TPU v7x, 32 devices: a whole 2x2x4 slice. The times are simulated.
32 devices in a mesh: seq: 4 (over y, core), fsdp: 8 (over z, x).
Axes of the slice: x: 2, y: 2, z: 4, core: 2. Of those that a mesh axis runs over, the one named last changes fastest.
Arguments:
- tokens: bfloat16 [2, 8, 1024, 1024], P(None, 'fsdp', 'seq'), may hold values from -6 to 6
- segment_ids: int32 [2, 8, 1024], P(None, 'fsdp'), may hold values from 0 to 8, never falling along the last dimension, each value on 1 to 512 neighbouring positions
- norm1_gain: bfloat16 [1024], P('fsdp'), may hold values from 0.5 to 1.5
- norm1_bias: bfloat16 [1024], P('fsdp'), may hold values from -3 to 3
- w_qkv: bfloat16 [1024, 3072], P('fsdp'), may hold values from -0.1875 to 0.1875
- w_out: bfloat16 [1024, 1024], P('fsdp'), may hold values from -1.5 to 1.5
- norm2_gain: bfloat16 [1024], P('fsdp'), may hold values from 0.5 to 1.5
- norm2_bias: bfloat16 [1024], P('fsdp'), may hold values from -3 to 3
- w_up: bfloat16 [1024, 4096], P('fsdp'), may hold values from -0.1875 to 0.1875
- w_down: bfloat16 [4096, 1024], P('fsdp'), may hold values from -0.125 to 0.125
- cotangent: bfloat16 [2, 8, 1024, 1024], P(None, 'fsdp', 'seq'), may hold values from -6 to 6
Outputs:
- output: bfloat16 [2, 8, 1024, 1024], P(None, 'fsdp', 'seq')
- grad_tokens: float32 [2, 8, 1024, 1024], P(None, 'fsdp', 'seq')
- grad_norm1_gain: float32 [1024], P('fsdp')
- grad_norm1_bias: float32 [1024], P('fsdp')
- grad_w_qkv: float32 [1024, 3072], P('fsdp')
- grad_w_out: float32 [1024, 1024], P('fsdp')
- grad_norm2_gain: float32 [1024], P('fsdp')
- grad_norm2_bias: float32 [1024], P('fsdp')
- grad_w_up: float32 [1024, 4096], P('fsdp')
- grad_w_down: float32 [4096, 1024], P('fsdp')
Inputs may be any that keep to these rules, and one draw needn't show every extreme that they name: `segment_ids`: in each sequence the ids start at 0 and rise by one at each new document; every document has 1 to 512 tokens, and in every sequence one has exactly 512.
All inputs are finite; a program needn't handle non-finite values.
Results may differ from a plain program's by a relative error of at most 0.018.
Values may be sent and summed in bfloat16 or wider, within the bound.
No kernel may reach another device: no remote copies, remote signals or barrier semaphores. Data moves between devices by JAX's collectives and lax.ppermute only.
A program may use at most 192 MiB of HBM per device.

v0:
```python
import math

import jax
import jax.numpy as jnp
from jax import lax
from jax.sharding import PartitionSpec as P

HEAD_DIM = 64
BLOCK = 512
BAND = 1


epsilon = 1e-05


def as_sent(value):

    def short(part):
        return part.astype(jnp.bfloat16) if part.dtype == jnp.float32 else part

    return jax.tree.map(short, value)


def normalize_rows(values, gain_row, bias_row):
    row_mean = jnp.mean(values, axis=-1, keepdims=True)
    centred = values - row_mean
    variance = jnp.mean(centred * centred, axis=-1, keepdims=True)
    inverse = lax.rsqrt(variance + epsilon)
    unit_rows = centred * inverse
    return (unit_rows * gain_row + bias_row, unit_rows, inverse)


def normalize_back(grad_rows, unit_rows, inverse, gain_row):
    grad_unit = grad_rows * gain_row
    mean_grad = jnp.mean(grad_unit, axis=-1, keepdims=True)
    mean_cross = jnp.mean(grad_unit * unit_rows, axis=-1, keepdims=True)
    return inverse * (grad_unit - mean_grad - unit_rows * mean_cross)


def smooth_gate(values):
    return jax.nn.gelu(values, approximate=False)


def contract_rows(left, right):
    return lax.dot_general(
        left, right, (((0,), (0,)), ((), ())), preferred_element_type=jnp.float32
    )


def contract_cols(left, right):
    return lax.dot_general(
        left, right, (((1,), (1,)), ((), ())), preferred_element_type=jnp.float32
    )


def split_heads(rows):
    return rows.reshape(rows.shape[0], -1, HEAD_DIM).transpose(1, 0, 2)


def merge_heads(per_head):
    return per_head.transpose(1, 0, 2).reshape(per_head.shape[1], -1)


def window_mask(block_index, segments_pad):
    padding = BAND * BLOCK
    window = (BAND + 1) * BLOCK
    row_start = block_index * BLOCK
    query_pos = row_start + jnp.arange(BLOCK, dtype=jnp.int32)
    key_pos = row_start - padding + jnp.arange(window, dtype=jnp.int32)
    query_seg = lax.dynamic_slice_in_dim(segments_pad, row_start + padding, BLOCK, 0)
    key_seg = lax.dynamic_slice_in_dim(segments_pad, row_start, window, 0)
    return (key_pos[None, :] <= query_pos[:, None]) & (key_seg[None, :] == query_seg[:, None])


def padded_inputs(key_heads, value_heads, segments):
    padding = BAND * BLOCK
    key_pad = jnp.pad(key_heads, ((0, 0), (padding, 0), (0, 0)))
    value_pad = jnp.pad(value_heads, ((0, 0), (padding, 0), (0, 0)))
    segments_pad = jnp.pad(segments, (padding, 0), constant_values=-1)
    return (key_pad, value_pad, segments_pad)


def attend_forward(query_heads, key_heads, value_heads, segments):
    head_count, length, head_width = query_heads.shape
    window = (BAND + 1) * BLOCK
    key_pad, value_pad, segments_pad = padded_inputs(key_heads, value_heads, segments)

    def one_block(block_index):
        row_start = block_index * BLOCK
        query_block = lax.dynamic_slice_in_dim(query_heads, row_start, BLOCK, 1)
        key_block = lax.dynamic_slice_in_dim(key_pad, row_start, window, 1)
        value_block = lax.dynamic_slice_in_dim(value_pad, row_start, window, 1)
        allowed = window_mask(block_index, segments_pad)
        scores = jnp.einsum(
            "hqd,hkd->hqk", query_block, key_block, preferred_element_type=jnp.float32
        )
        scores = jnp.where(allowed[None], scores, -1e30)
        row_top = jnp.max(scores, axis=-1, keepdims=True)
        exponent = jnp.exp(scores - row_top)
        row_total = jnp.sum(exponent, axis=-1, keepdims=True)
        probabilities = (exponent / row_total).astype(jnp.bfloat16)
        mixed_block = jnp.einsum(
            "hqk,hkd->hqd", probabilities, value_block, preferred_element_type=jnp.float32
        )
        return (mixed_block.astype(jnp.bfloat16), (row_top + jnp.log(row_total))[..., 0])

    indices = jnp.arange(length // BLOCK, dtype=jnp.int32)
    mixed_blocks, logsum = lax.map(one_block, indices)
    mixed_heads = mixed_blocks.transpose(1, 0, 2, 3).reshape(head_count, length, head_width)
    return (mixed_heads, logsum)


def attend_backward(query_heads, key_heads, value_heads, segments, logsum, grad_heads):
    head_count, length, head_width = query_heads.shape
    padding = BAND * BLOCK
    window = (BAND + 1) * BLOCK
    key_pad, value_pad, segments_pad = padded_inputs(key_heads, value_heads, segments)
    empty = jnp.zeros((head_count, length + padding, head_width), jnp.float32)

    def one_block(state_pair, inputs_pair):
        block_index, block_logsum = inputs_pair
        grad_keys, grad_values = state_pair
        row_start = block_index * BLOCK
        query_block = lax.dynamic_slice_in_dim(query_heads, row_start, BLOCK, 1)
        grad_block = lax.dynamic_slice_in_dim(grad_heads, row_start, BLOCK, 1)
        key_block = lax.dynamic_slice_in_dim(key_pad, row_start, window, 1)
        value_block = lax.dynamic_slice_in_dim(value_pad, row_start, window, 1)
        allowed = window_mask(block_index, segments_pad)
        scores = jnp.einsum(
            "hqd,hkd->hqk", query_block, key_block, preferred_element_type=jnp.float32
        )
        scores = jnp.where(allowed[None], scores, -1e30)
        probabilities = jnp.exp(scores - block_logsum[..., None])
        grad_probs = jnp.einsum(
            "hqd,hkd->hqk", grad_block, value_block, preferred_element_type=jnp.float32
        )
        inner_sum = jnp.sum(probabilities * grad_probs, axis=-1, keepdims=True)
        grad_scores = (probabilities * (grad_probs - inner_sum)).astype(jnp.bfloat16)
        grad_query = jnp.einsum(
            "hqk,hkd->hqd", grad_scores, key_block, preferred_element_type=jnp.float32
        )
        key_part = jnp.einsum(
            "hqk,hqd->hkd", grad_scores, query_block, preferred_element_type=jnp.float32
        )
        value_part = jnp.einsum(
            "hqk,hqd->hkd",
            probabilities.astype(jnp.bfloat16),
            grad_block,
            preferred_element_type=jnp.float32,
        )
        grad_keys = lax.dynamic_update_slice_in_dim(
            grad_keys,
            lax.dynamic_slice_in_dim(grad_keys, row_start, window, 1) + key_part,
            row_start,
            1,
        )
        grad_values = lax.dynamic_update_slice_in_dim(
            grad_values,
            lax.dynamic_slice_in_dim(grad_values, row_start, window, 1) + value_part,
            row_start,
            1,
        )
        return ((grad_keys, grad_values), grad_query.astype(jnp.bfloat16))

    indices = jnp.arange(length // BLOCK, dtype=jnp.int32)
    (grad_keys, grad_values), query_blocks = lax.scan(one_block, (empty, empty), (indices, logsum))
    grad_queries = query_blocks.transpose(1, 0, 2, 3).reshape(head_count, length, head_width)
    return (
        grad_queries,
        grad_keys[:, padding:].astype(jnp.bfloat16),
        grad_values[:, padding:].astype(jnp.bfloat16),
    )


def add_pairs(first_terms, second_terms):
    return tuple((left + right for left, right in zip(first_terms, second_terms)))


def owner_share(terms):
    return jax.tree.map(
        lambda part: part.astype(jnp.float32),
        lax.psum_scatter(as_sent(terms), "fsdp", scatter_dimension=0, tiled=True),
    )


def owner_finish(shares):
    return jax.tree.map(lambda part: part.astype(jnp.float32), lax.psum(as_sent(shares), "seq"))


def body(
    tokens,
    segment_ids,
    norm1_gain,
    norm1_bias,
    w_qkv,
    w_out,
    norm2_gain,
    norm2_bias,
    w_up,
    w_down,
    cotangent,
):
    model_width = w_qkv.shape[1] // 3
    score_scale = 1.0 / math.sqrt(HEAD_DIM)
    outputs = []
    input_grads = []
    local_sums = None
    owner_sums = None
    for micro_index in range(tokens.shape[0]):
        gathered = (
            lax.all_gather(norm1_gain, "fsdp", axis=0, tiled=True),
            lax.all_gather(norm1_bias, "fsdp", axis=0, tiled=True),
            lax.all_gather(w_qkv, "fsdp", axis=0, tiled=True),
            lax.all_gather(w_out, "fsdp", axis=0, tiled=True),
            lax.all_gather(norm2_gain, "fsdp", axis=0, tiled=True),
            lax.all_gather(norm2_bias, "fsdp", axis=0, tiled=True),
            lax.all_gather(w_up, "fsdp", axis=0, tiled=True),
            lax.all_gather(w_down, "fsdp", axis=0, tiled=True),
        )
        (
            gain_one,
            bias_one,
            joint_weight,
            output_weight,
            gain_two,
            bias_two,
            upward_weight,
            downward_weight,
        ) = gathered
        inputs = tokens[micro_index, 0].astype(jnp.float32)
        segments = segment_ids[micro_index, 0]
        normed, unit_one, inverse_one = normalize_rows(
            inputs, gain_one.astype(jnp.float32), bias_one.astype(jnp.float32)
        )
        normed_low = normed.astype(jnp.bfloat16)
        projected = jnp.dot(normed_low, joint_weight, preferred_element_type=jnp.float32)
        queries = (projected[:, :model_width] * score_scale).astype(jnp.bfloat16)
        key_rows = projected[:, model_width : 2 * model_width].astype(jnp.bfloat16)
        value_rows = projected[:, 2 * model_width :].astype(jnp.bfloat16)
        head_queries, head_keys, head_values = (
            lax.all_to_all(queries, "seq", split_axis=1, concat_axis=0, tiled=True),
            lax.all_to_all(key_rows, "seq", split_axis=1, concat_axis=0, tiled=True),
            lax.all_to_all(value_rows, "seq", split_axis=1, concat_axis=0, tiled=True),
        )
        query_heads = split_heads(head_queries)
        key_heads = split_heads(head_keys)
        value_heads = split_heads(head_values)
        mixed_heads, logsum = attend_forward(query_heads, key_heads, value_heads, segments)
        attended = lax.all_to_all(
            merge_heads(mixed_heads), "seq", split_axis=0, concat_axis=1, tiled=True
        )
        middle = inputs + jnp.dot(attended, output_weight, preferred_element_type=jnp.float32)
        normed_two, unit_two, inverse_two = normalize_rows(
            middle, gain_two.astype(jnp.float32), bias_two.astype(jnp.float32)
        )
        normed_two_low = normed_two.astype(jnp.bfloat16)
        pre_act = jnp.dot(normed_two_low, upward_weight, preferred_element_type=jnp.float32)
        activated, gate_pullback = jax.vjp(smooth_gate, pre_act)
        hidden = activated.astype(jnp.bfloat16)
        result = middle + jnp.dot(hidden, downward_weight, preferred_element_type=jnp.float32)
        outputs.append(result.astype(jnp.bfloat16))
        gathered = (
            lax.all_gather(norm1_gain, "fsdp", axis=0, tiled=True),
            lax.all_gather(norm1_bias, "fsdp", axis=0, tiled=True),
            lax.all_gather(w_qkv, "fsdp", axis=0, tiled=True),
            lax.all_gather(w_out, "fsdp", axis=0, tiled=True),
            lax.all_gather(norm2_gain, "fsdp", axis=0, tiled=True),
            lax.all_gather(norm2_bias, "fsdp", axis=0, tiled=True),
            lax.all_gather(w_up, "fsdp", axis=0, tiled=True),
            lax.all_gather(w_down, "fsdp", axis=0, tiled=True),
        )
        (
            gain_one,
            bias_one,
            joint_weight,
            output_weight,
            gain_two,
            bias_two,
            upward_weight,
            downward_weight,
        ) = gathered
        grad_result = cotangent[micro_index, 0]
        grad_down = contract_rows(hidden, grad_result)
        grad_hidden = contract_cols(grad_result, downward_weight)
        grad_pre = gate_pullback(grad_hidden)[0].astype(jnp.bfloat16)
        grad_up = contract_rows(normed_two_low, grad_pre)
        grad_normed_two = contract_cols(grad_pre, upward_weight)
        grad_gain_two = jnp.sum(grad_normed_two * unit_two, axis=0)
        grad_bias_two = jnp.sum(grad_normed_two, axis=0)
        grad_middle = grad_result.astype(jnp.float32) + normalize_back(
            grad_normed_two, unit_two, inverse_two, gain_two.astype(jnp.float32)
        )
        grad_branch = grad_middle.astype(jnp.bfloat16)
        grad_output_weight = contract_rows(attended, grad_branch)
        grad_attended = contract_cols(grad_branch, output_weight).astype(jnp.bfloat16)
        grad_heads = lax.all_to_all(grad_attended, "seq", split_axis=1, concat_axis=0, tiled=True)
        grad_query_heads, grad_key_heads, grad_value_heads = attend_backward(
            query_heads, key_heads, value_heads, segments, logsum, split_heads(grad_heads)
        )
        grad_queries, grad_keys, grad_values = (
            lax.all_to_all(
                merge_heads(grad_query_heads), "seq", split_axis=0, concat_axis=1, tiled=True
            ),
            lax.all_to_all(
                merge_heads(grad_key_heads), "seq", split_axis=0, concat_axis=1, tiled=True
            ),
            lax.all_to_all(
                merge_heads(grad_value_heads), "seq", split_axis=0, concat_axis=1, tiled=True
            ),
        )
        grad_projected = jnp.concatenate(
            [grad_queries * jnp.bfloat16(score_scale), grad_keys, grad_values], axis=1
        )
        grad_joint = contract_rows(normed_low, grad_projected)
        grad_normed = contract_cols(grad_projected, joint_weight)
        grad_gain_one = jnp.sum(grad_normed * unit_one, axis=0)
        grad_bias_one = jnp.sum(grad_normed, axis=0)
        grad_inputs = grad_middle + normalize_back(
            grad_normed, unit_one, inverse_one, gain_one.astype(jnp.float32)
        )
        input_grads.append(grad_inputs)
        grad_terms = (
            grad_gain_one,
            grad_bias_one,
            grad_joint,
            grad_output_weight,
            grad_gain_two,
            grad_bias_two,
            grad_up,
            grad_down,
        )
        local_sums = grad_terms if micro_index == 0 else add_pairs(local_sums, grad_terms)
    owner_sums = owner_share(local_sums)
    replicas = owner_finish(owner_sums)
    output = jnp.stack(outputs)[:, None]
    grad_tokens = jnp.stack(input_grads)[:, None]
    return (
        output,
        grad_tokens,
        replicas[0],
        replicas[1],
        replicas[2],
        replicas[3],
        replicas[4],
        replicas[5],
        replicas[6],
        replicas[7],
    )


def solution(mesh):
    return jax.shard_map(
        body,
        mesh=mesh,
        in_specs=(
            P(None, "fsdp", "seq", None),
            P(None, "fsdp", None),
            P("fsdp"),
            P("fsdp"),
            P("fsdp", None),
            P("fsdp", None),
            P("fsdp"),
            P("fsdp"),
            P("fsdp", None),
            P("fsdp", None),
            P(None, "fsdp", "seq", None),
        ),
        out_specs=(
            P(None, "fsdp", "seq", None),
            P(None, "fsdp", "seq", None),
            P("fsdp"),
            P("fsdp"),
            P("fsdp", None),
            P("fsdp", None),
            P("fsdp"),
            P("fsdp"),
            P("fsdp", None),
            P("fsdp", None),
        ),
        check_vma=False,
    )
```

profile of v0, /device:TPU:9, one launch (start us, length us, event | category | flops | bytes accessed | tf_op | source)
XLA Modules:
  0.0 1150.3 jit_solution(17831492155937469078)
XLA Ops:
  9.4 14.8 %all-gather.1 = bf16[8,1,128]{2,1,0:T(2,128)(2,1)S(1)} all-gather(bf16[1,1,128]{2,1,0:T(2,128)(2,1)} %bitcast.416), channel_id=1, replica_groups=mesh['seq'=4,'fsdp'=8] {'fsdp'}, dimensions={0}, use_global_device_ids=true | all-gather | bytes 2304 | tf_op jit(solution)/shard_map/all_gather | solution.py:212
  24.2 13.4 %all-gather = bf16[8,1,128]{2,1,0:T(2,128)(2,1)S(1)} all-gather(bf16[1,1,128]{2,1,0:T(2,128)(2,1)} %bitcast.417), channel_id=1, replica_groups=mesh['seq'=4,'fsdp'=8] {'fsdp'}, dimensions={0}, use_global_device_ids=true | all-gather | bytes 2304 | tf_op jit(solution)/shard_map/all_gather | solution.py:211
  40.7 67.5 %all-gather.9.cloned.1.call-done = bf16[1024,3072]{1,0:T(8,128)(2,1)} async-done(((bf16[128,3072]{1,0:T(8,128)(2,1)}), bf16[1024,3072]{1,0:T(8,128)(2,1)}) %all-gather.9.cloned.1.call-update) | async-done | bytes 6291472 | tf_op jit(solution)/shard_map/all_gather | solution.py:213
  108.2 5.8 fusion.179
  115.0 5.0 all-to-all-start.4
  122.0 6.0 all-to-all-done.4
  128.0 4.2 all-to-all-start.5
  133.1 7.2 all-to-all-done.5
  140.3 4.2 all-to-all-start.6
  144.5 5.9 fusion.181
  152.5 4.3 all-to-all-start
  158.9 5.9 all-to-all-done
  164.8 5.0 all-to-all-start.1
  170.3 13.6 %all-gather.3 = bf16[8,1,128]{2,1,0:T(2,128)(2,1)S(1)} all-gather(bf16[1,1,128]{2,1,0:T(2,128)(2,1)S(1)} %bitcast.418), channel_id=1, replica_groups=mesh['seq'=4,'fsdp'=8] {'fsdp'}, dimensions={0}, use_global_device_ids=true | all-gather | bytes 2304 | tf_op jit(solution)/shard_map/all_gather | solution.py:216
  184.5 13.6 %all-gather.2 = bf16[8,1,128]{2,1,0:T(2,128)(2,1)S(1)} all-gather(bf16[1,1,128]{2,1,0:T(2,128)(2,1)S(1)} %bitcast.419), channel_id=1, replica_groups=mesh['seq'=4,'fsdp'=8] {'fsdp'}, dimensions={0}, use_global_device_ids=true | all-gather | bytes 2304 | tf_op jit(solution)/shard_map/all_gather | solution.py:215
  201.7 10.9 all-to-all-start.2
  213.4 17.8 %while.61 = (s32[]{:T(128)}, bf16[2,4,512,64]{2,3,1,0:T(8,128)(2,1)}, f32[2,4,512]{2,1,0:T(4,128)S(1)}, s32[2]{0:T(128)S(1)}, s32[1536]{0:T(1024)S(1)}, /*index=...) while((s32[]{:T(128)}, ...), condition=%wide.region_13.14_spmd, body=%wide.region_10.13_spmd.sunk | while | flops 557448704 | bytes 33126788 | solution.py:108
  245.9 20.7 %while.60 = (s32[]{:T(128)}, bf16[2,4,512,64]{2,3,1,0:T(8,128)(2,1)}, f32[2,4,512]{2,1,0:T(4,128)}, s32[2]{0:T(128)S(1)}, s32[1536]{0:T(1024)S(1)}, /*index=5*/b...) while((s32[]{:T(128)}, ...), condition=%wide.region_5.6_spmd, body=%wide.region_2.5_spmd.sunk | while | flops 557448704 | bytes 28932428 | solution.py:108
  251.6 4.1 fusion.248
  261.9 4.1 fusion.248
  272.1 3.7 all-to-all-start.3
  279.6 4.2 all-to-all-done.3
  286.8 16.2 %multiply_convert_fusion.2 = (bf16[256,4096]{1,0:T(8,128)(2,1)}, f32[256,4096]{1,0:T(8,128)}, f32[256,4096]{1,0:T(8,128)}) fusion(bf16[1024,4096]{1,0:T(8,128)(2,1)} %all-gather.13.cloned.1.call-done, f32[256,1024]{1,0:T(8,128)} %copy-done.24, f32[256]{0:T(256)S(1)} %add_rsqrt_fusion, f32[256]{0:T(256)S(1)} %broadcast_multiply_fusion.10, ...), kind=kOutput, calls=%fused_computation.116 | convolution fusion | flops 2216951808 | bytes 19933184 | tf_op jit(solution)/shard_map/dot_general | solution.py:257
  303.1 16.2 %multiply_convert_fusion.3 = (bf16[256,4096]{1,0:T(8,128)(2,1)}, f32[256,4096]{1,0:T(8,128)}, f32[256,4096]{1,0:T(8,128)}) fusion(bf16[1024,4096]{1,0:T(8,128)(2,1)S(1)} %copy-done.99, f32[256,1024]{1,0:T(8,128)S(1)} %get-tuple-element.700, f32[1024]{0:T(1024)S(1)} %bitcast.411, f32[1024]{0:T(1024)S(1)} %bitcast.405, f32[256]{0:T(256)S(1)} %add_rsqrt_fusion.2, ...), kind=kOutput, calls=%fused_computation.129 | convolution fusion | flops 2216951808 | bytes 19933184 | tf_op jit(solution)/shard_map/dot_general | solution.py:257
  319.2 89.4 %all-gather.15.cloned.1.call-done = bf16[4096,1024]{1,0:T(8,128)(2,1)} async-done(((bf16[512,1024]{1,0:T(8,128)(2,1)}), bf16[4096,1024]{1,0:T(8,128)(2,1)}) %all-gather.15.cloned.1.call-update) | async-done | bytes 8388624 | tf_op jit(solution)/shard_map/all_gather | solution.py:218
  408.6 11.4 add_convert_fusion.4
  420.1 6.8 fusion.183
  426.9 6.2 add_convert_fusion.5
  433.2 8.0 multiply_reduce_fusion.3
  446.0 5.6 all-to-all-start.12
  459.7 5.0 all-to-all-start.8
  468.7 41.4 %while.63 = (s32[]{:T(128)}, f32[4,1536,64]{1,2,0:T(8,128)S(1)}, f32[4,1536,64]{1,2,0:T(8,128)}, bf16[2,4,512,64]{2,3,1,0:T(8,128)(2,1)}, s32[2]{0:T(128)S(1)}, ...) while((s32[]{:T(128)}, f32[4,1536,64]{1,2,0:T(8,128)S(1)}, ...), condition=%wide.region_27.28_spmd, body=%wide.region_25.27_spmd.sunk | while | flops 1369570816 | bytes 114121240 | solution.py:166
  470.0 4.7 fusion.272
  475.3 5.7 multiply_reduce_fusion.15
  490.7 4.7 fusion.272
  496.0 5.7 multiply_reduce_fusion.15
  517.0 4.1 all-to-all-start.15
  521.4 4.2 add_convert_fusion.3
  529.8 4.4 all-to-all-start.13
  536.6 43.1 %while.62 = (s32[]{:T(128)}, f32[4,1536,64]{1,2,0:T(8,128)S(1)}, f32[4,1536,64]{1,2,0:T(8,128)}, bf16[2,4,512,64]{2,3,1,0:T(8,128)(2,1)}, s32[2]{0:T(128)S(1)}, ...) while((s32[]{:T(128)}, f32[4,1536,64]{1,2,0:T(8,128)S(1)}, ...), condition=%wide.region_20.21_spmd, body=%wide.region_18.20_spmd.sunk | while | flops 1369570816 | bytes 114121240 | solution.py:166
  537.8 4.7 fusion.260
  543.9 5.8 multiply_reduce_fusion.14
  559.5 4.7 fusion.260
  565.5 5.8 multiply_reduce_fusion.14
  587.2 6.7 all-to-all-done.11
  593.9 5.0 all-to-all-start.9
  602.1 4.8 all-to-all-done.9
  606.9 4.7 all-to-all-start.10
  615.3 4.3 all-to-all-done.10
  619.6 4.3 all-to-all-start.14
  624.0 6.7 fusion.135
  632.7 9.5 add_convert_fusion.2
  643.5 10.4 fusion.171
  653.9 11.7 %add_convert_fusion.1 = bf16[1024,4096]{1,0:T(8,128)(2,1)} fusion(f32[1024,4096]{1,0:T(8,128)} %fusion.171, bf16[256,4096]{1,0:T(8,128)(2,1)S(1)} %copy-done.57, f32[256,1024]{1,0:T(8,128)S(1)} %copy-done.26, f32[256]{0:T(256)S(1)} %copy-done.90, f32[256]{0:T(256)S(1)} %copy-done.88, f32[1024]{0:T(1024)S(1)} %bitcast.413, f32[1024]{0:T(1024)S(1)} %bitcast.409), kind=kOutput, calls=%fused_computation.107 | convolution fusion | flops 2157182976 | bytes 28321792 | tf_op jit(solution)/shard_map/dot_general | solution.py:45
  665.9 10.3 fusion.146
  676.2 11.8 %add_convert_fusion = bf16[4096,1024]{1,0:T(8,128)(2,1)} fusion(f32[4096,1024]{1,0:T(8,128)} %fusion.146, bf16[256,4096]{1,0:T(8,128)(2,1)S(1)} %copy-done.28, bf16[2,1,256,1024]{3,2,1,0:T(8,128)(2,1)S(1)} %copy-done.35), kind=kOutput, calls=%fused_computation.106 | convolution fusion | flops 2155872256 | bytes 27787264 | tf_op jit(solution)/shard_map/dot_general | solution.py:45
  689.9 6.6 fusion.112
  696.6 6.1 fusion.113
  710.4 49.0 %reduce-scatter.5.cloned.1.call-done = bf16[128,3072]{1,0:T(8,128)(2,1)} async-done(((bf16[1024,3072]{1,0:T(8,128)(2,1)}), bf16[128,3072]{1,0:T(8,128)(2,1)}) %reduce-scatter.5.cloned.1.call-update) | async-done | bytes 786448 | tf_op jit(solution)/shard_map/reduce_scatter | solution.py:182
  759.4 151.2 %reduce-scatter.9.cloned.1.call-done = bf16[128,4096]{1,0:T(8,128)(2,1)} async-done(((bf16[1024,4096]{1,0:T(8,128)(2,1)}), bf16[128,4096]{1,0:T(8,128)(2,1)}) %reduce-scatter.9.cloned.1.call-update) | async-done | bytes 1048592 | tf_op jit(solution)/shard_map/reduce_scatter | solution.py:182
  910.6 152.1 %reduce-scatter.11.cloned.1.call-done = bf16[512,1024]{1,0:T(8,128)(2,1)} async-done(((bf16[4096,1024]{1,0:T(8,128)(2,1)}), bf16[512,1024]{1,0:T(8,128)(2,1)}) %reduce-scatter.11.cloned.1.call-update) | async-done | bytes 1048592 | tf_op jit(solution)/shard_map/reduce_scatter | solution.py:182
  1062.8 15.4 %all-reduce.10 = (bf16[1024]{0:T(1024)(128)(2,1)S(1)}, bf16[1024]{0:T(1024)(128)(2,1)S(1)}, bf16[1024]{0:T(1024)(128)(2,1)S(1)}, bf16[1024]{0:T(1024)(128)(2,1)S(1)}) all-reduce(bf16[1024]{0:T(1024)(128)(2,1)S(1)} %add_convert_fusion.11, ...), channel_id=2, replica_groups=mesh['seq'=4,'fsdp'=8] {'fsdp'}, use_global_device_ids=true, to_apply=%region_32.33.clone | all-reduce | flops 4096 | bytes 16384
  1078.5 9.0 all-reduce.11
  1093.4 41.5 %all-reduce.15.cloned.1.call-done = (bf16[128,3072]{1,0:T(8,128)(2,1)}, bf16[128,1024]{1,0:T(8,128)(2,1)}, bf16[128,4096]{1,0:T(8,128)(2,1)}, bf16[512,1024]{1,0:T(8,128)(2,1)}) async-done(((bf16[128,3072]{1,0:T(8,128)(2,1)}, bf16[128,1024]{1,0:T(8,128)(2,1)}, bf16[128,4096]{1,0:T(8,128)(2,1)}, bf16[512,1024]{1,0:T(8,128)(2,1)}), (bf16[128,3072]{1,0:T(8,128)(2,1)}, bf16[128,1024]{1,0:T(8,128)(2,1)}, ...) | async-done | bytes 3145744 | tf_op jit(solution)/shard_map/psum | solution.py:187
  (487 shorter events, 184.8 us)
Async XLA Ops:
  7.2 101.0 %copy-start.14 = (bf16[2,1,256,1024]{3,2,1,0:T(8,128)(2,1)S(1)}, bf16[2,1,256,1024]{3,2,1,0:T(8,128)(2,1)}, u32[]{:S(2)}) copy-start(bf16[2,1,256,1024]{3,2,1,0:T(8,128)(2,1)} %param.19) | copy-start | bytes 3145732
  7.2 101.0 %all-gather.9.cloned.1.call-start = ((), (), s32[]{:S(2)}) async-start(), calls=%async_computation.20 | async-start | bytes 7077888 | tf_op jit(solution)/shard_map/all_gather | solution.py:213
  7.9 267.8 %all-gather.11.cloned.1.call-start = ((), (), s32[]{:S(2)}) async-start(), calls=%async_computation.21 | async-start | bytes 2359296 | tf_op jit(solution)/shard_map/all_gather | solution.py:214
  8.7 278.1 %all-gather.13.cloned.1.call-start = ((), (), s32[]{:S(2)}) async-start(), calls=%async_computation.22 | async-start | bytes 9437184 | tf_op jit(solution)/shard_map/all_gather | solution.py:217
  24.2 120.3 %copy-start.67 = (f32[8,1,128]{2,1,0:T(1,128)}, f32[8,1,128]{2,1,0:T(1,128)S(1)}, u32[]{:S(2)}) copy-start(f32[8,1,128]{2,1,0:T(1,128)S(1)} %convert_element_type.270) | copy-start | bytes 12292
  37.6 106.9 %copy-start.65 = (f32[8,1,128]{2,1,0:T(1,128)}, f32[8,1,128]{2,1,0:T(1,128)S(1)}, u32[]{:S(2)}) copy-start(f32[8,1,128]{2,1,0:T(1,128)S(1)} %convert_element_type.269) | copy-start | bytes 12292
  39.0 75.0 %copy-start.79 = (f32[256]{0:T(256)}, f32[256]{0:T(256)S(1)}, u32[]{:S(2)}) copy-start(f32[256]{0:T(256)S(1)} %get-tuple-element.704) | copy-start | bytes 3076
  39.0 105.5 %copy-start.77 = (f32[256]{0:T(256)}, f32[256]{0:T(256)S(1)}, u32[]{:S(2)}) copy-start(f32[256]{0:T(256)S(1)} %get-tuple-element.705) | copy-start | bytes 3076
  40.7 73.4 %copy-start.85 = (f32[256]{0:T(256)}, f32[256]{0:T(256)S(1)}, u32[]{:S(2)}) copy-start(f32[256]{0:T(256)S(1)} %add_rsqrt_fusion.1) | copy-start | bytes 3076
  115.0 13.1 %all-to-all-start.4 = ((bf16[256,4,256]{2,0,1:T(8,128)(2,1)}), bf16[256,4,256]{2,0,1:T(8,128)(2,1)S(1)}, u32[]{:S(2)}, u32[]{:S(2)}) async-start(bf16[256,4,256]{2,0,1:T(8,128)(2,1)} %bitcast.311), calls=%async_computation.4 | async-start | bytes 1048576 | tf_op jit(solution)/shard_map/all_to_all | solution.py:241
  128.0 12.3 %all-to-all-start.5 = ((bf16[256,4,256]{2,0,1:T(8,128)(2,1)}), bf16[256,4,256]{2,0,1:T(8,128)(2,1)S(1)}, u32[]{:S(2)}, u32[]{:S(2)}) async-start(bf16[256,4,256]{2,0,1:T(8,128)(2,1)} %bitcast.310), calls=%async_computation.5 | async-start | bytes 1048576 | tf_op jit(solution)/shard_map/all_to_all | solution.py:242
  132.2 18.2 %copy-start.81 = (f32[256]{0:T(256)}, f32[256]{0:T(256)S(1)}, u32[]{:S(2)}) copy-start(f32[256]{0:T(256)S(1)} %add_rsqrt_fusion.3) | copy-start | bytes 3076
  140.3 12.2 %all-to-all-start.6 = ((bf16[256,4,256]{2,0,1:T(8,128)(2,1)}), bf16[256,4,256]{2,0,1:T(8,128)(2,1)S(1)}, u32[]{:S(2)}, u32[]{:S(2)}) async-start(bf16[256,4,256]{2,0,1:T(8,128)(2,1)} %bitcast.309), calls=%async_computation.6 | async-start | bytes 1048576 | tf_op jit(solution)/shard_map/all_to_all | solution.py:243
  150.4 19.9 %copy-start.96 = (bf16[128]{0:T(256)(128)(2,1)S(1)}, bf16[128]{0:T(256)(128)(2,1)}, u32[]{:S(2)}) copy-start(bf16[128]{0:T(256)(128)(2,1)} %param.26) | copy-start | bytes 772
  150.4 34.1 %copy-start.97 = (bf16[128]{0:T(256)(128)(2,1)S(1)}, bf16[128]{0:T(256)(128)(2,1)}, u32[]{:S(2)}) copy-start(bf16[128]{0:T(256)(128)(2,1)} %param.25) | copy-start | bytes 772
  150.4 48.3 %copy-start.91 = (s32[2,1,1024]{2,1,0:T(1,128)S(1)}, s32[2,1,1024]{2,1,0:T(1,128)}, u32[]{:S(2)}) copy-start(s32[2,1,1024]{2,1,0:T(1,128)} %param.20) | copy-start | bytes 24580
  152.5 12.3 %all-to-all-start = ((bf16[256,4,256]{2,0,1:T(8,128)(2,1)}), bf16[256,4,256]{2,0,1:T(8,128)(2,1)S(1)}, u32[]{:S(2)}, u32[]{:S(2)}) async-start(bf16[256,4,256]{2,0,1:T(8,128)(2,1)} %bitcast.314), calls=%async_computation | async-start | bytes 1048576 | tf_op jit(solution)/shard_map/all_to_all | solution.py:241
  164.8 35.4 %copy-start.47 = (bf16[256,4,256]{2,0,1:T(8,128)(2,1)}, bf16[256,4,256]{2,0,1:T(8,128)(2,1)S(1)}, u32[]{:S(2)}) copy-start(bf16[256,4,256]{2,0,1:T(8,128)(2,1)S(1)} %all-to-all-done) | copy-start | bytes 1572868
  164.8 36.9 %all-to-all-start.1 = ((bf16[256,4,256]{2,0,1:T(8,128)(2,1)}), bf16[256,4,256]{2,0,1:T(8,128)(2,1)}, u32[]{:S(2)}, u32[]{:S(2)}) async-start(bf16[256,4,256]{2,0,1:T(8,128)(2,1)} %bitcast.313), calls=%async_computation.1 | async-start | bytes 1048576 | tf_op jit(solution)/shard_map/all_to_all | solution.py:242
  169.7 238.9 %all-gather.15.cloned.1.call-start = ((), (), s32[]{:S(2)}) async-start(), calls=%async_computation.23 | async-start | bytes 9437184 | tf_op jit(solution)/shard_map/all_gather | solution.py:218
  201.7 36.5 %all-to-all-start.2 = ((bf16[256,4,256]{2,0,1:T(8,128)(2,1)}), bf16[256,4,256]{2,0,1:T(8,128)(2,1)}, u32[]{:S(2)}, u32[]{:S(2)}) async-start(bf16[256,4,256]{2,0,1:T(8,128)(2,1)} %bitcast.378), calls=%async_computation.2 | async-start | bytes 1048576 | tf_op jit(solution)/shard_map/all_to_all | solution.py:243
  213.4 22.4 %copy-start.48 = (bf16[256,4,256]{2,0,1:T(8,128)(2,1)S(1)}, bf16[256,4,256]{2,0,1:T(8,128)(2,1)}, u32[]{:S(2)}) copy-start(bf16[256,4,256]{2,0,1:T(8,128)(2,1)} %copy-done.47) | copy-start | bytes 1572868
  238.3 33.0 %all-to-all-start.7 = ((bf16[4,256,256]{1,2,0:T(8,128)(2,1)}), bf16[4,256,256]{1,2,0:T(8,128)(2,1)S(1)}, u32[]{:S(2)}, u32[]{:S(2)}) async-start(bf16[4,256,256]{1,2,0:T(8,128)(2,1)} %copy.116), calls=%async_computation.7 | async-start | bytes 1048576 | tf_op jit(solution)/shard_map/all_to_all | solution.py:249
  266.6 11.7 %copy-start = (bf16[4,1536,64]{1,2,0:T(8,128)(2,1)}, bf16[4,1536,64]{1,2,0:T(8,128)(2,1)S(1)}, u32[]{:S(2)}) copy-start(bf16[4,1536,64]{1,2,0:T(8,128)(2,1)S(1)} %get-tuple-element.1180) | copy-start | bytes 2359300
  266.6 11.8 %copy-start.4 = (bf16[4,1024,64]{1,2,0:T(8,128)(2,1)}, bf16[4,1024,64]{1,2,0:T(8,128)(2,1)S(1)}, u32[]{:S(2)}) copy-start(bf16[4,1024,64]{1,2,0:T(8,128)(2,1)S(1)} %get-tuple-element.1186) | copy-start | bytes 1572868
  266.6 11.8 %copy-start.61 = (s32[1536]{0:T(1024)}, s32[1536]{0:T(1024)S(1)}, u32[]{:S(2)}) copy-start(s32[1536]{0:T(1024)S(1)} %get-tuple-element.1230) | copy-start | bytes 18436
  272.1 11.7 %all-to-all-start.3 = ((bf16[4,256,256]{1,2,0:T(8,128)(2,1)}), bf16[4,256,256]{1,2,0:T(8,128)(2,1)S(1)}, u32[]{:S(2)}, u32[]{:S(2)}) async-start(bf16[4,256,256]{1,2,0:T(8,128)(2,1)} %copy.108), calls=%async_computation.3 | async-start | bytes 1048576 | tf_op jit(solution)/shard_map/all_to_all | solution.py:249
  278.4 162.8 %copy-start.87 = (f32[256]{0:T(256)}, f32[256]{0:T(256)S(1)}, u32[]{:S(2)}) copy-start(f32[256]{0:T(256)S(1)} %broadcast_multiply_fusion.10) | copy-start | bytes 3076
  283.8 19.2 %copy-start.29 = (bf16[4,256,256]{1,2,0:T(8,128)(2,1)}, bf16[4,256,256]{1,2,0:T(8,128)(2,1)S(1)}, u32[]{:S(2)}) copy-start(bf16[4,256,256]{1,2,0:T(8,128)(2,1)S(1)} %all-to-all-done.3) | copy-start | bytes 1572868
  286.4 146.7 %copy-start.17 = (f32[256,1024]{1,0:T(8,128)}, f32[256,1024]{1,0:T(8,128)S(1)}, u32[]{:S(2)}) copy-start(f32[256,1024]{1,0:T(8,128)S(1)} %get-tuple-element.700) | copy-start | bytes 3145732
  286.4 154.8 %copy-start.75 = (f32[256]{0:T(256)}, f32[256]{0:T(256)S(1)}, u32[]{:S(2)}) copy-start(f32[256]{0:T(256)S(1)} %broadcast_multiply_fusion.12) | copy-start | bytes 3076
  286.7 154.6 %copy-start.89 = (f32[256]{0:T(256)}, f32[256]{0:T(256)S(1)}, u32[]{:S(2)}) copy-start(f32[256]{0:T(256)S(1)} %add_rsqrt_fusion) | copy-start | bytes 3076
  286.7 154.5 %copy-start.83 = (f32[256]{0:T(256)}, f32[256]{0:T(256)S(1)}, u32[]{:S(2)}) copy-start(f32[256]{0:T(256)S(1)} %add_rsqrt_fusion.2) | copy-start | bytes 3076
  286.8 16.2 %copy-start.99 = (bf16[1024,4096]{1,0:T(8,128)(2,1)S(1)}, bf16[1024,4096]{1,0:T(8,128)(2,1)}, u32[]{:S(2)}) copy-start(bf16[1024,4096]{1,0:T(8,128)(2,1)} %all-gather.13.cloned.1.call-done) | copy-start | bytes 25165828
  303.0 105.6 %copy-start.33 = (bf16[2,1,256,1024]{3,2,1,0:T(8,128)(2,1)S(1)}, bf16[2,1,256,1024]{3,2,1,0:T(8,128)(2,1)}, u32[]{:S(2)}) copy-start(bf16[2,1,256,1024]{3,2,1,0:T(8,128)(2,1)} %param.29) | copy-start | bytes 3145732
  446.0 13.6 %all-to-all-start.12 = ((bf16[256,4,256]{2,0,1:T(8,128)(2,1)}), bf16[256,4,256]{2,0,1:T(8,128)(2,1)}, u32[]{:S(2)}, u32[]{:S(2)}) async-start(bf16[256,4,256]{2,0,1:T(8,128)(2,1)} %bitcast.382), calls=%async_computation.12 | async-start | bytes 1048576 | tf_op jit(solution)/shard_map/all_to_all | solution.py:296
  456.1 12.6 %copy-start.3 = (bf16[4,1536,64]{1,2,0:T(8,128)(2,1)S(1)}, bf16[4,1536,64]{1,2,0:T(8,128)(2,1)}, u32[]{:S(2)}) copy-start(bf16[4,1536,64]{1,2,0:T(8,128)(2,1)} %copy-done.2) | copy-start | bytes 2359300
  456.1 12.6 %copy-start.7 = (bf16[4,1024,64]{1,2,0:T(8,128)(2,1)S(1)}, bf16[4,1024,64]{1,2,0:T(8,128)(2,1)}, u32[]{:S(2)}) copy-start(bf16[4,1024,64]{1,2,0:T(8,128)(2,1)} %copy-done.6) | copy-start | bytes 1572868
  456.1 12.6 %copy-start.64 = (s32[1536]{0:T(1024)S(1)}, s32[1536]{0:T(1024)}, u32[]{:S(2)}) copy-start(s32[1536]{0:T(1024)} %copy-done.63) | copy-start | bytes 18436
  456.1 12.6 %copy-start.74 = (f32[2,4,512]{2,1,0:T(4,128)S(1)}, f32[2,4,512]{2,1,0:T(4,128)}, u32[]{:S(2)}) copy-start(f32[2,4,512]{2,1,0:T(4,128)} %copy-done.73) | copy-start | bytes 49156
  459.7 57.3 %all-to-all-start.8 = ((bf16[256,4,256]{2,0,1:T(8,128)(2,1)}), bf16[256,4,256]{2,0,1:T(8,128)(2,1)}, u32[]{:S(2)}, u32[]{:S(2)}) async-start(bf16[256,4,256]{2,0,1:T(8,128)(2,1)} %bitcast.308), calls=%async_computation.8 | async-start | bytes 1048576 | tf_op jit(solution)/shard_map/all_to_all | solution.py:296
  510.2 15.5 %copy-start.10 = (f32[4,1536,64]{1,2,0:T(8,128)}, f32[4,1536,64]{1,2,0:T(8,128)S(1)}, u32[]{:S(2)}) copy-start(f32[4,1536,64]{1,2,0:T(8,128)S(1)} %get-tuple-element.504) | copy-start | bytes 4718596
  517.0 12.7 %all-to-all-start.15 = ((bf16[4,256,256]{1,2,0:T(8,128)(2,1)}), bf16[4,256,256]{1,2,0:T(8,128)(2,1)}, u32[]{:S(2)}, u32[]{:S(2)}) async-start(bf16[4,256,256]{1,2,0:T(8,128)(2,1)} %copy.128), calls=%async_computation.15 | async-start | bytes 1048576 | tf_op jit(solution)/shard_map/all_to_all | solution.py:307
  521.2 189.3 %reduce-scatter.7.cloned.1.call-start = ((), (), s32[]{:S(2)}) async-start(), calls=%async_computation.25 | async-start | bytes 2359296 | tf_op jit(solution)/shard_map/reduce_scatter | solution.py:182
  529.8 52.6 %all-to-all-start.13 = ((bf16[4,256,256]{1,2,0:T(8,128)(2,1)}), bf16[4,256,256]{1,2,0:T(8,128)(2,1)}, u32[]{:S(2)}, u32[]{:S(2)}) async-start(bf16[4,256,256]{1,2,0:T(8,128)(2,1)} %copy.126), calls=%async_computation.13 | async-start | bytes 1048576 | tf_op jit(solution)/shard_map/all_to_all | solution.py:301
  582.3 11.5 %all-to-all-start.11 = ((bf16[4,256,256]{1,2,0:T(8,128)(2,1)}), bf16[4,256,256]{1,2,0:T(8,128)(2,1)S(1)}, u32[]{:S(2)}, u32[]{:S(2)}) async-start(bf16[4,256,256]{1,2,0:T(8,128)(2,1)} %copy.122), calls=%async_computation.11 | async-start | bytes 1048576 | tf_op jit(solution)/shard_map/all_to_all | solution.py:307
  593.9 30.0 %copy-start.41 = (bf16[4,256,256]{1,2,0:T(8,128)(2,1)}, bf16[4,256,256]{1,2,0:T(8,128)(2,1)S(1)}, u32[]{:S(2)}) copy-start(bf16[4,256,256]{1,2,0:T(8,128)(2,1)S(1)} %all-to-all-done.11) | copy-start | bytes 1572868
  593.9 13.0 %all-to-all-start.9 = ((bf16[4,256,256]{1,2,0:T(8,128)(2,1)}), bf16[4,256,256]{1,2,0:T(8,128)(2,1)}, u32[]{:S(2)}, u32[]{:S(2)}) async-start(bf16[4,256,256]{1,2,0:T(8,128)(2,1)} %copy.120), calls=%async_computation.9 | async-start | bytes 1048576 | tf_op jit(solution)/shard_map/all_to_all | solution.py:301
  599.7 24.2 %copy-start.16 = (bf16[2,1,256,1024]{3,2,1,0:T(8,128)(2,1)S(1)}, bf16[2,1,256,1024]{3,2,1,0:T(8,128)(2,1)}, u32[]{:S(2)}) copy-start(bf16[2,1,256,1024]{3,2,1,0:T(8,128)(2,1)} %param.19) | copy-start | bytes 3145732
  599.7 24.2 %copy-start.66 = (f32[8,1,128]{2,1,0:T(1,128)S(1)}, f32[8,1,128]{2,1,0:T(1,128)}, u32[]{:S(2)}) copy-start(f32[8,1,128]{2,1,0:T(1,128)} %copy-done.65) | copy-start | bytes 12292
  599.7 24.2 %copy-start.68 = (f32[8,1,128]{2,1,0:T(1,128)S(1)}, f32[8,1,128]{2,1,0:T(1,128)}, u32[]{:S(2)}) copy-start(f32[8,1,128]{2,1,0:T(1,128)} %copy-done.67) | copy-start | bytes 12292
  599.7 24.2 %copy-start.78 = (f32[256]{0:T(256)S(1)}, f32[256]{0:T(256)}, u32[]{:S(2)}) copy-start(f32[256]{0:T(256)} %copy-done.77) | copy-start | bytes 3076
  599.7 24.3 %copy-start.82 = (f32[256]{0:T(256)S(1)}, f32[256]{0:T(256)}, u32[]{:S(2)}) copy-start(f32[256]{0:T(256)} %copy-done.81) | copy-start | bytes 3076
  606.9 12.7 %all-to-all-start.10 = ((bf16[4,256,256]{1,2,0:T(8,128)(2,1)}), bf16[4,256,256]{1,2,0:T(8,128)(2,1)S(1)}, u32[]{:S(2)}, u32[]{:S(2)}) async-start(bf16[4,256,256]{1,2,0:T(8,128)(2,1)} %copy.121), calls=%async_computation.10 | async-start | bytes 1048576 | tf_op jit(solution)/shard_map/all_to_all | solution.py:304
  615.3 15.4 %copy-start.45 = (bf16[4,256,256]{1,2,0:T(8,128)(2,1)}, bf16[4,256,256]{1,2,0:T(8,128)(2,1)S(1)}, u32[]{:S(2)}) copy-start(bf16[4,256,256]{1,2,0:T(8,128)(2,1)S(1)} %broadcast_multiply_fusion.1) | copy-start | bytes 1572868
  619.6 12.3 %all-to-all-start.14 = ((bf16[4,256,256]{1,2,0:T(8,128)(2,1)}), bf16[4,256,256]{1,2,0:T(8,128)(2,1)S(1)}, u32[]{:S(2)}, u32[]{:S(2)}) async-start(bf16[4,256,256]{1,2,0:T(8,128)(2,1)} %copy.127), calls=%async_computation.14 | async-start | bytes 1048576 | tf_op jit(solution)/shard_map/all_to_all | solution.py:304
  623.9 135.5 %reduce-scatter.5.cloned.1.call-start = ((), (), s32[]{:S(2)}) async-start(), calls=%async_computation.24 | async-start | bytes 7077888 | tf_op jit(solution)/shard_map/reduce_scatter | solution.py:182
  642.3 11.6 %copy-start.26 = (f32[256,1024]{1,0:T(8,128)S(1)}, f32[256,1024]{1,0:T(8,128)}, u32[]{:S(2)}) copy-start(f32[256,1024]{1,0:T(8,128)} %copy-done.24) | copy-start | bytes 3145732
  642.3 268.3 %reduce-scatter.9.cloned.1.call-start = ((), (), s32[]{:S(2)}) async-start(), calls=%async_computation.26 | async-start | bytes 9437184 | tf_op jit(solution)/shard_map/reduce_scatter | solution.py:182
  665.6 397.1 %reduce-scatter.11.cloned.1.call-start = ((), (), s32[]{:S(2)}) async-start(), calls=%async_computation.27 | async-start | bytes 9437184 | tf_op jit(solution)/shard_map/reduce_scatter | solution.py:182
  688.0 446.9 %all-reduce.15.cloned.1.call-start = ((), (), s32[]{:S(2)}) async-start(), calls=%async_computation.28 | async-start | bytes 6291456 | tf_op jit(solution)/shard_map/psum | solution.py:187
  689.9 13.9 %slice-start.4 = ((s8[6291456]{0:T(1024)(128)(4,1)}), s8[4194304]{0:T(1024)(128)(4,1)S(1)}, s32[]{:S(2)}) async-start(s8[6291456]{0:T(1024)(128)(4,1)} %bitcast.420), calls=%async_computation.33 | async-start | bytes 8388608
  707.0 382.6 %copy-start.21 = (f32[256,1024]{1,0:T(8,128)S(1)}, f32[256,1024]{1,0:T(8,128)}, u32[]{:S(2)}) copy-start(f32[256,1024]{1,0:T(8,128)} %copy-done.19) | copy-start | bytes 3145732
  707.0 382.6 %copy-start.23 = (f32[256,1024]{1,0:T(8,128)S(1)}, f32[256,1024]{1,0:T(8,128)}, u32[]{:S(2)}) copy-start(f32[256,1024]{1,0:T(8,128)} %copy-done.22) | copy-start | bytes 3145732
  (82 other events, 407.8 us)
Sparse Core Ops, SparseCore 0:
  10.2 97.9 all-gather.8
  110.3 48.8 all-gather.10
  161.4 122.0 all-gather.12
  285.5 123.1 all-gather.14
  525.8 65.7 reduce-scatter.6
  642.4 116.9 reduce-scatter.4
  763.1 147.5 reduce-scatter.8
  914.7 147.9 reduce-scatter.10
  1065.3 69.5 all-reduce.14
where the time goes:
time: 1160 us; the launch traced here: 1150 us
  waiting for transfers between devices  597 us (51%)
  matrix products  249 us (21%)
  blocking collectives  79.8 us (7%)
  starting transfers between devices  78 us (7%)
  local copies, waits for them, and re-layouts  76.6 us (7%)
  other arithmetic  47.1 us (4%)
  between operations  16.1 us (1%)
    reduce_scatter x4, waiting for transfers between devices, owner_share(): lax.psum_scatter(as_sent(terms), 'fsdp', scatter_dimension=0, tiled=True)  352 us
    all_gather x1, waiting for transfers between devices, body(): lax.all_gather(w_down, 'fsdp', axis=0, tiled=True)  89.4 us
    all_gather x1, waiting for transfers between devices, body(): lax.all_gather(w_qkv, 'fsdp', axis=0, tiled=True)  67.5 us
    dot_general x8, matrix products, contract_rows(): lax.dot_general(left, right, (((0,), (0,)), ((), ())), preferred_element_...  67.4 us
    psum x1, waiting for transfers between devices, owner_finish(): lax.psum(as_sent(shares), 'seq')  41.5 us
    dot_general x8, matrix products, contract_cols(): lax.dot_general(left, right, (((1,), (1,)), ((), ())), preferred_element_...  40.4 us
    dot_general x2, matrix products, body(): jnp.dot(normed_two_low, upward_weight, preferred_element_type=jnp.float32)  32.4 us
    dot_general x8, matrix products, one_block(): jnp.einsum('hqd,hkd->hqk', query_block, key_block, preferred_element_type...  24.8 us
  transfers between devices with their start and end apart: 25, of which 16 were waited for; matrix products, arithmetic and copies ran while one was open for 27% of the time, Pallas kernels for 0%

commit v1 on v0

v1 whole, which is shorter than its diff:
```python
import functools
import math

import jax
import jax.numpy as jnp
from jax import lax
from jax.experimental import pallas as pl
from jax.experimental.pallas import tpu as pltpu
from jax.sharding import Mesh
from jax.sharding import PartitionSpec as P

HEAD_DIM = 64
DOC_MOST = 512
TILE = 256
LANES = 128
epsilon = 1e-05
SWAP = [(0, 1), (1, 0)]
f32 = jnp.float32
bf16 = jnp.bfloat16


def dot(left, right, dims):
    return lax.dot_general(left, right, (dims, ((), ())), preferred_element_type=f32)


def mm(left, right):
    return dot(left, right, ((1,), (0,)))


def mm_rows(left, right):
    return dot(left, right, ((0,), (0,)))


def mm_cols(left, right):
    return dot(left, right, ((1,), (1,)))


def pick(array, index, axis):
    return lax.dynamic_index_in_dim(array, index, axis, keepdims=False)


def swap(value, axis):
    return lax.ppermute(value, axis, SWAP)


def ordered(own, other, index, axis):
    first = jnp.where(index == 0, own, other)
    second = jnp.where(index == 0, other, own)
    return jnp.stack([first, second], axis)


def tile_spans(rows):
    tile = min(TILE, rows)
    spans = []
    for start in range(0, rows, tile):
        low = max(0, (start - DOC_MOST + 1) // tile * tile)
        spans.append((start, low, start + tile))
    return tile, spans


def fill_bias(bias, seg_col, seg_row, spans, tile):
    for i, (start, low, high) in enumerate(spans):
        width = high - low
        query_pos = start + lax.broadcasted_iota(jnp.int32, (tile, width), 0)
        key_pos = low + lax.broadcasted_iota(jnp.int32, (tile, width), 1)
        same = seg_col[start : start + tile, :] == seg_row[:, low:high]
        allowed = (key_pos <= query_pos) & same
        bias[i, :, :width] = jnp.where(allowed, 0.0, -1e30).astype(f32)


def attend_kernel(spans, tile, q_ref, k_ref, v_ref, seg_col, seg_row, out_ref, lse_ref, bias):
    @pl.when(pl.program_id(0) == 0)
    def _():
        fill_bias(bias, seg_col, seg_row, spans, tile)

    left = lax.broadcasted_iota(jnp.int32, (tile, LANES), 1) < HEAD_DIM
    for i, (start, low, high) in enumerate(spans):
        rows = slice(start, start + tile)
        queries = q_ref[rows, :]
        keys, values = k_ref[low:high, :], v_ref[low:high, :]
        mixed, logs = [], []
        for half in (left, ~left):
            scores = mm_cols(jnp.where(half, queries, jnp.zeros_like(queries)), keys)
            scores = scores + bias[i, :, : high - low]
            top = jnp.max(scores, axis=-1, keepdims=True)
            powers = jnp.exp(scores - top)
            total = jnp.sum(powers, axis=-1, keepdims=True)
            mixed.append(mm((powers * (1.0 / total)).astype(bf16), values))
            logs.append(top + jnp.log(total))
        out_ref[rows, :] = jnp.where(left, mixed[0], mixed[1]).astype(bf16)
        lse_ref[rows, :] = jnp.where(left, logs[0], logs[1])


def attend(joint, seg_col, seg_row):
    rows, width = joint.shape[0], joint.shape[1] // 3
    pairs = width // LANES
    tile, spans = tile_spans(rows)
    widest = max(high - low for _, low, high in spans)

    def part(which):
        return pl.BlockSpec((rows, LANES), lambda p: (0, which * pairs + p))

    return pl.pallas_call(
        functools.partial(attend_kernel, spans, tile),
        grid=(pairs,),
        in_specs=[
            part(0),
            part(1),
            part(2),
            pl.BlockSpec((rows, 1), lambda p: (0, 0)),
            pl.BlockSpec((1, rows), lambda p: (0, 0)),
        ],
        out_specs=[part(0), part(0)],
        out_shape=[
            jax.ShapeDtypeStruct((rows, width), bf16),
            jax.ShapeDtypeStruct((rows, width), f32),
        ],
        scratch_shapes=[pltpu.VMEM((len(spans), tile, widest), f32)],
        compiler_params=pltpu.CompilerParams(vmem_limit_bytes=40 * 1024 * 1024),
        name="attend",
    )(joint, joint, joint, seg_col, seg_row)


def attend_back_kernel(
    spans, tile, q_ref, k_ref, v_ref, g_ref, lse_ref, seg_col, seg_row, out_ref, bias, keys_sum, values_sum
):
    @pl.when((pl.program_id(0) == 0) & (pl.program_id(1) == 0))
    def _():
        fill_bias(bias, seg_col, seg_row, spans, tile)

    @pl.when(pl.program_id(1) == 0)
    def _():
        keys_sum[...] = jnp.zeros_like(keys_sum)
        values_sum[...] = jnp.zeros_like(values_sum)
        left = lax.broadcasted_iota(jnp.int32, (tile, LANES), 1) < HEAD_DIM
        for i, (start, low, high) in enumerate(spans):
            rows = slice(start, start + tile)
            queries, grads = q_ref[rows, :], g_ref[rows, :]
            keys, values = k_ref[low:high, :], v_ref[low:high, :]
            parts = []
            for half, lane in ((left, 0), (~left, HEAD_DIM)):
                own_queries = jnp.where(half, queries, jnp.zeros_like(queries))
                own_grads = jnp.where(half, grads, jnp.zeros_like(grads))
                scores = mm_cols(own_queries, keys) + bias[i, :, : high - low]
                probs = jnp.exp(scores - lse_ref[rows, lane : lane + 1])
                grad_probs = mm_cols(own_grads, values)
                inner = jnp.sum(probs * grad_probs, axis=-1, keepdims=True)
                grad_scores = (probs * (grad_probs - inner)).astype(bf16)
                parts.append(mm(grad_scores, keys))
                keys_sum[low:high, :] += mm_rows(grad_scores, own_queries)
                values_sum[low:high, :] += mm_rows(probs.astype(bf16), own_grads)
            grad_queries = jnp.where(left, parts[0], parts[1]).astype(bf16)
            out_ref[rows, :] = grad_queries * jnp.asarray(1.0 / math.sqrt(HEAD_DIM), bf16)

    @pl.when(pl.program_id(1) == 1)
    def _():
        out_ref[...] = keys_sum[...].astype(bf16)

    @pl.when(pl.program_id(1) == 2)
    def _():
        out_ref[...] = values_sum[...].astype(bf16)


def attend_back(joint, grads, lse, seg_col, seg_row):
    rows, width = joint.shape[0], joint.shape[1] // 3
    pairs = width // LANES
    tile, spans = tile_spans(rows)
    widest = max(high - low for _, low, high in spans)

    def part(which):
        return pl.BlockSpec((rows, LANES), lambda p, j: (0, which * pairs + p))

    return pl.pallas_call(
        functools.partial(attend_back_kernel, spans, tile),
        grid=(pairs, 3),
        in_specs=[
            part(0),
            part(1),
            part(2),
            part(0),
            part(0),
            pl.BlockSpec((rows, 1), lambda p, j: (0, 0)),
            pl.BlockSpec((1, rows), lambda p, j: (0, 0)),
        ],
        out_specs=pl.BlockSpec((rows, LANES), lambda p, j: (0, j * pairs + p)),
        out_shape=jax.ShapeDtypeStruct((rows, 3 * width), bf16),
        scratch_shapes=[
            pltpu.VMEM((len(spans), tile, widest), f32),
            pltpu.VMEM((rows, LANES), f32),
            pltpu.VMEM((rows, LANES), f32),
        ],
        compiler_params=pltpu.CompilerParams(vmem_limit_bytes=48 * 1024 * 1024),
        name="attend_back",
    )(joint, joint, joint, grads, lse, seg_col, seg_row)


def gather(own, depth):
    h = lax.axis_index("hi")
    rows, columns = own.shape
    halves = own.reshape(2, rows // 2, columns)
    half = pick(halves, h, 0)
    far = [lax.ppermute(half, "fz", [(i, (i + k) % depth) for i in range(depth)]) for k in range(1, depth)]
    spots = [(0, 0, None), (0, 1, None)]
    pieces = [halves, swap(halves, "fx")]
    for k, piece in enumerate(far, 1):
        side = swap(piece, "fx")
        spots += [(k, 0, 0), (k, 0, 1), (k, 1, 0), (k, 1, 1)]
        pieces += [piece, swap(piece, "hi"), side, swap(side, "hi")]
    return spots, pieces


def load(spots, depth, place, pieces, sems, targets):
    z, x, h = place[0], place[1], place[2]
    copies = []
    for first, columns, where in targets:
        for (k, other_x, other_h), piece in zip(spots, pieces):
            shard = lax.rem(z - k + depth, depth) * 2 + (1 - x if other_x else x)
            for part in range(2) if other_h is None else (None,):
                if part is None:
                    half, source = (1 - h if other_h else h), piece
                else:
                    half, source = part, piece.at[part]
                if columns != source.shape[1]:
                    source = source.at[:, first : first + columns]
                copy = pltpu.make_async_copy(source, where(shard, half), sems.at[len(copies)])
                copy.start()
                copies.append(copy)
    return copies


def below(weight, half_rows):
    def where(shard, half):
        return weight.at[pl.ds(pl.multiple_of((shard * 2 + half) * half_rows, half_rows), half_rows), :]

    return where


def beside(weight, rows, columns):
    def where(shard, half):
        return weight.at[
            pl.ds(pl.multiple_of(shard * rows, rows), rows),
            pl.ds(pl.multiple_of(half * columns, columns), columns),
        ]

    return where


def plus(left, right):
    return (left.astype(f32) + right.astype(f32)).astype(bf16)


def reduce(full, depth):
    z, x, h = lax.axis_index("fz"), lax.axis_index("fx"), lax.axis_index("hi")
    columns = full.shape[1]
    rows = full.shape[0] // (2 * depth)
    view = full.reshape(depth, 2, 2, 2, rows // 4, columns)
    first, second = view[:, :, 0], view[:, :, 1]
    first = plus(pick(first, x, 1), swap(pick(first, 1 - x, 1), "fx"))
    second = plus(pick(second, h, 2), swap(pick(second, 1 - h, 2), "hi"))
    first = plus(pick(first, h, 1), swap(pick(first, 1 - h, 1), "hi"))
    second = plus(pick(second, x, 1), swap(pick(second, 1 - x, 1), "fx"))
    both = jnp.stack([first, second], 1)
    total = pick(both, z, 0).astype(f32)
    for k in range(1, depth):
        ring = [(i, (i + k) % depth) for i in range(depth)]
        total = total + lax.ppermute(pick(both, (z + k) % depth, 0), "fz", ring).astype(f32)
    total = total.astype(bf16)
    return ordered(total, swap(total, "hi"), h, 1).reshape(rows, columns)


def row_block(tile, width):
    return pl.BlockSpec((tile, width), lambda i: (i, 0))


def whole_block(*shape):
    return pl.BlockSpec(shape, lambda i: (0,) * len(shape))


def weight_call(name, step, tiles, place, inputs, sets, outs, scratch, copies, flops):
    pieces = [piece for _, held in sets for piece in held]
    moved = sum(math.prod(v.shape) * v.dtype.itemsize for v in pieces)
    moved += sum(math.prod(v.shape) * v.dtype.itemsize for v, _ in inputs)
    moved += sum(math.prod(v.shape) * v.dtype.itemsize for v, _ in outs)

    def kernel(place_ref, *refs):
        refs = list(refs)

        def take(count):
            taken = refs[:count]
            del refs[:count]
            return taken

        given = take(len(inputs))
        held = [take(len(one)) for _, one in sets]
        made = take(len(outs))
        step(place_ref, given, held, made, refs[:-1], refs[-1])

    return pl.pallas_call(
        kernel,
        grid=(tiles,),
        in_specs=[pl.BlockSpec(memory_space=pltpu.SMEM)]
        + [spec for _, spec in inputs]
        + [pl.BlockSpec(memory_space=pl.ANY)] * len(pieces),
        out_specs=[spec for _, spec in outs],
        out_shape=[shape for shape, _ in outs],
        scratch_shapes=list(scratch) + [pltpu.SemaphoreType.DMA(copies if isinstance(copies, tuple) else (copies,))],
        compiler_params=pltpu.CompilerParams(vmem_limit_bytes=56 * 1024 * 1024),
        cost_estimate=pl.CostEstimate(flops=flops, bytes_accessed=moved, transcendentals=0),
        name=name,
    )(place, *[v for v, _ in inputs], *pieces)


def shape_of(*shape, dtype=bf16):
    return jax.ShapeDtypeStruct(shape, dtype)


def unit_of(values):
    centred = values - jnp.mean(values, axis=-1, keepdims=True)
    variance = jnp.mean(centred * centred, axis=-1, keepdims=True)
    inverse = lax.rsqrt(variance + epsilon)
    return centred * inverse, inverse


def unit_back(grad_unit, unit_rows, inverse):
    mean_grad = jnp.mean(grad_unit, axis=-1, keepdims=True)
    mean_cross = jnp.mean(grad_unit * unit_rows, axis=-1, keepdims=True)
    return inverse * (grad_unit - mean_grad - unit_rows * mean_cross)


def bell_and_slope(values):
    size = jnp.abs(values)
    t = 1.0 / (1.0 + (0.3275911 * math.sqrt(0.5)) * size)
    bell = jnp.exp(values * values * -0.5)
    series = 0.5 * 1.061405429
    for term in (-1.453152027, 1.421413741, -0.284496736, 0.254829592):
        series = series * t + 0.5 * term
    tail = series * t * bell
    phi = jnp.where(values < 0, tail, 1.0 - tail)
    return values * phi, phi + values * bell * (1.0 / math.sqrt(2.0 * math.pi))


def body(
    group,
    depth,
    tokens,
    segment_ids,
    norm1_gain,
    norm1_bias,
    w_qkv,
    w_out,
    norm2_gain,
    norm2_bias,
    w_up,
    w_down,
    cotangent,
):
    h, lo = lax.axis_index("hi"), lax.axis_index("lo")
    z, x = lax.axis_index("fz"), lax.axis_index("fx")
    micro, _, chunk, model = tokens.shape
    shards = 2 * depth
    rows = micro * group * chunk
    own_rows = w_out.shape[0]
    inner = w_up.shape[1] // group
    split_out = (own_rows // HEAD_DIM) % group == 0
    joined = split_out and group == 2
    head_columns = model // group
    tile = min(TILE, rows)
    tiles = rows // tile

    def whole_group(value, axis):
        if group == 2:
            return ordered(value, swap(value, "lo"), lo, axis)
        return lax.all_gather(value, "lo", axis=axis)

    def sequence(array):
        kept = pick(array[:, 0], h, 0)
        came = swap(pick(array[:, 0], 1 - h, 0), "hi")
        return whole_group(ordered(kept, came, h, 0), 1).reshape(rows, model)

    def placed(array):
        came = swap(pick(array, 1 - h, 0).astype(bf16), "hi").astype(array.dtype)
        return ordered(pick(array, h, 0), came, h, 0)[:, None]

    def other_part(partial):
        if group == 2:
            return swap(partial, "lo")
        return (lax.psum(partial, "lo").astype(f32) - partial.astype(f32)).astype(bf16)

    def sum_own(partial):
        parts = partial.reshape(micro, group, chunk, model)
        if group == 2:
            came = swap(pick(parts, 1 - lo, 1), "lo").astype(f32)
            return pick(parts, lo, 1).astype(f32) + came
        return lax.psum_scatter(parts, "lo", scatter_dimension=1).astype(f32)

    def own_chunks(full):
        return pick(full.reshape(micro, group, chunk, -1), lo, 1)

    if split_out:
        qkv_part = pick(w_qkv.reshape(own_rows, 3, shards, group, -1), lo, 3).reshape(own_rows, -1)
        out_part = pick(w_out.reshape(group, own_rows // group, model), lo, 0)
    else:
        qkv_part = pick(w_qkv.reshape(own_rows, 3, group, -1), lo, 2).reshape(own_rows, -1)
        out_part = w_out
    up_part = pick(w_up.reshape(own_rows, shards, group, -1), lo, 2).reshape(own_rows, -1)
    down_part = pick(w_down.reshape(group, -1, model), lo, 0)
    out_rows, down_rows = out_part.shape[0], down_part.shape[0]

    vectors = jnp.stack([norm1_gain, norm1_bias, norm2_gain, norm2_bias], axis=1)
    parts = [qkv_part, jnp.pad(vectors, ((0, 0), (0, LANES - 4)))]
    if joined:
        parts.append(jnp.concatenate([out_part[:, : model // 2], out_part[:, model // 2 :]], axis=0))
    place = jnp.stack([z, x, h, lo]).astype(jnp.int32)
    scale_at, out_at = 3 * head_columns, 3 * head_columns + LANES

    inputs = sequence(tokens)
    first_set = gather(jnp.concatenate(parts, axis=1), depth)
    out_set = first_set if joined else gather(out_part, depth)
    up_set = gather(up_part, depth)
    down_set = gather(down_part, depth)
    grad_result = sequence(cotangent)

    segments = pick(segment_ids[:, 0], h, 0)
    seg_col, seg_row = segments[:, None], segments[None, :]
    half_rows = own_rows // 2
    copies = 4 * shards

    def load_out(place_ref, pieces, weight, sems):
        if joined:
            targets = [(out_at, model // 2, beside(weight, out_rows, model // 2))]
        else:
            targets = [(0, model, below(weight, out_rows // 2))]
        return load(out_set[0], depth, place_ref, pieces, sems, targets)

    def out_weight(weight, place_ref):
        if split_out:
            return weight[...]
        return weight[pl.ds(pl.multiple_of(place_ref[3] * head_columns, head_columns), head_columns), :]

    def project(place_ref, given, held, made, scratch, sems):
        (rows_ref,), (normed_ref, joint_ref, scales_ref) = given, made
        weight, columns = scratch

        @pl.when(pl.program_id(0) == 0)
        def _():
            targets = [
                (0, 3 * head_columns, below(weight, half_rows)),
                (scale_at, LANES, below(columns, half_rows)),
            ]
            for copy in load(first_set[0], depth, place_ref, held[0], sems, targets):
                copy.wait()
            scales_ref[...] = columns[...].astype(f32).T[:8, :]

        unit_rows, _ = unit_of(rows_ref[...].astype(f32))
        normed = (unit_rows * scales_ref[0:1, :] + scales_ref[1:2, :]).astype(bf16)
        normed_ref[...] = normed
        for at in range(0, 3 * head_columns, head_columns):
            part = mm(normed, weight[:, at : at + head_columns])
            if at == 0:
                part = part * (1.0 / math.sqrt(HEAD_DIM))
            joint_ref[:, at : at + head_columns] = part.astype(bf16)

    normed, joint, scales = weight_call(
        "project",
        project,
        tiles,
        place,
        [(inputs, row_block(tile, model))],
        [first_set],
        [
            (shape_of(rows, model), row_block(tile, model)),
            (shape_of(rows, 3 * head_columns), row_block(tile, 3 * head_columns)),
            (shape_of(8, model, dtype=f32), whole_block(8, model)),
        ],
        [pltpu.VMEM((model, 3 * head_columns), bf16), pltpu.VMEM((model, LANES), bf16)],
        copies,
        6 * rows * model * head_columns,
    )
    attended, lse = attend(joint, seg_col, seg_row)

    def leave(place_ref, given, held, made, scratch, sems):
        (rows_ref,), (out_ref,), (weight,) = given, made, scratch

        @pl.when(pl.program_id(0) == 0)
        def _():
            for copy in load_out(place_ref, held[0], weight, sems):
                copy.wait()

        out_ref[...] = mm(rows_ref[...], out_weight(weight, place_ref)).astype(bf16)

    (branch,) = weight_call(
        "leave",
        leave,
        tiles,
        place,
        [(attended, row_block(tile, head_columns))],
        [out_set],
        [(shape_of(rows, model), row_block(tile, model))],
        [pltpu.VMEM((out_rows * shards, model), bf16)],
        copies,
        2 * rows * model * head_columns,
    )
    branch_other = other_part(branch)
    wide = min(512, inner)

    def widen(place_ref, given, held, made, scratch, sems):
        rows_ref, own_ref, other_ref, scales_ref = given
        middle_ref, normed_ref, hidden_ref, slope_ref = made
        (weight,) = scratch

        @pl.when(pl.program_id(0) == 0)
        def _():
            targets = [(0, inner, below(weight, half_rows))]
            for copy in load(up_set[0], depth, place_ref, held[0], sems, targets):
                copy.wait()

        added = own_ref[...].astype(f32) + other_ref[...].astype(f32)
        middle = rows_ref[...].astype(f32) + added
        middle_ref[...] = middle
        unit_rows, _ = unit_of(middle)
        normed = (unit_rows * scales_ref[2:3, :] + scales_ref[3:4, :]).astype(bf16)
        normed_ref[...] = normed
        for at in range(0, inner, wide):
            hidden, slope = bell_and_slope(mm(normed, weight[:, at : at + wide]))
            hidden_ref[:, at : at + wide] = hidden.astype(bf16)
            slope_ref[:, at : at + wide] = slope.astype(bf16)

    middle, normed_two, hidden, slope = weight_call(
        "widen",
        widen,
        tiles,
        place,
        [
            (inputs, row_block(tile, model)),
            (branch, row_block(tile, model)),
            (branch_other, row_block(tile, model)),
            (scales, whole_block(8, model)),
        ],
        [up_set],
        [
            (shape_of(rows, model, dtype=f32), row_block(tile, model)),
            (shape_of(rows, model), row_block(tile, model)),
            (shape_of(rows, inner), row_block(tile, inner)),
            (shape_of(rows, inner), row_block(tile, inner)),
        ],
        [pltpu.VMEM((model, inner), bf16)],
        copies,
        2 * rows * model * inner,
    )
    grad_down = mm_rows(hidden, grad_result).astype(bf16)

    def narrow(place_ref, given, held, made, scratch, sems):
        hidden_ref, grad_ref, slope_ref = given
        out_ref, pre_ref, back_ref = made
        upward, downward = scratch

        @pl.when(pl.program_id(0) == 0)
        def _():
            targets = [(0, inner, below(upward, half_rows))]
            ups = load(up_set[0], depth, place_ref, held[0], sems.at[0], targets)
            targets = [(0, model, below(downward, down_rows // 2))]
            for copy in ups + load(down_set[0], depth, place_ref, held[1], sems.at[1], targets):
                copy.wait()

        out_ref[...] = mm(hidden_ref[...], downward[...]).astype(bf16)
        total = jnp.zeros(back_ref.shape, f32)
        for at in range(0, inner, wide):
            grad = mm_cols(grad_ref[...], downward[at : at + wide, :])
            grad = (grad * slope_ref[:, at : at + wide].astype(f32)).astype(bf16)
            pre_ref[:, at : at + wide] = grad
            total = total + mm_cols(grad, upward[:, at : at + wide])
        back_ref[...] = total.astype(bf16)

    result, grad_pre, back = weight_call(
        "narrow",
        narrow,
        tiles,
        place,
        [
            (hidden, row_block(tile, inner)),
            (grad_result, row_block(tile, model)),
            (slope, row_block(tile, inner)),
        ],
        [up_set, down_set],
        [
            (shape_of(rows, model), row_block(tile, model)),
            (shape_of(rows, inner), row_block(tile, inner)),
            (shape_of(rows, model), row_block(tile, model)),
        ],
        [pltpu.VMEM((model, inner), bf16), pltpu.VMEM((inner, model), bf16)],
        (2, copies),
        6 * rows * model * inner,
    )
    back_other = other_part(back)
    grad_up = mm_rows(normed_two, grad_pre).astype(bf16)

    def between(place_ref, given, held, made, scratch, sems):
        grad_ref, own_ref, other_ref, middle_ref, scales_ref = given
        middle_grad_ref, branch_ref, attended_ref, sums_ref = made
        (weight,) = scratch

        @pl.when(pl.program_id(0) == 0)
        def _():
            sums_ref[...] = jnp.zeros_like(sums_ref)
            for copy in load_out(place_ref, held[0], weight, sems):
                copy.wait()

        unit_rows, inverse = unit_of(middle_ref[...])
        back_rows = own_ref[...].astype(f32) + other_ref[...].astype(f32)
        sums_ref[0:1, :] += jnp.sum(back_rows * unit_rows, axis=0, keepdims=True)
        sums_ref[1:2, :] += jnp.sum(back_rows, axis=0, keepdims=True)
        grads = grad_ref[...].astype(f32) + unit_back(back_rows * scales_ref[2:3, :], unit_rows, inverse)
        middle_grad_ref[...] = grads
        low = grads.astype(bf16)
        branch_ref[...] = low
        attended_ref[...] = mm_cols(low, out_weight(weight, place_ref)).astype(bf16)

    grad_middle, grad_branch, grad_attended, sums_two = weight_call(
        "between",
        between,
        tiles,
        place,
        [
            (grad_result, row_block(tile, model)),
            (back, row_block(tile, model)),
            (back_other, row_block(tile, model)),
            (middle, row_block(tile, model)),
            (scales, whole_block(8, model)),
        ],
        [out_set],
        [
            (shape_of(rows, model, dtype=f32), row_block(tile, model)),
            (shape_of(rows, model), row_block(tile, model)),
            (shape_of(rows, head_columns), row_block(tile, head_columns)),
            (shape_of(8, model, dtype=f32), whole_block(8, model)),
        ],
        [pltpu.VMEM((out_rows * shards, model), bf16)],
        copies,
        2 * rows * model * head_columns,
    )
    grad_joint = attend_back(joint, grad_attended, lse, seg_col, seg_row)
    grad_out = mm_rows(attended, grad_branch).astype(bf16)

    def enter(place_ref, given, held, made, scratch, sems):
        (rows_ref,), (out_ref,), (weight,) = given, made, scratch

        @pl.when(pl.program_id(0) == 0)
        def _():
            targets = [(0, 3 * head_columns, below(weight, half_rows))]
            for copy in load(first_set[0], depth, place_ref, held[0], sems, targets):
                copy.wait()

        out_ref[...] = mm_cols(rows_ref[...], weight[...]).astype(bf16)

    (entered,) = weight_call(
        "enter",
        enter,
        tiles,
        place,
        [(grad_joint, row_block(tile, 3 * head_columns))],
        [first_set],
        [(shape_of(rows, model), row_block(tile, model))],
        [pltpu.VMEM((model, 3 * head_columns), bf16)],
        copies,
        6 * rows * model * head_columns,
    )
    grad_qkv = mm_rows(normed, grad_joint).astype(bf16)

    output = placed((own_chunks(middle) + sum_own(result)).astype(bf16))
    grad_normed = sum_own(entered)
    unit_own, inverse_own = unit_of(own_chunks(inputs).astype(f32))
    grad_gain_one = jnp.sum(grad_normed * unit_own, axis=(0, 1))
    grad_bias_one = jnp.sum(grad_normed, axis=(0, 1))
    grad_tokens = placed(own_chunks(grad_middle) + unit_back(grad_normed * scales[0], unit_own, inverse_own))

    if not split_out:
        empty = jnp.zeros((model, model), bf16)
        grad_out = lax.dynamic_update_slice_in_dim(empty, grad_out, lo * head_columns, 0)
    down_own = reduce(grad_down, depth)
    up_own = reduce(grad_up, depth)
    out_own = reduce(grad_out, depth)
    qkv_own = reduce(grad_qkv, depth)

    down_all = whole_group(down_own, 0).reshape(-1, model).astype(f32)
    up_all = whole_group(up_own.reshape(own_rows, shards, -1), 2).reshape(own_rows, -1).astype(f32)
    if split_out:
        out_all = whole_group(out_own, 0).reshape(own_rows, model).astype(f32)
        qkv_all = whole_group(qkv_own.reshape(own_rows, 3, shards, -1), 3)
    else:
        out_all = lax.psum(out_own, "lo").astype(f32)
        qkv_all = whole_group(qkv_own.reshape(own_rows, 3, -1), 2)
    qkv_all = qkv_all.reshape(own_rows, -1).astype(f32)

    once = jnp.where(lo == 0, 1.0, 0.0).astype(f32)
    sums = jnp.stack([grad_gain_one, grad_bias_one, sums_two[0] * once, sums_two[1] * once])
    sums = lax.psum(sums, ("hi", "lo", "fz", "fx")).reshape(4, shards, own_rows)
    sums = pick(sums, z * 2 + x, 1)

    return (
        output,
        grad_tokens,
        sums[0],
        sums[1],
        qkv_all,
        out_all,
        sums[2],
        sums[3],
        up_all,
        down_all,
    )


def solution(mesh):
    seq, fsdp = mesh.shape["seq"], mesh.shape["fsdp"]
    group, depth = seq // 2, fsdp // 2
    fine = Mesh(mesh.devices.reshape(2, group, depth, 2), ("hi", "lo", "fz", "fx"))
    s, f = ("hi", "lo"), ("fz", "fx")
    return jax.shard_map(
        functools.partial(body, group, depth),
        mesh=fine,
        in_specs=(
            P(None, f, s, None),
            P(None, f, None),
            P(f),
            P(f),
            P(f, None),
            P(f, None),
            P(f),
            P(f),
            P(f, None),
            P(f, None),
            P(None, f, s, None),
        ),
        out_specs=(
            P(None, f, s, None),
            P(None, f, s, None),
            P(f),
            P(f),
            P(f, None),
            P(f, None),
            P(f),
            P(f),
            P(f, None),
            P(f, None),
        ),
        check_vma=False,
    )
```

time: 1160 us -> 604 us (0.52)
  waiting for transfers between devices: 597 us -> 229 us
  matrix products: 249 us -> 21 us
  Pallas kernels: 0 us -> 122 us
  blocking collectives: 79.8 us -> 46.7 us
  local copies, waits for them, and re-layouts: 76.6 us -> 49 us
  starting transfers between devices: 78 us -> 95.3 us
  other arithmetic: 47.1 us -> 30 us
  between operations: 16.1 us -> 2.21 us
    reduce_scatter x4 -> x0, waiting for transfers between devices: 352 us -> none  [owner_share(): lax.psum_scatter(as_sent(terms), 'fsdp', scatter_dimension=0, tiled=True)]
    ppermute x0 -> x85, waiting for transfers between devices: none -> 229 us  [the longest x64 144 us: swap(): return lax.ppermute(value, axis, SWAP)]
    dot_general x52 -> x4, matrix products: 249 us -> 21 us  [dot(): lax.dot_general(left, right, (dims, ((), ())), preferred_element_type=f32)]
    all_gather x4 -> x0, waiting for transfers between devices: 157 us -> none  [the longest x1 89.4 us: body(): lax.all_gather(w_down, 'fsdp', axis=0, tiled=True)]
    pallas_call x0 -> x8, Pallas kernels: none -> 122 us  [the longest x6 75.2 us: weight_call(): pl.pallas_call(kernel, grid=(tiles,), in_specs=[pl.BlockSpec(memory_space...]
    ppermute x0 -> x85, starting transfers between devices: none -> 95.3 us  [the longest x64 65.4 us: swap(): return lax.ppermute(value, axis, SWAP)]
    all_to_all x16 -> x0, starting transfers between devices: 77.4 us -> none  [the longest x2 15.1 us: body(): lax.all_to_all(value_rows, 'seq', split_axis=1, concat_axis=0, tiled=True)]
    all_gather x4 -> x0, blocking collectives: 55.3 us -> none  [the longest x1 14.8 us: body(): lax.all_gather(norm1_bias, 'fsdp', axis=0, tiled=True)]
  transfers between devices with their start and end apart: 25 -> 85, of which waited for: 16 -> 41; matrix products, arithmetic and copies ran while one was open for 27% -> 14% of each run, Pallas kernels for 0% -> 17%
where the time goes in v1:
time: 604 us; the launch traced here: 595 us
  waiting for transfers between devices  229 us (38%)
  Pallas kernels  122 us (20%)
  starting transfers between devices  95.3 us (16%)
  local copies, waits for them, and re-layouts  49 us (8%)
  blocking collectives  46.7 us (8%)
  other arithmetic  30 us (5%)
  matrix products  21 us (3%)
    ppermute x64, waiting for transfers between devices, swap(): return lax.ppermute(value, axis, SWAP)  144 us
    pallas_call x6, Pallas kernels, weight_call(): pl.pallas_call(kernel, grid=(tiles,), in_specs=[pl.BlockSpec(memory_space...  75.2 us
    ppermute x64, starting transfers between devices, swap(): return lax.ppermute(value, axis, SWAP)  65.4 us
    psum x1, blocking collectives, body(): sums = lax.psum(sums, ('hi', 'lo', 'fz', 'fx')).reshape(4, shards, own_rows)  46.7 us
    ppermute x12, waiting for transfers between devices, reduce(): lax.ppermute(pick(both, (z + k) % depth, 0), 'fz', ring).astype(f32)  44 us
    ppermute x9, waiting for transfers between devices, gather(): lax.ppermute(half, 'fz', [(i, (i + k) % depth) for i in range(depth)])  41.1 us
    pallas_call x1, Pallas kernels, attend_back(): pl.pallas_call(functools.partial(attend_back_kernel, spans, tile), grid=(...  30.1 us
    dot_general x4, matrix products, dot(): lax.dot_general(left, right, (dims, ((), ())), preferred_element_type=f32)  21 us
  transfers between devices with their start and end apart: 85, of which 41 were waited for; matrix products, arithmetic and copies ran while one was open for 14% of the time, Pallas kernels for 17%

profile of v1, /device:TPU:9, one launch (start us, length us, event | category | flops | bytes accessed | tf_op | source)
XLA Modules:
  0.0 595.3 jit_solution(1778954878318916959)
XLA Ops:
  0.7 2.0 dynamic-slice_bitcast_fusion.8
  8.1 7.7 %collective-permute-done = bf16[256,1024]{1,0:T(8,128)(2,1)} collective-permute-done((bf16[256,1024]{1,0:T(8,128)(2,1)}, bf16[256,1024]{1,0:T(8,128)(2,1)}, u32[]{:S(2)}, u32[]{:S(2)}) %collective-permute-start) | collective-permute-done | bytes 524320 | tf_op jit(solution)/shard_map/ppermute | solution.py:43
  21.9 2.3 collective-permute-start.7
  25.5 11.3 %collective-permute-done.7.refs_7_.refs_11_ = bf16[64,2176]{1,0:T(8,128)(2,1)} collective-permute-done((bf16[64,2176]{1,0:T(8,128)(2,1)}, bf16[64,2176]{1,0:T(8,128)(2,1)}, u32[]{:S(2)}, u32[]{:S(2)}) %collective-permute-start.7) | collective-permute-done | bytes 278560 | tf_op jit(solution)/shard_map/ppermute | solution.py:202
  37.9 4.8 collective-permute-done.3.refs_3_.refs_7_
  52.2 4.4 collective-permute-done.5.refs_5_.refs_9_
  62.1 2.8 collective-permute-start.30
  64.9 3.7 collective-permute-done.2.refs_2_.refs_6_
  68.8 6.0 %collective-permute-done.6.refs_6_.refs_10_ = bf16[64,2176]{1,0:T(8,128)(2,1)S(1)} collective-permute-done((bf16[64,2176]{1,0:T(8,128)(2,1)S(1)}, bf16[64,2176]{1,0:T(8,128)(2,1)S(1)}, u32[]{:S(2)}, u32[]{:S(2)}) %collective-permute-start.6) | collective-permute-done | bytes 278560 | tf_op jit(solution)/shard_map/ppermute | solution.py:43
  75.5 9.4 %project.1 = (bf16[1024,1024]{1,0:T(8,128)(2,1)}, bf16[1024,1536]{1,0:T(8,128)(2,1)}, f32[8,1024]{1,0:T(8,128)}) custom-call(s32[4]{0:T(128)} %pad_add_fusion.place_ref, bf16[1024,1024]{1,0:T(8,128)(2,1)} %bitcast.413, bf16[2,64,2176]{2,1,0:T(8,128)(2,1)} %copy-done.12, bf16[2,64,2176]{2,1,0:T(8,128)(2,1)} %copy-done.25, ...), custom_call_target="tpu_custom_call" | custom-call | flops 3221225472 | bytes 11829248 | tf_op jit(solution)/shard_map/project/pallas_call | solution.py:298
  86.7 17.1 %attend.1 = (bf16[1024,512]{1,0:T(8,128)(2,1)S(1)}, f32[1024,512]{1,0:T(8,128)S(1)}) custom-call(bf16[1024,1536]{1,0:T(8,128)(2,1)S(1)} %copy-done.2, bf16[1024,1536]{1,0:T(8,128)(2,1)S(1)} %copy-done.2, bf16[1024,1536]{1,0:T(8,128)(2,1)S(1)} %copy-done.2, s32[1024,1]{1,0:T(8,128)S(1)} %copy.119.seg_col, s32[1,1024]{1,0:T(1,128)S(1)} %get-tuple-element.160.seg_row), custom_call_target="tpu_custom_call" | custom-call | tf_op jit(solution)/shard_map/attend/pallas_call | solution.py:103
  106.2 5.9 leave.1.refs_1_
  112.1 3.2 collective-permute-start.15
  116.1 4.3 collective-permute-start.40
  121.8 2.6 reshape.216
  124.4 4.4 dynamic-slice_reduce_fusion
  131.1 6.4 %collective-permute-done.36.refs_23_ = bf16[128,1024]{1,0:T(8,128)(2,1)} collective-permute-done((bf16[128,1024]{1,0:T(8,128)(2,1)S(1)}, bf16[128,1024]{1,0:T(8,128)(2,1)}, u32[]{:S(2)}, u32[]{:S(2)}) %collective-permute-start.36) | collective-permute-done | bytes 262176 | tf_op jit(solution)/shard_map/ppermute | solution.py:202
  137.5 3.3 collective-permute-start.21
  140.8 13.5 %collective-permute-done.32.refs_19_ = bf16[128,1024]{1,0:T(8,128)(2,1)} collective-permute-done((bf16[128,1024]{1,0:T(8,128)(2,1)S(1)}, bf16[128,1024]{1,0:T(8,128)(2,1)}, u32[]{:S(2)}, u32[]{:S(2)}) %collective-permute-start.32) | collective-permute-done | bytes 262176 | tf_op jit(solution)/shard_map/ppermute | solution.py:202
  154.3 2.3 collective-permute-start.17
  156.6 2.2 collective-permute-done.25.refs_14_.refs_13_
  162.7 2.9 collective-permute-done.17.refs_6_.refs_5_
  168.3 3.1 collective-permute-done.23.refs_12_.refs_11_
  173.4 3.7 collective-permute-done.19.refs_8_.refs_7_
  180.5 7.8 %collective-permute-done.16.refs_5_.refs_4_ = bf16[2,64,2048]{2,1,0:T(8,128)(2,1)S(1)} collective-permute-done((bf16[2,64,2048]{2,1,0:T(8,128)(2,1)S(1)}, bf16[2,64,2048]{2,1,0:T(8,128)(2,1)S(1)}, u32[]{:S(2)}, u32[]{:S(2)}) %collective-permute-start.16) | collective-permute-done | bytes 524320 | tf_op jit(solution)/shard_map/ppermute | solution.py:43
  191.1 4.7 collective-permute-done.20.refs_9_.refs_8_
  197.1 18.8 %widen.1 = (f32[1024,1024]{1,0:T(8,128)}, bf16[1024,1024]{1,0:T(8,128)(2,1)}, bf16[1024,2048]{1,0:T(8,128)(2,1)}, bf16[1024,2048]{1,0:T(8,128)(2,1)}) custom-call(s32[4]{0:T(128)} %pad_add_fusion.place_ref, bf16[1024,1024]{1,0:T(8,128)(2,1)} %bitcast.414, bf16[1024,1024]{1,0:T(8,128)(2,1)} %leave.1.refs_1_, ...), custom_call_target="tpu_custom_call" | custom-call | flops 4294967296 | bytes 25198592 | tf_op jit(solution)/shard_map/widen/pallas_call | solution.py:298
  215.9 7.1 %convolution_convert_fusion.1 = bf16[2048,1024]{1,0:T(8,128)(2,1)S(1)} fusion(bf16[1024,2048]{1,0:T(8,128)(2,1)} %get-tuple-element.30.refs_0_, bf16[1024,1024]{1,0:T(8,128)(2,1)S(1)} %bitcast.401), kind=kOutput, calls=%fused_computation.1 | convolution fusion | flops 4297064448 | bytes 10485760 | tf_op jit(solution)/shard_map/dot_general | solution.py:23
  229.2 4.6 collective-permute-done.31.refs_18_
  234.9 4.9 collective-permute-done.39.refs_26_
  240.5 4.9 collective-permute-done.35.refs_22_
  246.1 21.4 %narrow.1 = (bf16[1024,1024]{1,0:T(8,128)(2,1)}, bf16[1024,2048]{1,0:T(8,128)(2,1)}, bf16[1024,1024]{1,0:T(8,128)(2,1)}) custom-call(s32[4]{0:T(128)} %pad_add_fusion.place_ref, bf16[1024,2048]{1,0:T(8,128)(2,1)} %get-tuple-element.30.refs_0_, bf16[1024,1024]{1,0:T(8,128)(2,1)} %bitcast.402, bf16[1024,2048]{1,0:T(8,128)(2,1)} %get-tuple-element.31.refs_2_, ...), custom_call_target="tpu_custom_call" | custom-call | flops 12884901888 | bytes 27262976 | tf_op jit(solution)/shard_map/narrow/pallas_call | solution.py:298
  268.8 3.9 collective-permute-start.44
  277.0 5.3 convolution_convert_fusion.2
  287.3 10.4 %collective-permute-done.78 = bf16[4,2,64,1024]{3,2,0,1:T(8,128)(2,1)S(1)} collective-permute-done((bf16[4,2,64,1024]{3,2,0,1:T(8,128)(2,1)}, bf16[4,2,64,1024]{3,2,0,1:T(8,128)(2,1)S(1)}, u32[]{:S(2)}, u32[]{:S(2)}) %collective-permute-start.78) | collective-permute-done | bytes 1048608 | tf_op jit(solution)/shard_map/ppermute | solution.py:43
  301.0 19.2 %collective-permute-done.69 = bf16[4,2,32,2048]{3,2,0,1:T(8,128)(2,1)S(1)} collective-permute-done((bf16[4,2,32,2048]{3,2,0,1:T(8,128)(2,1)S(1)}, bf16[4,2,32,2048]{3,2,0,1:T(8,128)(2,1)S(1)}, u32[]{:S(2)}, u32[]{:S(2)}) %collective-permute-start.69) | collective-permute-done | bytes 1048608 | tf_op jit(solution)/shard_map/ppermute | solution.py:43
  323.5 9.1 %collective-permute-done.79 = bf16[4,64,1024]{2,1,0:T(8,128)(2,1)S(1)} collective-permute-done((bf16[4,64,1024]{2,1,0:T(8,128)(2,1)S(1)}, bf16[4,64,1024]{2,1,0:T(8,128)(2,1)S(1)}, u32[]{:S(2)}, u32[]{:S(2)}) %collective-permute-start.79) | collective-permute-done | bytes 524320 | tf_op jit(solution)/shard_map/ppermute | solution.py:43
  333.0 9.7 %collective-permute-done.77 = bf16[4,64,1024]{2,1,0:T(8,128)(2,1)S(1)} collective-permute-done((bf16[4,64,1024]{2,1,0:T(8,128)(2,1)S(1)}, bf16[4,64,1024]{2,1,0:T(8,128)(2,1)S(1)}, u32[]{:S(2)}, u32[]{:S(2)}) %collective-permute-start.77) | collective-permute-done | bytes 524320 | tf_op jit(solution)/shard_map/ppermute | solution.py:43
  343.0 2.3 collective-permute-start.80
  346.7 7.2 %collective-permute-done.68 = bf16[4,32,2048]{2,1,0:T(8,128)(2,1)S(1)} collective-permute-done((bf16[4,32,2048]{2,1,0:T(8,128)(2,1)S(1)}, bf16[4,32,2048]{2,1,0:T(8,128)(2,1)S(1)}, u32[]{:S(2)}, u32[]{:S(2)}) %collective-permute-start.68) | collective-permute-done | bytes 524320 | tf_op jit(solution)/shard_map/ppermute | solution.py:43
  356.5 4.0 collective-permute-start.72
  360.5 5.9 collective-permute-done.81
  367.5 13.6 %collective-permute-done.82 = bf16[2,64,1024]{2,1,0:T(8,128)(2,1)S(1)} collective-permute-done((bf16[2,64,1024]{2,1,0:T(8,128)(2,1)S(1)}, bf16[2,64,1024]{2,1,0:T(8,128)(2,1)S(1)}, u32[]{:S(2)}, u32[]{:S(2)}) %collective-permute-start.82) | collective-permute-done | bytes 262176 | tf_op jit(solution)/shard_map/ppermute | solution.py:266
  382.1 6.8 %collective-permute-done.72 = bf16[2,32,2048]{2,1,0:T(8,128)(2,1)S(1)} collective-permute-done((bf16[2,32,2048]{2,1,0:T(8,128)(2,1)S(1)}, bf16[2,32,2048]{2,1,0:T(8,128)(2,1)S(1)}, u32[]{:S(2)}, u32[]{:S(2)}) %collective-permute-start.72) | collective-permute-done | bytes 262176 | tf_op jit(solution)/shard_map/ppermute | solution.py:266
  388.9 3.5 collective-permute-done.73
  394.6 5.3 collective-permute-done.74
  401.6 11.1 %between.1 = (f32[1024,1024]{1,0:T(8,128)}, bf16[1024,1024]{1,0:T(8,128)(2,1)}, bf16[1024,512]{1,0:T(8,128)(2,1)}, f32[8,1024]{1,0:T(8,128)}) custom-call(s32[4]{0:T(128)} %pad_add_fusion.place_ref, bf16[1024,1024]{1,0:T(8,128)(2,1)} %bitcast.403, bf16[1024,1024]{1,0:T(8,128)(2,1)} %get-tuple-element.33.refs_1_, ...), custom_call_target="tpu_custom_call" | custom-call | flops 1073741824 | bytes 22347776 | tf_op jit(solution)/shard_map/between/pallas_call | solution.py:298
  412.8 3.0 convolution_convert_fusion.3
  415.8 30.1 %attend_back.1.refs_0_ = bf16[1024,1536]{1,0:T(8,128)(2,1)} custom-call(bf16[1024,1536]{1,0:T(8,128)(2,1)} %get-tuple-element.26.q_ref.k_ref.v_ref, bf16[1024,1536]{1,0:T(8,128)(2,1)} %get-tuple-element.26.q_ref.k_ref.v_ref, bf16[1024,1536]{1,0:T(8,128)(2,1)} %get-tuple-element.26.q_ref.k_ref.v_ref, bf16[1024,512]{1,0:T(8,128)(2,1)S(1)} %copy-done.7, ...), custom_call_target="tpu_custom_call" | custom-call | tf_op jit(solution)/shard_map/attend_back/pallas_call | solution.py:173
  445.9 5.6 convolution_convert_fusion
  456.1 8.6 %enter.1 = bf16[1024,1024]{1,0:T(8,128)(2,1)} custom-call(s32[4]{0:T(128)} %pad_add_fusion.place_ref, bf16[1024,1536]{1,0:T(8,128)(2,1)} %attend_back.1.refs_0_, bf16[2,64,2176]{2,1,0:T(8,128)(2,1)} %copy-done.12, bf16[2,64,2176]{2,1,0:T(8,128)(2,1)} %copy-done.25, bf16[64,2176]{1,0:T(8,128)(2,1)} %collective-permute-done.3.refs_3_.refs_7_, ...), custom_call_target="tpu_custom_call" | custom-call | flops 3221225472 | bytes 9699328 | tf_op jit(solution)/shard_map/enter/pallas_call | solution.py:298
  466.9 3.4 collective-permute-done.61
  476.6 3.0 collective-permute-start.47
  482.9 10.5 %collective-permute-done.65 = bf16[2,16,1024]{2,1,0:T(8,128)(2,1)S(1)} collective-permute-done((bf16[2,16,1024]{2,1,0:T(8,128)(2,1)S(1)}, bf16[2,16,1024]{2,1,0:T(8,128)(2,1)S(1)}, u32[]{:S(2)}, u32[]{:S(2)}) %collective-permute-start.65) | collective-permute-done | bytes 65568 | tf_op jit(solution)/shard_map/ppermute | solution.py:43
  493.5 3.3 collective-permute-start.66
  498.8 3.0 copy.141
  507.1 2.6 fusion.10
  509.8 5.1 collective-permute-done.52
  515.0 2.3 collective-permute-done.50
  518.7 3.0 collective-permute-start.54
  521.7 2.1 fusion.9
  523.8 11.1 %collective-permute-done.54 = bf16[2,32,1536]{2,1,0:T(8,128)(2,1)S(1)} collective-permute-done((bf16[2,32,1536]{2,1,0:T(8,128)(2,1)S(1)}, bf16[2,32,1536]{2,1,0:T(8,128)(2,1)S(1)}, u32[]{:S(2)}, u32[]{:S(2)}) %collective-permute-start.54) | collective-permute-done | bytes 196640 | tf_op jit(solution)/shard_map/ppermute | solution.py:266
  534.9 3.1 collective-permute-done.55
  540.5 46.7 %psum.7 = f32[4,8,128]{2,1,0:T(8,128)S(1)} all-reduce(f32[4,8,128]{2,1,0:T(8,128)S(1)} %bitcast.432), channel_id=1, replica_groups=mesh['hi'=2,'lo'=2,'fz'=4,'fx'=2] {'hi','lo','fz','fx'}, use_global_device_ids=true, to_apply=%region_6.7 | all-reduce | flops 4096 | bytes 32768 | tf_op jit(solution)/shard_map/psum | solution.py:696
  (386 shorter events, 125.9 us)
Async XLA Ops:
  2.7 13.1 %collective-permute-start = (bf16[256,1024]{1,0:T(8,128)(2,1)}, bf16[256,1024]{1,0:T(8,128)(2,1)}, u32[]{:S(2)}, u32[]{:S(2)}) collective-permute-start(bf16[256,1024]{1,0:T(8,128)(2,1)} %dynamic-slice_bitcast_fusion.8), channel_id=1, source_target_pairs={{0,16},{16,0},{1,17},{17,1},{2,18},{18,2},{3,19},{19,3},{4,20},{20... | collective-permute-start | bytes 1572872 | tf_op jit(solution)/shard_map/ppermute | solution.py:43
  7.9 16.3 %collective-permute-start.11 = (bf16[64,2176]{1,0:T(8,128)(2,1)}, bf16[64,2176]{1,0:T(8,128)(2,1)S(1)}, u32[]{:S(2)}, u32[]{:S(2)}) collective-permute-start(bf16[64,2176]{1,0:T(8,128)(2,1)} %dynamic-slice_bitcast_fusion.11), channel_id=1, source_target_pairs={{0,6},{2,0},{4,2},{6,4},{1,7},{3,1},{5,3},{7,5},{8,14},{10,8},{12,... | collective-permute-start | bytes 835592 | tf_op jit(solution)/shard_map/ppermute | solution.py:202
  18.3 38.6 %collective-permute-start.1 = (bf16[2,256,1024]{2,1,0:T(8,128)(2,1)}, bf16[2,256,1024]{2,1,0:T(8,128)(2,1)}, u32[]{:S(2)}, u32[]{:S(2)}) collective-permute-start(bf16[2,256,1024]{2,1,0:T(8,128)(2,1)} %pad_maximum_fusion.2), channel_id=1, source_target_pairs={{0,8},{8,0},{1,9},{9,1},{2,10},{10,2},{3,11},{11,3},{4,12},{12,4},... | collective-permute-start | bytes 3145736 | tf_op jit(solution)/shard_map/ppermute | solution.py:43
  20.6 23.3 %collective-permute-start.29 = (bf16[256,1024]{1,0:T(8,128)(2,1)}, bf16[256,1024]{1,0:T(8,128)(2,1)}, u32[]{:S(2)}, u32[]{:S(2)}) collective-permute-start(bf16[256,1024]{1,0:T(8,128)(2,1)} %dynamic-slice_bitcast_fusion.7), channel_id=1, source_target_pairs={{0,16},{16,0},{1,17},{17,1},{2,18},{18,2},{3,19},{19,3},{4,20},{20... | collective-permute-start | bytes 1572872 | tf_op jit(solution)/shard_map/ppermute | solution.py:43
  21.9 14.9 %collective-permute-start.7 = (bf16[64,2176]{1,0:T(8,128)(2,1)}, bf16[64,2176]{1,0:T(8,128)(2,1)}, u32[]{:S(2)}, u32[]{:S(2)}) collective-permute-start(bf16[64,2176]{1,0:T(8,128)(2,1)} %dynamic-slice_bitcast_fusion.11), channel_id=1, source_target_pairs={{0,4},{2,6},{4,0},{6,2},{1,5},{3,7},{5,1},{7,3},{8,12},{10,14},{12... | collective-permute-start | bytes 835592 | tf_op jit(solution)/shard_map/ppermute | solution.py:202
  24.2 18.5 %collective-permute-start.3 = (bf16[64,2176]{1,0:T(8,128)(2,1)}, bf16[64,2176]{1,0:T(8,128)(2,1)}, u32[]{:S(2)}, u32[]{:S(2)}) collective-permute-start(bf16[64,2176]{1,0:T(8,128)(2,1)} %dynamic-slice_bitcast_fusion.11), channel_id=1, source_target_pairs={{0,2},{2,4},{4,6},{6,0},{1,3},{3,5},{5,7},{7,1},{8,10},{10,12},{12... | collective-permute-start | bytes 835592 | tf_op jit(solution)/shard_map/ppermute | solution.py:202
  24.2 20.0 %collective-permute-start.13 = (bf16[64,2176]{1,0:T(8,128)(2,1)S(1)}, bf16[64,2176]{1,0:T(8,128)(2,1)S(1)}, u32[]{:S(2)}, u32[]{:S(2)}) collective-permute-start(bf16[64,2176]{1,0:T(8,128)(2,1)S(1)} %collective-permute-done.11.refs_11_.refs_15_), channel_id=1, source_target_pairs={{0,1},{1,0},{2,3},{3,2},{4,5},{5,4},{6,7},{7,6},{8,9},{9,8},{10,11... | collective-permute-start | bytes 835592 | tf_op jit(solution)/shard_map/ppermute | solution.py:43
  44.9 11.8 %collective-permute-start.5 = (bf16[64,2176]{1,0:T(8,128)(2,1)}, bf16[64,2176]{1,0:T(8,128)(2,1)S(1)}, u32[]{:S(2)}, u32[]{:S(2)}) collective-permute-start(bf16[64,2176]{1,0:T(8,128)(2,1)} %collective-permute-done.3.refs_3_.refs_7_), channel_id=1, source_target_pairs={{0,1},{1,0},{2,3},{3,2},{4,5},{5,4},{6,7},{7,6},{8,9},{9,8},{10,11... | collective-permute-start | bytes 835592 | tf_op jit(solution)/shard_map/ppermute | solution.py:43
  46.5 22.1 %collective-permute-start.2 = (bf16[2,64,2176]{2,1,0:T(8,128)(2,1)S(1)}, bf16[2,64,2176]{2,1,0:T(8,128)(2,1)S(1)}, u32[]{:S(2)}, u32[]{:S(2)}) collective-permute-start(bf16[2,64,2176]{2,1,0:T(8,128)(2,1)S(1)} %pad_maximum_fusion.6.refs_1_.refs_5_), channel_id=1, source_target_pairs={{0,1},{1,0},{2,3},{3,2},{4,5},{5,4},{6,7},{7,6},{8,9},{9,8},{10,11... | collective-permute-start | bytes 1671176 | tf_op jit(solution)/shard_map/ppermute | solution.py:43
  50.7 11.4 %collective-permute-start.4 = (bf16[64,2176]{1,0:T(8,128)(2,1)}, bf16[64,2176]{1,0:T(8,128)(2,1)S(1)}, u32[]{:S(2)}, u32[]{:S(2)}) collective-permute-start(bf16[64,2176]{1,0:T(8,128)(2,1)} %collective-permute-done.3.refs_3_.refs_7_), channel_id=1, source_target_pairs={{0,16},{16,0},{1,17},{17,1},{2,18},{18,2},{3,19},{19,3},{4,20},{20... | collective-permute-start | bytes 835592 | tf_op jit(solution)/shard_map/ppermute | solution.py:43
  51.6 17.0 %collective-permute-start.14 = (bf16[64,2176]{1,0:T(8,128)(2,1)S(1)}, bf16[64,2176]{1,0:T(8,128)(2,1)S(1)}, u32[]{:S(2)}, u32[]{:S(2)}) collective-permute-start(bf16[64,2176]{1,0:T(8,128)(2,1)S(1)} %copy-done.33), channel_id=1, source_target_pairs={{0,16},{16,0},{1,17},{17,1},{2,18},{18,2},{3,19},{19,3},{4,20},{20... | collective-permute-start | bytes 835592 | tf_op jit(solution)/shard_map/ppermute | solution.py:43
  56.7 12.1 %collective-permute-start.10 = (bf16[64,2176]{1,0:T(8,128)(2,1)S(1)}, bf16[64,2176]{1,0:T(8,128)(2,1)S(1)}, u32[]{:S(2)}, u32[]{:S(2)}) collective-permute-start(bf16[64,2176]{1,0:T(8,128)(2,1)S(1)} %collective-permute-done.9.refs_9_.refs_13_), channel_id=1, source_target_pairs={{0,16},{16,0},{1,17},{17,1},{2,18},{18,2},{3,19},{19,3},{4,20},{20... | collective-permute-start | bytes 835592 | tf_op jit(solution)/shard_map/ppermute | solution.py:43
  56.9 17.8 %collective-permute-start.6 = (bf16[64,2176]{1,0:T(8,128)(2,1)S(1)}, bf16[64,2176]{1,0:T(8,128)(2,1)S(1)}, u32[]{:S(2)}, u32[]{:S(2)}) collective-permute-start(bf16[64,2176]{1,0:T(8,128)(2,1)S(1)} %collective-permute-done.5.refs_5_.refs_9_), channel_id=1, source_target_pairs={{0,16},{16,0},{1,17},{17,1},{2,18},{18,2},{3,19},{19,3},{4,20},{20... | collective-permute-start | bytes 835592 | tf_op jit(solution)/shard_map/ppermute | solution.py:43
  62.1 98.0 %collective-permute-start.30 = (bf16[2,256,1024]{2,1,0:T(8,128)(2,1)}, bf16[2,256,1024]{2,1,0:T(8,128)(2,1)}, u32[]{:S(2)}, u32[]{:S(2)}) collective-permute-start(bf16[2,256,1024]{2,1,0:T(8,128)(2,1)} %pad_maximum_fusion.3), channel_id=1, source_target_pairs={{0,8},{8,0},{1,9},{9,1},{2,10},{10,2},{3,11},{11,3},{4,12},{12,4},... | collective-permute-start | bytes 3145736 | tf_op jit(solution)/shard_map/ppermute | solution.py:43
  112.1 83.9 %collective-permute-start.15 = (bf16[1024,1024]{1,0:T(8,128)(2,1)}, bf16[1024,1024]{1,0:T(8,128)(2,1)}, u32[]{:S(2)}, u32[]{:S(2)}) collective-permute-start(bf16[1024,1024]{1,0:T(8,128)(2,1)} %leave.1.refs_1_), channel_id=1, source_target_pairs={{0,8},{8,0},{1,9},{9,1},{2,10},{10,2},{3,11},{11,3},{4,12},{12,4},... | collective-permute-start | bytes 6291464 | tf_op jit(solution)/shard_map/ppermute | solution.py:43
  116.1 14.7 %collective-permute-start.40 = (bf16[128,1024]{1,0:T(8,128)(2,1)S(1)}, bf16[128,1024]{1,0:T(8,128)(2,1)}, u32[]{:S(2)}, u32[]{:S(2)}) collective-permute-start(bf16[128,1024]{1,0:T(8,128)(2,1)S(1)} %dynamic-slice_bitcast_fusion.12), channel_id=1, source_target_pairs={{0,6},{2,0},{4,2},{6,4},{1,7},{3,1},{5,3},{7,5},{8,14},{10,8},{12,... | collective-permute-start | bytes 786440 | tf_op jit(solution)/shard_map/ppermute | solution.py:202
  120.4 17.1 %collective-permute-start.36 = (bf16[128,1024]{1,0:T(8,128)(2,1)S(1)}, bf16[128,1024]{1,0:T(8,128)(2,1)}, u32[]{:S(2)}, u32[]{:S(2)}) collective-permute-start(bf16[128,1024]{1,0:T(8,128)(2,1)S(1)} %dynamic-slice_bitcast_fusion.12), channel_id=1, source_target_pairs={{0,4},{2,6},{4,0},{6,2},{1,5},{3,7},{5,1},{7,3},{8,12},{10,14},{12... | collective-permute-start | bytes 786440 | tf_op jit(solution)/shard_map/ppermute | solution.py:202
  120.4 33.9 %collective-permute-start.32 = (bf16[128,1024]{1,0:T(8,128)(2,1)S(1)}, bf16[128,1024]{1,0:T(8,128)(2,1)}, u32[]{:S(2)}, u32[]{:S(2)}) collective-permute-start(bf16[128,1024]{1,0:T(8,128)(2,1)S(1)} %dynamic-slice_bitcast_fusion.12), channel_id=1, source_target_pairs={{0,2},{2,4},{4,6},{6,0},{1,3},{3,5},{5,7},{7,1},{8,10},{10,12},{12... | collective-permute-start | bytes 786440 | tf_op jit(solution)/shard_map/ppermute | solution.py:202
  130.8 28.0 %collective-permute-start.25 = (bf16[64,2048]{1,0:T(8,128)(2,1)S(1)}, bf16[64,2048]{1,0:T(8,128)(2,1)S(1)}, u32[]{:S(2)}, u32[]{:S(2)}) collective-permute-start(bf16[64,2048]{1,0:T(8,128)(2,1)S(1)} %dynamic-slice_bitcast_fusion.13), channel_id=1, source_target_pairs={{0,6},{2,0},{4,2},{6,4},{1,7},{3,1},{5,3},{7,5},{8,14},{10,8},{12,... | collective-permute-start | bytes 786440 | tf_op jit(solution)/shard_map/ppermute | solution.py:202
  137.5 24.2 %collective-permute-start.21 = (bf16[64,2048]{1,0:T(8,128)(2,1)S(1)}, bf16[64,2048]{1,0:T(8,128)(2,1)S(1)}, u32[]{:S(2)}, u32[]{:S(2)}) collective-permute-start(bf16[64,2048]{1,0:T(8,128)(2,1)S(1)} %dynamic-slice_bitcast_fusion.13), channel_id=1, source_target_pairs={{0,4},{2,6},{4,0},{6,2},{1,5},{3,7},{5,1},{7,3},{8,12},{10,14},{12... | collective-permute-start | bytes 786440 | tf_op jit(solution)/shard_map/ppermute | solution.py:202
  154.3 11.3 %collective-permute-start.17 = (bf16[64,2048]{1,0:T(8,128)(2,1)S(1)}, bf16[64,2048]{1,0:T(8,128)(2,1)S(1)}, u32[]{:S(2)}, u32[]{:S(2)}) collective-permute-start(bf16[64,2048]{1,0:T(8,128)(2,1)S(1)} %dynamic-slice_bitcast_fusion.13), channel_id=1, source_target_pairs={{0,2},{2,4},{4,6},{6,0},{1,3},{3,5},{5,7},{7,1},{8,10},{10,12},{12... | collective-permute-start | bytes 786440 | tf_op jit(solution)/shard_map/ppermute | solution.py:202
  166.0 11.1 %collective-permute-start.19 = (bf16[64,2048]{1,0:T(8,128)(2,1)S(1)}, bf16[64,2048]{1,0:T(8,128)(2,1)S(1)}, u32[]{:S(2)}, u32[]{:S(2)}) collective-permute-start(bf16[64,2048]{1,0:T(8,128)(2,1)S(1)} %collective-permute-done.17.refs_6_.refs_5_), channel_id=1, source_target_pairs={{0,1},{1,0},{2,3},{3,2},{4,5},{5,4},{6,7},{7,6},{8,9},{9,8},{10,11... | collective-permute-start | bytes 786440 | tf_op jit(solution)/shard_map/ppermute | solution.py:43
  167.1 11.8 %collective-permute-start.18 = (bf16[64,2048]{1,0:T(8,128)(2,1)S(1)}, bf16[64,2048]{1,0:T(8,128)(2,1)S(1)}, u32[]{:S(2)}, u32[]{:S(2)}) collective-permute-start(bf16[64,2048]{1,0:T(8,128)(2,1)S(1)} %collective-permute-done.17.refs_6_.refs_5_), channel_id=1, source_target_pairs={{0,16},{16,0},{1,17},{17,1},{2,18},{18,2},{3,19},{19,3},{4,20},{20... | collective-permute-start | bytes 786440 | tf_op jit(solution)/shard_map/ppermute | solution.py:43
  171.5 16.8 %collective-permute-start.16 = (bf16[2,64,2048]{2,1,0:T(8,128)(2,1)S(1)}, bf16[2,64,2048]{2,1,0:T(8,128)(2,1)S(1)}, u32[]{:S(2)}, u32[]{:S(2)}) collective-permute-start(bf16[2,64,2048]{2,1,0:T(8,128)(2,1)S(1)} %copy-done.28), channel_id=1, source_target_pairs={{0,1},{1,0},{2,3},{3,2},{4,5},{5,4},{6,7},{7,6},{8,9},{9,8},{10,11... | collective-permute-start | bytes 1572872 | tf_op jit(solution)/shard_map/ppermute | solution.py:43
  173.3 16.3 %collective-permute-start.28 = (bf16[64,2048]{1,0:T(8,128)(2,1)S(1)}, bf16[64,2048]{1,0:T(8,128)(2,1)S(1)}, u32[]{:S(2)}, u32[]{:S(2)}) collective-permute-start(bf16[64,2048]{1,0:T(8,128)(2,1)S(1)} %collective-permute-done.27.refs_16_.refs_15_), channel_id=1, source_target_pairs={{0,16},{16,0},{1,17},{17,1},{2,18},{18,2},{3,19},{19,3},{4,20},{20... | collective-permute-start | bytes 786440 | tf_op jit(solution)/shard_map/ppermute | solution.py:43
  177.1 13.0 %collective-permute-start.24 = (bf16[64,2048]{1,0:T(8,128)(2,1)S(1)}, bf16[64,2048]{1,0:T(8,128)(2,1)S(1)}, u32[]{:S(2)}, u32[]{:S(2)}) collective-permute-start(bf16[64,2048]{1,0:T(8,128)(2,1)S(1)} %collective-permute-done.23.refs_12_.refs_11_), channel_id=1, source_target_pairs={{0,16},{16,0},{1,17},{17,1},{2,18},{18,2},{3,19},{19,3},{4,20},{20... | collective-permute-start | bytes 786440 | tf_op jit(solution)/shard_map/ppermute | solution.py:43
  178.9 17.0 %collective-permute-start.20 = (bf16[64,2048]{1,0:T(8,128)(2,1)S(1)}, bf16[64,2048]{1,0:T(8,128)(2,1)S(1)}, u32[]{:S(2)}, u32[]{:S(2)}) collective-permute-start(bf16[64,2048]{1,0:T(8,128)(2,1)S(1)} %collective-permute-done.19.refs_8_.refs_7_), channel_id=1, source_target_pairs={{0,16},{16,0},{1,17},{17,1},{2,18},{18,2},{3,19},{19,3},{4,20},{20... | collective-permute-start | bytes 786440 | tf_op jit(solution)/shard_map/ppermute | solution.py:43
  188.3 34.7 %collective-permute-start.42 = (bf16[128,1024]{1,0:T(8,128)(2,1)}, bf16[128,1024]{1,0:T(8,128)(2,1)}, u32[]{:S(2)}, u32[]{:S(2)}) collective-permute-start(bf16[128,1024]{1,0:T(8,128)(2,1)} %collective-permute-done.40.refs_27_), channel_id=1, source_target_pairs={{0,1},{1,0},{2,3},{3,2},{4,5},{5,4},{6,7},{7,6},{8,9},{9,8},{10,11... | collective-permute-start | bytes 786440 | tf_op jit(solution)/shard_map/ppermute | solution.py:43
  189.6 33.9 %collective-permute-start.41 = (bf16[128,1024]{1,0:T(8,128)(2,1)}, bf16[128,1024]{1,0:T(8,128)(2,1)S(1)}, u32[]{:S(2)}, u32[]{:S(2)}) collective-permute-start(bf16[128,1024]{1,0:T(8,128)(2,1)} %collective-permute-done.40.refs_27_), channel_id=1, source_target_pairs={{0,16},{16,0},{1,17},{17,1},{2,18},{18,2},{3,19},{19,3},{4,20},{20... | collective-permute-start | bytes 786440 | tf_op jit(solution)/shard_map/ppermute | solution.py:43
  190.1 34.7 %collective-permute-start.38 = (bf16[128,1024]{1,0:T(8,128)(2,1)}, bf16[128,1024]{1,0:T(8,128)(2,1)}, u32[]{:S(2)}, u32[]{:S(2)}) collective-permute-start(bf16[128,1024]{1,0:T(8,128)(2,1)} %collective-permute-done.36.refs_23_), channel_id=1, source_target_pairs={{0,1},{1,0},{2,3},{3,2},{4,5},{5,4},{6,7},{7,6},{8,9},{9,8},{10,11... | collective-permute-start | bytes 786440 | tf_op jit(solution)/shard_map/ppermute | solution.py:43
  195.8 29.1 %collective-permute-start.37 = (bf16[128,1024]{1,0:T(8,128)(2,1)}, bf16[128,1024]{1,0:T(8,128)(2,1)S(1)}, u32[]{:S(2)}, u32[]{:S(2)}) collective-permute-start(bf16[128,1024]{1,0:T(8,128)(2,1)} %collective-permute-done.36.refs_23_), channel_id=1, source_target_pairs={{0,16},{16,0},{1,17},{17,1},{2,18},{18,2},{3,19},{19,3},{4,20},{20... | collective-permute-start | bytes 786440 | tf_op jit(solution)/shard_map/ppermute | solution.py:43
  196.0 30.2 %collective-permute-start.34 = (bf16[128,1024]{1,0:T(8,128)(2,1)}, bf16[128,1024]{1,0:T(8,128)(2,1)}, u32[]{:S(2)}, u32[]{:S(2)}) collective-permute-start(bf16[128,1024]{1,0:T(8,128)(2,1)} %collective-permute-done.32.refs_19_), channel_id=1, source_target_pairs={{0,1},{1,0},{2,3},{3,2},{4,5},{5,4},{6,7},{7,6},{8,9},{9,8},{10,11... | collective-permute-start | bytes 786440 | tf_op jit(solution)/shard_map/ppermute | solution.py:43
  225.0 14.8 %collective-permute-start.39 = (bf16[128,1024]{1,0:T(8,128)(2,1)}, bf16[128,1024]{1,0:T(8,128)(2,1)S(1)}, u32[]{:S(2)}, u32[]{:S(2)}) collective-permute-start(bf16[128,1024]{1,0:T(8,128)(2,1)} %collective-permute-done.38.refs_25_), channel_id=1, source_target_pairs={{0,16},{16,0},{1,17},{17,1},{2,18},{18,2},{3,19},{19,3},{4,20},{20... | collective-permute-start | bytes 786440 | tf_op jit(solution)/shard_map/ppermute | solution.py:43
  226.2 19.1 %collective-permute-start.35 = (bf16[128,1024]{1,0:T(8,128)(2,1)}, bf16[128,1024]{1,0:T(8,128)(2,1)S(1)}, u32[]{:S(2)}, u32[]{:S(2)}) collective-permute-start(bf16[128,1024]{1,0:T(8,128)(2,1)} %collective-permute-done.34.refs_21_), channel_id=1, source_target_pairs={{0,16},{16,0},{1,17},{17,1},{2,18},{18,2},{3,19},{19,3},{4,20},{20... | collective-permute-start | bytes 786440 | tf_op jit(solution)/shard_map/ppermute | solution.py:43
  268.8 16.0 %collective-permute-start.44 = (bf16[2,256,1024]{2,1,0:T(8,128)(2,1)S(1)}, bf16[2,256,1024]{2,1,0:T(8,128)(2,1)S(1)}, u32[]{:S(2)}, u32[]{:S(2)}) collective-permute-start(bf16[2,256,1024]{2,1,0:T(8,128)(2,1)S(1)} %dynamic-slice_bitcast_fusion.1), channel_id=1, source_target_pairs={{0,8},{8,0},{1,9},{9,1},{2,10},{10,2},{3,11},{11,3},{4,12},{12,4},... | collective-permute-start | bytes 3145736 | tf_op jit(solution)/shard_map/ppermute | solution.py:43
  272.8 24.9 %collective-permute-start.78 = (bf16[4,2,64,1024]{3,2,0,1:T(8,128)(2,1)}, bf16[4,2,64,1024]{3,2,0,1:T(8,128)(2,1)S(1)}, u32[]{:S(2)}, u32[]{:S(2)}) collective-permute-start(bf16[4,2,64,1024]{3,2,0,1:T(8,128)(2,1)} %bitcast.389), channel_id=1, source_target_pairs={{0,16},{16,0},{1,17},{17,1},{2,18},{18,2},{3,19},{19,3},{4,20},{20... | collective-permute-start | bytes 3145736 | tf_op jit(solution)/shard_map/ppermute | solution.py:43
  274.4 25.1 %collective-permute-start.76 = (bf16[4,2,64,1024]{3,2,0,1:T(8,128)(2,1)S(1)}, bf16[4,2,64,1024]{3,2,0,1:T(8,128)(2,1)S(1)}, u32[]{:S(2)}, u32[]{:S(2)}) collective-permute-start(bf16[4,2,64,1024]{3,2,0,1:T(8,128)(2,1)S(1)} %bitcast.422), channel_id=1, source_target_pairs={{0,1},{1,0},{2,3},{3,2},{4,5},{5,4},{6,7},{7,6},{8,9},{9,8},{10,11... | collective-permute-start | bytes 3145736 | tf_op jit(solution)/shard_map/ppermute | solution.py:43
  283.2 37.0 %collective-permute-start.69 = (bf16[4,2,32,2048]{3,2,0,1:T(8,128)(2,1)S(1)}, bf16[4,2,32,2048]{3,2,0,1:T(8,128)(2,1)S(1)}, u32[]{:S(2)}, u32[]{:S(2)}) collective-permute-start(bf16[4,2,32,2048]{3,2,0,1:T(8,128)(2,1)S(1)} %bitcast.424), channel_id=1, source_target_pairs={{0,16},{16,0},{1,17},{17,1},{2,18},{18,2},{3,19},{19,3},{4,20},{20... | collective-permute-start | bytes 3145736 | tf_op jit(solution)/shard_map/ppermute | solution.py:43
  283.7 38.2 %collective-permute-start.67 = (bf16[4,2,32,2048]{3,2,0,1:T(8,128)(2,1)S(1)}, bf16[4,2,32,2048]{3,2,0,1:T(8,128)(2,1)S(1)}, u32[]{:S(2)}, u32[]{:S(2)}) collective-permute-start(bf16[4,2,32,2048]{3,2,0,1:T(8,128)(2,1)S(1)} %bitcast.423), channel_id=1, source_target_pairs={{0,1},{1,0},{2,3},{3,2},{4,5},{5,4},{6,7},{7,6},{8,9},{9,8},{10,11... | collective-permute-start | bytes 3145736 | tf_op jit(solution)/shard_map/ppermute | solution.py:43
  284.9 116.7 %collective-permute-start.46 = (bf16[1024,1024]{1,0:T(8,128)(2,1)S(1)}, bf16[1024,1024]{1,0:T(8,128)(2,1)}, u32[]{:S(2)}, u32[]{:S(2)}) collective-permute-start(bf16[1024,1024]{1,0:T(8,128)(2,1)S(1)} %copy-done.27), channel_id=1, source_target_pairs={{0,8},{8,0},{1,9},{9,1},{2,10},{10,2},{3,11},{11,3},{4,12},{12,4},... | collective-permute-start | bytes 6291464 | tf_op jit(solution)/shard_map/ppermute | solution.py:43
  297.7 57.6 %collective-permute-start.45 = (bf16[256,1024]{1,0:T(8,128)(2,1)S(1)}, bf16[256,1024]{1,0:T(8,128)(2,1)S(1)}, u32[]{:S(2)}, u32[]{:S(2)}) collective-permute-start(bf16[256,1024]{1,0:T(8,128)(2,1)S(1)} %dynamic-slice_bitcast_fusion.6), channel_id=1, source_target_pairs={{0,16},{16,0},{1,17},{17,1},{2,18},{18,2},{3,19},{19,3},{4,20},{20... | collective-permute-start | bytes 1572872 | tf_op jit(solution)/shard_map/ppermute | solution.py:43
  299.5 33.1 %collective-permute-start.79 = (bf16[4,64,1024]{2,1,0:T(8,128)(2,1)S(1)}, bf16[4,64,1024]{2,1,0:T(8,128)(2,1)S(1)}, u32[]{:S(2)}, u32[]{:S(2)}) collective-permute-start(bf16[4,64,1024]{2,1,0:T(8,128)(2,1)S(1)} %dynamic-slice_bitcast_fusion.2), channel_id=1, source_target_pairs={{0,1},{1,0},{2,3},{3,2},{4,5},{5,4},{6,7},{7,6},{8,9},{9,8},{10,11... | collective-permute-start | bytes 1572872 | tf_op jit(solution)/shard_map/ppermute | solution.py:43
  320.2 22.5 %collective-permute-start.77 = (bf16[4,64,1024]{2,1,0:T(8,128)(2,1)S(1)}, bf16[4,64,1024]{2,1,0:T(8,128)(2,1)S(1)}, u32[]{:S(2)}, u32[]{:S(2)}) collective-permute-start(bf16[4,64,1024]{2,1,0:T(8,128)(2,1)S(1)} %dynamic-slice_bitcast_fusion.3), channel_id=1, source_target_pairs={{0,16},{16,0},{1,17},{17,1},{2,18},{18,2},{3,19},{19,3},{4,20},{20... | collective-permute-start | bytes 1572872 | tf_op jit(solution)/shard_map/ppermute | solution.py:43
  322.0 23.3 %collective-permute-start.70 = (bf16[4,32,2048]{2,1,0:T(8,128)(2,1)S(1)}, bf16[4,32,2048]{2,1,0:T(8,128)(2,1)S(1)}, u32[]{:S(2)}, u32[]{:S(2)}) collective-permute-start(bf16[4,32,2048]{2,1,0:T(8,128)(2,1)S(1)} %dynamic-slice_bitcast_fusion.4), channel_id=1, source_target_pairs={{0,1},{1,0},{2,3},{3,2},{4,5},{5,4},{6,7},{7,6},{8,9},{9,8},{10,11... | collective-permute-start | bytes 1572872 | tf_op jit(solution)/shard_map/ppermute | solution.py:43
  332.6 21.3 %collective-permute-start.68 = (bf16[4,32,2048]{2,1,0:T(8,128)(2,1)S(1)}, bf16[4,32,2048]{2,1,0:T(8,128)(2,1)S(1)}, u32[]{:S(2)}, u32[]{:S(2)}) collective-permute-start(bf16[4,32,2048]{2,1,0:T(8,128)(2,1)S(1)} %dynamic-slice_bitcast_fusion.5), channel_id=1, source_target_pairs={{0,16},{16,0},{1,17},{17,1},{2,18},{18,2},{3,19},{19,3},{4,20},{20... | collective-permute-start | bytes 1572872 | tf_op jit(solution)/shard_map/ppermute | solution.py:43
  343.0 13.5 %collective-permute-start.80 = (bf16[2,64,1024]{2,1,0:T(8,128)(2,1)S(1)}, bf16[2,64,1024]{2,1,0:T(8,128)(2,1)S(1)}, u32[]{:S(2)}, u32[]{:S(2)}) collective-permute-start(bf16[2,64,1024]{2,1,0:T(8,128)(2,1)S(1)} %get-tuple-element.120), channel_id=1, source_target_pairs={{0,2},{2,4},{4,6},{6,0},{1,3},{3,5},{5,7},{7,1},{8,10},{10,12},{12... | collective-permute-start | bytes 786440 | tf_op jit(solution)/shard_map/ppermute | solution.py:266
  345.3 21.1 %collective-permute-start.81 = (bf16[2,64,1024]{2,1,0:T(8,128)(2,1)S(1)}, bf16[2,64,1024]{2,1,0:T(8,128)(2,1)S(1)}, u32[]{:S(2)}, u32[]{:S(2)}) collective-permute-start(bf16[2,64,1024]{2,1,0:T(8,128)(2,1)S(1)} %get-tuple-element.121), channel_id=1, source_target_pairs={{0,4},{2,6},{4,0},{6,2},{1,5},{3,7},{5,1},{7,3},{8,12},{10,14},{12... | collective-permute-start | bytes 786440 | tf_op jit(solution)/shard_map/ppermute | solution.py:266
  353.9 27.2 %collective-permute-start.82 = (bf16[2,64,1024]{2,1,0:T(8,128)(2,1)S(1)}, bf16[2,64,1024]{2,1,0:T(8,128)(2,1)S(1)}, u32[]{:S(2)}, u32[]{:S(2)}) collective-permute-start(bf16[2,64,1024]{2,1,0:T(8,128)(2,1)S(1)} %get-tuple-element.122), channel_id=1, source_target_pairs={{0,6},{2,0},{4,2},{6,4},{1,7},{3,1},{5,3},{7,5},{8,14},{10,8},{12,... | collective-permute-start | bytes 786440 | tf_op jit(solution)/shard_map/ppermute | solution.py:266
  355.3 26.8 %collective-permute-start.71 = (bf16[2,32,2048]{2,1,0:T(8,128)(2,1)S(1)}, bf16[2,32,2048]{2,1,0:T(8,128)(2,1)S(1)}, u32[]{:S(2)}, u32[]{:S(2)}) collective-permute-start(bf16[2,32,2048]{2,1,0:T(8,128)(2,1)S(1)} %get-tuple-element.125), channel_id=1, source_target_pairs={{0,2},{2,4},{4,6},{6,0},{1,3},{3,5},{5,7},{7,1},{8,10},{10,12},{12... | collective-permute-start | bytes 786440 | tf_op jit(solution)/shard_map/ppermute | solution.py:266
  356.5 32.4 %collective-permute-start.72 = (bf16[2,32,2048]{2,1,0:T(8,128)(2,1)S(1)}, bf16[2,32,2048]{2,1,0:T(8,128)(2,1)S(1)}, u32[]{:S(2)}, u32[]{:S(2)}) collective-permute-start(bf16[2,32,2048]{2,1,0:T(8,128)(2,1)S(1)} %get-tuple-element.126), channel_id=1, source_target_pairs={{0,4},{2,6},{4,0},{6,2},{1,5},{3,7},{5,1},{7,3},{8,12},{10,14},{12... | collective-permute-start | bytes 786440 | tf_op jit(solution)/shard_map/ppermute | solution.py:266
  366.4 26.0 %collective-permute-start.73 = (bf16[2,32,2048]{2,1,0:T(8,128)(2,1)S(1)}, bf16[2,32,2048]{2,1,0:T(8,128)(2,1)S(1)}, u32[]{:S(2)}, u32[]{:S(2)}) collective-permute-start(bf16[2,32,2048]{2,1,0:T(8,128)(2,1)S(1)} %get-tuple-element.127), channel_id=1, source_target_pairs={{0,6},{2,0},{4,2},{6,4},{1,7},{3,1},{5,3},{7,5},{8,14},{10,8},{12,... | collective-permute-start | bytes 786440 | tf_op jit(solution)/shard_map/ppermute | solution.py:266
  381.3 12.1 %collective-permute-start.83 = (bf16[2,64,1024]{2,1,0:T(8,128)(2,1)S(1)}, bf16[2,64,1024]{2,1,0:T(8,128)(2,1)S(1)}, u32[]{:S(2)}, u32[]{:S(2)}) collective-permute-start(bf16[2,64,1024]{2,1,0:T(8,128)(2,1)S(1)} %fusion.39), channel_id=1, source_target_pairs={{0,16},{16,0},{1,17},{17,1},{2,18},{18,2},{3,19},{19,3},{4,20},{20... | collective-permute-start | bytes 786440 | tf_op jit(solution)/shard_map/ppermute | solution.py:43
  393.5 86.2 %collective-permute-start.84 = (bf16[256,1024]{1,0:T(8,128)(2,1)S(1)}, bf16[256,1024]{1,0:T(8,128)(2,1)S(1)}, u32[]{:S(2)}, u32[]{:S(2)}) collective-permute-start(bf16[256,1024]{1,0:T(8,128)(2,1)S(1)} %bitcast.411), channel_id=1, source_target_pairs={{0,8},{8,0},{1,9},{9,1},{2,10},{10,2},{3,11},{11,3},{4,12},{12,4},... | collective-permute-start | bytes 1572872 | tf_op jit(solution)/shard_map/ppermute | solution.py:43
  400.2 82.6 %collective-permute-start.75 = (bf16[128,8,256]{2,1,0:T(8,128)(2,1)S(1)}, bf16[128,8,256]{2,1,0:T(8,128)(2,1)S(1)}, u32[]{:S(2)}, u32[]{:S(2)}) collective-permute-start(bf16[128,8,256]{2,1,0:T(8,128)(2,1)S(1)} %bitcast.412), channel_id=1, source_target_pairs={{0,8},{8,0},{1,9},{9,1},{2,10},{10,2},{3,11},{11,3},{4,12},{12,4},... | collective-permute-start | bytes 1572872 | tf_op jit(solution)/shard_map/ppermute | solution.py:43
  453.0 12.7 %collective-permute-start.60 = (bf16[4,2,16,1024]{3,2,0,1:T(8,128)(2,1)S(1)}, bf16[4,2,16,1024]{3,2,0,1:T(8,128)(2,1)S(1)}, u32[]{:S(2)}, u32[]{:S(2)}) collective-permute-start(bf16[4,2,16,1024]{3,2,0,1:T(8,128)(2,1)S(1)} %bitcast.429), channel_id=1, source_target_pairs={{0,16},{16,0},{1,17},{17,1},{2,18},{18,2},{3,19},{19,3},{4,20},{20... | collective-permute-start | bytes 786440 | tf_op jit(solution)/shard_map/ppermute | solution.py:43
  453.9 12.2 %collective-permute-start.58 = (bf16[4,2,16,1024]{3,2,0,1:T(8,128)(2,1)S(1)}, bf16[4,2,16,1024]{3,2,0,1:T(8,128)(2,1)S(1)}, u32[]{:S(2)}, u32[]{:S(2)}) collective-permute-start(bf16[4,2,16,1024]{3,2,0,1:T(8,128)(2,1)S(1)} %bitcast.428), channel_id=1, source_target_pairs={{0,1},{1,0},{2,3},{3,2},{4,5},{5,4},{6,7},{7,6},{8,9},{9,8},{10,11... | collective-permute-start | bytes 786440 | tf_op jit(solution)/shard_map/ppermute | solution.py:43
  475.1 27.6 %collective-permute-start.51 = (bf16[4,2,32,1536]{3,2,0,1:T(8,128)(2,1)}, bf16[4,2,32,1536]{3,2,0,1:T(8,128)(2,1)}, u32[]{:S(2)}, u32[]{:S(2)}) collective-permute-start(bf16[4,2,32,1536]{3,2,0,1:T(8,128)(2,1)} %bitcast.393), channel_id=1, source_target_pairs={{0,16},{16,0},{1,17},{17,1},{2,18},{18,2},{3,19},{19,3},{4,20},{20... | collective-permute-start | bytes 2359304 | tf_op jit(solution)/shard_map/ppermute | solution.py:43
  475.8 29.6 %collective-permute-start.49 = (bf16[4,2,32,1536]{3,2,0,1:T(8,128)(2,1)}, bf16[4,2,32,1536]{3,2,0,1:T(8,128)(2,1)}, u32[]{:S(2)}, u32[]{:S(2)}) collective-permute-start(bf16[4,2,32,1536]{3,2,0,1:T(8,128)(2,1)} %bitcast.394), channel_id=1, source_target_pairs={{0,1},{1,0},{2,3},{3,2},{4,5},{5,4},{6,7},{7,6},{8,9},{9,8},{10,11... | collective-permute-start | bytes 2359304 | tf_op jit(solution)/shard_map/ppermute | solution.py:43
  476.6 30.5 %collective-permute-start.47 = (bf16[2,256,1024]{2,1,0:T(8,128)(2,1)}, bf16[2,256,1024]{2,1,0:T(8,128)(2,1)}, u32[]{:S(2)}, u32[]{:S(2)}) collective-permute-start(bf16[2,256,1024]{2,1,0:T(8,128)(2,1)} %dynamic-slice_bitcast_fusion), channel_id=1, source_target_pairs={{0,8},{8,0},{1,9},{9,1},{2,10},{10,2},{3,11},{11,3},{4,12},{12,4},... | collective-permute-start | bytes 3145736 | tf_op jit(solution)/shard_map/ppermute | solution.py:43
  479.6 13.8 %collective-permute-start.65 = (bf16[2,16,1024]{2,1,0:T(8,128)(2,1)S(1)}, bf16[2,16,1024]{2,1,0:T(8,128)(2,1)S(1)}, u32[]{:S(2)}, u32[]{:S(2)}) collective-permute-start(bf16[2,16,1024]{2,1,0:T(8,128)(2,1)S(1)} %fusion.86), channel_id=1, source_target_pairs={{0,16},{16,0},{1,17},{17,1},{2,18},{18,2},{3,19},{19,3},{4,20},{20... | collective-permute-start | bytes 196616 | tf_op jit(solution)/shard_map/ppermute | solution.py:43
  518.7 16.2 %collective-permute-start.54 = (bf16[2,32,1536]{2,1,0:T(8,128)(2,1)S(1)}, bf16[2,32,1536]{2,1,0:T(8,128)(2,1)S(1)}, u32[]{:S(2)}, u32[]{:S(2)}) collective-permute-start(bf16[2,32,1536]{2,1,0:T(8,128)(2,1)S(1)} %get-tuple-element.133), channel_id=1, source_target_pairs={{0,4},{2,6},{4,0},{6,2},{1,5},{3,7},{5,1},{7,3},{8,12},{10,14},{12... | collective-permute-start | bytes 589832 | tf_op jit(solution)/shard_map/ppermute | solution.py:266
  521.7 16.3 %collective-permute-start.55 = (bf16[2,32,1536]{2,1,0:T(8,128)(2,1)S(1)}, bf16[2,32,1536]{2,1,0:T(8,128)(2,1)S(1)}, u32[]{:S(2)}, u32[]{:S(2)}) collective-permute-start(bf16[2,32,1536]{2,1,0:T(8,128)(2,1)S(1)} %get-tuple-element.134), channel_id=1, source_target_pairs={{0,6},{2,0},{4,2},{6,4},{1,7},{3,1},{5,3},{7,5},{8,14},{10,8},{12,... | collective-permute-start | bytes 589832 | tf_op jit(solution)/shard_map/ppermute | solution.py:266
  538.1 49.6 %collective-permute-start.56 = (bf16[2,32,1536]{2,1,0:T(8,128)(2,1)S(1)}, bf16[2,32,1536]{2,1,0:T(8,128)(2,1)S(1)}, u32[]{:S(2)}, u32[]{:S(2)}) collective-permute-start(bf16[2,32,1536]{2,1,0:T(8,128)(2,1)S(1)} %fusion.55), channel_id=1, source_target_pairs={{0,16},{16,0},{1,17},{17,1},{2,18},{18,2},{3,19},{19,3},{4,20},{20... | collective-permute-start | bytes 589832 | tf_op jit(solution)/shard_map/ppermute | solution.py:43
  539.4 51.0 %collective-permute-start.48 = (bf16[256,1024]{1,0:T(8,128)(2,1)}, bf16[256,1024]{1,0:T(8,128)(2,1)}, u32[]{:S(2)}, u32[]{:S(2)}) collective-permute-start(bf16[256,1024]{1,0:T(8,128)(2,1)} %fusion.32), channel_id=1, source_target_pairs={{0,16},{16,0},{1,17},{17,1},{2,18},{18,2},{3,19},{19,3},{4,20},{20... | collective-permute-start | bytes 1572872 | tf_op jit(solution)/shard_map/ppermute | solution.py:43
  (89 other events, 882.3 us)

commit v2 on v1

--- a/solution.py
+++ b/solution.py
@@ -33,6 +33,14 @@
 
 def mm_cols(left, right):
     return dot(left, right, ((1,), (1,)))
+
+
+def cost(micros):
+    return pl.CostEstimate(flops=int(micros * 1.1e9), bytes_accessed=1, transcendentals=0)
+
+
+def sync(*values):
+    return lax.optimization_barrier(values)
 
 
 def pick(array, index, axis):
@@ -117,6 +125,7 @@
         ],
         scratch_shapes=[pltpu.VMEM((len(spans), tile, widest), f32)],
         compiler_params=pltpu.CompilerParams(vmem_limit_bytes=40 * 1024 * 1024),
+        cost_estimate=cost(4.3 * pairs),
         name="attend",
     )(joint, joint, joint, seg_col, seg_row)
 
@@ -161,18 +170,18 @@
         out_ref[...] = values_sum[...].astype(bf16)
 
 
-def attend_back(joint, grads, lse, seg_col, seg_row):
+def attend_back(joint, grads, lse, seg_col, seg_row, begin, count):
     rows, width = joint.shape[0], joint.shape[1] // 3
     pairs = width // LANES
     tile, spans = tile_spans(rows)
     widest = max(high - low for _, low, high in spans)
 
     def part(which):
-        return pl.BlockSpec((rows, LANES), lambda p, j: (0, which * pairs + p))
+        return pl.BlockSpec((rows, LANES), lambda p, j: (0, which * pairs + begin + p))
 
     return pl.pallas_call(
         functools.partial(attend_back_kernel, spans, tile),
-        grid=(pairs, 3),
+        grid=(count, 3),
         in_specs=[
             part(0),
             part(1),
@@ -182,49 +191,39 @@
             pl.BlockSpec((rows, 1), lambda p, j: (0, 0)),
             pl.BlockSpec((1, rows), lambda p, j: (0, 0)),
         ],
-        out_specs=pl.BlockSpec((rows, LANES), lambda p, j: (0, j * pairs + p)),
-        out_shape=jax.ShapeDtypeStruct((rows, 3 * width), bf16),
+        out_specs=pl.BlockSpec((rows, LANES), lambda p, j: (0, j * count + p)),
+        out_shape=jax.ShapeDtypeStruct((rows, 3 * count * LANES), bf16),
         scratch_shapes=[
             pltpu.VMEM((len(spans), tile, widest), f32),
             pltpu.VMEM((rows, LANES), f32),
             pltpu.VMEM((rows, LANES), f32),
         ],
         compiler_params=pltpu.CompilerParams(vmem_limit_bytes=48 * 1024 * 1024),
+        cost_estimate=cost(7.5 * count),
         name="attend_back",
     )(joint, joint, joint, grads, lse, seg_col, seg_row)
 
 
-def gather(own, depth):
-    h = lax.axis_index("hi")
-    rows, columns = own.shape
-    halves = own.reshape(2, rows // 2, columns)
-    half = pick(halves, h, 0)
-    far = [lax.ppermute(half, "fz", [(i, (i + k) % depth) for i in range(depth)]) for k in range(1, depth)]
-    spots = [(0, 0, None), (0, 1, None)]
-    pieces = [halves, swap(halves, "fx")]
-    for k, piece in enumerate(far, 1):
-        side = swap(piece, "fx")
-        spots += [(k, 0, 0), (k, 0, 1), (k, 1, 0), (k, 1, 1)]
-        pieces += [piece, swap(piece, "hi"), side, swap(side, "hi")]
-    return spots, pieces
-
-
-def load(spots, depth, place, pieces, sems, targets):
+def along(value, axis, depth, step):
+    return lax.ppermute(value, axis, [(i, (i + step) % depth) for i in range(depth)])
+
+
+def load(depth, place, pieces, sems, targets):
     z, x, h = place[0], place[1], place[2]
     copies = []
-    for first, columns, where in targets:
-        for (k, other_x, other_h), piece in zip(spots, pieces):
-            shard = lax.rem(z - k + depth, depth) * 2 + (1 - x if other_x else x)
-            for part in range(2) if other_h is None else (None,):
-                if part is None:
-                    half, source = (1 - h if other_h else h), piece
-                else:
-                    half, source = part, piece.at[part]
-                if columns != source.shape[1]:
-                    source = source.at[:, first : first + columns]
-                copy = pltpu.make_async_copy(source, where(shard, half), sems.at[len(copies)])
-                copy.start()
-                copies.append(copy)
+
+    def put(source, shard, half):
+        for first, columns, where in targets:
+            taken = source if columns == source.shape[1] else source.at[:, first : first + columns]
+            copies.append(pltpu.make_async_copy(taken, where(shard, half), sems.at[len(copies)]))
+            copies[-1].start()
+
+    for at_x, piece in ((x, pieces[0]), (1 - x, pieces[1])):
+        for half in range(2):
+            put(piece.at[half], z * 2 + at_x, half)
+    for at_x, at_h, piece in ((x, h, pieces[2]), (1 - x, h, pieces[3]), (x, 1 - h, pieces[4]), (1 - x, 1 - h, pieces[5])):
+        for k in range(1, depth):
+            put(piece.at[k - 1], lax.rem(z - k + depth, depth) * 2 + at_x, at_h)
     return copies
 
 
@@ -235,37 +234,36 @@
     return where
 
 
-def beside(weight, rows, columns):
-    def where(shard, half):
-        return weight.at[
-            pl.ds(pl.multiple_of(shard * rows, rows), rows),
-            pl.ds(pl.multiple_of(half * columns, columns), columns),
-        ]
-
-    return where
-
-
 def plus(left, right):
     return (left.astype(f32) + right.astype(f32)).astype(bf16)
 
 
-def reduce(full, depth):
-    z, x, h = lax.axis_index("fz"), lax.axis_index("fx"), lax.axis_index("hi")
-    columns = full.shape[1]
-    rows = full.shape[0] // (2 * depth)
+def cut(full, depth, x, h):
+    rows, columns = full.shape[0] // (2 * depth), full.shape[1]
     view = full.reshape(depth, 2, 2, 2, rows // 4, columns)
     first, second = view[:, :, 0], view[:, :, 1]
-    first = plus(pick(first, x, 1), swap(pick(first, 1 - x, 1), "fx"))
-    second = plus(pick(second, h, 2), swap(pick(second, 1 - h, 2), "hi"))
-    first = plus(pick(first, h, 1), swap(pick(first, 1 - h, 1), "hi"))
-    second = plus(pick(second, x, 1), swap(pick(second, 1 - x, 1), "fx"))
-    both = jnp.stack([first, second], 1)
-    total = pick(both, z, 0).astype(f32)
-    for k in range(1, depth):
-        ring = [(i, (i + k) % depth) for i in range(depth)]
-        total = total + lax.ppermute(pick(both, (z + k) % depth, 0), "fz", ring).astype(f32)
-    total = total.astype(bf16)
-    return ordered(total, swap(total, "hi"), h, 1).reshape(rows, columns)
+    keep = pick(first, x, 1), pick(second, h, 2)
+    send = pick(first, 1 - x, 1), pick(second, 1 - h, 2)
+    return keep, send
+
+
+def cut_again(keep, came, x, h):
+    first, second = plus(keep[0], came[0]), plus(keep[1], came[1])
+    keep = pick(first, h, 1), pick(second, x, 1)
+    send = pick(first, 1 - h, 1), pick(second, 1 - x, 1)
+    return keep, send
+
+
+def along_z(keep, came, depth, z):
+    both = jnp.stack([plus(keep[0], came[0]), plus(keep[1], came[1])], 1)
+    return pick(both, z, 0), [pick(both, (z + k) % depth, 0) for k in range(1, depth)]
+
+
+def add_up(own, came):
+    total = own.astype(f32)
+    for piece in came:
+        total = total + piece.astype(f32)
+    return total.astype(bf16)
 
 
 def row_block(tile, width):
@@ -276,11 +274,8 @@
     return pl.BlockSpec(shape, lambda i: (0,) * len(shape))
 
 
-def weight_call(name, step, tiles, place, inputs, sets, outs, scratch, copies, flops):
-    pieces = [piece for _, held in sets for piece in held]
-    moved = sum(math.prod(v.shape) * v.dtype.itemsize for v in pieces)
-    moved += sum(math.prod(v.shape) * v.dtype.itemsize for v, _ in inputs)
-    moved += sum(math.prod(v.shape) * v.dtype.itemsize for v, _ in outs)
+def weight_call(name, step, tiles, place, inputs, sets, outs, scratch, copies, micros):
+    pieces = [piece for held in sets for piece in held]
 
     def kernel(place_ref, *refs):
         refs = list(refs)
@@ -291,7 +286,7 @@
             return taken
 
         given = take(len(inputs))
-        held = [take(len(one)) for _, one in sets]
+        held = [take(len(one)) for one in sets]
         made = take(len(outs))
         step(place_ref, given, held, made, refs[:-1], refs[-1])
 
@@ -303,9 +298,9 @@
         + [pl.BlockSpec(memory_space=pl.ANY)] * len(pieces),
         out_specs=[spec for _, spec in outs],
         out_shape=[shape for shape, _ in outs],
-        scratch_shapes=list(scratch) + [pltpu.SemaphoreType.DMA(copies if isinstance(copies, tuple) else (copies,))],
+        scratch_shapes=list(scratch) + [pltpu.SemaphoreType.DMA((copies,))],
         compiler_params=pltpu.CompilerParams(vmem_limit_bytes=56 * 1024 * 1024),
-        cost_estimate=pl.CostEstimate(flops=flops, bytes_accessed=moved, transcendentals=0),
+        cost_estimate=cost(micros),
         name=name,
     )(place, *[v for v, _ in inputs], *pieces)
 
@@ -362,39 +357,33 @@
     own_rows = w_out.shape[0]
     inner = w_up.shape[1] // group
     split_out = (own_rows // HEAD_DIM) % group == 0
-    joined = split_out and group == 2
     head_columns = model // group
+    half_rows = own_rows // 2
     tile = min(TILE, rows)
     tiles = rows // tile
+    scale_at = 3 * head_columns
+    copies = 4 * shards
+    wide = min(512, inner)
+    shard_axes = ("fz", "fx")
 
     def whole_group(value, axis):
         if group == 2:
             return ordered(value, swap(value, "lo"), lo, axis)
         return lax.all_gather(value, "lo", axis=axis)
 
-    def sequence(array):
-        kept = pick(array[:, 0], h, 0)
-        came = swap(pick(array[:, 0], 1 - h, 0), "hi")
-        return whole_group(ordered(kept, came, h, 0), 1).reshape(rows, model)
-
-    def placed(array):
-        came = swap(pick(array, 1 - h, 0).astype(bf16), "hi").astype(array.dtype)
-        return ordered(pick(array, h, 0), came, h, 0)[:, None]
-
     def other_part(partial):
         if group == 2:
             return swap(partial, "lo")
         return (lax.psum(partial, "lo").astype(f32) - partial.astype(f32)).astype(bf16)
 
-    def sum_own(partial):
+    def own_chunks(full):
+        return pick(full.reshape(micro, group, chunk, -1), lo, 1)
+
+    def other_own(partial):
         parts = partial.reshape(micro, group, chunk, model)
         if group == 2:
-            came = swap(pick(parts, 1 - lo, 1), "lo").astype(f32)
-            return pick(parts, lo, 1).astype(f32) + came
-        return lax.psum_scatter(parts, "lo", scatter_dimension=1).astype(f32)
-
-    def own_chunks(full):
-        return pick(full.reshape(micro, group, chunk, -1), lo, 1)
+            return swap(pick(parts, 1 - lo, 1), "lo")
+        return plus(lax.psum_scatter(parts, "lo", scatter_dimension=1), -pick(parts, lo, 1))
 
     if split_out:
         qkv_part = pick(w_qkv.reshape(own_rows, 3, shards, group, -1), lo, 3).reshape(own_rows, -1)
@@ -404,38 +393,41 @@
         out_part = w_out
     up_part = pick(w_up.reshape(own_rows, shards, group, -1), lo, 2).reshape(own_rows, -1)
     down_part = pick(w_down.reshape(group, -1, model), lo, 0)
-    out_rows, down_rows = out_part.shape[0], down_part.shape[0]
-
     vectors = jnp.stack([norm1_gain, norm1_bias, norm2_gain, norm2_bias], axis=1)
-    parts = [qkv_part, jnp.pad(vectors, ((0, 0), (0, LANES - 4)))]
-    if joined:
-        parts.append(jnp.concatenate([out_part[:, : model // 2], out_part[:, model // 2 :]], axis=0))
+    first_part = jnp.concatenate([qkv_part, jnp.pad(vectors, ((0, 0), (0, LANES - 4)))], axis=1)
     place = jnp.stack([z, x, h, lo]).astype(jnp.int32)
-    scale_at, out_at = 3 * head_columns, 3 * head_columns + LANES
-
-    inputs = sequence(tokens)
-    first_set = gather(jnp.concatenate(parts, axis=1), depth)
-    out_set = first_set if joined else gather(out_part, depth)
-    up_set = gather(up_part, depth)
-    down_set = gather(down_part, depth)
-    grad_result = sequence(cotangent)
+    first_own = first_part.reshape(2, half_rows, -1)
+    up_own = up_part.reshape(2, half_rows, -1)
+    rest = range(1, depth)
+
+    out_weight = lax.all_gather(out_part, shard_axes, axis=0, tiled=True)
+    first_half = pick(first_own, h, 0)
+    first_far = [along(first_half, "fz", depth, k) for k in rest]
+    first_side_own = swap(first_own, "fx")
+    came = swap(pick(tokens[:, 0], 1 - h, 0), "hi")
+    first_far, first_side_own, came, up_own, tokens = sync(
+        first_far, first_side_own, came, up_own, tokens
+    )
+
+    first_far = jnp.stack(first_far)
+    first_side, first_near = swap(first_far, "fx"), swap(first_far, "hi")
+    inputs = whole_group(ordered(pick(tokens[:, 0], h, 0), came, h, 0), 1).reshape(rows, model)
+    up_half = pick(up_own, h, 0)
+    odd = [along(up_half, "fz", depth, k) for k in rest if k % 2]
+    first_side, first_near, inputs, odd, up_half, up_own, down_part = sync(
+        first_side, first_near, inputs, odd, up_half, up_own, down_part
+    )
+
+    downward = lax.all_gather(down_part, shard_axes, axis=0, tiled=True)
+    first_last = swap(first_side, "hi")
+    up_side_own = swap(up_own, "fx")
+    even = [along(up_half, "fz", depth, k) for k in rest if k % 2 == 0]
+    first_last, up_side_own, even, odd, inputs = sync(first_last, up_side_own, even, odd, inputs)
+    first_set = [first_own, first_side_own, first_far, first_side, first_near, first_last]
+    up_far = jnp.stack([odd[k // 2] if k % 2 else even[k // 2 - 1] for k in rest])
 
     segments = pick(segment_ids[:, 0], h, 0)
     seg_col, seg_row = segments[:, None], segments[None, :]
-    half_rows = own_rows // 2
-    copies = 4 * shards
-
-    def load_out(place_ref, pieces, weight, sems):
-        if joined:
-            targets = [(out_at, model // 2, beside(weight, out_rows, model // 2))]
-        else:
-            targets = [(0, model, below(weight, out_rows // 2))]
-        return load(out_set[0], depth, place_ref, pieces, sems, targets)
-
-    def out_weight(weight, place_ref):
-        if split_out:
-            return weight[...]
-        return weight[pl.ds(pl.multiple_of(place_ref[3] * head_columns, head_columns), head_columns), :]
 
     def project(place_ref, given, held, made, scratch, sems):
         (rows_ref,), (normed_ref, joint_ref, scales_ref) = given, made
@@ -447,7 +439,7 @@
                 (0, 3 * head_columns, below(weight, half_rows)),
                 (scale_at, LANES, below(columns, half_rows)),
             ]
-            for copy in load(first_set[0], depth, place_ref, held[0], sems, targets):
+            for copy in load(depth, place_ref, held[0], sems, targets):
                 copy.wait()
             scales_ref[...] = columns[...].astype(f32).T[:8, :]
 
@@ -474,34 +466,40 @@
         ],
         [pltpu.VMEM((model, 3 * head_columns), bf16), pltpu.VMEM((model, LANES), bf16)],
         copies,
-        6 * rows * model * head_columns,
+        9,
     )
     attended, lse = attend(joint, seg_col, seg_row)
+    up_side, up_near = swap(up_far, "fx"), swap(up_far, "hi")
+    attended, up_side, up_near, cotangent = sync(attended, up_side, up_near, cotangent)
 
     def leave(place_ref, given, held, made, scratch, sems):
-        (rows_ref,), (out_ref,), (weight,) = given, made, scratch
-
-        @pl.when(pl.program_id(0) == 0)
-        def _():
-            for copy in load_out(place_ref, held[0], weight, sems):
-                copy.wait()
-
-        out_ref[...] = mm(rows_ref[...], out_weight(weight, place_ref)).astype(bf16)
+        (rows_ref, weight), (out_ref,) = given, made
+        out_ref[...] = mm(rows_ref[...], own_out(weight, place_ref)).astype(bf16)
+
+    def own_out(weight, place_ref):
+        if split_out:
+            return weight[...]
+        return weight[pl.ds(pl.multiple_of(place_ref[3] * head_columns, head_columns), head_columns), :]
 
     (branch,) = weight_call(
         "leave",
         leave,
         tiles,
         place,
-        [(attended, row_block(tile, head_columns))],
-        [out_set],
+        [(attended, row_block(tile, head_columns)), (out_weight, whole_block(*out_weight.shape))],
+        [],
         [(shape_of(rows, model), row_block(tile, model))],
-        [pltpu.VMEM((out_rows * shards, model), bf16)],
-        copies,
-        2 * rows * model * head_columns,
+        [],
+        1,
+        4,
     )
     branch_other = other_part(branch)
-    wide = min(512, inner)
+    up_last = swap(up_side, "hi")
+    came = swap(pick(cotangent[:, 0], 1 - h, 0), "hi")
+    branch, branch_other, up_last, cotangent = sync(branch, branch_other, up_last, cotangent)
+    up_set = [up_own, up_side_own, up_far, up_side, up_near, up_last]
+
+    grad_result = whole_group(ordered(pick(cotangent[:, 0], h, 0), came, h, 0), 1).reshape(rows, model)
 
     def widen(place_ref, given, held, made, scratch, sems):
         rows_ref, own_ref, other_ref, scales_ref = given
@@ -511,7 +509,7 @@
         @pl.when(pl.program_id(0) == 0)
         def _():
             targets = [(0, inner, below(weight, half_rows))]
-            for copy in load(up_set[0], depth, place_ref, held[0], sems, targets):
+            for copy in load(depth, place_ref, held[0], sems, targets):
                 copy.wait()
 
         added = own_ref[...].astype(f32) + other_ref[...].astype(f32)
@@ -545,27 +543,29 @@
         ],
         [pltpu.VMEM((model, inner), bf16)],
         copies,
-        2 * rows * model * inner,
-    )
+        18,
+    )
+    hidden, slope, grad_result = sync(hidden, slope, grad_result)
+
     grad_down = mm_rows(hidden, grad_result).astype(bf16)
+    hidden, slope, grad_down = sync(hidden, slope, grad_down)
+    down_own = lax.psum_scatter(grad_down, shard_axes, scatter_dimension=0, tiled=True)
 
     def narrow(place_ref, given, held, made, scratch, sems):
-        hidden_ref, grad_ref, slope_ref = given
+        hidden_ref, grad_ref, slope_ref, down_ref = given
         out_ref, pre_ref, back_ref = made
-        upward, downward = scratch
+        (upward,) = scratch
 
         @pl.when(pl.program_id(0) == 0)
         def _():
             targets = [(0, inner, below(upward, half_rows))]
-            ups = load(up_set[0], depth, place_ref, held[0], sems.at[0], targets)
-            targets = [(0, model, below(downward, down_rows // 2))]
-            for copy in ups + load(down_set[0], depth, place_ref, held[1], sems.at[1], targets):
+            for copy in load(depth, place_ref, held[0], sems, targets):
                 copy.wait()
 
-        out_ref[...] = mm(hidden_ref[...], downward[...]).astype(bf16)
+        out_ref[...] = mm(hidden_ref[...], down_ref[...]).astype(bf16)
         total = jnp.zeros(back_ref.shape, f32)
         for at in range(0, inner, wide):
-            grad = mm_cols(grad_ref[...], downward[at : at + wide, :])
+            grad = mm_cols(grad_ref[...], down_ref[at : at + wide, :])
             grad = (grad * slope_ref[:, at : at + wide].astype(f32)).astype(bf16)
             pre_ref[:, at : at + wide] = grad
             total = total + mm_cols(grad, upward[:, at : at + wide])
@@ -580,40 +580,47 @@
             (hidden, row_block(tile, inner)),
             (grad_result, row_block(tile, model)),
             (slope, row_block(tile, inner)),
-        ],
-        [up_set, down_set],
+            (downward, whole_block(inner, model)),
+        ],
+        [up_set],
         [
             (shape_of(rows, model), row_block(tile, model)),
             (shape_of(rows, inner), row_block(tile, inner)),
             (shape_of(rows, model), row_block(tile, model)),
         ],
-        [pltpu.VMEM((model, inner), bf16), pltpu.VMEM((inner, model), bf16)],
-        (2, copies),
-        6 * rows * model * inner,
-    )
+        [pltpu.VMEM((model, inner), bf16)],
+        copies,
+        21,
+    )
+    result, grad_pre, back = sync(result, grad_pre, back)
+
     back_other = other_part(back)
     grad_up = mm_rows(normed_two, grad_pre).astype(bf16)
+    up_keep, up_send = cut(grad_up, depth, x, h)
+    back, back_other, up_keep, up_send, result = sync(back, back_other, up_keep, up_send, result)
+
+    pairs = head_columns // LANES
+    pieces = 2 if pairs % 2 == 0 else 1
+    count = pairs // pieces
 
     def between(place_ref, given, held, made, scratch, sems):
-        grad_ref, own_ref, other_ref, middle_ref, scales_ref = given
+        grad_ref, own_ref, other_ref, middle_ref, scales_ref, weight = given
         middle_grad_ref, branch_ref, attended_ref, sums_ref = made
-        (weight,) = scratch
 
         @pl.when(pl.program_id(0) == 0)
         def _():
             sums_ref[...] = jnp.zeros_like(sums_ref)
-            for copy in load_out(place_ref, held[0], weight, sems):
-                copy.wait()
 
         unit_rows, inverse = unit_of(middle_ref[...])
-        back_rows = own_ref[...].astype(f32) + other_ref[...].astype(f32)
-        sums_ref[0:1, :] += jnp.sum(back_rows * unit_rows, axis=0, keepdims=True)
-        sums_ref[1:2, :] += jnp.sum(back_rows, axis=0, keepdims=True)
+        own_back = own_ref[...].astype(f32)
+        back_rows = own_back + other_ref[...].astype(f32)
+        sums_ref[0:1, :] += jnp.sum(own_back * unit_rows, axis=0, keepdims=True)
+        sums_ref[1:2, :] += jnp.sum(own_back, axis=0, keepdims=True)
         grads = grad_ref[...].astype(f32) + unit_back(back_rows * scales_ref[2:3, :], unit_rows, inverse)
         middle_grad_ref[...] = grads
         low = grads.astype(bf16)
         branch_ref[...] = low
-        attended_ref[...] = mm_cols(low, out_weight(weight, place_ref)).astype(bf16)
+        attended_ref[...] = mm_cols(low, own_out(weight, place_ref)).astype(bf16)
 
     grad_middle, grad_branch, grad_attended, sums_two = weight_call(
         "between",
@@ -626,75 +633,154 @@
             (back_other, row_block(tile, model)),
             (middle, row_block(tile, model)),
             (scales, whole_block(8, model)),
-        ],
-        [out_set],
+            (out_weight, whole_block(*out_weight.shape)),
+        ],
+        [],
         [
             (shape_of(rows, model, dtype=f32), row_block(tile, model)),
             (shape_of(rows, model), row_block(tile, model)),
             (shape_of(rows, head_columns), row_block(tile, head_columns)),
             (shape_of(8, model, dtype=f32), whole_block(8, model)),
         ],
-        [pltpu.VMEM((out_rows * shards, model), bf16)],
-        copies,
-        2 * rows * model * head_columns,
-    )
-    grad_joint = attend_back(joint, grad_attended, lse, seg_col, seg_row)
+        [],
+        1,
+        10,
+    )
+    grad_joints = [attend_back(joint, grad_attended, lse, seg_col, seg_row, 0, count)]
+    up_came = swap(up_send[0], "fx"), swap(up_send[1], "hi")
+    result_other = other_own(result)
+    grad_joints, grad_attended, grad_branch, up_came, result_other = sync(
+        grad_joints, grad_attended, grad_branch, up_came, result_other
+    )
+
     grad_out = mm_rows(attended, grad_branch).astype(bf16)
+    if not split_out:
+        empty = jnp.zeros((model, model), bf16)
+        grad_out = lax.dynamic_update_slice_in_dim(empty, grad_out, lo * head_columns, 0)
+    up_keep, up_send = cut_again(up_keep, up_came, x, h)
+    for piece in range(1, pieces):
+        grad_joints.append(
+            attend_back(joint, grad_attended, lse, seg_col, seg_row, piece * count, count)
+        )
+    fused_out = split_out and group == 2
+    parts = [mm_rows(normed, grad_joints[0]).astype(bf16)]
+    if fused_out:
+        halves = grad_out.reshape(shards, own_rows // group, group, model // group).transpose(0, 2, 1, 3)
+        parts.append(halves.reshape(model, model // group))
+    one_keep, one_send = cut(jnp.concatenate(parts, axis=1), depth, x, h)
+    up_came = swap(up_send[0], "hi"), swap(up_send[1], "fx")
+    grad_joints, up_came, one_keep, one_send = sync(grad_joints, up_came, one_keep, one_send)
+
+    up_own_sum, up_send = along_z(up_keep, up_came, depth, z)
+    one_came = swap(one_send[0], "fx"), swap(one_send[1], "hi")
+    up_came = [along(value, "fz", depth, k) for k, value in zip(rest, up_send)]
+    part_columns = count * LANES
 
     def enter(place_ref, given, held, made, scratch, sems):
-        (rows_ref,), (out_ref,), (weight,) = given, made, scratch
+        *parts_refs, inputs_ref = given
+        (out_ref, sums_ref), (weight,) = made, scratch
 
         @pl.when(pl.program_id(0) == 0)
         def _():
+            sums_ref[...] = jnp.zeros_like(sums_ref)
             targets = [(0, 3 * head_columns, below(weight, half_rows))]
-            for copy in load(first_set[0], depth, place_ref, held[0], sems, targets):
+            for copy in load(depth, place_ref, held[0], sems, targets):
                 copy.wait()
 
-        out_ref[...] = mm_cols(rows_ref[...], weight[...]).astype(bf16)
-
-    (entered,) = weight_call(
+        unit_rows, _ = unit_of(inputs_ref[...].astype(f32))
+        grads = jnp.zeros(out_ref.shape, f32)
+        for piece, part_ref in enumerate(parts_refs):
+            for j in range(3):
+                at = j * head_columns + piece * part_columns
+                grads = grads + mm_cols(
+                    part_ref[:, j * part_columns : (j + 1) * part_columns], weight[:, at : at + part_columns]
+                )
+        out_ref[...] = grads.astype(bf16)
+        sums_ref[0:1, :] += jnp.sum(grads * unit_rows, axis=0, keepdims=True)
+        sums_ref[1:2, :] += jnp.sum(grads, axis=0, keepdims=True)
+
+    entered, sums_one = weight_call(
         "enter",
         enter,
         tiles,
         place,
-        [(grad_joint, row_block(tile, 3 * head_columns))],
+        [(value, row_block(tile, 3 * part_columns)) for value in grad_joints] + [(inputs, row_block(tile, model))],
         [first_set],
-        [(shape_of(rows, model), row_block(tile, model))],
+        [
+            (shape_of(rows, model), row_block(tile, model)),
+            (shape_of(8, model, dtype=f32), whole_block(8, model)),
+        ],
         [pltpu.VMEM((model, 3 * head_columns), bf16)],
         copies,
-        6 * rows * model * head_columns,
-    )
-    grad_qkv = mm_rows(normed, grad_joint).astype(bf16)
-
-    output = placed((own_chunks(middle) + sum_own(result)).astype(bf16))
-    grad_normed = sum_own(entered)
+        9,
+    )
+    sums = jnp.stack([sums_one[0], sums_one[1], sums_two[0], sums_two[1]], axis=1).astype(bf16)
+    parts = [mm_rows(normed, value).astype(bf16) for value in grad_joints[1:]]
+    parts.append(jnp.pad(sums, ((0, 0), (0, LANES - 4))))
+    two_keep, two_send = cut(jnp.concatenate(parts, axis=1), depth, x, h)
+    entered, one_came, up_came, two_keep, two_send, down_own = sync(
+        entered, one_came, up_came, two_keep, two_send, down_own
+    )
+
+    one_keep, one_send = cut_again(one_keep, one_came, x, h)
+    one_came = swap(one_send[0], "hi"), swap(one_send[1], "fx")
+    two_came = swap(two_send[0], "fx"), swap(two_send[1], "hi")
+    up_sum = add_up(up_own_sum, up_came)
+    entered_other = other_own(entered)
+    output = (own_chunks(middle) + own_chunks(result).astype(f32) + result_other.astype(f32)).astype(bf16)
+    entered_other, one_came, two_came, up_sum, output, down_own = sync(
+        entered_other, one_came, two_came, up_sum, output, down_own
+    )
+
+    one_own_sum, one_send = along_z(one_keep, one_came, depth, z)
+    one_came = [along(value, "fz", depth, k) for k, value in zip(rest, one_send)]
+    two_keep, two_send = cut_again(two_keep, two_came, x, h)
+    two_came = swap(two_send[0], "hi"), swap(two_send[1], "fx")
+    grad_normed = own_chunks(entered).astype(f32) + entered_other.astype(f32)
     unit_own, inverse_own = unit_of(own_chunks(inputs).astype(f32))
-    grad_gain_one = jnp.sum(grad_normed * unit_own, axis=(0, 1))
-    grad_bias_one = jnp.sum(grad_normed, axis=(0, 1))
-    grad_tokens = placed(own_chunks(grad_middle) + unit_back(grad_normed * scales[0], unit_own, inverse_own))
-
-    if not split_out:
-        empty = jnp.zeros((model, model), bf16)
-        grad_out = lax.dynamic_update_slice_in_dim(empty, grad_out, lo * head_columns, 0)
-    down_own = reduce(grad_down, depth)
-    up_own = reduce(grad_up, depth)
-    out_own = reduce(grad_out, depth)
-    qkv_own = reduce(grad_qkv, depth)
-
+    grad_tokens = own_chunks(grad_middle) + unit_back(grad_normed * scales[0], unit_own, inverse_own)
+    one_came, two_came, grad_tokens, output, up_sum, down_own = sync(
+        one_came, two_came, grad_tokens, output, up_sum, down_own
+    )
+
+    two_own_sum, two_send = along_z(two_keep, two_came, depth, z)
+    two_came = [along(value, "fz", depth, k) for k, value in zip(rest, two_send)]
+    one_sum = add_up(one_own_sum, one_came)
+    grad_came = swap(pick(grad_tokens, 1 - h, 0).astype(bf16), "hi").astype(f32)
+    output_came = swap(pick(output, 1 - h, 0), "hi")
+    two_came, one_sum, grad_came, output_came, up_sum, down_own = sync(
+        two_came, one_sum, grad_came, output_came, up_sum, down_own
+    )
+    output = ordered(pick(output, h, 0), output_came, h, 0)[:, None]
+    grad_tokens = ordered(pick(grad_tokens, h, 0), grad_came, h, 0)[:, None]
+
+    down_own = plus(down_own, swap(down_own, "hi"))
+    two_sum = add_up(two_own_sum, two_came)
+
+    def both_halves(value):
+        return ordered(value, swap(value, "hi"), h, 1).reshape(own_rows, -1)
+
+    up_own, one_own, two_own = both_halves(up_sum), both_halves(one_sum), both_halves(two_sum)
     down_all = whole_group(down_own, 0).reshape(-1, model).astype(f32)
     up_all = whole_group(up_own.reshape(own_rows, shards, -1), 2).reshape(own_rows, -1).astype(f32)
+    qkv_owns = [one_own[:, : 3 * part_columns]]
+    if pieces == 2:
+        qkv_owns.append(two_own[:, : 3 * part_columns])
+    sums_own = two_own[:, -LANES : 4 - LANES]
+    sums = jnp.sum(whole_group(sums_own, 0).astype(f32), axis=0).T
+    if fused_out:
+        out_own = one_own[:, 3 * part_columns :].reshape(group, own_rows // group, -1)
+        out_all = whole_group(out_own, 0).transpose(0, 2, 1, 3).reshape(own_rows, model).astype(f32)
+    else:
+        out_own = lax.psum(lax.psum_scatter(grad_out, shard_axes, scatter_dimension=0, tiled=True), "hi")
+        out_all = whole_group(out_own, 0).reshape(own_rows, model) if split_out else lax.psum(out_own, "lo")
+        out_all = out_all.astype(f32)
+    qkv_own = jnp.concatenate([value.reshape(own_rows, 3, part_columns) for value in qkv_owns], axis=2)
     if split_out:
-        out_all = whole_group(out_own, 0).reshape(own_rows, model).astype(f32)
         qkv_all = whole_group(qkv_own.reshape(own_rows, 3, shards, -1), 3)
     else:
-        out_all = lax.psum(out_own, "lo").astype(f32)
-        qkv_all = whole_group(qkv_own.reshape(own_rows, 3, -1), 2)
+        qkv_all = whole_group(qkv_own, 2)
     qkv_all = qkv_all.reshape(own_rows, -1).astype(f32)
-
-    once = jnp.where(lo == 0, 1.0, 0.0).astype(f32)
-    sums = jnp.stack([grad_gain_one, grad_bias_one, sums_two[0] * once, sums_two[1] * once])
-    sums = lax.psum(sums, ("hi", "lo", "fz", "fx")).reshape(4, shards, own_rows)
-    sums = pick(sums, z * 2 + x, 1)
 
     return (
         output,

time: 604 us -> 464 us (0.77)
  waiting for transfers between devices: 229 us -> 160 us
  blocking collectives: 46.7 us -> 0 us
  starting transfers between devices: 95.3 us -> 52.3 us
  between operations: 2.21 us -> 15.5 us
  other arithmetic: 30 us -> 36.6 us
    ppermute x64 -> x39, waiting for transfers between devices: 144 us -> 83.2 us  [swap(): return lax.ppermute(value, axis, SWAP)]
    psum x1 -> x0, blocking collectives: 46.7 us -> none  [body(): sums = lax.psum(sums, ('hi', 'lo', 'fz', 'fx')).reshape(4, shards, own_rows)]
    ppermute x64 -> x39, starting transfers between devices: 65.4 us -> 31.7 us  [swap(): return lax.ppermute(value, axis, SWAP)]
    ppermute x21 -> x15, starting transfers between devices: 29.9 us -> 20.3 us  [along(): lax.ppermute(value, axis, [(i, (i + step) % depth) for i in range(depth)])]
    ppermute x21 -> x15, waiting for transfers between devices: 85.1 us -> 76.5 us  [along(): lax.ppermute(value, axis, [(i, (i + step) % depth) for i in range(depth)])]
    pallas_call x1 -> x2, Pallas kernels: 30.1 us -> 28.2 us  [attend_back(): pl.pallas_call(functools.partial(attend_back_kernel, spans, tile), grid=(...]
    dot_general x4 -> x5, matrix products: 21 us -> 19.7 us  [dot(): lax.dot_general(left, right, (dims, ((), ())), preferred_element_type=f32)]
    unnamed x150 -> x117, local copies, waits for them, and re-layouts: 20.6 us -> 21.5 us
  transfers between devices with their start and end apart: 85 -> 57, of which waited for: 41 -> 21; matrix products, arithmetic and copies ran while one was open for 14% -> 19% of each run, Pallas kernels for 17% -> 26%
where the time goes in v2:
time: 464 us; the launch traced here: 457 us
  waiting for transfers between devices  160 us (34%)
  Pallas kernels  119 us (26%)
  local copies, waits for them, and re-layouts  54.3 us (12%)
  starting transfers between devices  52.3 us (11%)
  other arithmetic  36.6 us (8%)
  matrix products  19.7 us (4%)
  between operations  15.5 us (3%)
    ppermute x39, waiting for transfers between devices, swap(): return lax.ppermute(value, axis, SWAP)  83.2 us
    ppermute x15, waiting for transfers between devices, along(): lax.ppermute(value, axis, [(i, (i + step) % depth) for i in range(depth)])  76.5 us
    pallas_call x6, Pallas kernels, weight_call(): pl.pallas_call(kernel, grid=(tiles,), in_specs=[pl.BlockSpec(memory_space...  73.7 us
    ppermute x39, starting transfers between devices, swap(): return lax.ppermute(value, axis, SWAP)  31.7 us
    pallas_call x2, Pallas kernels, attend_back(): pl.pallas_call(functools.partial(attend_back_kernel, spans, tile), grid=(...  28.2 us
    unnamed x117, local copies, waits for them, and re-layouts  21.5 us
    ppermute x15, starting transfers between devices, along(): lax.ppermute(value, axis, [(i, (i + step) % depth) for i in range(depth)])  20.3 us
    dot_general x5, matrix products, dot(): lax.dot_general(left, right, (dims, ((), ())), preferred_element_type=f32)  19.7 us
  transfers between devices with their start and end apart: 57, of which 21 were waited for; matrix products, arithmetic and copies ran while one was open for 19% of the time, Pallas kernels for 26%

profile of v2, /device:TPU:9, one launch (start us, length us, event | category | flops | bytes accessed | tf_op | source)
XLA Modules:
  0.0 457.1 jit_solution(14679643532904833759)
XLA Ops:
  7.2 1.9 dynamic-slice_bitcast_fusion.11
  10.4 1.6 copy.122
  18.2 1.5 collective-permute-start.2
  20.5 3.1 dynamic-slice_reduce_fusion
  23.8 10.7 %collective-permute-done.1 = bf16[64,1664]{1,0:T(8,128)(2,1)} collective-permute-done((bf16[64,1664]{1,0:T(8,128)(2,1)}, bf16[64,1664]{1,0:T(8,128)(2,1)}, u32[]{:S(2)}, u32[]{:S(2)}) %collective-permute-start.1) | collective-permute-done | bytes 213024 | tf_op jit(solution)/shard_map/ppermute | solution.py:208
  34.5 3.4 collective-permute-done.2
  44.1 1.5 collective-permute-start.9
  47.2 1.5 copy.126
  48.7 4.2 collective-permute-done.8
  52.9 9.2 %collective-permute-done.9 = bf16[64,2048]{1,0:T(8,128)(2,1)S(1)} collective-permute-done((bf16[64,2048]{1,0:T(8,128)(2,1)S(1)}, bf16[64,2048]{1,0:T(8,128)(2,1)S(1)}, u32[]{:S(2)}, u32[]{:S(2)}) %collective-permute-start.9) | collective-permute-done | bytes 262176 | tf_op jit(solution)/shard_map/ppermute | solution.py:208
  67.0 15.8 %collective-permute-done.12 = bf16[64,2048]{1,0:T(8,128)(2,1)S(1)} collective-permute-done((bf16[64,2048]{1,0:T(8,128)(2,1)S(1)}, bf16[64,2048]{1,0:T(8,128)(2,1)S(1)}, u32[]{:S(2)}, u32[]{:S(2)}) %collective-permute-start.12) | collective-permute-done | bytes 262176 | tf_op jit(solution)/shard_map/ppermute | solution.py:208
  83.8 9.5 %project.1 = (bf16[1024,1024]{1,0:T(8,128)(2,1)}, bf16[1024,1536]{1,0:T(8,128)(2,1)}, f32[8,1024]{1,0:T(8,128)}) custom-call(s32[4]{0:T(128)} %pad_add_fusion.place_ref, bf16[1024,1024]{1,0:T(8,128)(2,1)} %bitcast.339, bf16[2,64,1664]{2,1,0:T(8,128)(2,1)} %pad_maximum_fusion.8.refs_1_.refs_3_, bf16[2,64,1664]{2,1,0:T(8,128)(2,1)} %collective-permute-done.3.refs_2_.refs_4_, ...), custom_call_target="tpu_custom_call" | custom-call | flops 9900000256 | bytes 1 | tf_op jit(solution)/shard_map/project/pallas_call | solution.py:293
  93.3 1.9 copy-done.7
  95.2 17.1 %attend.1 = (bf16[1024,512]{1,0:T(8,128)(2,1)S(1)}, f32[1024,512]{1,0:T(8,128)S(1)}) custom-call(bf16[1024,1536]{1,0:T(8,128)(2,1)S(1)} %copy-done.7, bf16[1024,1536]{1,0:T(8,128)(2,1)S(1)} %copy-done.7, bf16[1024,1536]{1,0:T(8,128)(2,1)S(1)} %copy-done.7, s32[1024,1]{1,0:T(8,128)S(1)} %copy.127.seg_col, s32[1,1024]{1,0:T(1,128)S(1)} %get-tuple-element.333.seg_row), custom_call_target="tpu_custom_call" | custom-call | flops 18919999488 | bytes 1 | tf_op jit(solution)/shard_map/attend/pallas_call | solution.py:111
  115.5 4.9 %leave.1.refs_1_ = bf16[1024,1024]{1,0:T(8,128)(2,1)} custom-call(s32[4]{0:T(128)} %pad_add_fusion.place_ref, bf16[1024,512]{1,0:T(8,128)(2,1)} %copy-done.2, bf16[512,1024]{1,0:T(8,128)(2,1)} %bitcast.391), custom_call_target="tpu_custom_call" | custom-call | flops 4400000000 | bytes 1 | tf_op jit(solution)/shard_map/leave/pallas_call | solution.py:293
  120.5 1.9 collective-permute-start.15
  127.8 14.0 %collective-permute-done.16.refs_9_ = bf16[3,64,2048]{2,1,0:T(8,128)(2,1)} collective-permute-done((bf16[3,64,2048]{2,1,0:T(8,128)(2,1)}, bf16[3,64,2048]{2,1,0:T(8,128)(2,1)}, u32[]{:S(2)}, u32[]{:S(2)}) %collective-permute-start.16) | collective-permute-done | bytes 786464 | tf_op jit(solution)/shard_map/ppermute | solution.py:51
  141.8 11.2 %collective-permute-done.17 = bf16[256,1024]{1,0:T(8,128)(2,1)S(1)} collective-permute-done((bf16[256,1024]{1,0:T(8,128)(2,1)S(1)}, bf16[256,1024]{1,0:T(8,128)(2,1)S(1)}, u32[]{:S(2)}, u32[]{:S(2)}) %collective-permute-start.17) | collective-permute-done | bytes 524320 | tf_op jit(solution)/shard_map/ppermute | solution.py:51
  154.0 18.5 %widen.1 = (f32[1024,1024]{1,0:T(8,128)}, bf16[1024,1024]{1,0:T(8,128)(2,1)}, bf16[1024,2048]{1,0:T(8,128)(2,1)}, bf16[1024,2048]{1,0:T(8,128)(2,1)}) custom-call(s32[4]{0:T(128)} %pad_add_fusion.place_ref, bf16[1024,1024]{1,0:T(8,128)(2,1)} %bitcast.340, bf16[1024,1024]{1,0:T(8,128)(2,1)} %leave.1.refs_1_, ...), custom_call_target="tpu_custom_call" | custom-call | flops 19800000512 | bytes 1 | tf_op jit(solution)/shard_map/widen/pallas_call | solution.py:293
  173.1 2.7 copy-done.53
  175.9 6.6 %convolution_convert_fusion.1 = bf16[2048,1024]{1,0:T(8,128)(2,1)} fusion(bf16[1024,2048]{1,0:T(8,128)(2,1)S(1)} %copy-done.53, bf16[1024,1024]{1,0:T(8,128)(2,1)S(1)} %bitcast.357), kind=kOutput, calls=%fused_computation.1 | convolution fusion | flops 4297064448 | bytes 10485760 | tf_op jit(solution)/shard_map/dot_general | solution.py:23
  182.5 21.7 %narrow.1 = (bf16[1024,1024]{1,0:T(8,128)(2,1)}, bf16[1024,2048]{1,0:T(8,128)(2,1)}, bf16[1024,1024]{1,0:T(8,128)(2,1)}) custom-call(s32[4]{0:T(128)} %pad_add_fusion.place_ref, bf16[1024,2048]{1,0:T(8,128)(2,1)} %get-tuple-element.156.refs_0_, bf16[1024,1024]{1,0:T(8,128)(2,1)} %bitcast.358, bf16[1024,2048]{1,0:T(8,128)(2,1)} %get-tuple-element.157.refs_2_, ...), custom_call_target="tpu_custom_call" | custom-call | flops 23100000256 | bytes 1 | tf_op jit(solution)/shard_map/narrow/pallas_call | solution.py:293
  204.4 7.0 %convolution_convert_fusion = bf16[1024,2048]{1,0:T(8,128)(2,1)S(1)} fusion(bf16[1024,1024]{1,0:T(8,128)(2,1)S(1)} %copy-done.52, bf16[1024,2048]{1,0:T(8,128)(2,1)} %get-tuple-element.161), kind=kOutput, calls=%fused_computation | convolution fusion | flops 4297064448 | bytes 10485760 | tf_op jit(solution)/shard_map/dot_general | solution.py:23
  212.3 1.6 dynamic-slice_bitcast_fusion.2
  219.3 9.9 %between.1 = (f32[1024,1024]{1,0:T(8,128)}, bf16[1024,1024]{1,0:T(8,128)(2,1)}, bf16[1024,512]{1,0:T(8,128)(2,1)}, f32[8,1024]{1,0:T(8,128)}) custom-call(s32[4]{0:T(128)} %pad_add_fusion.place_ref, bf16[1024,1024]{1,0:T(8,128)(2,1)} %bitcast.359, bf16[1024,1024]{1,0:T(8,128)(2,1)} %get-tuple-element.163.refs_1_, bf16[1024,1024]{1,0:T(8,128)(2,1)} %copy-done.46, ...), custom_call_target="tpu_custom_call" | custom-call | flops 11000000512 | bytes 1 | tf_op jit(solution)/shard_map/between/pallas_call | solution.py:293
  231.3 14.0 %attend_back.2.refs_0_ = bf16[1024,768]{1,0:T(8,128)(2,1)S(1)} custom-call(bf16[1024,1536]{1,0:T(8,128)(2,1)} %get-tuple-element.136.q_ref.k_ref.v_ref, bf16[1024,1536]{1,0:T(8,128)(2,1)} %get-tuple-element.136.q_ref.k_ref.v_ref, bf16[1024,1536]{1,0:T(8,128)(2,1)} %get-tuple-element.136.q_ref.k_ref.v_ref, bf16[1024,512]{1,0:T(8,128)(2,1)S(1)} %copy-done.8, ...), custom_call_target="tpu_custom_call" | custom-call | flops 16499999744 | bytes 1 | tf_op jit(solution)/shard_map/attend_back/pallas_call | solution.py:182
  245.3 8.1 %collective-permute-done.20 = bf16[4,2,32,2048]{3,2,1,0:T(8,128)(2,1)} collective-permute-done((bf16[4,2,32,2048]{3,2,1,0:T(8,128)(2,1)}, bf16[4,2,32,2048]{3,2,1,0:T(8,128)(2,1)}, u32[]{:S(2)}, u32[]{:S(2)}) %collective-permute-start.20) | collective-permute-done | bytes 1048608 | tf_op jit(solution)/shard_map/ppermute | solution.py:51
  253.4 2.2 convolution_convert_fusion.4
  255.7 2.6 reshape.192
  258.3 1.6 copy.134
  260.2 1.9 convolution_convert_fusion.3
  264.0 1.7 add_convert_fusion
  265.9 1.6 add_convert_fusion.1
  267.6 1.5 collective-permute-start.23
  269.5 14.1 %attend_back.3.refs_1_ = bf16[1024,768]{1,0:T(8,128)(2,1)S(1)} custom-call(bf16[1024,1536]{1,0:T(8,128)(2,1)} %get-tuple-element.136.q_ref.k_ref.v_ref, bf16[1024,1536]{1,0:T(8,128)(2,1)} %get-tuple-element.136.q_ref.k_ref.v_ref, bf16[1024,1536]{1,0:T(8,128)(2,1)} %get-tuple-element.136.q_ref.k_ref.v_ref, bf16[1024,512]{1,0:T(8,128)(2,1)S(1)} %copy-done.9, ...), custom_call_target="tpu_custom_call" | custom-call | flops 16499999744 | bytes 1 | tf_op jit(solution)/shard_map/attend_back/pallas_call | solution.py:182
  284.8 1.5 copy-done.21
  286.3 2.7 fusion.11
  289.0 9.1 %enter.1 = (bf16[1024,1024]{1,0:T(8,128)(2,1)}, f32[8,1024]{1,0:T(8,128)}) custom-call(s32[4]{0:T(128)} %pad_add_fusion.place_ref, bf16[1024,768]{1,0:T(8,128)(2,1)} %copy-done.6, bf16[1024,768]{1,0:T(8,128)(2,1)} %copy-done.4, bf16[1024,1024]{1,0:T(8,128)(2,1)} %bitcast.341, bf16[2,64,1664]{2,1,0:T(8,128)(2,1)} %pad_maximum_fusion.8.refs_1_.refs_3_, ...), custom_call_target="tpu_custom_call" | custom-call | flops 9900000256 | bytes 1 | tf_op jit(solution)/shard_map/enter/pallas_call | solution.py:293
  298.9 1.4 collective-permute-start.25
  304.2 1.9 convolution_convert_fusion.2
  307.5 3.1 copy.137
  310.5 3.3 collective-permute-start.27
  313.8 5.0 %collective-permute-start.28 = (bf16[2,32,2048]{2,1,0:T(8,128)(2,1)}, bf16[2,32,2048]{2,1,0:T(8,128)(2,1)}, u32[]{:S(2)}, u32[]{:S(2)}) collective-permute-start(bf16[2,32,2048]{2,1,0:T(8,128)(2,1)} %get-tuple-element.306), channel_id=1, source_target_pairs={{0,4},{2,6},{4,0},{6,2},{1,5},{3,7},{5,1},{7,3},{8,12},{10,14},{12... | collective-permute-start | bytes 786440 | tf_op jit(solution)/shard_map/ppermute | solution.py:208
  322.2 13.6 %collective-permute-done.28 = bf16[2,32,2048]{2,1,0:T(8,128)(2,1)} collective-permute-done((bf16[2,32,2048]{2,1,0:T(8,128)(2,1)}, bf16[2,32,2048]{2,1,0:T(8,128)(2,1)}, u32[]{:S(2)}, u32[]{:S(2)}) %collective-permute-start.28) | collective-permute-done | bytes 262176 | tf_op jit(solution)/shard_map/ppermute | solution.py:208
  335.8 5.3 %collective-permute-done.29 = bf16[2,32,2048]{2,1,0:T(8,128)(2,1)} collective-permute-done((bf16[2,32,2048]{2,1,0:T(8,128)(2,1)S(1)}, bf16[2,32,2048]{2,1,0:T(8,128)(2,1)}, u32[]{:S(2)}, u32[]{:S(2)}) %collective-permute-start.29) | collective-permute-done | bytes 262176 | tf_op jit(solution)/shard_map/ppermute | solution.py:208
  341.1 1.5 add_convert_fusion.2
  344.2 1.7 collective-permute-start.30
  347.4 1.5 collective-permute-start.34
  350.5 6.1 %collective-permute-done.31 = bf16[4,32,1280]{2,1,0:T(8,128)(2,1)S(1)} collective-permute-done((bf16[4,32,1280]{2,1,0:T(8,128)(2,1)S(1)}, bf16[4,32,1280]{2,1,0:T(8,128)(2,1)S(1)}, u32[]{:S(2)}, u32[]{:S(2)}) %collective-permute-start.31) | collective-permute-done | bytes 327712 | tf_op jit(solution)/shard_map/ppermute | solution.py:51
  356.6 9.8 %collective-permute-done.34 = bf16[4,2,32,896]{3,2,0,1:T(8,128)(2,1)S(1)} collective-permute-done((bf16[4,2,32,896]{3,2,0,1:T(8,128)(2,1)S(1)}, bf16[4,2,32,896]{3,2,0,1:T(8,128)(2,1)S(1)}, u32[]{:S(2)}, u32[]{:S(2)}) %collective-permute-start.34) | collective-permute-done | bytes 458784 | tf_op jit(solution)/shard_map/ppermute | solution.py:51
  370.8 1.9 collective-permute-done.35
  372.7 8.3 %collective-permute-done.36 = bf16[2,32,1280]{2,1,0:T(8,128)(2,1)S(1)} collective-permute-done((bf16[2,32,1280]{2,1,0:T(8,128)(2,1)S(1)}, bf16[2,32,1280]{2,1,0:T(8,128)(2,1)S(1)}, u32[]{:S(2)}, u32[]{:S(2)}) %collective-permute-start.36) | collective-permute-done | bytes 163872 | tf_op jit(solution)/shard_map/ppermute | solution.py:208
  382.1 1.5 collective-permute-start.43
  384.0 2.3 collective-permute-start.41
  387.8 6.6 %collective-permute-done.43 = bf16[256,1024]{1,0:T(8,128)(2,1)S(1)} collective-permute-done((bf16[256,1024]{1,0:T(8,128)(2,1)S(1)}, bf16[256,1024]{1,0:T(8,128)(2,1)S(1)}, u32[]{:S(2)}, u32[]{:S(2)}) %collective-permute-start.43) | collective-permute-done | bytes 524320 | tf_op jit(solution)/shard_map/ppermute | solution.py:51
  394.5 2.1 collective-permute-done.42
  396.6 9.0 %collective-permute-done.44 = bf16[256,1024]{1,0:T(8,128)(2,1)S(1)} collective-permute-done((bf16[256,1024]{1,0:T(8,128)(2,1)S(1)}, bf16[256,1024]{1,0:T(8,128)(2,1)S(1)}, u32[]{:S(2)}, u32[]{:S(2)}) %collective-permute-start.44) | collective-permute-done | bytes 524320 | tf_op jit(solution)/shard_map/ppermute | solution.py:51
  409.0 1.5 maximum_bitcast_fusion
  410.4 18.2 %collective-permute-done.45 = bf16[2,32,896]{2,1,0:T(8,128)(2,1)S(1)} collective-permute-done((bf16[2,32,896]{2,1,0:T(8,128)(2,1)S(1)}, bf16[2,32,896]{2,1,0:T(8,128)(2,1)S(1)}, u32[]{:S(2)}, u32[]{:S(2)}) %collective-permute-start.45) | collective-permute-done | bytes 114720 | tf_op jit(solution)/shard_map/ppermute | solution.py:51
  428.7 3.0 collective-permute-start.46
  440.6 1.6 copy.154
  442.5 1.9 copy.153
  444.4 2.9 copy.155
  448.5 1.6 bitcast_convert_fusion
  (311 shorter events, 79.5 us)
Async XLA Ops:
  7.2 34.3 %copy-start = (bf16[512,1024]{1,0:T(8,128)(2,1)S(1)}, bf16[512,1024]{1,0:T(8,128)(2,1)}, u32[]{:S(2)}) copy-start(bf16[512,1024]{1,0:T(8,128)(2,1)} %param.20) | copy-start | bytes 3145732
  7.2 108.3 %all-gather.6.cloned.1.call-start = ((), (), s32[]{:S(2)}) async-start(), calls=%async_computation.3 | async-start | bytes 1179648 | tf_op jit(solution)/shard_map/all_gather | solution.py:403
  9.2 28.7 %collective-permute-start.4 = (bf16[256,1024]{1,0:T(8,128)(2,1)}, bf16[256,1024]{1,0:T(8,128)(2,1)}, u32[]{:S(2)}, u32[]{:S(2)}) collective-permute-start(bf16[256,1024]{1,0:T(8,128)(2,1)} %dynamic-slice_bitcast_fusion.11), channel_id=1, source_target_pairs={{0,16},{16,0},{1,17},{17,1},{2,18},{18,2},{3,19},{19,3},{4,20},{20... | collective-permute-start | bytes 1572872 | tf_op jit(solution)/shard_map/ppermute | solution.py:51
  14.0 23.9 %collective-permute-start.3 = (bf16[2,64,1664]{2,1,0:T(8,128)(2,1)}, bf16[2,64,1664]{2,1,0:T(8,128)(2,1)}, u32[]{:S(2)}, u32[]{:S(2)}) collective-permute-start(bf16[2,64,1664]{2,1,0:T(8,128)(2,1)} %pad_maximum_fusion.8.refs_1_.refs_3_), channel_id=1, source_target_pairs={{0,1},{1,0},{2,3},{3,2},{4,5},{5,4},{6,7},{7,6},{8,9},{9,8},{10,11... | collective-permute-start | bytes 1277960 | tf_op jit(solution)/shard_map/ppermute | solution.py:51
  15.9 7.9 %collective-permute-start = (bf16[64,1664]{1,0:T(8,128)(2,1)}, bf16[64,1664]{1,0:T(8,128)(2,1)S(1)}, u32[]{:S(2)}, u32[]{:S(2)}) collective-permute-start(bf16[64,1664]{1,0:T(8,128)(2,1)} %fusion.62), channel_id=1, source_target_pairs={{0,2},{2,4},{4,6},{6,0},{1,3},{3,5},{5,7},{7,1},{8,10},{10,12},{12... | collective-permute-start | bytes 638984 | tf_op jit(solution)/shard_map/ppermute | solution.py:208
  17.2 17.3 %collective-permute-start.1 = (bf16[64,1664]{1,0:T(8,128)(2,1)}, bf16[64,1664]{1,0:T(8,128)(2,1)}, u32[]{:S(2)}, u32[]{:S(2)}) collective-permute-start(bf16[64,1664]{1,0:T(8,128)(2,1)} %fusion.62), channel_id=1, source_target_pairs={{0,4},{2,6},{4,0},{6,2},{1,5},{3,7},{5,1},{7,3},{8,12},{10,14},{12... | collective-permute-start | bytes 638984 | tf_op jit(solution)/shard_map/ppermute | solution.py:208
  18.2 19.7 %collective-permute-start.2 = (bf16[64,1664]{1,0:T(8,128)(2,1)}, bf16[64,1664]{1,0:T(8,128)(2,1)}, u32[]{:S(2)}, u32[]{:S(2)}) collective-permute-start(bf16[64,1664]{1,0:T(8,128)(2,1)} %fusion.62), channel_id=1, source_target_pairs={{0,6},{2,0},{4,2},{6,4},{1,7},{3,1},{5,3},{7,5},{8,14},{10,8},{12,... | collective-permute-start | bytes 638984 | tf_op jit(solution)/shard_map/ppermute | solution.py:208
  23.8 39.6 %copy-start.27 = (bf16[2,64,2048]{2,1,0:T(8,128)(2,1)}, bf16[2,64,2048]{2,1,0:T(8,128)(2,1)S(1)}, u32[]{:S(2)}) copy-start(bf16[2,64,2048]{2,1,0:T(8,128)(2,1)S(1)} %reshape_reshape.6.refs_4_) | copy-start | bytes 1572868
  40.3 5.3 %collective-permute-start.7 = (bf16[2,256,1024]{2,1,0:T(8,128)(2,1)}, bf16[2,256,1024]{2,1,0:T(8,128)(2,1)}, u32[]{:S(2)}, u32[]{:S(2)}) collective-permute-start(bf16[2,256,1024]{2,1,0:T(8,128)(2,1)} %pad_maximum_fusion.3), channel_id=1, source_target_pairs={{0,8},{8,0},{1,9},{9,1},{2,10},{10,2},{3,11},{11,3},{4,12},{12,4},... | collective-permute-start | bytes 3145736 | tf_op jit(solution)/shard_map/ppermute | solution.py:51
  41.5 141.1 %all-gather.4.cloned.1.call-start = ((), (), s32[]{:S(2)}) async-start(), calls=%async_computation.1 | async-start | bytes 4718592 | tf_op jit(solution)/shard_map/all_gather | solution.py:421
  43.5 18.6 %collective-permute-start.5 = (bf16[3,64,1664]{2,1,0:T(8,128)(2,1)S(1)}, bf16[3,64,1664]{2,1,0:T(8,128)(2,1)}, u32[]{:S(2)}, u32[]{:S(2)}) collective-permute-start(bf16[3,64,1664]{2,1,0:T(8,128)(2,1)S(1)} %pad_maximum_fusion.7.refs_3_.refs_5_), channel_id=1, source_target_pairs={{0,1},{1,0},{2,3},{3,2},{4,5},{5,4},{6,7},{7,6},{8,9},{9,8},{10,11... | collective-permute-start | bytes 1916936 | tf_op jit(solution)/shard_map/ppermute | solution.py:51
  43.8 18.3 %collective-permute-start.6 = (bf16[3,64,1664]{2,1,0:T(8,128)(2,1)S(1)}, bf16[3,64,1664]{2,1,0:T(8,128)(2,1)S(1)}, u32[]{:S(2)}, u32[]{:S(2)}) collective-permute-start(bf16[3,64,1664]{2,1,0:T(8,128)(2,1)S(1)} %pad_maximum_fusion.7.refs_3_.refs_5_), channel_id=1, source_target_pairs={{0,16},{16,0},{1,17},{17,1},{2,18},{18,2},{3,19},{19,3},{4,20},{20... | collective-permute-start | bytes 1916936 | tf_op jit(solution)/shard_map/ppermute | solution.py:51
  44.1 8.8 %collective-permute-start.8 = (bf16[64,2048]{1,0:T(8,128)(2,1)S(1)}, bf16[64,2048]{1,0:T(8,128)(2,1)S(1)}, u32[]{:S(2)}, u32[]{:S(2)}) collective-permute-start(bf16[64,2048]{1,0:T(8,128)(2,1)S(1)} %dynamic-slice_bitcast_fusion.18), channel_id=1, source_target_pairs={{0,2},{2,4},{4,6},{6,0},{1,3},{3,5},{5,7},{7,1},{8,10},{10,12},{12... | collective-permute-start | bytes 786440 | tf_op jit(solution)/shard_map/ppermute | solution.py:208
  44.1 17.9 %collective-permute-start.9 = (bf16[64,2048]{1,0:T(8,128)(2,1)S(1)}, bf16[64,2048]{1,0:T(8,128)(2,1)S(1)}, u32[]{:S(2)}, u32[]{:S(2)}) collective-permute-start(bf16[64,2048]{1,0:T(8,128)(2,1)S(1)} %dynamic-slice_bitcast_fusion.18), channel_id=1, source_target_pairs={{0,6},{2,0},{4,2},{6,4},{1,7},{3,1},{5,3},{7,5},{8,14},{10,8},{12,... | collective-permute-start | bytes 786440 | tf_op jit(solution)/shard_map/ppermute | solution.py:208
  62.1 20.8 %collective-permute-start.10 = (bf16[3,64,1664]{2,1,0:T(8,128)(2,1)}, bf16[3,64,1664]{2,1,0:T(8,128)(2,1)S(1)}, u32[]{:S(2)}, u32[]{:S(2)}) collective-permute-start(bf16[3,64,1664]{2,1,0:T(8,128)(2,1)} %collective-permute-done.5.refs_4_.refs_6_), channel_id=1, source_target_pairs={{0,16},{16,0},{1,17},{17,1},{2,18},{18,2},{3,19},{19,3},{4,20},{20... | collective-permute-start | bytes 1916936 | tf_op jit(solution)/shard_map/ppermute | solution.py:51
  63.4 19.5 %collective-permute-start.11 = (bf16[2,64,2048]{2,1,0:T(8,128)(2,1)S(1)}, bf16[2,64,2048]{2,1,0:T(8,128)(2,1)}, u32[]{:S(2)}, u32[]{:S(2)}) collective-permute-start(bf16[2,64,2048]{2,1,0:T(8,128)(2,1)S(1)} %reshape_reshape.6.refs_4_), channel_id=1, source_target_pairs={{0,1},{1,0},{2,3},{3,2},{4,5},{5,4},{6,7},{7,6},{8,9},{9,8},{10,11... | collective-permute-start | bytes 1572872 | tf_op jit(solution)/shard_map/ppermute | solution.py:51
  64.6 18.2 %collective-permute-start.12 = (bf16[64,2048]{1,0:T(8,128)(2,1)S(1)}, bf16[64,2048]{1,0:T(8,128)(2,1)S(1)}, u32[]{:S(2)}, u32[]{:S(2)}) collective-permute-start(bf16[64,2048]{1,0:T(8,128)(2,1)S(1)} %dynamic-slice_bitcast_fusion.18), channel_id=1, source_target_pairs={{0,4},{2,6},{4,0},{6,2},{1,5},{3,7},{5,1},{7,3},{8,12},{10,14},{12... | collective-permute-start | bytes 786440 | tf_op jit(solution)/shard_map/ppermute | solution.py:208
  66.8 274.3 %reduce-scatter.2.cloned.1.call-start = ((), (), s32[]{:S(2)}) async-start(), calls=%async_computation.2 | async-start | bytes 4718592 | tf_op jit(solution)/shard_map/reduce_scatter | solution.py:552
  83.0 31.7 %collective-permute-start.13 = (bf16[3,64,2048]{2,1,0:T(8,128)(2,1)S(1)}, bf16[3,64,2048]{2,1,0:T(8,128)(2,1)}, u32[]{:S(2)}, u32[]{:S(2)}) collective-permute-start(bf16[3,64,2048]{2,1,0:T(8,128)(2,1)S(1)} %pad_maximum_fusion.6.refs_6_), channel_id=1, source_target_pairs={{0,1},{1,0},{2,3},{3,2},{4,5},{5,4},{6,7},{7,6},{8,9},{9,8},{10,11... | collective-permute-start | bytes 2359304 | tf_op jit(solution)/shard_map/ppermute | solution.py:51
  83.3 31.4 %collective-permute-start.14 = (bf16[3,64,2048]{2,1,0:T(8,128)(2,1)S(1)}, bf16[3,64,2048]{2,1,0:T(8,128)(2,1)S(1)}, u32[]{:S(2)}, u32[]{:S(2)}) collective-permute-start(bf16[3,64,2048]{2,1,0:T(8,128)(2,1)S(1)} %pad_maximum_fusion.6.refs_6_), channel_id=1, source_target_pairs={{0,16},{16,0},{1,17},{17,1},{2,18},{18,2},{3,19},{19,3},{4,20},{20... | collective-permute-start | bytes 2359304 | tf_op jit(solution)/shard_map/ppermute | solution.py:51
  120.5 21.3 %collective-permute-start.15 = (bf16[1024,1024]{1,0:T(8,128)(2,1)}, bf16[1024,1024]{1,0:T(8,128)(2,1)}, u32[]{:S(2)}, u32[]{:S(2)}) collective-permute-start(bf16[1024,1024]{1,0:T(8,128)(2,1)} %leave.1.refs_1_), channel_id=1, source_target_pairs={{0,8},{8,0},{1,9},{9,1},{2,10},{10,2},{3,11},{11,3},{4,12},{12,4},... | collective-permute-start | bytes 6291464 | tf_op jit(solution)/shard_map/ppermute | solution.py:51
  122.4 19.4 %collective-permute-start.16 = (bf16[3,64,2048]{2,1,0:T(8,128)(2,1)}, bf16[3,64,2048]{2,1,0:T(8,128)(2,1)}, u32[]{:S(2)}, u32[]{:S(2)}) collective-permute-start(bf16[3,64,2048]{2,1,0:T(8,128)(2,1)} %collective-permute-done.13.refs_7_), channel_id=1, source_target_pairs={{0,16},{16,0},{1,17},{17,1},{2,18},{18,2},{3,19},{19,3},{4,20},{20... | collective-permute-start | bytes 2359304 | tf_op jit(solution)/shard_map/ppermute | solution.py:51
  123.6 29.4 %copy-start.30 = (bf16[2,1,256,1024]{3,2,1,0:T(8,128)(2,1)S(1)}, bf16[2,1,256,1024]{3,2,1,0:T(8,128)(2,1)}, u32[]{:S(2)}) copy-start(bf16[2,1,256,1024]{3,2,1,0:T(8,128)(2,1)} %param.21) | copy-start | bytes 3145732
  126.4 26.6 %collective-permute-start.17 = (bf16[256,1024]{1,0:T(8,128)(2,1)S(1)}, bf16[256,1024]{1,0:T(8,128)(2,1)S(1)}, u32[]{:S(2)}, u32[]{:S(2)}) collective-permute-start(bf16[256,1024]{1,0:T(8,128)(2,1)S(1)} %dynamic-slice_bitcast_fusion.9), channel_id=1, source_target_pairs={{0,16},{16,0},{1,17},{17,1},{2,18},{18,2},{3,19},{19,3},{4,20},{20... | collective-permute-start | bytes 1572872 | tf_op jit(solution)/shard_map/ppermute | solution.py:51
  126.8 26.4 %copy-start.38 = (f32[2,256]{1,0:T(2,128)}, f32[2,256]{1,0:T(2,128)S(1)}, u32[]{:S(2)}) copy-start(f32[2,256]{1,0:T(2,128)S(1)} %broadcast_multiply_fusion.2) | copy-start | bytes 6148
  153.2 19.3 %collective-permute-start.18 = (bf16[2,256,1024]{2,1,0:T(8,128)(2,1)S(1)}, bf16[2,256,1024]{2,1,0:T(8,128)(2,1)S(1)}, u32[]{:S(2)}, u32[]{:S(2)}) collective-permute-start(bf16[2,256,1024]{2,1,0:T(8,128)(2,1)S(1)} %pad_maximum_fusion.4), channel_id=1, source_target_pairs={{0,8},{8,0},{1,9},{9,1},{2,10},{10,2},{3,11},{11,3},{4,12},{12,4},... | collective-permute-start | bytes 3145736 | tf_op jit(solution)/shard_map/ppermute | solution.py:51
  204.3 11.0 %collective-permute-start.19 = (bf16[1024,1024]{1,0:T(8,128)(2,1)}, bf16[1024,1024]{1,0:T(8,128)(2,1)S(1)}, u32[]{:S(2)}, u32[]{:S(2)}) collective-permute-start(bf16[1024,1024]{1,0:T(8,128)(2,1)} %get-tuple-element.163.refs_1_), channel_id=1, source_target_pairs={{0,8},{8,0},{1,9},{9,1},{2,10},{10,2},{3,11},{11,3},{4,12},{12,4},... | collective-permute-start | bytes 6291464 | tf_op jit(solution)/shard_map/ppermute | solution.py:51
  217.3 28.0 %collective-permute-start.22 = (bf16[2,256,1024]{2,1,0:T(8,128)(2,1)}, bf16[2,256,1024]{2,1,0:T(8,128)(2,1)}, u32[]{:S(2)}, u32[]{:S(2)}) collective-permute-start(bf16[2,256,1024]{2,1,0:T(8,128)(2,1)} %dynamic-slice_bitcast_fusion.1), channel_id=1, source_target_pairs={{0,8},{8,0},{1,9},{9,1},{2,10},{10,2},{3,11},{11,3},{4,12},{12,4},... | collective-permute-start | bytes 3145736 | tf_op jit(solution)/shard_map/ppermute | solution.py:51
  217.8 35.6 %collective-permute-start.20 = (bf16[4,2,32,2048]{3,2,1,0:T(8,128)(2,1)}, bf16[4,2,32,2048]{3,2,1,0:T(8,128)(2,1)}, u32[]{:S(2)}, u32[]{:S(2)}) collective-permute-start(bf16[4,2,32,2048]{3,2,1,0:T(8,128)(2,1)} %get-tuple-element.169), channel_id=1, source_target_pairs={{0,1},{1,0},{2,3},{3,2},{4,5},{5,4},{6,7},{7,6},{8,9},{9,8},{10,11... | collective-permute-start | bytes 3145736 | tf_op jit(solution)/shard_map/ppermute | solution.py:51
  218.1 35.4 %collective-permute-start.21 = (bf16[4,2,32,2048]{3,2,0,1:T(8,128)(2,1)}, bf16[4,2,32,2048]{3,2,0,1:T(8,128)(2,1)}, u32[]{:S(2)}, u32[]{:S(2)}) collective-permute-start(bf16[4,2,32,2048]{3,2,0,1:T(8,128)(2,1)} %get-tuple-element.170), channel_id=1, source_target_pairs={{0,16},{16,0},{1,17},{17,1},{2,18},{18,2},{3,19},{19,3},{4,20},{20... | collective-permute-start | bytes 3145736 | tf_op jit(solution)/shard_map/ppermute | solution.py:51
  231.2 22.2 %copy-start.3 = (bf16[1024,512]{1,0:T(8,128)(2,1)S(1)}, bf16[1024,512]{1,0:T(8,128)(2,1)}, u32[]{:S(2)}) copy-start(bf16[1024,512]{1,0:T(8,128)(2,1)} %copy-done.2) | copy-start | bytes 3145732
  231.2 22.2 %copy-start.23 = (bf16[1024,1024]{1,0:T(8,128)(2,1)S(1)}, bf16[1024,1024]{1,0:T(8,128)(2,1)}, u32[]{:S(2)}) copy-start(bf16[1024,1024]{1,0:T(8,128)(2,1)} %get-tuple-element.179) | copy-start | bytes 6291460
  265.8 23.2 %collective-permute-start.24 = (bf16[4,32,2048]{2,1,0:T(8,128)(2,1)S(1)}, bf16[4,32,2048]{2,1,0:T(8,128)(2,1)S(1)}, u32[]{:S(2)}, u32[]{:S(2)}) collective-permute-start(bf16[4,32,2048]{2,1,0:T(8,128)(2,1)S(1)} %dynamic-slice_bitcast_fusion.7), channel_id=1, source_target_pairs={{0,1},{1,0},{2,3},{3,2},{4,5},{5,4},{6,7},{7,6},{8,9},{9,8},{10,11... | collective-permute-start | bytes 1572872 | tf_op jit(solution)/shard_map/ppermute | solution.py:51
  267.6 21.4 %collective-permute-start.23 = (bf16[4,32,2048]{2,1,0:T(8,128)(2,1)S(1)}, bf16[4,32,2048]{2,1,0:T(8,128)(2,1)}, u32[]{:S(2)}, u32[]{:S(2)}) collective-permute-start(bf16[4,32,2048]{2,1,0:T(8,128)(2,1)S(1)} %dynamic-slice_bitcast_fusion.8), channel_id=1, source_target_pairs={{0,16},{16,0},{1,17},{17,1},{2,18},{18,2},{3,19},{19,3},{4,20},{20... | collective-permute-start | bytes 1572872 | tf_op jit(solution)/shard_map/ppermute | solution.py:51
  298.9 42.1 %collective-permute-start.25 = (bf16[4,2,32,1280]{3,2,1,0:T(8,128)(2,1)}, bf16[4,2,32,1280]{3,2,1,0:T(8,128)(2,1)}, u32[]{:S(2)}, u32[]{:S(2)}) collective-permute-start(bf16[4,2,32,1280]{3,2,1,0:T(8,128)(2,1)} %get-tuple-element.184), channel_id=1, source_target_pairs={{0,1},{1,0},{2,3},{3,2},{4,5},{5,4},{6,7},{7,6},{8,9},{9,8},{10,11... | collective-permute-start | bytes 1966088 | tf_op jit(solution)/shard_map/ppermute | solution.py:51
  300.4 40.7 %collective-permute-start.26 = (bf16[4,2,32,1280]{3,2,0,1:T(8,128)(2,1)}, bf16[4,2,32,1280]{3,2,0,1:T(8,128)(2,1)}, u32[]{:S(2)}, u32[]{:S(2)}) collective-permute-start(bf16[4,2,32,1280]{3,2,0,1:T(8,128)(2,1)} %bitcast.336), channel_id=1, source_target_pairs={{0,16},{16,0},{1,17},{17,1},{2,18},{18,2},{3,19},{19,3},{4,20},{20... | collective-permute-start | bytes 1966088 | tf_op jit(solution)/shard_map/ppermute | solution.py:51
  310.5 11.7 %collective-permute-start.27 = (bf16[2,32,2048]{2,1,0:T(8,128)(2,1)}, bf16[2,32,2048]{2,1,0:T(8,128)(2,1)}, u32[]{:S(2)}, u32[]{:S(2)}) collective-permute-start(bf16[2,32,2048]{2,1,0:T(8,128)(2,1)} %get-tuple-element.305), channel_id=1, source_target_pairs={{0,2},{2,4},{4,6},{6,0},{1,3},{3,5},{5,7},{7,1},{8,10},{10,12},{12... | collective-permute-start | bytes 786440 | tf_op jit(solution)/shard_map/ppermute | solution.py:208
  313.8 22.0 %collective-permute-start.28 = (bf16[2,32,2048]{2,1,0:T(8,128)(2,1)}, bf16[2,32,2048]{2,1,0:T(8,128)(2,1)}, u32[]{:S(2)}, u32[]{:S(2)}) collective-permute-start(bf16[2,32,2048]{2,1,0:T(8,128)(2,1)} %get-tuple-element.306), channel_id=1, source_target_pairs={{0,4},{2,6},{4,0},{6,2},{1,5},{3,7},{5,1},{7,3},{8,12},{10,14},{12... | collective-permute-start | bytes 786440 | tf_op jit(solution)/shard_map/ppermute | solution.py:208
  318.8 22.3 %collective-permute-start.29 = (bf16[2,32,2048]{2,1,0:T(8,128)(2,1)S(1)}, bf16[2,32,2048]{2,1,0:T(8,128)(2,1)}, u32[]{:S(2)}, u32[]{:S(2)}) collective-permute-start(bf16[2,32,2048]{2,1,0:T(8,128)(2,1)S(1)} %get-tuple-element.304), channel_id=1, source_target_pairs={{0,6},{2,0},{4,2},{6,4},{1,7},{3,1},{5,3},{7,5},{8,14},{10,8},{12,... | collective-permute-start | bytes 786440 | tf_op jit(solution)/shard_map/ppermute | solution.py:208
  320.2 23.9 %copy-start.15 = (bf16[1024,1024]{1,0:T(8,128)(2,1)S(1)}, bf16[1024,1024]{1,0:T(8,128)(2,1)}, u32[]{:S(2)}) copy-start(bf16[1024,1024]{1,0:T(8,128)(2,1)} %get-tuple-element.192) | copy-start | bytes 6291460
  342.6 7.9 %collective-permute-start.32 = (bf16[4,32,1280]{2,1,0:T(8,128)(2,1)S(1)}, bf16[4,32,1280]{2,1,0:T(8,128)(2,1)S(1)}, u32[]{:S(2)}, u32[]{:S(2)}) collective-permute-start(bf16[4,32,1280]{2,1,0:T(8,128)(2,1)S(1)} %dynamic-slice_bitcast_fusion.16), channel_id=1, source_target_pairs={{0,1},{1,0},{2,3},{3,2},{4,5},{5,4},{6,7},{7,6},{8,9},{9,8},{10,11... | collective-permute-start | bytes 983048 | tf_op jit(solution)/shard_map/ppermute | solution.py:51
  344.2 22.3 %collective-permute-start.30 = (bf16[2,256,1024]{2,1,0:T(8,128)(2,1)S(1)}, bf16[2,256,1024]{2,1,0:T(8,128)(2,1)S(1)}, u32[]{:S(2)}, u32[]{:S(2)}) collective-permute-start(bf16[2,256,1024]{2,1,0:T(8,128)(2,1)S(1)} %dynamic-slice_bitcast_fusion), channel_id=1, source_target_pairs={{0,8},{8,0},{1,9},{9,1},{2,10},{10,2},{3,11},{11,3},{4,12},{12,4},... | collective-permute-start | bytes 3145736 | tf_op jit(solution)/shard_map/ppermute | solution.py:51
  347.2 9.3 %collective-permute-start.31 = (bf16[4,32,1280]{2,1,0:T(8,128)(2,1)S(1)}, bf16[4,32,1280]{2,1,0:T(8,128)(2,1)S(1)}, u32[]{:S(2)}, u32[]{:S(2)}) collective-permute-start(bf16[4,32,1280]{2,1,0:T(8,128)(2,1)S(1)} %dynamic-slice_bitcast_fusion.17), channel_id=1, source_target_pairs={{0,16},{16,0},{1,17},{17,1},{2,18},{18,2},{3,19},{19,3},{4,20},{20... | collective-permute-start | bytes 983048 | tf_op jit(solution)/shard_map/ppermute | solution.py:51
  347.4 19.0 %collective-permute-start.34 = (bf16[4,2,32,896]{3,2,0,1:T(8,128)(2,1)S(1)}, bf16[4,2,32,896]{3,2,0,1:T(8,128)(2,1)S(1)}, u32[]{:S(2)}, u32[]{:S(2)}) collective-permute-start(bf16[4,2,32,896]{3,2,0,1:T(8,128)(2,1)S(1)} %copy.138), channel_id=1, source_target_pairs={{0,16},{16,0},{1,17},{17,1},{2,18},{18,2},{3,19},{19,3},{4,20},{20... | collective-permute-start | bytes 1376264 | tf_op jit(solution)/shard_map/ppermute | solution.py:51
  348.9 17.5 %collective-permute-start.33 = (bf16[4,2,32,896]{3,2,1,0:T(8,128)(2,1)S(1)}, bf16[4,2,32,896]{3,2,1,0:T(8,128)(2,1)S(1)}, u32[]{:S(2)}, u32[]{:S(2)}) collective-permute-start(bf16[4,2,32,896]{3,2,1,0:T(8,128)(2,1)S(1)} %copy-done.35), channel_id=1, source_target_pairs={{0,1},{1,0},{2,3},{3,2},{4,5},{5,4},{6,7},{7,6},{8,9},{9,8},{10,11... | collective-permute-start | bytes 1376264 | tf_op jit(solution)/shard_map/ppermute | solution.py:51
  367.5 14.5 %collective-permute-start.39 = (bf16[4,32,896]{2,1,0:T(8,128)(2,1)S(1)}, bf16[4,32,896]{2,1,0:T(8,128)(2,1)S(1)}, u32[]{:S(2)}, u32[]{:S(2)}) collective-permute-start(bf16[4,32,896]{2,1,0:T(8,128)(2,1)S(1)} %dynamic-slice_bitcast_fusion.19), channel_id=1, source_target_pairs={{0,1},{1,0},{2,3},{3,2},{4,5},{5,4},{6,7},{7,6},{8,9},{9,8},{10,11... | collective-permute-start | bytes 688136 | tf_op jit(solution)/shard_map/ppermute | solution.py:51
  367.8 14.1 %collective-permute-start.38 = (bf16[4,32,896]{2,1,0:T(8,128)(2,1)S(1)}, bf16[4,32,896]{2,1,0:T(8,128)(2,1)S(1)}, u32[]{:S(2)}, u32[]{:S(2)}) collective-permute-start(bf16[4,32,896]{2,1,0:T(8,128)(2,1)S(1)} %dynamic-slice_bitcast_fusion.20), channel_id=1, source_target_pairs={{0,16},{16,0},{1,17},{17,1},{2,18},{18,2},{3,19},{19,3},{4,20},{20... | collective-permute-start | bytes 688136 | tf_op jit(solution)/shard_map/ppermute | solution.py:51
  368.2 4.5 collective-permute-start.35
  368.2 12.7 %collective-permute-start.36 = (bf16[2,32,1280]{2,1,0:T(8,128)(2,1)S(1)}, bf16[2,32,1280]{2,1,0:T(8,128)(2,1)S(1)}, u32[]{:S(2)}, u32[]{:S(2)}) collective-permute-start(bf16[2,32,1280]{2,1,0:T(8,128)(2,1)S(1)} %get-tuple-element.315), channel_id=1, source_target_pairs={{0,4},{2,6},{4,0},{6,2},{1,5},{3,7},{5,1},{7,3},{8,12},{10,14},{12... | collective-permute-start | bytes 491528 | tf_op jit(solution)/shard_map/ppermute | solution.py:208
  368.3 13.7 %collective-permute-start.37 = (bf16[2,32,1280]{2,1,0:T(8,128)(2,1)S(1)}, bf16[2,32,1280]{2,1,0:T(8,128)(2,1)S(1)}, u32[]{:S(2)}, u32[]{:S(2)}) collective-permute-start(bf16[2,32,1280]{2,1,0:T(8,128)(2,1)S(1)} %get-tuple-element.313), channel_id=1, source_target_pairs={{0,6},{2,0},{4,2},{6,4},{1,7},{3,1},{5,3},{7,5},{8,14},{10,8},{12,... | collective-permute-start | bytes 491528 | tf_op jit(solution)/shard_map/ppermute | solution.py:208
  382.1 12.3 %collective-permute-start.43 = (bf16[256,1024]{1,0:T(8,128)(2,1)S(1)}, bf16[256,1024]{1,0:T(8,128)(2,1)S(1)}, u32[]{:S(2)}, u32[]{:S(2)}) collective-permute-start(bf16[256,1024]{1,0:T(8,128)(2,1)S(1)} %fusion.22), channel_id=1, source_target_pairs={{0,16},{16,0},{1,17},{17,1},{2,18},{18,2},{3,19},{19,3},{4,20},{20... | collective-permute-start | bytes 1572872 | tf_op jit(solution)/shard_map/ppermute | solution.py:51
  383.6 22.0 %collective-permute-start.44 = (bf16[256,1024]{1,0:T(8,128)(2,1)S(1)}, bf16[256,1024]{1,0:T(8,128)(2,1)S(1)}, u32[]{:S(2)}, u32[]{:S(2)}) collective-permute-start(bf16[256,1024]{1,0:T(8,128)(2,1)S(1)} %dynamic-slice_bitcast_fusion.6), channel_id=1, source_target_pairs={{0,16},{16,0},{1,17},{17,1},{2,18},{18,2},{3,19},{19,3},{4,20},{20... | collective-permute-start | bytes 1572872 | tf_op jit(solution)/shard_map/ppermute | solution.py:51
  383.9 10.6 %collective-permute-start.40 = (bf16[2,32,896]{2,1,0:T(8,128)(2,1)S(1)}, bf16[2,32,896]{2,1,0:T(8,128)(2,1)S(1)}, u32[]{:S(2)}, u32[]{:S(2)}) collective-permute-start(bf16[2,32,896]{2,1,0:T(8,128)(2,1)S(1)} %get-tuple-element.319), channel_id=1, source_target_pairs={{0,2},{2,4},{4,6},{6,0},{1,3},{3,5},{5,7},{7,1},{8,10},{10,12},{12... | collective-permute-start | bytes 344072 | tf_op jit(solution)/shard_map/ppermute | solution.py:208
  384.0 10.5 %collective-permute-start.41 = (bf16[2,32,896]{2,1,0:T(8,128)(2,1)S(1)}, bf16[2,32,896]{2,1,0:T(8,128)(2,1)S(1)}, u32[]{:S(2)}, u32[]{:S(2)}) collective-permute-start(bf16[2,32,896]{2,1,0:T(8,128)(2,1)S(1)} %get-tuple-element.320), channel_id=1, source_target_pairs={{0,4},{2,6},{4,0},{6,2},{1,5},{3,7},{5,1},{7,3},{8,12},{10,14},{12... | collective-permute-start | bytes 344072 | tf_op jit(solution)/shard_map/ppermute | solution.py:208
  386.3 10.3 %collective-permute-start.42 = (bf16[2,32,896]{2,1,0:T(8,128)(2,1)S(1)}, bf16[2,32,896]{2,1,0:T(8,128)(2,1)S(1)}, u32[]{:S(2)}, u32[]{:S(2)}) collective-permute-start(bf16[2,32,896]{2,1,0:T(8,128)(2,1)S(1)} %get-tuple-element.318), channel_id=1, source_target_pairs={{0,6},{2,0},{4,2},{6,4},{1,7},{3,1},{5,3},{7,5},{8,14},{10,8},{12,... | collective-permute-start | bytes 344072 | tf_op jit(solution)/shard_map/ppermute | solution.py:208
  405.6 33.9 %collective-permute-start.52 = (bf16[256,1024]{1,0:T(8,128)(2,1)S(1)}, bf16[256,1024]{1,0:T(8,128)(2,1)S(1)}, u32[]{:S(2)}, u32[]{:S(2)}) collective-permute-start(bf16[256,1024]{1,0:T(8,128)(2,1)S(1)} %copy-done.34), channel_id=1, source_target_pairs={{0,16},{16,0},{1,17},{17,1},{2,18},{18,2},{3,19},{19,3},{4,20},{20... | collective-permute-start | bytes 1572872 | tf_op jit(solution)/shard_map/ppermute | solution.py:51
  407.0 29.0 %collective-permute-start.50 = (bf16[2,32,2048]{2,1,0:T(8,128)(2,1)S(1)}, bf16[2,32,2048]{2,1,0:T(8,128)(2,1)}, u32[]{:S(2)}, u32[]{:S(2)}) collective-permute-start(bf16[2,32,2048]{2,1,0:T(8,128)(2,1)S(1)} %fusion.31), channel_id=1, source_target_pairs={{0,16},{16,0},{1,17},{17,1},{2,18},{18,2},{3,19},{19,3},{4,20},{20... | collective-permute-start | bytes 786440 | tf_op jit(solution)/shard_map/ppermute | solution.py:51
  407.1 27.0 %collective-permute-start.47 = (bf16[2,32,1280]{2,1,0:T(8,128)(2,1)S(1)}, bf16[2,32,1280]{2,1,0:T(8,128)(2,1)}, u32[]{:S(2)}, u32[]{:S(2)}) collective-permute-start(bf16[2,32,1280]{2,1,0:T(8,128)(2,1)S(1)} %fusion.44), channel_id=1, source_target_pairs={{0,16},{16,0},{1,17},{17,1},{2,18},{18,2},{3,19},{19,3},{4,20},{20... | collective-permute-start | bytes 491528 | tf_op jit(solution)/shard_map/ppermute | solution.py:51
  408.5 20.1 %collective-permute-start.45 = (bf16[2,32,896]{2,1,0:T(8,128)(2,1)S(1)}, bf16[2,32,896]{2,1,0:T(8,128)(2,1)S(1)}, u32[]{:S(2)}, u32[]{:S(2)}) collective-permute-start(bf16[2,32,896]{2,1,0:T(8,128)(2,1)S(1)} %fusion.60), channel_id=1, source_target_pairs={{0,16},{16,0},{1,17},{17,1},{2,18},{18,2},{3,19},{19,3},{4,20},{20... | collective-permute-start | bytes 344072 | tf_op jit(solution)/shard_map/ppermute | solution.py:51
  428.7 4.2 collective-permute-start.46
  435.1 2.2 collective-permute-start.49
  435.4 4.9 %collective-permute-start.48 = (bf16[128,3,8,64]{0,3,2,1:T(8,128)(2,1)S(1)}, bf16[128,3,8,64]{0,3,2,1:T(8,128)(2,1)S(1)}, u32[]{:S(2)}, u32[]{:S(2)}) collective-permute-start(bf16[128,3,8,64]{0,3,2,1:T(8,128)(2,1)S(1)} %pad_maximum_fusion.10), channel_id=1, source_target_pairs={{0,8},{8,0},{1,9},{9,1},{2,10},{10,2},{3,11},{11,3},{4,12},{12,4},... | collective-permute-start | bytes 1179656 | tf_op jit(solution)/shard_map/ppermute | solution.py:51
  437.2 5.1 %collective-permute-start.51 = (bf16[128,8,256]{2,1,0:T(8,128)(2,1)S(1)}, bf16[128,8,256]{2,1,0:T(8,128)(2,1)S(1)}, u32[]{:S(2)}, u32[]{:S(2)}) collective-permute-start(bf16[128,8,256]{2,1,0:T(8,128)(2,1)S(1)} %bitcast.354), channel_id=1, source_target_pairs={{0,8},{8,0},{1,9},{9,1},{2,10},{10,2},{3,11},{11,3},{4,12},{12,4},... | collective-permute-start | bytes 1572872 | tf_op jit(solution)/shard_map/ppermute | solution.py:51
  439.7 7.5 %collective-permute-start.53 = (bf16[256,1024]{1,0:T(8,128)(2,1)S(1)}, bf16[256,1024]{1,0:T(8,128)(2,1)}, u32[]{:S(2)}, u32[]{:S(2)}) collective-permute-start(bf16[256,1024]{1,0:T(8,128)(2,1)S(1)} %add_convert_fusion.4), channel_id=1, source_target_pairs={{0,8},{8,0},{1,9},{9,1},{2,10},{10,2},{3,11},{11,3},{4,12},{12,4},... | collective-permute-start | bytes 1572872 | tf_op jit(solution)/shard_map/ppermute | solution.py:51
  (47 other events, 336.7 us)
Sparse Core Ops, SparseCore 0:
  41.6 45.7 all-gather.5
  90.1 72.0 all-gather.3
  182.6 101.9 reduce-scatter.1

commit v3 on v2

--- a/solution.py
+++ b/solution.py
@@ -35,8 +35,7 @@
     return dot(left, right, ((1,), (1,)))
 
 
-def cost(micros):
-    return pl.CostEstimate(flops=int(micros * 1.1e9), bytes_accessed=1, transcendentals=0)
+TINY = pl.CostEstimate(flops=1000, bytes_accessed=1000, transcendentals=0)
 
 
 def sync(*values):
@@ -99,18 +98,19 @@
         lse_ref[rows, :] = jnp.where(left, logs[0], logs[1])
 
 
-def attend(joint, seg_col, seg_row):
+def attend(joint, seg_col, seg_row, begin, count):
     rows, width = joint.shape[0], joint.shape[1] // 3
     pairs = width // LANES
     tile, spans = tile_spans(rows)
     widest = max(high - low for _, low, high in spans)
 
     def part(which):
-        return pl.BlockSpec((rows, LANES), lambda p: (0, which * pairs + p))
-
+        return pl.BlockSpec((rows, LANES), lambda p: (0, which * pairs + begin + p))
+
+    out = pl.BlockSpec((rows, LANES), lambda p: (0, p))
     return pl.pallas_call(
         functools.partial(attend_kernel, spans, tile),
-        grid=(pairs,),
+        grid=(count,),
         in_specs=[
             part(0),
             part(1),
@@ -118,14 +118,14 @@
             pl.BlockSpec((rows, 1), lambda p: (0, 0)),
             pl.BlockSpec((1, rows), lambda p: (0, 0)),
         ],
-        out_specs=[part(0), part(0)],
+        out_specs=[out, out],
         out_shape=[
-            jax.ShapeDtypeStruct((rows, width), bf16),
-            jax.ShapeDtypeStruct((rows, width), f32),
+            jax.ShapeDtypeStruct((rows, count * LANES), bf16),
+            jax.ShapeDtypeStruct((rows, count * LANES), f32),
         ],
         scratch_shapes=[pltpu.VMEM((len(spans), tile, widest), f32)],
         compiler_params=pltpu.CompilerParams(vmem_limit_bytes=40 * 1024 * 1024),
-        cost_estimate=cost(4.3 * pairs),
+        cost_estimate=TINY,
         name="attend",
     )(joint, joint, joint, seg_col, seg_row)
 
@@ -187,7 +187,7 @@
             part(1),
             part(2),
             part(0),
-            part(0),
+            pl.BlockSpec((rows, LANES), lambda p, j: (0, p)),
             pl.BlockSpec((rows, 1), lambda p, j: (0, 0)),
             pl.BlockSpec((1, rows), lambda p, j: (0, 0)),
         ],
@@ -199,7 +199,7 @@
             pltpu.VMEM((rows, LANES), f32),
         ],
         compiler_params=pltpu.CompilerParams(vmem_limit_bytes=48 * 1024 * 1024),
-        cost_estimate=cost(7.5 * count),
+        cost_estimate=TINY,
         name="attend_back",
     )(joint, joint, joint, grads, lse, seg_col, seg_row)
 
@@ -208,47 +208,156 @@
     return lax.ppermute(value, axis, [(i, (i + step) % depth) for i in range(depth)])
 
 
-def load(depth, place, pieces, sems, targets):
+def load(depth, place, pieces, sems, targets, base=0):
     z, x, h = place[0], place[1], place[2]
     copies = []
 
-    def put(source, shard, half):
+    def put(source, shard, half, at, shift=0):
         for first, columns, where in targets:
-            taken = source if columns == source.shape[1] else source.at[:, first : first + columns]
-            copies.append(pltpu.make_async_copy(taken, where(shard, half), sems.at[len(copies)]))
+            taken = source
+            if columns != source.shape[1]:
+                taken = source.at[:, shift + first : shift + first + columns]
+            copies.append(pltpu.make_async_copy(taken, where(shard, half, at, source.shape[0]), sems.at[len(copies)]))
             copies[-1].start()
 
-    for at_x, piece in ((x, pieces[0]), (1 - x, pieces[1])):
+    own, side_own, far, side, near, last_side, last_near = pieces
+    quarter = last_side.shape[1]
+    for at_x, piece in ((x, own), (1 - x, side_own)):
         for half in range(2):
-            put(piece.at[half], z * 2 + at_x, half)
-    for at_x, at_h, piece in ((x, h, pieces[2]), (1 - x, h, pieces[3]), (x, 1 - h, pieces[4]), (1 - x, 1 - h, pieces[5])):
+            put(piece.at[half], z * 2 + at_x, half, 0, base)
+    for at_x, at_h, at, piece in (
+        (x, h, 0, far),
+        (1 - x, h, 0, side),
+        (x, 1 - h, 0, near),
+        (1 - x, 1 - h, 0, last_side),
+        (1 - x, 1 - h, quarter, last_near),
+    ):
         for k in range(1, depth):
-            put(piece.at[k - 1], lax.rem(z - k + depth, depth) * 2 + at_x, at_h)
+            put(piece.at[k - 1], lax.rem(z - k + depth, depth) * 2 + at_x, at_h, at)
     return copies
 
 
 def below(weight, half_rows):
-    def where(shard, half):
-        return weight.at[pl.ds(pl.multiple_of((shard * 2 + half) * half_rows, half_rows), half_rows), :]
+    def where(shard, half, at, count):
+        first = pl.multiple_of((shard * 2 + half) * half_rows + at, math.gcd(half_rows, at))
+        return weight.at[pl.ds(first, count), :]
 
     return where
+
+
+def prepare(place, shards, w_qkv, w_out, w_up, vectors):
+    rows, model = w_out.shape
+    half, blocks = rows // 2, w_qkv.shape[1] // LANES
+    qkv_columns, wide = w_qkv.shape[1] // 2, w_up.shape[1] // 2
+    scale_at = qkv_columns
+    out_at = scale_at + LANES
+    up_at = out_at + model // 2
+    unit = wide // shards
+
+    def kernel(place_ref, qkv_ref, out_ref, up_ref, vectors_ref, own_ref, first_ref, up_half_ref):
+        lo, h = place_ref[3], place_ref[2]
+        left = lax.broadcasted_iota(jnp.int32, (rows, LANES), 1) < HEAD_DIM
+
+        def put(at, value):
+            own_ref[0, :, at : at + value.shape[1]] = value[:half]
+            own_ref[1, :, at : at + value.shape[1]] = value[half:]
+
+        for block in range(0, blocks, 2):
+            one = qkv_ref[:, block * LANES : (block + 1) * LANES].astype(f32)
+            two = qkv_ref[:, (block + 1) * LANES : (block + 2) * LANES].astype(f32)
+            even = jnp.where(left, one, pltpu.roll(two, HEAD_DIM, 1))
+            odd = jnp.where(left, pltpu.roll(one, HEAD_DIM, 1), two)
+            put(block // 2 * LANES, jnp.where(lo == 0, even, odd).astype(bf16))
+        columns = jnp.concatenate([vectors_ref[...].astype(f32), jnp.zeros((LANES - 4, rows), f32)], axis=0)
+        put(scale_at, columns.T.astype(bf16))
+        outs = jnp.where(lo == 0, out_ref[:half, :], out_ref[half:, :])
+        put(out_at, jnp.concatenate([outs[:, : model // 2], outs[:, model // 2 :]], axis=0))
+        for shard in range(shards):
+            at = shard * 2 * unit
+            put(up_at + shard * unit, jnp.where(lo == 0, up_ref[:, at : at + unit], up_ref[:, at + unit : at + 2 * unit]))
+        first_ref[...] = own_ref[h, :, :up_at]
+        up_half_ref[...] = own_ref[h, :, up_at:]
+
+    return pl.pallas_call(
+        kernel,
+        in_specs=[pl.BlockSpec(memory_space=pltpu.SMEM)] + [pl.BlockSpec(memory_space=pltpu.VMEM)] * 4,
+        out_specs=[pl.BlockSpec(memory_space=pltpu.VMEM)] * 3,
+        out_shape=[shape_of(2, half, up_at + wide), shape_of(half, up_at), shape_of(half, wide)],
+        compiler_params=pltpu.CompilerParams(vmem_limit_bytes=40 * 1024 * 1024),
+        cost_estimate=TINY,
+        name="prepare",
+    )(place, w_qkv, w_out, w_up, vectors)
+
+
+def finish_up(place, shards, own, other):
+    rows, columns = own.shape
+    unit = columns // shards
+
+    def kernel(place_ref, own_ref, other_ref, out_ref):
+        lo = place_ref[3]
+        for shard in range(shards):
+            at, mine, theirs = shard * 2 * unit, own_ref, other_ref
+            one = mine[:, shard * unit : (shard + 1) * unit].astype(f32)
+            two = theirs[:, shard * unit : (shard + 1) * unit].astype(f32)
+            out_ref[:, at : at + unit] = jnp.where(lo == 0, one, two)
+            out_ref[:, at + unit : at + 2 * unit] = jnp.where(lo == 0, two, one)
+
+    return pl.pallas_call(
+        kernel,
+        in_specs=[pl.BlockSpec(memory_space=pltpu.SMEM)] + [pl.BlockSpec(memory_space=pltpu.VMEM)] * 2,
+        out_specs=pl.BlockSpec(memory_space=pltpu.VMEM),
+        out_shape=shape_of(rows, 2 * columns, dtype=f32),
+        cost_estimate=TINY,
+        name="finish_up",
+    )(place, own, other)
+
+
+def finish_qkv(place, owns, others, out_own, out_other):
+    rows = out_own.shape[0]
+    half = rows // 2
+    columns = sum(own.shape[1] for own in owns)
+    model = 2 * out_own.shape[1]
+    pieces = len(owns)
+
+    def kernel(place_ref, *refs):
+        lo = place_ref[3]
+        owns_refs, others_refs = refs[:pieces], refs[pieces : 2 * pieces]
+        out_own_ref, out_other_ref, qkv_ref, out_ref = refs[2 * pieces :]
+        left = lax.broadcasted_iota(jnp.int32, (rows, LANES), 1) < HEAD_DIM
+        at = 0
+        for j in range(3):
+            for own_ref, other_ref in zip(owns_refs, others_refs):
+                third = own_ref.shape[1] // 3
+                for first in range(j * third, (j + 1) * third, LANES):
+                    mine = own_ref[:, first : first + LANES].astype(f32)
+                    theirs = other_ref[:, first : first + LANES].astype(f32)
+                    one, two = jnp.where(lo == 0, mine, theirs), jnp.where(lo == 0, theirs, mine)
+                    qkv_ref[:, at : at + LANES] = jnp.where(left, one, pltpu.roll(two, HEAD_DIM, 1))
+                    qkv_ref[:, at + LANES : at + 2 * LANES] = jnp.where(left, pltpu.roll(one, HEAD_DIM, 1), two)
+                    at += 2 * LANES
+        mine, theirs = out_own_ref[...].astype(f32), out_other_ref[...].astype(f32)
+        for at, value in ((0, jnp.where(lo == 0, mine, theirs)), (half, jnp.where(lo == 0, theirs, mine))):
+            out_ref[at : at + half, : model // 2] = value[:half]
+            out_ref[at : at + half, model // 2 :] = value[half:]
+
+    return pl.pallas_call(
+        kernel,
+        in_specs=[pl.BlockSpec(memory_space=pltpu.SMEM)] + [pl.BlockSpec(memory_space=pltpu.VMEM)] * (2 * pieces + 2),
+        out_specs=[pl.BlockSpec(memory_space=pltpu.VMEM)] * 2,
+        out_shape=[shape_of(rows, 2 * columns, dtype=f32), shape_of(rows, model, dtype=f32)],
+        compiler_params=pltpu.CompilerParams(vmem_limit_bytes=40 * 1024 * 1024),
+        cost_estimate=TINY,
+        name="finish_qkv",
+    )(place, *owns, *others, out_own, out_other)
 
 
 def plus(left, right):
     return (left.astype(f32) + right.astype(f32)).astype(bf16)
 
 
-def cut(full, depth, x, h):
-    rows, columns = full.shape[0] // (2 * depth), full.shape[1]
-    view = full.reshape(depth, 2, 2, 2, rows // 4, columns)
-    first, second = view[:, :, 0], view[:, :, 1]
-    keep = pick(first, x, 1), pick(second, h, 2)
-    send = pick(first, 1 - x, 1), pick(second, 1 - h, 2)
-    return keep, send
-
-
 def cut_again(keep, came, x, h):
     first, second = plus(keep[0], came[0]), plus(keep[1], came[1])
+    first = first.reshape(second.shape)
     keep = pick(first, h, 1), pick(second, x, 1)
     send = pick(first, 1 - h, 1), pick(second, 1 - x, 1)
     return keep, send
@@ -274,7 +383,7 @@
     return pl.BlockSpec(shape, lambda i: (0,) * len(shape))
 
 
-def weight_call(name, step, tiles, place, inputs, sets, outs, scratch, copies, micros):
+def weight_call(name, step, tiles, place, inputs, sets, outs, scratch, copies):
     pieces = [piece for held in sets for piece in held]
 
     def kernel(place_ref, *refs):
@@ -300,7 +409,7 @@
         out_shape=[shape for shape, _ in outs],
         scratch_shapes=list(scratch) + [pltpu.SemaphoreType.DMA((copies,))],
         compiler_params=pltpu.CompilerParams(vmem_limit_bytes=56 * 1024 * 1024),
-        cost_estimate=cost(micros),
+        cost_estimate=TINY,
         name=name,
     )(place, *[v for v, _ in inputs], *pieces)
 
@@ -324,7 +433,9 @@
 
 def bell_and_slope(values):
     size = jnp.abs(values)
-    t = 1.0 / (1.0 + (0.3275911 * math.sqrt(0.5)) * size)
+    base = 1.0 + (0.3275911 * math.sqrt(0.5)) * size
+    t = pl.reciprocal(base, approx=True)
+    t = t * (2.0 - base * t)
     bell = jnp.exp(values * values * -0.5)
     series = 0.5 * 1.061405429
     for term in (-1.453152027, 1.421413741, -0.284496736, 0.254829592):
@@ -332,6 +443,84 @@
     tail = series * t * bell
     phi = jnp.where(values < 0, tail, 1.0 - tail)
     return values * phi, phi + values * bell * (1.0 / math.sqrt(2.0 * math.pi))
+
+
+def outer_whole(left, right):
+    rows, across = left.shape
+    block = min(256, across)
+
+    def kernel(left_ref, right_ref, out_ref):
+        out_ref[...] = mm_rows(left_ref[...], right_ref[...]).astype(bf16)
+
+    return pl.pallas_call(
+        kernel,
+        grid=(across // block,),
+        in_specs=[pl.BlockSpec((rows, block), lambda i: (0, i)), whole_block(*right.shape)],
+        out_specs=row_block(block, right.shape[1]),
+        out_shape=shape_of(across, right.shape[1]),
+        compiler_params=pltpu.CompilerParams(vmem_limit_bytes=56 * 1024 * 1024),
+        cost_estimate=TINY,
+        name="outer_whole",
+    )(left, right)
+
+
+def outer(place, depth, left, right, out_pair=None, sums=None):
+    rows, own_rows = left.shape[0], left.shape[1] // (2 * depth)
+    top, low = own_rows // 2, own_rows // 4
+    columns = right.shape[1]
+    given = [left, right]
+    specs = [pl.BlockSpec((rows, 2 * own_rows), lambda i: (0, i)), whole_block(*right.shape)]
+    if out_pair is not None:
+        out_block = out_pair[0].shape[1] // depth
+        given += out_pair
+        specs += [pl.BlockSpec((rows, out_block), lambda i: (0, i)), whole_block(*out_pair[1].shape)]
+        half = out_pair[1].shape[1] // 2
+    if sums is not None:
+        given += sums
+        specs += [pl.BlockSpec((8, 2 * own_rows), lambda i: (0, i))] * 2
+    total = columns + (half if out_pair is not None else 0) + (LANES if sums is not None else 0)
+
+    def kernel(place_ref, *refs):
+        ins, outs = list(refs[: len(given)]), refs[len(given) :]
+        at_x, at_h = place_ref[1] == 0, place_ref[2] == 0
+        keep_first, send_first, keep_second, send_second = outs
+
+        def put(first, value):
+            where = slice(first, first + value.shape[2])
+            heads = value[:, :top].astype(bf16)
+            keep_first[0, :, where] = jnp.where(at_x, heads[0], heads[1])
+            send_first[0, :, where] = jnp.where(at_x, heads[1], heads[0])
+            lower, upper = value[:, top : top + low].astype(bf16), value[:, top + low :].astype(bf16)
+            keep_second[0, :, :, where] = jnp.where(at_h, lower, upper)
+            send_second[0, :, :, where] = jnp.where(at_h, upper, lower)
+
+        product = mm_rows(ins.pop(0)[...], ins.pop(0)[...])
+        put(0, product.reshape(2, own_rows, columns))
+        first = columns
+        if out_pair is not None:
+            product = mm_rows(ins.pop(0)[...], ins.pop(0)[...]).reshape(2, top, 2 * half)
+            put(first, jnp.concatenate([product[:, :, :half], product[:, :, half:]], axis=1))
+            first += half
+        if sums is not None:
+            stacked = jnp.concatenate([ref[0:2, :] for ref in ins], axis=0)
+            stacked = jnp.concatenate([stacked, jnp.zeros((LANES - 4, 2 * own_rows), f32)], axis=0)
+            put(first, stacked.T.reshape(2, own_rows, LANES))
+
+    def spec(*block):
+        return pl.BlockSpec((1, *block), lambda i: (i,) + (0,) * len(block))
+
+    first_shape, second_shape = (top, total), (2, low, total)
+    made = pl.pallas_call(
+        kernel,
+        grid=(depth,),
+        in_specs=[pl.BlockSpec(memory_space=pltpu.SMEM)] + specs,
+        out_specs=[spec(*first_shape)] * 2 + [spec(*second_shape)] * 2,
+        out_shape=[shape_of(depth, *first_shape)] * 2 + [shape_of(depth, *second_shape)] * 2,
+        compiler_params=pltpu.CompilerParams(vmem_limit_bytes=56 * 1024 * 1024),
+        cost_estimate=TINY,
+        name="outer",
+    )(place, *given)
+    return (made[0], made[2]), (made[1], made[3])
 
 
 def body(
@@ -385,53 +574,59 @@
             return swap(pick(parts, 1 - lo, 1), "lo")
         return plus(lax.psum_scatter(parts, "lo", scatter_dimension=1), -pick(parts, lo, 1))
 
-    if split_out:
-        qkv_part = pick(w_qkv.reshape(own_rows, 3, shards, group, -1), lo, 3).reshape(own_rows, -1)
-        out_part = pick(w_out.reshape(group, own_rows // group, model), lo, 0)
+    fused_out = split_out and group == 2
+    out_rows, half_model = own_rows // group, model // 2
+    place = jnp.stack([z, x, h, lo]).astype(jnp.int32)
+    rest = range(1, depth)
+    came = swap(jnp.stack([pick(tokens[:, 0], 1 - h, 0), pick(cotangent[:, 0], 1 - h, 0)]), "hi")
+    vectors = jnp.stack([norm1_gain, norm1_bias, norm2_gain, norm2_bias])
+    if fused_out:
+        both_own, first_half, up_half = prepare(place, shards, w_qkv, w_out, w_up, vectors)
     else:
-        qkv_part = pick(w_qkv.reshape(own_rows, 3, group, -1), lo, 2).reshape(own_rows, -1)
-        out_part = w_out
-    up_part = pick(w_up.reshape(own_rows, shards, group, -1), lo, 2).reshape(own_rows, -1)
+        if split_out:
+            qkv_part = pick(w_qkv.reshape(own_rows, 3, shards, group, -1), lo, 3).reshape(own_rows, -1)
+            out_part = pick(w_out.reshape(group, out_rows, model), lo, 0)
+        else:
+            qkv_part = pick(w_qkv.reshape(own_rows, 3, group, -1), lo, 2).reshape(own_rows, -1)
+            out_part = w_out
+        up_part = pick(w_up.reshape(own_rows, shards, group, -1), lo, 2).reshape(own_rows, -1)
+        parts = [qkv_part, jnp.pad(vectors.T, ((0, 0), (0, LANES - 4)))]
+        both_own = jnp.concatenate(parts + [up_part], axis=1).reshape(2, half_rows, -1)
+        half = pick(both_own, h, 0)
+        first_half, up_half = half[:, : scale_at + LANES], half[:, scale_at + LANES :]
+        out_weight = lax.all_gather(out_part, shard_axes, axis=0, tiled=True)
+    up_at = first_half.shape[1]
     down_part = pick(w_down.reshape(group, -1, model), lo, 0)
-    vectors = jnp.stack([norm1_gain, norm1_bias, norm2_gain, norm2_bias], axis=1)
-    first_part = jnp.concatenate([qkv_part, jnp.pad(vectors, ((0, 0), (0, LANES - 4)))], axis=1)
-    place = jnp.stack([z, x, h, lo]).astype(jnp.int32)
-    first_own = first_part.reshape(2, half_rows, -1)
-    up_own = up_part.reshape(2, half_rows, -1)
-    rest = range(1, depth)
-
-    out_weight = lax.all_gather(out_part, shard_axes, axis=0, tiled=True)
-    first_half = pick(first_own, h, 0)
     first_far = [along(first_half, "fz", depth, k) for k in rest]
-    first_side_own = swap(first_own, "fx")
-    came = swap(pick(tokens[:, 0], 1 - h, 0), "hi")
-    first_far, first_side_own, came, up_own, tokens = sync(
-        first_far, first_side_own, came, up_own, tokens
-    )
+    side_own = swap(both_own, "fx")
+    first_far, side_own, came, up_half = sync(first_far, side_own, came, up_half)
+
+    def last_quarters(side, near):
+        quarter = side.shape[1] // 2
+        return swap(side[:, :quarter], "hi"), swap(near[:, quarter:], "fx")
 
     first_far = jnp.stack(first_far)
     first_side, first_near = swap(first_far, "fx"), swap(first_far, "hi")
-    inputs = whole_group(ordered(pick(tokens[:, 0], h, 0), came, h, 0), 1).reshape(rows, model)
-    up_half = pick(up_own, h, 0)
+    inputs = whole_group(ordered(pick(tokens[:, 0], h, 0), came[0], h, 0), 1).reshape(rows, model)
     odd = [along(up_half, "fz", depth, k) for k in rest if k % 2]
-    first_side, first_near, inputs, odd, up_half, up_own, down_part = sync(
-        first_side, first_near, inputs, odd, up_half, up_own, down_part
-    )
-
+    first_side, first_near, inputs, odd, up_half, came = sync(first_side, first_near, inputs, odd, up_half, came)
+
+    first_last = last_quarters(first_side, first_near)
+    even = [along(up_half, "fz", depth, k) for k in rest if k % 2 == 0]
+    grad_result = whole_group(ordered(pick(cotangent[:, 0], h, 0), came[1], h, 0), 1).reshape(rows, model)
+    first_last, even, odd, inputs, grad_result, down_part = sync(
+        first_last, even, odd, inputs, grad_result, down_part
+    )
     downward = lax.all_gather(down_part, shard_axes, axis=0, tiled=True)
-    first_last = swap(first_side, "hi")
-    up_side_own = swap(up_own, "fx")
-    even = [along(up_half, "fz", depth, k) for k in rest if k % 2 == 0]
-    first_last, up_side_own, even, odd, inputs = sync(first_last, up_side_own, even, odd, inputs)
-    first_set = [first_own, first_side_own, first_far, first_side, first_near, first_last]
+    first_set = [both_own, side_own, first_far, first_side, first_near, *first_last]
     up_far = jnp.stack([odd[k // 2] if k % 2 else even[k // 2 - 1] for k in rest])
 
     segments = pick(segment_ids[:, 0], h, 0)
     seg_col, seg_row = segments[:, None], segments[None, :]
 
     def project(place_ref, given, held, made, scratch, sems):
-        (rows_ref,), (normed_ref, joint_ref, scales_ref) = given, made
-        weight, columns = scratch
+        (rows_ref,), (normed_ref, joint_ref, scales_ref, *outs) = given, made
+        weight, columns, *beside = scratch
 
         @pl.when(pl.program_id(0) == 0)
         def _():
@@ -439,9 +634,17 @@
                 (0, 3 * head_columns, below(weight, half_rows)),
                 (scale_at, LANES, below(columns, half_rows)),
             ]
+            if fused_out:
+                targets.append((scale_at + LANES, half_model, below(beside[0], half_rows)))
             for copy in load(depth, place_ref, held[0], sems, targets):
                 copy.wait()
             scales_ref[...] = columns[...].astype(f32).T[:8, :]
+            for shard in range(shards if fused_out else 0):
+                for part in range(2):
+                    at = shard * own_rows + part * out_rows
+                    outs[0][
+                        shard * out_rows : (shard + 1) * out_rows, part * half_model : (part + 1) * half_model
+                    ] = beside[0][at : at + out_rows, :]
 
         unit_rows, _ = unit_of(rows_ref[...].astype(f32))
         normed = (unit_rows * scales_ref[0:1, :] + scales_ref[1:2, :]).astype(bf16)
@@ -452,7 +655,11 @@
                 part = part * (1.0 / math.sqrt(HEAD_DIM))
             joint_ref[:, at : at + head_columns] = part.astype(bf16)
 
-    normed, joint, scales = weight_call(
+    out_shapes, out_scratch = [], []
+    if fused_out:
+        out_shapes = [(shape_of(head_columns, model), whole_block(head_columns, model))]
+        out_scratch = [pltpu.VMEM((model, half_model), bf16)]
+    normed, joint, scales, *outs = weight_call(
         "project",
         project,
         tiles,
@@ -463,44 +670,60 @@
             (shape_of(rows, model), row_block(tile, model)),
             (shape_of(rows, 3 * head_columns), row_block(tile, 3 * head_columns)),
             (shape_of(8, model, dtype=f32), whole_block(8, model)),
-        ],
-        [pltpu.VMEM((model, 3 * head_columns), bf16), pltpu.VMEM((model, LANES), bf16)],
-        copies,
-        9,
-    )
-    attended, lse = attend(joint, seg_col, seg_row)
+        ]
+        + out_shapes,
+        [pltpu.VMEM((model, 3 * head_columns), bf16), pltpu.VMEM((model, LANES), bf16)] + out_scratch,
+        3 * copies,
+    )
+    if fused_out:
+        (out_weight,) = outs
+    pairs = head_columns // LANES
+    pieces = 2 if pairs % 2 == 0 else 1
+    count = pairs // pieces
+    part_columns = count * LANES
+    mixed = [attend(joint, seg_col, seg_row, 0, count)]
     up_side, up_near = swap(up_far, "fx"), swap(up_far, "hi")
-    attended, up_side, up_near, cotangent = sync(attended, up_side, up_near, cotangent)
+    mixed, joint, up_side, up_near, scales, out_weight = sync(mixed, joint, up_side, up_near, scales, out_weight)
+
+    up_last = last_quarters(up_side, up_near)
+    for piece in range(1, pieces):
+        mixed.append(attend(joint, seg_col, seg_row, piece * count, count))
+    mixed, up_last, out_weight = sync(mixed, up_last, out_weight)
+    up_set = [both_own, side_own, up_far, up_side, up_near, *up_last]
+    lses = [lse for _, lse in mixed]
 
     def leave(place_ref, given, held, made, scratch, sems):
-        (rows_ref, weight), (out_ref,) = given, made
-        out_ref[...] = mm(rows_ref[...], own_out(weight, place_ref)).astype(bf16)
+        *parts_refs, weight = given
+        out_ref, attended_ref = made
+        weight = own_out(weight, place_ref)
+        total = jnp.zeros(out_ref.shape, f32)
+        for piece, part_ref in enumerate(parts_refs):
+            at = slice(piece * part_columns, (piece + 1) * part_columns)
+            attended_ref[:, at] = part_ref[...]
+            total = total + mm(part_ref[...], weight[at, :])
+        out_ref[...] = total.astype(bf16)
 
     def own_out(weight, place_ref):
         if split_out:
             return weight[...]
         return weight[pl.ds(pl.multiple_of(place_ref[3] * head_columns, head_columns), head_columns), :]
 
-    (branch,) = weight_call(
+    branch, attended = weight_call(
         "leave",
         leave,
         tiles,
         place,
-        [(attended, row_block(tile, head_columns)), (out_weight, whole_block(*out_weight.shape))],
+        [(value, row_block(tile, part_columns)) for value, _ in mixed]
+        + [(out_weight, whole_block(*out_weight.shape))],
         [],
-        [(shape_of(rows, model), row_block(tile, model))],
+        [
+            (shape_of(rows, model), row_block(tile, model)),
+            (shape_of(rows, head_columns), row_block(tile, head_columns)),
+        ],
         [],
         1,
-        4,
     )
     branch_other = other_part(branch)
-    up_last = swap(up_side, "hi")
-    came = swap(pick(cotangent[:, 0], 1 - h, 0), "hi")
-    branch, branch_other, up_last, cotangent = sync(branch, branch_other, up_last, cotangent)
-    up_set = [up_own, up_side_own, up_far, up_side, up_near, up_last]
-
-    grad_result = whole_group(ordered(pick(cotangent[:, 0], h, 0), came, h, 0), 1).reshape(rows, model)
-
     def widen(place_ref, given, held, made, scratch, sems):
         rows_ref, own_ref, other_ref, scales_ref = given
         middle_ref, normed_ref, hidden_ref, slope_ref = made
@@ -509,7 +732,7 @@
         @pl.when(pl.program_id(0) == 0)
         def _():
             targets = [(0, inner, below(weight, half_rows))]
-            for copy in load(depth, place_ref, held[0], sems, targets):
+            for copy in load(depth, place_ref, held[0], sems, targets, up_at):
                 copy.wait()
 
         added = own_ref[...].astype(f32) + other_ref[...].astype(f32)
@@ -543,12 +766,10 @@
         ],
         [pltpu.VMEM((model, inner), bf16)],
         copies,
-        18,
-    )
-    hidden, slope, grad_result = sync(hidden, slope, grad_result)
-
-    grad_down = mm_rows(hidden, grad_result).astype(bf16)
-    hidden, slope, grad_down = sync(hidden, slope, grad_down)
+    )
+
+    grad_down = outer_whole(hidden, grad_result)
+    hidden, slope, grad_down, normed_two = sync(hidden, slope, grad_down, normed_two)
     down_own = lax.psum_scatter(grad_down, shard_axes, scatter_dimension=0, tiled=True)
 
     def narrow(place_ref, given, held, made, scratch, sems):
@@ -559,17 +780,14 @@
         @pl.when(pl.program_id(0) == 0)
         def _():
             targets = [(0, inner, below(upward, half_rows))]
-            for copy in load(depth, place_ref, held[0], sems, targets):
+            for copy in load(depth, place_ref, held[0], sems, targets, up_at):
                 copy.wait()
 
-        out_ref[...] = mm(hidden_ref[...], down_ref[...]).astype(bf16)
-        total = jnp.zeros(back_ref.shape, f32)
         for at in range(0, inner, wide):
             grad = mm_cols(grad_ref[...], down_ref[at : at + wide, :])
-            grad = (grad * slope_ref[:, at : at + wide].astype(f32)).astype(bf16)
-            pre_ref[:, at : at + wide] = grad
-            total = total + mm_cols(grad, upward[:, at : at + wide])
-        back_ref[...] = total.astype(bf16)
+            pre_ref[:, at : at + wide] = (grad * slope_ref[:, at : at + wide].astype(f32)).astype(bf16)
+        back_ref[...] = mm_cols(pre_ref[...], upward[...]).astype(bf16)
+        out_ref[...] = mm(hidden_ref[...], down_ref[...]).astype(bf16)
 
     result, grad_pre, back = weight_call(
         "narrow",
@@ -590,18 +808,13 @@
         ],
         [pltpu.VMEM((model, inner), bf16)],
         copies,
-        21,
-    )
-    result, grad_pre, back = sync(result, grad_pre, back)
+    )
+    result, grad_pre, back, normed_two = sync(result, grad_pre, back, normed_two)
 
     back_other = other_part(back)
-    grad_up = mm_rows(normed_two, grad_pre).astype(bf16)
-    up_keep, up_send = cut(grad_up, depth, x, h)
-    back, back_other, up_keep, up_send, result = sync(back, back_other, up_keep, up_send, result)
-
-    pairs = head_columns // LANES
-    pieces = 2 if pairs % 2 == 0 else 1
-    count = pairs // pieces
+    result_other = other_own(result)
+    up_keep, up_send = outer(place, depth, normed_two, grad_pre)
+    back, back_other, up_keep, up_send, result_other = sync(back, back_other, up_keep, up_send, result_other)
 
     def between(place_ref, given, held, made, scratch, sems):
         grad_ref, own_ref, other_ref, middle_ref, scales_ref, weight = given
@@ -644,37 +857,43 @@
         ],
         [],
         1,
-        10,
-    )
-    grad_joints = [attend_back(joint, grad_attended, lse, seg_col, seg_row, 0, count)]
+    )
+    grad_joints = [attend_back(joint, grad_attended, lses[0], seg_col, seg_row, 0, count)]
     up_came = swap(up_send[0], "fx"), swap(up_send[1], "hi")
-    result_other = other_own(result)
-    grad_joints, grad_attended, grad_branch, up_came, result_other = sync(
-        grad_joints, grad_attended, grad_branch, up_came, result_other
-    )
-
-    grad_out = mm_rows(attended, grad_branch).astype(bf16)
-    if not split_out:
-        empty = jnp.zeros((model, model), bf16)
-        grad_out = lax.dynamic_update_slice_in_dim(empty, grad_out, lo * head_columns, 0)
+    grad_joints, grad_attended, grad_branch, up_came = sync(grad_joints, grad_attended, grad_branch, up_came)
+
     up_keep, up_send = cut_again(up_keep, up_came, x, h)
+    up_came = swap(up_send[0], "hi"), swap(up_send[1], "fx")
+    one_keep, one_send = outer(
+        place, depth, normed, grad_joints[0], out_pair=[attended, grad_branch] if fused_out else None
+    )
+    output = (own_chunks(middle) + own_chunks(result).astype(f32) + result_other.astype(f32)).astype(bf16)
+    up_came, one_keep, one_send, grad_attended, output = sync(up_came, one_keep, one_send, grad_attended, output)
+
+    up_own_sum, up_send = along_z(up_keep, up_came, depth, z)
+    up_send = dict(zip(rest, up_send))
     for piece in range(1, pieces):
         grad_joints.append(
-            attend_back(joint, grad_attended, lse, seg_col, seg_row, piece * count, count)
+            attend_back(joint, grad_attended, lses[piece], seg_col, seg_row, piece * count, count)
         )
-    fused_out = split_out and group == 2
-    parts = [mm_rows(normed, grad_joints[0]).astype(bf16)]
-    if fused_out:
-        halves = grad_out.reshape(shards, own_rows // group, group, model // group).transpose(0, 2, 1, 3)
-        parts.append(halves.reshape(model, model // group))
-    one_keep, one_send = cut(jnp.concatenate(parts, axis=1), depth, x, h)
-    up_came = swap(up_send[0], "hi"), swap(up_send[1], "fx")
-    grad_joints, up_came, one_keep, one_send = sync(grad_joints, up_came, one_keep, one_send)
-
-    up_own_sum, up_send = along_z(up_keep, up_came, depth, z)
     one_came = swap(one_send[0], "fx"), swap(one_send[1], "hi")
-    up_came = [along(value, "fz", depth, k) for k, value in zip(rest, up_send)]
-    part_columns = count * LANES
+    odd = [along(up_send[k], "fz", depth, k) for k in rest if k % 2]
+    output_came = swap(pick(output, 1 - h, 0), "hi")
+    grad_joints, odd, up_send, one_keep, one_came, output_came = sync(
+        grad_joints, odd, up_send, one_keep, one_came, output_came
+    )
+
+    if pieces == 2:
+        two_keep, two_send = outer(place, depth, normed, grad_joints[1])
+        two_keep, two_send, grad_joints, one_keep, one_came, up_send = sync(
+            two_keep, two_send, grad_joints, one_keep, one_came, up_send
+        )
+        two_came = swap(two_send[0], "fx"), swap(two_send[1], "hi")
+    else:
+        two_keep, two_came = one_keep, one_came
+    one_keep, one_send = cut_again(one_keep, one_came, x, h)
+    one_came = swap(one_send[0], "hi"), swap(one_send[1], "fx")
+    even = [along(up_send[k], "fz", depth, k) for k in rest if k % 2 == 0]
 
     def enter(place_ref, given, held, made, scratch, sems):
         *parts_refs, inputs_ref = given
@@ -712,75 +931,72 @@
         ],
         [pltpu.VMEM((model, 3 * head_columns), bf16)],
         copies,
-        9,
-    )
-    sums = jnp.stack([sums_one[0], sums_one[1], sums_two[0], sums_two[1]], axis=1).astype(bf16)
-    parts = [mm_rows(normed, value).astype(bf16) for value in grad_joints[1:]]
-    parts.append(jnp.pad(sums, ((0, 0), (0, LANES - 4))))
-    two_keep, two_send = cut(jnp.concatenate(parts, axis=1), depth, x, h)
-    entered, one_came, up_came, two_keep, two_send, down_own = sync(
-        entered, one_came, up_came, two_keep, two_send, down_own
-    )
-
-    one_keep, one_send = cut_again(one_keep, one_came, x, h)
-    one_came = swap(one_send[0], "hi"), swap(one_send[1], "fx")
-    two_came = swap(two_send[0], "fx"), swap(two_send[1], "hi")
-    up_sum = add_up(up_own_sum, up_came)
-    entered_other = other_own(entered)
-    output = (own_chunks(middle) + own_chunks(result).astype(f32) + result_other.astype(f32)).astype(bf16)
-    entered_other, one_came, two_came, up_sum, output, down_own = sync(
-        entered_other, one_came, two_came, up_sum, output, down_own
-    )
-
+    )
+    sums = jnp.concatenate([sums_one[:2], sums_two[:2]]).reshape(4, depth, 2, own_rows)
+    two_came, one_came, even, entered, sums, down_own = sync(two_came, one_came, even, entered, sums, down_own)
+
+    def both_halves(value):
+        return ordered(value, swap(value, "hi"), h, 1).reshape(own_rows, -1)
+
+    two_keep, two_send = cut_again(two_keep, two_came, x, h)
+    two_came = swap(two_send[0], "hi"), swap(two_send[1], "fx")
     one_own_sum, one_send = along_z(one_keep, one_came, depth, z)
     one_came = [along(value, "fz", depth, k) for k, value in zip(rest, one_send)]
-    two_keep, two_send = cut_again(two_keep, two_came, x, h)
-    two_came = swap(two_send[0], "hi"), swap(two_send[1], "fx")
+    entered_other = other_own(entered)
+    down_own = plus(down_own, swap(down_own, "hi"))
+    sums = pick(sums, x, 2) + swap(pick(sums, 1 - x, 2), "fx")
+    two_came, one_came, entered_other, sums, odd, even, down_own = sync(
+        two_came, one_came, entered_other, sums, odd, even, down_own
+    )
+
+    two_own_sum, two_send = along_z(two_keep, two_came, depth, z)
+    two_came = [along(value, "fz", depth, k) for k, value in zip(rest, two_send)]
+    up_own = both_halves(add_up(up_own_sum, odd + even))
     grad_normed = own_chunks(entered).astype(f32) + entered_other.astype(f32)
     unit_own, inverse_own = unit_of(own_chunks(inputs).astype(f32))
     grad_tokens = own_chunks(grad_middle) + unit_back(grad_normed * scales[0], unit_own, inverse_own)
-    one_came, two_came, grad_tokens, output, up_sum, down_own = sync(
-        one_came, two_came, grad_tokens, output, up_sum, down_own
-    )
-
-    two_own_sum, two_send = along_z(two_keep, two_came, depth, z)
-    two_came = [along(value, "fz", depth, k) for k, value in zip(rest, two_send)]
-    one_sum = add_up(one_own_sum, one_came)
-    grad_came = swap(pick(grad_tokens, 1 - h, 0).astype(bf16), "hi").astype(f32)
-    output_came = swap(pick(output, 1 - h, 0), "hi")
-    two_came, one_sum, grad_came, output_came, up_sum, down_own = sync(
-        two_came, one_sum, grad_came, output_came, up_sum, down_own
-    )
+    grad_came = swap(pick(grad_tokens, 1 - h, 0).astype(bf16), "hi")
+    sums = sums + swap(sums, "hi")
+    two_came, up_own, grad_tokens, grad_came, sums, one_came, down_own = sync(
+        two_came, up_own, grad_tokens, grad_came, sums, one_came, down_own
+    )
+
+    one_own = both_halves(add_up(one_own_sum, one_came))
+    two_own = both_halves(add_up(two_own_sum, two_came))
+    sums_came = [along(pick(sums, (z + k) % depth, 1), "fz", depth, k) for k in rest]
+    sums = pick(sums, z, 1)
+    for piece in sums_came:
+        sums = sums + piece
     output = ordered(pick(output, h, 0), output_came, h, 0)[:, None]
-    grad_tokens = ordered(pick(grad_tokens, h, 0), grad_came, h, 0)[:, None]
-
-    down_own = plus(down_own, swap(down_own, "hi"))
-    two_sum = add_up(two_own_sum, two_came)
-
-    def both_halves(value):
-        return ordered(value, swap(value, "hi"), h, 1).reshape(own_rows, -1)
-
-    up_own, one_own, two_own = both_halves(up_sum), both_halves(one_sum), both_halves(two_sum)
+    grad_tokens = ordered(pick(grad_tokens, h, 0), grad_came.astype(f32), h, 0)[:, None]
+
     down_all = whole_group(down_own, 0).reshape(-1, model).astype(f32)
-    up_all = whole_group(up_own.reshape(own_rows, shards, -1), 2).reshape(own_rows, -1).astype(f32)
-    qkv_owns = [one_own[:, : 3 * part_columns]]
-    if pieces == 2:
-        qkv_owns.append(two_own[:, : 3 * part_columns])
-    sums_own = two_own[:, -LANES : 4 - LANES]
-    sums = jnp.sum(whole_group(sums_own, 0).astype(f32), axis=0).T
+    sums = jnp.sum(whole_group(sums, 0), axis=0)
     if fused_out:
-        out_own = one_own[:, 3 * part_columns :].reshape(group, own_rows // group, -1)
-        out_all = whole_group(out_own, 0).transpose(0, 2, 1, 3).reshape(own_rows, model).astype(f32)
+        up_all = finish_up(place, shards, up_own, swap(up_own, "lo"))
+        owns = [value[:, : 3 * part_columns] for value in ((one_own, two_own) if pieces == 2 else (one_own,))]
+        one_other = swap(one_own, "lo")
+        others = [one_other[:, : 3 * part_columns]]
+        if pieces == 2:
+            others.append(swap(two_own, "lo"))
+        out_own, out_other = one_own[:, 3 * part_columns :], one_other[:, 3 * part_columns :]
+        qkv_all, out_all = finish_qkv(place, owns, others, out_own, out_other)
     else:
+        up_all = whole_group(up_own.reshape(own_rows, shards, -1), 2).reshape(own_rows, -1).astype(f32)
+        qkv_owns = [one_own] + ([two_own] if pieces == 2 else [])
+        qkv_own = jnp.concatenate([value.reshape(own_rows, 3, part_columns) for value in qkv_owns], axis=2)
+        if split_out:
+            qkv_all = whole_group(qkv_own.reshape(own_rows, 3, shards, -1), 3)
+        else:
+            qkv_all = whole_group(qkv_own, 2)
+        qkv_all = qkv_all.reshape(own_rows, -1).astype(f32)
+        grad_out = outer_whole(attended, grad_branch)
+        if not split_out:
+            empty = jnp.zeros((model, model), bf16)
+            grad_out = lax.dynamic_update_slice_in_dim(empty, grad_out, lo * head_columns, 0)
         out_own = lax.psum(lax.psum_scatter(grad_out, shard_axes, scatter_dimension=0, tiled=True), "hi")
         out_all = whole_group(out_own, 0).reshape(own_rows, model) if split_out else lax.psum(out_own, "lo")
         out_all = out_all.astype(f32)
-    qkv_own = jnp.concatenate([value.reshape(own_rows, 3, part_columns) for value in qkv_owns], axis=2)
-    if split_out:
-        qkv_all = whole_group(qkv_own.reshape(own_rows, 3, shards, -1), 3)
-    else:
-        qkv_all = whole_group(qkv_own, 2)
-    qkv_all = qkv_all.reshape(own_rows, -1).astype(f32)
 
     return (
         output,

time: 464 us -> 394 us (0.85)
  waiting for transfers between devices: 160 us -> 92.1 us
  Pallas kernels: 119 us -> 159 us
  local copies, waits for them, and re-layouts: 54.3 us -> 29.2 us
  matrix products: 19.7 us -> 0 us
    ppermute x39 -> x41, waiting for transfers between devices: 83.2 us -> 43.4 us  [swap(): return lax.ppermute(value, axis, SWAP)]
    pallas_call x1 -> x9, Pallas kernels: 17.1 us -> 55.2 us  [the longest x3 21.8 us: outer(): pl.pallas_call(kernel, grid=(depth,), in_specs=[pl.BlockSpec(memory_space...]
    ppermute x15 -> x18, waiting for transfers between devices: 76.5 us -> 48.7 us  [along(): lax.ppermute(value, axis, [(i, (i + step) % depth) for i in range(depth)])]
    dot_general x5 -> x0, matrix products: 19.7 us -> none  [dot(): lax.dot_general(left, right, (dims, ((), ())), preferred_element_type=f32)]
    unnamed x117 -> x124, local copies, waits for them, and re-layouts: 21.5 us -> 13.2 us
    ppermute x39 -> x41, starting transfers between devices: 31.7 us -> 38.8 us  [swap(): return lax.ppermute(value, axis, SWAP)]
    squeeze x18 -> x11, local copies, waits for them, and re-layouts: 11.6 us -> 5.52 us  [pick(): return lax.dynamic_index_in_dim(array, index, axis, keepdims=False)]
    ppermute x15 -> x18, starting transfers between devices: 20.3 us -> 17.8 us  [along(): lax.ppermute(value, axis, [(i, (i + step) % depth) for i in range(depth)])]
  transfers between devices with their start and end apart: 57 -> 61, of which waited for: 21 -> 18; matrix products, arithmetic and copies ran while one was open for 19% -> 12% of each run, Pallas kernels for 26% -> 35%
where the time goes in v3:
time: 394 us; the launch traced here: 386 us
  Pallas kernels  159 us (40%)
  waiting for transfers between devices  92.1 us (23%)
  starting transfers between devices  56.9 us (14%)
  other arithmetic  34.2 us (9%)
  local copies, waits for them, and re-layouts  29.2 us (7%)
  between operations  15.4 us (4%)
    pallas_call x6, Pallas kernels, weight_call(): pl.pallas_call(kernel, grid=(tiles,), in_specs=[pl.BlockSpec(memory_space...  75.1 us
    ppermute x18, waiting for transfers between devices, along(): lax.ppermute(value, axis, [(i, (i + step) % depth) for i in range(depth)])  48.7 us
    ppermute x41, waiting for transfers between devices, swap(): return lax.ppermute(value, axis, SWAP)  43.4 us
    ppermute x41, starting transfers between devices, swap(): return lax.ppermute(value, axis, SWAP)  38.8 us
    pallas_call x2, Pallas kernels, attend_back(): pl.pallas_call(functools.partial(attend_back_kernel, spans, tile), grid=(...  28.4 us
    pallas_call x3, Pallas kernels, outer(): pl.pallas_call(kernel, grid=(depth,), in_specs=[pl.BlockSpec(memory_space...  21.8 us
    ppermute x18, starting transfers between devices, along(): lax.ppermute(value, axis, [(i, (i + step) % depth) for i in range(depth)])  17.8 us
    pallas_call x2, Pallas kernels, attend(): pl.pallas_call(functools.partial(attend_kernel, spans, tile), grid=(count...  17.3 us
  transfers between devices with their start and end apart: 61, of which 18 were waited for; matrix products, arithmetic and copies ran while one was open for 12% of the time, Pallas kernels for 35%

profile of v3, /device:TPU:9, one launch (start us, length us, event | category | flops | bytes accessed | tf_op | source)
XLA Modules:
  0.0 386.4 jit_solution(5014418015522157631)
XLA Ops:
  19.6 1.5 collective-permute-start.2
  21.1 3.2 collective-permute-done
  24.3 16.9 %collective-permute-done.1 = bf16[64,2176]{1,0:T(8,128)(2,1)S(1)} collective-permute-done((bf16[64,2176]{1,0:T(8,128)(2,1)S(1)}, bf16[64,2176]{1,0:T(8,128)(2,1)S(1)}, u32[]{:S(2)}, u32[]{:S(2)}) %collective-permute-start.1) | collective-permute-done | bytes 278560 | tf_op jit(solution)/shard_map/ppermute | solution.py:208
  41.2 3.6 collective-permute-done.2
  44.8 1.3 bitcast_select_fusion.5
  49.4 1.5 collective-permute-start.9
  50.8 1.4 select_bitcast_fusion.3
  52.2 1.5 pad_maximum_fusion
  53.7 3.0 collective-permute-done.8
  56.8 7.0 %collective-permute-done.9 = bf16[64,2048]{1,0:T(8,128)(2,1)S(1)} collective-permute-done((bf16[64,2048]{1,0:T(8,128)(2,1)S(1)}, bf16[64,2048]{1,0:T(8,128)(2,1)S(1)}, u32[]{:S(2)}, u32[]{:S(2)}) %collective-permute-start.9) | collective-permute-done | bytes 262176 | tf_op jit(solution)/shard_map/ppermute | solution.py:208
  63.7 5.4 %collective-permute-done.5.refs_4_.refs_6_ = bf16[3,64,2176]{2,1,0:T(8,128)(2,1)} collective-permute-done((bf16[3,64,2176]{2,1,0:T(8,128)(2,1)S(1)}, bf16[3,64,2176]{2,1,0:T(8,128)(2,1)}, u32[]{:S(2)}, u32[]{:S(2)}) %collective-permute-start.5) | collective-permute-done | bytes 835616 | tf_op jit(solution)/shard_map/ppermute | solution.py:50
  76.9 1.9 collective-permute-start.12
  78.8 1.4 select_bitcast_fusion.1
  80.3 1.5 copy.29
  81.8 6.7 %collective-permute-done.12 = bf16[64,2048]{1,0:T(8,128)(2,1)S(1)} collective-permute-done((bf16[64,2048]{1,0:T(8,128)(2,1)S(1)}, bf16[64,2048]{1,0:T(8,128)(2,1)S(1)}, u32[]{:S(2)}, u32[]{:S(2)}) %collective-permute-start.12) | collective-permute-done | bytes 262176 | tf_op jit(solution)/shard_map/ppermute | solution.py:208
  90.9 10.5 %project.1 = (bf16[1024,1024]{1,0:T(8,128)(2,1)}, bf16[1024,1536]{1,0:T(8,128)(2,1)}, f32[8,1024]{1,0:T(8,128)}, bf16[512,1024]{1,0:T(8,128)(2,1)}) custom-call(s32[4]{0:T(128)} %copy-done.13, bf16[1024,1024]{1,0:T(8,128)(2,1)} %bitcast.246, bf16[2,64,4224]{2,1,0:T(8,128)(2,1)} %copy-done.3, ...), custom_call_target="tpu_custom_call" | custom-call | flops 1000 | bytes 1000 | tf_op jit(solution)/shard_map/project/pallas_call | solution.py:402
  101.4 1.9 copy-done.2
  103.3 8.6 %attend.2 = (bf16[1024,256]{1,0:T(8,128)(2,1)S(1)}, f32[1024,256]{1,0:T(8,128)S(1)}) custom-call(bf16[1024,1536]{1,0:T(8,128)(2,1)S(1)} %copy-done.2, bf16[1024,1536]{1,0:T(8,128)(2,1)S(1)} %copy-done.2, bf16[1024,1536]{1,0:T(8,128)(2,1)S(1)} %copy-done.2, s32[1024,1]{1,0:T(8,128)S(1)} %copy.30.seg_col, s32[1,1024]{1,0:T(1,128)S(1)} %get-tuple-element.353.seg_row), custom_call_target="tpu_custom_call" | custom-call | flops 1000 | bytes 1000 | tf_op jit(solution)/shard_map/attend/pallas_call | solution.py:111
  112.0 1.3 collective-permute-done.14.refs_7_
  113.3 1.3 collective-permute-start.16
  116.1 8.7 %attend.3 = (bf16[1024,256]{1,0:T(8,128)(2,1)S(1)}, f32[1024,256]{1,0:T(8,128)S(1)}) custom-call(bf16[1024,1536]{1,0:T(8,128)(2,1)S(1)} %copy-done.2, bf16[1024,1536]{1,0:T(8,128)(2,1)S(1)} %copy-done.2, bf16[1024,1536]{1,0:T(8,128)(2,1)S(1)} %copy-done.2, s32[1024,1]{1,0:T(8,128)S(1)} %copy.30.seg_col, s32[1,1024]{1,0:T(1,128)S(1)} %get-tuple-element.353.seg_row), custom_call_target="tpu_custom_call" | custom-call | flops 1000 | bytes 1000 | tf_op jit(solution)/shard_map/attend/pallas_call | solution.py:111
  125.6 5.2 %leave.1 = (bf16[1024,1024]{1,0:T(8,128)(2,1)}, bf16[1024,512]{1,0:T(8,128)(2,1)}) custom-call(s32[4]{0:T(128)} %copy-done.13, bf16[1024,256]{1,0:T(8,128)(2,1)} %copy-done.10, bf16[1024,256]{1,0:T(8,128)(2,1)} %copy-done.11, bf16[512,1024]{1,0:T(8,128)(2,1)} %get-tuple-element.201.refs_2_.refs_5_), custom_call_target="tpu_custom_call" | custom-call | flops 1000 | bytes 1000 | tf_op jit(solution)/shard_map/leave/pallas_call | solution.py:402
  130.7 2.1 collective-permute-start.18
  132.8 4.0 %collective-permute-done.18.refs_2_ = bf16[1024,1024]{1,0:T(8,128)(2,1)S(1)} collective-permute-done((bf16[1024,1024]{1,0:T(8,128)(2,1)}, bf16[1024,1024]{1,0:T(8,128)(2,1)S(1)}, u32[]{:S(2)}, u32[]{:S(2)}) %collective-permute-start.18) | collective-permute-done | bytes 2097184 | tf_op jit(solution)/shard_map/ppermute | solution.py:50
  138.1 19.7 %widen.1 = (f32[1024,1024]{1,0:T(8,128)}, bf16[1024,1024]{1,0:T(8,128)(2,1)}, bf16[1024,2048]{1,0:T(8,128)(2,1)}, bf16[1024,2048]{1,0:T(8,128)(2,1)}) custom-call(s32[4]{0:T(128)} %copy-done.13, bf16[1024,1024]{1,0:T(8,128)(2,1)} %bitcast.247, bf16[1024,1024]{1,0:T(8,128)(2,1)} %get-tuple-element.202.refs_1_, bf16[1024,1024]{1,0:T(8,128)(2,1)} %copy-done.26, ...), custom_call_target="tpu_custom_call" | custom-call | flops 1000 | bytes 1000 | tf_op jit(solution)/shard_map/widen/pallas_call | solution.py:402
  157.9 10.2 %outer_whole.1 = bf16[2048,1024]{1,0:T(8,128)(2,1)} custom-call(bf16[1024,2048]{1,0:T(8,128)(2,1)} %get-tuple-element.210.left_ref.refs_0_, bf16[1024,1024]{1,0:T(8,128)(2,1)} %bitcast.249), custom_call_target="tpu_custom_call" | custom-call | flops 1000 | bytes 1000 | tf_op jit(solution)/shard_map/outer_whole/pallas_call | solution.py:455
  168.0 20.7 %narrow.1 = (bf16[1024,1024]{1,0:T(8,128)(2,1)}, bf16[1024,2048]{1,0:T(8,128)(2,1)}, bf16[1024,1024]{1,0:T(8,128)(2,1)}) custom-call(s32[4]{0:T(128)} %copy-done.13, bf16[1024,2048]{1,0:T(8,128)(2,1)} %get-tuple-element.210.left_ref.refs_0_, bf16[1024,1024]{1,0:T(8,128)(2,1)} %bitcast.250, bf16[1024,2048]{1,0:T(8,128)(2,1)} %get-tuple-element.211.refs_2_, ...), custom_call_target="tpu_custom_call" | custom-call | flops 1000 | bytes 1000 | tf_op jit(solution)/shard_map/narrow/pallas_call | solution.py:402
  190.7 8.7 %outer.3 = (bf16[4,64,2048]{2,1,0:T(8,128)(2,1)}, bf16[4,64,2048]{2,1,0:T(8,128)(2,1)}, bf16[4,2,32,2048]{3,2,1,0:T(8,128)(2,1)}, bf16[4,2,32,2048]{3,2,1,0:T(8,128)(2,1)}) custom-call(s32[4]{0:T(128)} %copy-done.13, bf16[1024,1024]{1,0:T(8,128)(2,1)} %get-tuple-element.218.refs_0_, bf16[1024,2048]{1,0:T(8,128)(2,1)} %get-tuple-element.219.refs_1_), custom_call_target="tpu_custom_call" | custom-call | flops 1000 | bytes 1000 | tf_op jit(solution)/shard_map/outer/pallas_call | solution.py:513
  202.1 9.8 %between.1 = (f32[1024,1024]{1,0:T(8,128)}, bf16[1024,1024]{1,0:T(8,128)(2,1)}, bf16[1024,512]{1,0:T(8,128)(2,1)}, f32[8,1024]{1,0:T(8,128)}) custom-call(s32[4]{0:T(128)} %copy-done.13, bf16[1024,1024]{1,0:T(8,128)(2,1)} %bitcast.251, bf16[1024,1024]{1,0:T(8,128)(2,1)} %get-tuple-element.226.refs_1_, bf16[1024,1024]{1,0:T(8,128)(2,1)} %collective-permute-done.19.refs_2_, ...), custom_call_target="tpu_custom_call" | custom-call | flops 1000 | bytes 1000 | tf_op jit(solution)/shard_map/between/pallas_call | solution.py:402
  213.1 14.4 %attend_back.2.refs_1_.refs_0_ = bf16[1024,768]{1,0:T(8,128)(2,1)S(1)} custom-call(bf16[1024,1536]{1,0:T(8,128)(2,1)} %get-tuple-element.193.q_ref.k_ref.v_ref, bf16[1024,1536]{1,0:T(8,128)(2,1)} %get-tuple-element.193.q_ref.k_ref.v_ref, bf16[1024,1536]{1,0:T(8,128)(2,1)} %get-tuple-element.193.q_ref.k_ref.v_ref, bf16[1024,512]{1,0:T(8,128)(2,1)S(1)} %copy-done.6, ...), custom_call_target="tpu_custom_call" | custom-call | flops 1000 | bytes 1000 | tf_op jit(solution)/shard_map/attend_back/pallas_call | solution.py:182
  227.6 5.2 %collective-permute-done.21 = bf16[4,64,2048]{2,1,0:T(8,128)(2,1)} collective-permute-done((bf16[4,64,2048]{2,1,0:T(8,128)(2,1)}, bf16[4,64,2048]{2,1,0:T(8,128)(2,1)}, u32[]{:S(2)}, u32[]{:S(2)}) %collective-permute-start.21) | collective-permute-done | bytes 1048608 | tf_op jit(solution)/shard_map/ppermute | solution.py:50
  232.8 1.8 add_convert_fusion
  235.7 1.8 add_convert_fusion.1
  238.3 1.4 collective-permute-start.23
  240.6 7.6 %outer.4 = (bf16[4,64,1280]{2,1,0:T(8,128)(2,1)}, bf16[4,64,1280]{2,1,0:T(8,128)(2,1)}, bf16[4,2,32,1280]{3,2,1,0:T(8,128)(2,1)}, bf16[4,2,32,1280]{3,2,1,0:T(8,128)(2,1)}) custom-call(s32[4]{0:T(128)} %copy-done.13, bf16[1024,1024]{1,0:T(8,128)(2,1)} %get-tuple-element.237.refs_0_, bf16[1024,768]{1,0:T(8,128)(2,1)} %copy-done.4, ...), custom_call_target="tpu_custom_call" | custom-call | flops 1000 | bytes 1000 | tf_op jit(solution)/shard_map/outer/pallas_call | solution.py:513
  248.1 7.5 %collective-permute-done.24 = bf16[4,32,2048]{2,1,0:T(8,128)(2,1)S(1)} collective-permute-done((bf16[4,32,2048]{2,1,0:T(8,128)(2,1)}, bf16[4,32,2048]{2,1,0:T(8,128)(2,1)S(1)}, u32[]{:S(2)}, u32[]{:S(2)}) %collective-permute-start.24) | collective-permute-done | bytes 524320 | tf_op jit(solution)/shard_map/ppermute | solution.py:50
  256.5 1.8 collective-permute-start.29
  263.2 1.4 slice.59
  265.3 13.9 %attend_back.3.refs_1_ = bf16[1024,768]{1,0:T(8,128)(2,1)S(1)} custom-call(bf16[1024,1536]{1,0:T(8,128)(2,1)} %get-tuple-element.193.q_ref.k_ref.v_ref, bf16[1024,1536]{1,0:T(8,128)(2,1)} %get-tuple-element.193.q_ref.k_ref.v_ref, bf16[1024,1536]{1,0:T(8,128)(2,1)} %get-tuple-element.193.q_ref.k_ref.v_ref, bf16[1024,512]{1,0:T(8,128)(2,1)S(1)} %copy-done.7, ...), custom_call_target="tpu_custom_call" | custom-call | flops 1000 | bytes 1000 | tf_op jit(solution)/shard_map/attend_back/pallas_call | solution.py:182
  281.2 2.0 collective-permute-done.28
  283.2 5.5 %outer.5 = (bf16[4,64,768]{2,1,0:T(8,128)(2,1)}, bf16[4,64,768]{2,1,0:T(8,128)(2,1)}, bf16[4,2,32,768]{3,2,1,0:T(8,128)(2,1)}, bf16[4,2,32,768]{3,2,1,0:T(8,128)(2,1)}) custom-call(s32[4]{0:T(128)} %copy-done.13, bf16[1024,1024]{1,0:T(8,128)(2,1)} %get-tuple-element.237.refs_0_, bf16[1024,768]{1,0:T(8,128)(2,1)} %copy-done.5), custom_call_target="tpu_custom_call" | custom-call | flops 1000 | bytes 1000 | tf_op jit(solution)/shard_map/outer/pallas_call | solution.py:513
  288.8 1.3 add_convert_fusion.2
  290.9 5.1 %collective-permute-start.33 = (bf16[4,32,1280]{2,1,0:T(8,128)(2,1)}, bf16[4,32,1280]{2,1,0:T(8,128)(2,1)}, u32[]{:S(2)}, u32[]{:S(2)}) collective-permute-start(bf16[4,32,1280]{2,1,0:T(8,128)(2,1)} %dynamic-slice_bitcast_fusion.8), channel_id=1, source_target_pairs={{0,1},{1,0},{2,3},{3,2},{4,5},{5,4},{6,7},{7,6},{8,9},{9,8},{10,11... | collective-permute-start | bytes 983048 | tf_op jit(solution)/shard_map/ppermute | solution.py:50
  296.9 1.5 collective-permute-start.32
  299.3 9.1 %enter.1 = (bf16[1024,1024]{1,0:T(8,128)(2,1)}, f32[8,1024]{1,0:T(8,128)}) custom-call(s32[4]{0:T(128)} %copy-done.13, bf16[1024,768]{1,0:T(8,128)(2,1)} %copy-done.4, bf16[1024,768]{1,0:T(8,128)(2,1)} %copy-done.5, bf16[1024,1024]{1,0:T(8,128)(2,1)} %bitcast.248, bf16[2,64,4224]{2,1,0:T(8,128)(2,1)} %copy-done.3, ...), custom_call_target="tpu_custom_call" | custom-call | flops 1000 | bytes 1000 | tf_op jit(solution)/shard_map/enter/pallas_call | solution.py:402
  310.5 2.1 maximum_bitcast_fusion.1
  313.9 1.5 collective-permute-start.42
  318.0 2.4 collective-permute-start.38
  320.5 3.0 collective-permute-start.40
  324.8 1.7 collective-permute-start.39
  327.3 8.2 %collective-permute-done.39 = bf16[2,32,1280]{2,1,0:T(8,128)(2,1)S(1)} collective-permute-done((bf16[2,32,1280]{2,1,0:T(8,128)(2,1)S(1)}, bf16[2,32,1280]{2,1,0:T(8,128)(2,1)S(1)}, u32[]{:S(2)}, u32[]{:S(2)}) %collective-permute-start.39) | collective-permute-done | bytes 163872 | tf_op jit(solution)/shard_map/ppermute | solution.py:208
  337.7 1.4 collective-permute-start.47
  339.7 2.2 collective-permute-start.44
  342.1 13.9 %collective-permute-done.46 = bf16[2,32,2048]{2,1,0:T(8,128)(2,1)S(1)} collective-permute-done((bf16[2,32,2048]{2,1,0:T(8,128)(2,1)S(1)}, bf16[2,32,2048]{2,1,0:T(8,128)(2,1)S(1)}, u32[]{:S(2)}, u32[]{:S(2)}) %collective-permute-start.46) | collective-permute-done | bytes 262176 | tf_op jit(solution)/shard_map/ppermute | solution.py:50
  356.2 1.7 collective-permute-start.58
  358.1 2.2 collective-permute-start.50
  360.8 1.5 collective-permute-start.54
  362.9 2.0 collective-permute-start.52
  364.9 1.5 maximum_bitcast_fusion
  366.4 1.8 collective-permute-done.53
  368.3 1.8 collective-permute-start.55
  371.7 2.3 finish_qkv.1
  374.2 1.6 bitcast_convert_fusion
  376.6 2.7 finish_up.1
  (294 shorter events, 63.7 us)
Async XLA Ops:
  7.2 65.3 %copy-start = (bf16[512,1024]{1,0:T(8,128)(2,1)S(1)}, bf16[512,1024]{1,0:T(8,128)(2,1)}, u32[]{:S(2)}) copy-start(bf16[512,1024]{1,0:T(8,128)(2,1)} %param.20) | copy-start | bytes 3145732
  7.2 160.8 %all-gather.2.cloned.1.call-start = ((), (), s32[]{:S(2)}) async-start(), calls=%async_computation.1 | async-start | bytes 4718592 | tf_op jit(solution)/shard_map/all_gather | solution.py:620
  12.4 32.4 %collective-permute-start.3 = (bf16[2,64,4224]{2,1,0:T(8,128)(2,1)S(1)}, bf16[2,64,4224]{2,1,0:T(8,128)(2,1)}, u32[]{:S(2)}, u32[]{:S(2)}) collective-permute-start(bf16[2,64,4224]{2,1,0:T(8,128)(2,1)S(1)} %get-tuple-element.165.refs_1_.refs_4_.refs_3_), channel_id=1, source_target_pairs={{0,1},{1,0},{2,3},{3,2},{4,5},{5,4},{6,7},{7,6},{8,9},{9,8},{10,11... | collective-permute-start | bytes 3244040 | tf_op jit(solution)/shard_map/ppermute | solution.py:50
  16.0 28.7 %collective-permute-start.4 = (bf16[2,256,1024]{2,1,0:T(8,128)(2,1)}, bf16[2,256,1024]{2,1,0:T(8,128)(2,1)}, u32[]{:S(2)}, u32[]{:S(2)}) collective-permute-start(bf16[2,256,1024]{2,1,0:T(8,128)(2,1)} %pad_maximum_fusion.2), channel_id=1, source_target_pairs={{0,16},{16,0},{1,17},{17,1},{2,18},{18,2},{3,19},{19,3},{4,20},{20... | collective-permute-start | bytes 3145736 | tf_op jit(solution)/shard_map/ppermute | solution.py:50
  17.3 7.0 %collective-permute-start = (bf16[64,2176]{1,0:T(8,128)(2,1)S(1)}, bf16[64,2176]{1,0:T(8,128)(2,1)S(1)}, u32[]{:S(2)}, u32[]{:S(2)}) collective-permute-start(bf16[64,2176]{1,0:T(8,128)(2,1)S(1)} %get-tuple-element.164), channel_id=1, source_target_pairs={{0,2},{2,4},{4,6},{6,0},{1,3},{3,5},{5,7},{7,1},{8,10},{10,12},{12... | collective-permute-start | bytes 835592 | tf_op jit(solution)/shard_map/ppermute | solution.py:208
  18.6 22.6 %collective-permute-start.1 = (bf16[64,2176]{1,0:T(8,128)(2,1)S(1)}, bf16[64,2176]{1,0:T(8,128)(2,1)S(1)}, u32[]{:S(2)}, u32[]{:S(2)}) collective-permute-start(bf16[64,2176]{1,0:T(8,128)(2,1)S(1)} %get-tuple-element.164), channel_id=1, source_target_pairs={{0,4},{2,6},{4,0},{6,2},{1,5},{3,7},{5,1},{7,3},{8,12},{10,14},{12... | collective-permute-start | bytes 835592 | tf_op jit(solution)/shard_map/ppermute | solution.py:208
  19.6 25.2 %collective-permute-start.2 = (bf16[64,2176]{1,0:T(8,128)(2,1)S(1)}, bf16[64,2176]{1,0:T(8,128)(2,1)}, u32[]{:S(2)}, u32[]{:S(2)}) collective-permute-start(bf16[64,2176]{1,0:T(8,128)(2,1)S(1)} %get-tuple-element.164), channel_id=1, source_target_pairs={{0,6},{2,0},{4,2},{6,4},{1,7},{3,1},{5,3},{7,5},{8,14},{10,8},{12,... | collective-permute-start | bytes 835592 | tf_op jit(solution)/shard_map/ppermute | solution.py:208
  47.2 3.6 collective-permute-start.7
  48.8 20.4 %collective-permute-start.5 = (bf16[3,64,2176]{2,1,0:T(8,128)(2,1)S(1)}, bf16[3,64,2176]{2,1,0:T(8,128)(2,1)}, u32[]{:S(2)}, u32[]{:S(2)}) collective-permute-start(bf16[3,64,2176]{2,1,0:T(8,128)(2,1)S(1)} %pad_maximum_fusion.6.refs_3_.refs_5_), channel_id=1, source_target_pairs={{0,1},{1,0},{2,3},{3,2},{4,5},{5,4},{6,7},{7,6},{8,9},{9,8},{10,11... | collective-permute-start | bytes 2506760 | tf_op jit(solution)/shard_map/ppermute | solution.py:50
  49.1 20.0 %collective-permute-start.6 = (bf16[3,64,2176]{2,1,0:T(8,128)(2,1)S(1)}, bf16[3,64,2176]{2,1,0:T(8,128)(2,1)}, u32[]{:S(2)}, u32[]{:S(2)}) collective-permute-start(bf16[3,64,2176]{2,1,0:T(8,128)(2,1)S(1)} %pad_maximum_fusion.6.refs_3_.refs_5_), channel_id=1, source_target_pairs={{0,16},{16,0},{1,17},{17,1},{2,18},{18,2},{3,19},{19,3},{4,20},{20... | collective-permute-start | bytes 2506760 | tf_op jit(solution)/shard_map/ppermute | solution.py:50
  49.4 7.4 %collective-permute-start.8 = (bf16[64,2048]{1,0:T(8,128)(2,1)S(1)}, bf16[64,2048]{1,0:T(8,128)(2,1)S(1)}, u32[]{:S(2)}, u32[]{:S(2)}) collective-permute-start(bf16[64,2048]{1,0:T(8,128)(2,1)S(1)} %get-tuple-element.174), channel_id=1, source_target_pairs={{0,2},{2,4},{4,6},{6,0},{1,3},{3,5},{5,7},{7,1},{8,10},{10,12},{12... | collective-permute-start | bytes 786440 | tf_op jit(solution)/shard_map/ppermute | solution.py:208
  49.4 14.4 %collective-permute-start.9 = (bf16[64,2048]{1,0:T(8,128)(2,1)S(1)}, bf16[64,2048]{1,0:T(8,128)(2,1)S(1)}, u32[]{:S(2)}, u32[]{:S(2)}) collective-permute-start(bf16[64,2048]{1,0:T(8,128)(2,1)S(1)} %get-tuple-element.174), channel_id=1, source_target_pairs={{0,6},{2,0},{4,2},{6,4},{1,7},{3,1},{5,3},{7,5},{8,14},{10,8},{12,... | collective-permute-start | bytes 786440 | tf_op jit(solution)/shard_map/ppermute | solution.py:208
  71.4 7.4 %collective-permute-start.13 = (bf16[2,256,1024]{2,1,0:T(8,128)(2,1)}, bf16[2,256,1024]{2,1,0:T(8,128)(2,1)}, u32[]{:S(2)}, u32[]{:S(2)}) collective-permute-start(bf16[2,256,1024]{2,1,0:T(8,128)(2,1)} %pad_maximum_fusion.4), channel_id=1, source_target_pairs={{0,8},{8,0},{1,9},{9,1},{2,10},{10,2},{3,11},{11,3},{4,12},{12,4},... | collective-permute-start | bytes 3145736 | tf_op jit(solution)/shard_map/ppermute | solution.py:50
  74.3 14.3 %collective-permute-start.10 = (bf16[3,32,2176]{2,1,0:T(8,128)(2,1)S(1)}, bf16[3,32,2176]{2,1,0:T(8,128)(2,1)S(1)}, u32[]{:S(2)}, u32[]{:S(2)}) collective-permute-start(bf16[3,32,2176]{2,1,0:T(8,128)(2,1)S(1)} %slice.52), channel_id=1, source_target_pairs={{0,16},{16,0},{1,17},{17,1},{2,18},{18,2},{3,19},{19,3},{4,20},{20... | collective-permute-start | bytes 1253384 | tf_op jit(solution)/shard_map/ppermute | solution.py:50
  75.6 12.9 %collective-permute-start.11 = (bf16[3,32,2176]{2,1,0:T(8,128)(2,1)S(1)}, bf16[3,32,2176]{2,1,0:T(8,128)(2,1)}, u32[]{:S(2)}, u32[]{:S(2)}) collective-permute-start(bf16[3,32,2176]{2,1,0:T(8,128)(2,1)S(1)} %slice.53), channel_id=1, source_target_pairs={{0,1},{1,0},{2,3},{3,2},{4,5},{5,4},{6,7},{7,6},{8,9},{9,8},{10,11... | collective-permute-start | bytes 1253384 | tf_op jit(solution)/shard_map/ppermute | solution.py:50
  76.9 11.7 %collective-permute-start.12 = (bf16[64,2048]{1,0:T(8,128)(2,1)S(1)}, bf16[64,2048]{1,0:T(8,128)(2,1)S(1)}, u32[]{:S(2)}, u32[]{:S(2)}) collective-permute-start(bf16[64,2048]{1,0:T(8,128)(2,1)S(1)} %get-tuple-element.174), channel_id=1, source_target_pairs={{0,4},{2,6},{4,0},{6,2},{1,5},{3,7},{5,1},{7,3},{8,12},{10,14},{12... | collective-permute-start | bytes 786440 | tf_op jit(solution)/shard_map/ppermute | solution.py:208
  88.6 224.0 %reduce-scatter.2.cloned.1.call-start = ((), (), s32[]{:S(2)}) async-start(), calls=%async_computation.2 | async-start | bytes 4718592 | tf_op jit(solution)/shard_map/reduce_scatter | solution.py:773
  89.0 24.3 %collective-permute-start.14 = (bf16[3,64,2048]{2,1,0:T(8,128)(2,1)S(1)}, bf16[3,64,2048]{2,1,0:T(8,128)(2,1)S(1)}, u32[]{:S(2)}, u32[]{:S(2)}) collective-permute-start(bf16[3,64,2048]{2,1,0:T(8,128)(2,1)S(1)} %pad_maximum_fusion.7.refs_6_), channel_id=1, source_target_pairs={{0,1},{1,0},{2,3},{3,2},{4,5},{5,4},{6,7},{7,6},{8,9},{9,8},{10,11... | collective-permute-start | bytes 2359304 | tf_op jit(solution)/shard_map/ppermute | solution.py:50
  89.4 23.9 %collective-permute-start.15 = (bf16[3,64,2048]{2,1,0:T(8,128)(2,1)S(1)}, bf16[3,64,2048]{2,1,0:T(8,128)(2,1)}, u32[]{:S(2)}, u32[]{:S(2)}) collective-permute-start(bf16[3,64,2048]{2,1,0:T(8,128)(2,1)S(1)} %pad_maximum_fusion.7.refs_6_), channel_id=1, source_target_pairs={{0,16},{16,0},{1,17},{17,1},{2,18},{18,2},{3,19},{19,3},{4,20},{20... | collective-permute-start | bytes 2359304 | tf_op jit(solution)/shard_map/ppermute | solution.py:50
  113.3 12.2 %collective-permute-start.16 = (bf16[3,32,2048]{2,1,0:T(8,128)(2,1)S(1)}, bf16[3,32,2048]{2,1,0:T(8,128)(2,1)S(1)}, u32[]{:S(2)}, u32[]{:S(2)}) collective-permute-start(bf16[3,32,2048]{2,1,0:T(8,128)(2,1)S(1)} %slice.55), channel_id=1, source_target_pairs={{0,16},{16,0},{1,17},{17,1},{2,18},{18,2},{3,19},{19,3},{4,20},{20... | collective-permute-start | bytes 1179656 | tf_op jit(solution)/shard_map/ppermute | solution.py:50
  115.7 9.9 %collective-permute-start.17 = (bf16[3,32,2048]{2,1,0:T(8,128)(2,1)S(1)}, bf16[3,32,2048]{2,1,0:T(8,128)(2,1)S(1)}, u32[]{:S(2)}, u32[]{:S(2)}) collective-permute-start(bf16[3,32,2048]{2,1,0:T(8,128)(2,1)S(1)} %slice.56), channel_id=1, source_target_pairs={{0,1},{1,0},{2,3},{3,2},{4,5},{5,4},{6,7},{7,6},{8,9},{9,8},{10,11... | collective-permute-start | bytes 1179656 | tf_op jit(solution)/shard_map/ppermute | solution.py:50
  130.7 6.1 %collective-permute-start.18 = (bf16[1024,1024]{1,0:T(8,128)(2,1)}, bf16[1024,1024]{1,0:T(8,128)(2,1)S(1)}, u32[]{:S(2)}, u32[]{:S(2)}) collective-permute-start(bf16[1024,1024]{1,0:T(8,128)(2,1)} %get-tuple-element.202.refs_1_), channel_id=1, source_target_pairs={{0,8},{8,0},{1,9},{9,1},{2,10},{10,2},{3,11},{11,3},{4,12},{12,4},... | collective-permute-start | bytes 6291464 | tf_op jit(solution)/shard_map/ppermute | solution.py:50
  188.8 11.6 %collective-permute-start.19 = (bf16[1024,1024]{1,0:T(8,128)(2,1)}, bf16[1024,1024]{1,0:T(8,128)(2,1)}, u32[]{:S(2)}, u32[]{:S(2)}) collective-permute-start(bf16[1024,1024]{1,0:T(8,128)(2,1)} %get-tuple-element.226.refs_1_), channel_id=1, source_target_pairs={{0,8},{8,0},{1,9},{9,1},{2,10},{10,2},{3,11},{11,3},{4,12},{12,4},... | collective-permute-start | bytes 6291464 | tf_op jit(solution)/shard_map/ppermute | solution.py:50
  190.5 8.9 %collective-permute-start.20 = (bf16[2,256,1024]{2,1,0:T(8,128)(2,1)S(1)}, bf16[2,256,1024]{2,1,0:T(8,128)(2,1)S(1)}, u32[]{:S(2)}, u32[]{:S(2)}) collective-permute-start(bf16[2,256,1024]{2,1,0:T(8,128)(2,1)S(1)} %dynamic-slice_bitcast_fusion.1), channel_id=1, source_target_pairs={{0,8},{8,0},{1,9},{9,1},{2,10},{10,2},{3,11},{11,3},{4,12},{12,4},... | collective-permute-start | bytes 3145736 | tf_op jit(solution)/shard_map/ppermute | solution.py:50
  200.4 32.4 %collective-permute-start.21 = (bf16[4,64,2048]{2,1,0:T(8,128)(2,1)}, bf16[4,64,2048]{2,1,0:T(8,128)(2,1)}, u32[]{:S(2)}, u32[]{:S(2)}) collective-permute-start(bf16[4,64,2048]{2,1,0:T(8,128)(2,1)} %get-tuple-element.232), channel_id=1, source_target_pairs={{0,1},{1,0},{2,3},{3,2},{4,5},{5,4},{6,7},{7,6},{8,9},{9,8},{10,11... | collective-permute-start | bytes 3145736 | tf_op jit(solution)/shard_map/ppermute | solution.py:50
  201.6 31.2 %collective-permute-start.22 = (bf16[4,2,32,2048]{3,2,1,0:T(8,128)(2,1)}, bf16[4,2,32,2048]{3,2,1,0:T(8,128)(2,1)}, u32[]{:S(2)}, u32[]{:S(2)}) collective-permute-start(bf16[4,2,32,2048]{3,2,1,0:T(8,128)(2,1)} %get-tuple-element.233), channel_id=1, source_target_pairs={{0,16},{16,0},{1,17},{17,1},{2,18},{18,2},{3,19},{19,3},{4,20},{20... | collective-permute-start | bytes 3145736 | tf_op jit(solution)/shard_map/ppermute | solution.py:50
  213.1 22.6 %copy-start.30 = (bf16[4,64,2048]{2,1,0:T(8,128)(2,1)S(1)}, bf16[4,64,2048]{2,1,0:T(8,128)(2,1)}, u32[]{:S(2)}) copy-start(bf16[4,64,2048]{2,1,0:T(8,128)(2,1)} %get-tuple-element.225) | copy-start | bytes 3145732
  235.5 20.2 %collective-permute-start.24 = (bf16[4,32,2048]{2,1,0:T(8,128)(2,1)}, bf16[4,32,2048]{2,1,0:T(8,128)(2,1)S(1)}, u32[]{:S(2)}, u32[]{:S(2)}) collective-permute-start(bf16[4,32,2048]{2,1,0:T(8,128)(2,1)} %dynamic-slice_bitcast_fusion.3), channel_id=1, source_target_pairs={{0,1},{1,0},{2,3},{3,2},{4,5},{5,4},{6,7},{7,6},{8,9},{9,8},{10,11... | collective-permute-start | bytes 1572872 | tf_op jit(solution)/shard_map/ppermute | solution.py:50
  238.3 17.3 %collective-permute-start.23 = (bf16[4,32,2048]{2,1,0:T(8,128)(2,1)}, bf16[4,32,2048]{2,1,0:T(8,128)(2,1)S(1)}, u32[]{:S(2)}, u32[]{:S(2)}) collective-permute-start(bf16[4,32,2048]{2,1,0:T(8,128)(2,1)} %dynamic-slice_bitcast_fusion.4), channel_id=1, source_target_pairs={{0,16},{16,0},{1,17},{17,1},{2,18},{18,2},{3,19},{19,3},{4,20},{20... | collective-permute-start | bytes 1572872 | tf_op jit(solution)/shard_map/ppermute | solution.py:50
  239.9 22.2 %copy-start.58 = (f32[2,256]{1,0:T(2,128)}, f32[2,256]{1,0:T(2,128)S(1)}, u32[]{:S(2)}) copy-start(f32[2,256]{1,0:T(2,128)S(1)} %broadcast_multiply_fusion.2) | copy-start | bytes 6148
  256.5 23.9 %collective-permute-start.29 = (bf16[256,1024]{1,0:T(8,128)(2,1)S(1)}, bf16[256,1024]{1,0:T(8,128)(2,1)S(1)}, u32[]{:S(2)}, u32[]{:S(2)}) collective-permute-start(bf16[256,1024]{1,0:T(8,128)(2,1)S(1)} %dynamic-slice_bitcast_fusion.2), channel_id=1, source_target_pairs={{0,16},{16,0},{1,17},{17,1},{2,18},{18,2},{3,19},{19,3},{4,20},{20... | collective-permute-start | bytes 1572872 | tf_op jit(solution)/shard_map/ppermute | solution.py:50
  258.2 22.2 %collective-permute-start.27 = (bf16[4,64,1280]{2,1,0:T(8,128)(2,1)}, bf16[4,64,1280]{2,1,0:T(8,128)(2,1)S(1)}, u32[]{:S(2)}, u32[]{:S(2)}) collective-permute-start(bf16[4,64,1280]{2,1,0:T(8,128)(2,1)} %get-tuple-element.254), channel_id=1, source_target_pairs={{0,1},{1,0},{2,3},{3,2},{4,5},{5,4},{6,7},{7,6},{8,9},{9,8},{10,11... | collective-permute-start | bytes 1966088 | tf_op jit(solution)/shard_map/ppermute | solution.py:50
  258.2 25.0 %collective-permute-start.28 = (bf16[4,2,32,1280]{3,2,1,0:T(8,128)(2,1)}, bf16[4,2,32,1280]{3,2,1,0:T(8,128)(2,1)}, u32[]{:S(2)}, u32[]{:S(2)}) collective-permute-start(bf16[4,2,32,1280]{3,2,1,0:T(8,128)(2,1)} %get-tuple-element.255), channel_id=1, source_target_pairs={{0,16},{16,0},{1,17},{17,1},{2,18},{18,2},{3,19},{19,3},{4,20},{20... | collective-permute-start | bytes 1966088 | tf_op jit(solution)/shard_map/ppermute | solution.py:50
  260.4 20.0 %collective-permute-start.25 = (bf16[2,32,2048]{2,1,0:T(8,128)(2,1)S(1)}, bf16[2,32,2048]{2,1,0:T(8,128)(2,1)S(1)}, u32[]{:S(2)}, u32[]{:S(2)}) collective-permute-start(bf16[2,32,2048]{2,1,0:T(8,128)(2,1)S(1)} %get-tuple-element.335), channel_id=1, source_target_pairs={{0,2},{2,4},{4,6},{6,0},{1,3},{3,5},{5,7},{7,1},{8,10},{10,12},{12... | collective-permute-start | bytes 786440 | tf_op jit(solution)/shard_map/ppermute | solution.py:208
  261.6 18.8 %collective-permute-start.26 = (bf16[2,32,2048]{2,1,0:T(8,128)(2,1)S(1)}, bf16[2,32,2048]{2,1,0:T(8,128)(2,1)S(1)}, u32[]{:S(2)}, u32[]{:S(2)}) collective-permute-start(bf16[2,32,2048]{2,1,0:T(8,128)(2,1)S(1)} %get-tuple-element.336), channel_id=1, source_target_pairs={{0,6},{2,0},{4,2},{6,4},{1,7},{3,1},{5,3},{7,5},{8,14},{10,8},{12,... | collective-permute-start | bytes 786440 | tf_op jit(solution)/shard_map/ppermute | solution.py:208
  290.9 21.8 %collective-permute-start.33 = (bf16[4,32,1280]{2,1,0:T(8,128)(2,1)}, bf16[4,32,1280]{2,1,0:T(8,128)(2,1)}, u32[]{:S(2)}, u32[]{:S(2)}) collective-permute-start(bf16[4,32,1280]{2,1,0:T(8,128)(2,1)} %dynamic-slice_bitcast_fusion.8), channel_id=1, source_target_pairs={{0,1},{1,0},{2,3},{3,2},{4,5},{5,4},{6,7},{7,6},{8,9},{9,8},{10,11... | collective-permute-start | bytes 983048 | tf_op jit(solution)/shard_map/ppermute | solution.py:50
  296.9 15.8 %collective-permute-start.32 = (bf16[4,32,1280]{2,1,0:T(8,128)(2,1)}, bf16[4,32,1280]{2,1,0:T(8,128)(2,1)}, u32[]{:S(2)}, u32[]{:S(2)}) collective-permute-start(bf16[4,32,1280]{2,1,0:T(8,128)(2,1)} %dynamic-slice_bitcast_fusion.9), channel_id=1, source_target_pairs={{0,16},{16,0},{1,17},{17,1},{2,18},{18,2},{3,19},{19,3},{4,20},{20... | collective-permute-start | bytes 983048 | tf_op jit(solution)/shard_map/ppermute | solution.py:50
  298.4 14.3 %collective-permute-start.30 = (bf16[4,64,768]{2,1,0:T(8,128)(2,1)}, bf16[4,64,768]{2,1,0:T(8,128)(2,1)S(1)}, u32[]{:S(2)}, u32[]{:S(2)}) collective-permute-start(bf16[4,64,768]{2,1,0:T(8,128)(2,1)} %get-tuple-element.269), channel_id=1, source_target_pairs={{0,1},{1,0},{2,3},{3,2},{4,5},{5,4},{6,7},{7,6},{8,9},{9,8},{10,11... | collective-permute-start | bytes 1179656 | tf_op jit(solution)/shard_map/ppermute | solution.py:50
  298.4 15.5 %collective-permute-start.31 = (bf16[4,2,32,768]{3,2,1,0:T(8,128)(2,1)}, bf16[4,2,32,768]{3,2,1,0:T(8,128)(2,1)}, u32[]{:S(2)}, u32[]{:S(2)}) collective-permute-start(bf16[4,2,32,768]{3,2,1,0:T(8,128)(2,1)} %get-tuple-element.270), channel_id=1, source_target_pairs={{0,16},{16,0},{1,17},{17,1},{2,18},{18,2},{3,19},{19,3},{4,20},{20... | collective-permute-start | bytes 1179656 | tf_op jit(solution)/shard_map/ppermute | solution.py:50
  298.4 14.2 %collective-permute-start.34 = (bf16[2,32,2048]{2,1,0:T(8,128)(2,1)}, bf16[2,32,2048]{2,1,0:T(8,128)(2,1)S(1)}, u32[]{:S(2)}, u32[]{:S(2)}) collective-permute-start(bf16[2,32,2048]{2,1,0:T(8,128)(2,1)} %get-tuple-element.275), channel_id=1, source_target_pairs={{0,4},{2,6},{4,0},{6,2},{1,5},{3,7},{5,1},{7,3},{8,12},{10,14},{12... | collective-permute-start | bytes 786440 | tf_op jit(solution)/shard_map/ppermute | solution.py:208
  313.9 12.8 %collective-permute-start.42 = (bf16[256,1024]{1,0:T(8,128)(2,1)}, bf16[256,1024]{1,0:T(8,128)(2,1)S(1)}, u32[]{:S(2)}, u32[]{:S(2)}) collective-permute-start(bf16[256,1024]{1,0:T(8,128)(2,1)} %reduce-scatter.2.cloned.1.call-done), channel_id=1, source_target_pairs={{0,16},{16,0},{1,17},{17,1},{2,18},{18,2},{3,19},{19,3},{4,20},{20... | collective-permute-start | bytes 1572872 | tf_op jit(solution)/shard_map/ppermute | solution.py:50
  315.4 9.4 %collective-permute-start.41 = (f32[4,4,128]{2,1,0:T(4,128)S(1)}, f32[4,4,128]{2,1,0:T(4,128)S(1)}, u32[]{:S(2)}, u32[]{:S(2)}) collective-permute-start(f32[4,4,128]{2,1,0:T(4,128)S(1)} %fusion.65), channel_id=1, source_target_pairs={{0,1},{1,0},{2,3},{3,2},{4,5},{5,4},{6,7},{7,6},{8,9},{9,8},{10,11... | collective-permute-start | bytes 24584 | tf_op jit(solution)/shard_map/ppermute | solution.py:50
  317.9 8.6 %collective-permute-start.37 = (bf16[2,32,1280]{2,1,0:T(8,128)(2,1)S(1)}, bf16[2,32,1280]{2,1,0:T(8,128)(2,1)S(1)}, u32[]{:S(2)}, u32[]{:S(2)}) collective-permute-start(bf16[2,32,1280]{2,1,0:T(8,128)(2,1)S(1)} %get-tuple-element.338), channel_id=1, source_target_pairs={{0,2},{2,4},{4,6},{6,0},{1,3},{3,5},{5,7},{7,1},{8,10},{10,12},{12... | collective-permute-start | bytes 491528 | tf_op jit(solution)/shard_map/ppermute | solution.py:208
  318.0 9.3 %collective-permute-start.38 = (bf16[2,32,1280]{2,1,0:T(8,128)(2,1)S(1)}, bf16[2,32,1280]{2,1,0:T(8,128)(2,1)S(1)}, u32[]{:S(2)}, u32[]{:S(2)}) collective-permute-start(bf16[2,32,1280]{2,1,0:T(8,128)(2,1)S(1)} %get-tuple-element.339), channel_id=1, source_target_pairs={{0,4},{2,6},{4,0},{6,2},{1,5},{3,7},{5,1},{7,3},{8,12},{10,14},{12... | collective-permute-start | bytes 491528 | tf_op jit(solution)/shard_map/ppermute | solution.py:208
  320.5 15.0 %collective-permute-start.40 = (bf16[2,256,1024]{2,1,0:T(8,128)(2,1)S(1)}, bf16[2,256,1024]{2,1,0:T(8,128)(2,1)S(1)}, u32[]{:S(2)}, u32[]{:S(2)}) collective-permute-start(bf16[2,256,1024]{2,1,0:T(8,128)(2,1)S(1)} %dynamic-slice_bitcast_fusion), channel_id=1, source_target_pairs={{0,8},{8,0},{1,9},{9,1},{2,10},{10,2},{3,11},{11,3},{4,12},{12,4},... | collective-permute-start | bytes 3145736 | tf_op jit(solution)/shard_map/ppermute | solution.py:50
  324.8 10.8 %collective-permute-start.39 = (bf16[2,32,1280]{2,1,0:T(8,128)(2,1)S(1)}, bf16[2,32,1280]{2,1,0:T(8,128)(2,1)S(1)}, u32[]{:S(2)}, u32[]{:S(2)}) collective-permute-start(bf16[2,32,1280]{2,1,0:T(8,128)(2,1)S(1)} %get-tuple-element.337), channel_id=1, source_target_pairs={{0,6},{2,0},{4,2},{6,4},{1,7},{3,1},{5,3},{7,5},{8,14},{10,8},{12,... | collective-permute-start | bytes 491528 | tf_op jit(solution)/shard_map/ppermute | solution.py:208
  326.6 9.0 %collective-permute-start.36 = (bf16[4,32,768]{2,1,0:T(8,128)(2,1)S(1)}, bf16[4,32,768]{2,1,0:T(8,128)(2,1)S(1)}, u32[]{:S(2)}, u32[]{:S(2)}) collective-permute-start(bf16[4,32,768]{2,1,0:T(8,128)(2,1)S(1)} %dynamic-slice_bitcast_fusion.10), channel_id=1, source_target_pairs={{0,1},{1,0},{2,3},{3,2},{4,5},{5,4},{6,7},{7,6},{8,9},{9,8},{10,11... | collective-permute-start | bytes 589832 | tf_op jit(solution)/shard_map/ppermute | solution.py:50
  326.7 8.9 %collective-permute-start.35 = (bf16[4,32,768]{2,1,0:T(8,128)(2,1)S(1)}, bf16[4,32,768]{2,1,0:T(8,128)(2,1)S(1)}, u32[]{:S(2)}, u32[]{:S(2)}) collective-permute-start(bf16[4,32,768]{2,1,0:T(8,128)(2,1)S(1)} %dynamic-slice_bitcast_fusion.11), channel_id=1, source_target_pairs={{0,16},{16,0},{1,17},{17,1},{2,18},{18,2},{3,19},{19,3},{4,20},{20... | collective-permute-start | bytes 589832 | tf_op jit(solution)/shard_map/ppermute | solution.py:50
  335.6 6.3 %collective-permute-start.48 = (f32[4,4,128]{2,1,0:T(4,128)S(1)}, f32[4,4,128]{2,1,0:T(4,128)S(1)}, u32[]{:S(2)}, u32[]{:S(2)}) collective-permute-start(f32[4,4,128]{2,1,0:T(4,128)S(1)} %fusion.64), channel_id=1, source_target_pairs={{0,16},{16,0},{1,17},{17,1},{2,18},{18,2},{3,19},{19,3},{4,20},{20... | collective-permute-start | bytes 24584 | tf_op jit(solution)/shard_map/ppermute | solution.py:50
  337.7 18.6 %collective-permute-start.47 = (bf16[256,1024]{1,0:T(8,128)(2,1)S(1)}, bf16[256,1024]{1,0:T(8,128)(2,1)S(1)}, u32[]{:S(2)}, u32[]{:S(2)}) collective-permute-start(bf16[256,1024]{1,0:T(8,128)(2,1)S(1)} %fusion.19), channel_id=1, source_target_pairs={{0,16},{16,0},{1,17},{17,1},{2,18},{18,2},{3,19},{19,3},{4,20},{20... | collective-permute-start | bytes 1572872 | tf_op jit(solution)/shard_map/ppermute | solution.py:50
  339.3 16.8 %collective-permute-start.46 = (bf16[2,32,2048]{2,1,0:T(8,128)(2,1)S(1)}, bf16[2,32,2048]{2,1,0:T(8,128)(2,1)S(1)}, u32[]{:S(2)}, u32[]{:S(2)}) collective-permute-start(bf16[2,32,2048]{2,1,0:T(8,128)(2,1)S(1)} %fusion.24), channel_id=1, source_target_pairs={{0,16},{16,0},{1,17},{17,1},{2,18},{18,2},{3,19},{19,3},{4,20},{20... | collective-permute-start | bytes 786440 | tf_op jit(solution)/shard_map/ppermute | solution.py:50
  339.6 16.6 %collective-permute-start.43 = (bf16[2,32,768]{2,1,0:T(8,128)(2,1)S(1)}, bf16[2,32,768]{2,1,0:T(8,128)(2,1)S(1)}, u32[]{:S(2)}, u32[]{:S(2)}) collective-permute-start(bf16[2,32,768]{2,1,0:T(8,128)(2,1)S(1)} %get-tuple-element.343), channel_id=1, source_target_pairs={{0,2},{2,4},{4,6},{6,0},{1,3},{3,5},{5,7},{7,1},{8,10},{10,12},{12... | collective-permute-start | bytes 294920 | tf_op jit(solution)/shard_map/ppermute | solution.py:208
  339.7 16.6 %collective-permute-start.44 = (bf16[2,32,768]{2,1,0:T(8,128)(2,1)S(1)}, bf16[2,32,768]{2,1,0:T(8,128)(2,1)S(1)}, u32[]{:S(2)}, u32[]{:S(2)}) collective-permute-start(bf16[2,32,768]{2,1,0:T(8,128)(2,1)S(1)} %get-tuple-element.344), channel_id=1, source_target_pairs={{0,4},{2,6},{4,0},{6,2},{1,5},{3,7},{5,1},{7,3},{8,12},{10,14},{12... | collective-permute-start | bytes 294920 | tf_op jit(solution)/shard_map/ppermute | solution.py:208
  341.9 14.3 %collective-permute-start.45 = (bf16[2,32,768]{2,1,0:T(8,128)(2,1)S(1)}, bf16[2,32,768]{2,1,0:T(8,128)(2,1)S(1)}, u32[]{:S(2)}, u32[]{:S(2)}) collective-permute-start(bf16[2,32,768]{2,1,0:T(8,128)(2,1)S(1)} %get-tuple-element.342), channel_id=1, source_target_pairs={{0,6},{2,0},{4,2},{6,4},{1,7},{3,1},{5,3},{7,5},{8,14},{10,8},{12,... | collective-permute-start | bytes 294920 | tf_op jit(solution)/shard_map/ppermute | solution.py:208
  356.2 17.7 %collective-permute-start.58 = (bf16[256,1024]{1,0:T(8,128)(2,1)S(1)}, bf16[256,1024]{1,0:T(8,128)(2,1)S(1)}, u32[]{:S(2)}, u32[]{:S(2)}) collective-permute-start(bf16[256,1024]{1,0:T(8,128)(2,1)S(1)} %add_convert_fusion.4), channel_id=1, source_target_pairs={{0,8},{8,0},{1,9},{9,1},{2,10},{10,2},{3,11},{11,3},{4,12},{12,4},... | collective-permute-start | bytes 1572872 | tf_op jit(solution)/shard_map/ppermute | solution.py:50
  358.0 17.8 %collective-permute-start.57 = (bf16[128,2048]{1,0:T(8,128)(2,1)S(1)}, bf16[128,2048]{1,0:T(8,128)(2,1)S(1)}, u32[]{:S(2)}, u32[]{:S(2)}) collective-permute-start(bf16[128,2048]{1,0:T(8,128)(2,1)S(1)} %bitcast.262), channel_id=1, source_target_pairs={{0,8},{8,0},{1,9},{9,1},{2,10},{10,2},{3,11},{11,3},{4,12},{12,4},... | collective-permute-start | bytes 1572872 | tf_op jit(solution)/shard_map/ppermute | solution.py:50
  358.1 2.7 collective-permute-start.49
  358.1 4.2 %collective-permute-start.50 = (f32[4,128]{1,0:T(4,128)S(1)}, f32[4,128]{1,0:T(4,128)S(1)}, u32[]{:S(2)}, u32[]{:S(2)}) collective-permute-start(f32[4,128]{1,0:T(4,128)S(1)} %bitcast.279), channel_id=1, source_target_pairs={{0,4},{2,6},{4,0},{6,2},{1,5},{3,7},{5,1},{7,3},{8,12},{10,14},{12... | collective-permute-start | bytes 6152 | tf_op jit(solution)/shard_map/ppermute | solution.py:208
  360.3 2.5 collective-permute-start.51
  360.8 5.6 %collective-permute-start.54 = (bf16[2,32,768]{2,1,0:T(8,128)(2,1)S(1)}, bf16[2,32,768]{2,1,0:T(8,128)(2,1)S(1)}, u32[]{:S(2)}, u32[]{:S(2)}) collective-permute-start(bf16[2,32,768]{2,1,0:T(8,128)(2,1)S(1)} %fusion.46), channel_id=1, source_target_pairs={{0,16},{16,0},{1,17},{17,1},{2,18},{18,2},{3,19},{19,3},{4,20},{20... | collective-permute-start | bytes 294920 | tf_op jit(solution)/shard_map/ppermute | solution.py:50
  362.3 5.9 %collective-permute-start.53 = (bf16[2,32,1280]{2,1,0:T(8,128)(2,1)S(1)}, bf16[2,32,1280]{2,1,0:T(8,128)(2,1)S(1)}, u32[]{:S(2)}, u32[]{:S(2)}) collective-permute-start(bf16[2,32,1280]{2,1,0:T(8,128)(2,1)S(1)} %fusion.33), channel_id=1, source_target_pairs={{0,16},{16,0},{1,17},{17,1},{2,18},{18,2},{3,19},{19,3},{4,20},{20... | collective-permute-start | bytes 491528 | tf_op jit(solution)/shard_map/ppermute | solution.py:50
  362.9 3.5 collective-permute-start.52
  368.3 3.1 collective-permute-start.55
  370.2 1.5 collective-permute-start.56
  (59 other events, 400.8 us)
Sparse Core Ops, SparseCore 0:
  88.7 75.7 all-gather.1
  189.3 104.5 reduce-scatter.1

commit v4 on v3

--- a/solution.py
+++ b/solution.py
@@ -13,6 +13,7 @@
 DOC_MOST = 512
 TILE = 256
 LANES = 128
+VMEM = 30 * 1024 * 1024
 epsilon = 1e-05
 SWAP = [(0, 1), (1, 0)]
 f32 = jnp.float32
@@ -35,7 +36,12 @@
     return dot(left, right, ((1,), (1,)))
 
 
-TINY = pl.CostEstimate(flops=1000, bytes_accessed=1000, transcendentals=0)
+def cost(micros):
+    return pl.CostEstimate(flops=int(micros * 1.1e9), bytes_accessed=1000, transcendentals=0)
+
+
+def far(array):
+    return pltpu.with_memory_space_constraint(array, pltpu.HBM)
 
 
 def sync(*values):
@@ -124,10 +130,10 @@
             jax.ShapeDtypeStruct((rows, count * LANES), f32),
         ],
         scratch_shapes=[pltpu.VMEM((len(spans), tile, widest), f32)],
-        compiler_params=pltpu.CompilerParams(vmem_limit_bytes=40 * 1024 * 1024),
-        cost_estimate=TINY,
+        compiler_params=pltpu.CompilerParams(vmem_limit_bytes=VMEM),
+        cost_estimate=cost(4 * count),
         name="attend",
-    )(joint, joint, joint, seg_col, seg_row)
+    )(far(joint), far(joint), far(joint), seg_col, seg_row)
 
 
 def attend_back_kernel(
@@ -198,17 +204,17 @@
             pltpu.VMEM((rows, LANES), f32),
             pltpu.VMEM((rows, LANES), f32),
         ],
-        compiler_params=pltpu.CompilerParams(vmem_limit_bytes=48 * 1024 * 1024),
-        cost_estimate=TINY,
+        compiler_params=pltpu.CompilerParams(vmem_limit_bytes=VMEM),
+        cost_estimate=cost(6 * count),
         name="attend_back",
-    )(joint, joint, joint, grads, lse, seg_col, seg_row)
+    )(far(joint), far(joint), far(joint), grads, lse, seg_col, seg_row)
 
 
 def along(value, axis, depth, step):
     return lax.ppermute(value, axis, [(i, (i + step) % depth) for i in range(depth)])
 
 
-def load(depth, place, pieces, sems, targets, base=0):
+def load(depth, place, pieces, sems, targets, base=0, sem=0):
     z, x, h = place[0], place[1], place[2]
     copies = []
 
@@ -217,7 +223,7 @@
             taken = source
             if columns != source.shape[1]:
                 taken = source.at[:, shift + first : shift + first + columns]
-            copies.append(pltpu.make_async_copy(taken, where(shard, half, at, source.shape[0]), sems.at[len(copies)]))
+            copies.append(pltpu.make_async_copy(taken, where(shard, half, at, source.shape[0]), sems.at[sem + len(copies)]))
             copies[-1].start()
 
     own, side_own, far, side, near, last_side, last_near = pieces
@@ -245,6 +251,25 @@
     return where
 
 
+def halve(side, near):
+    count, rows, columns = side.shape
+    half = rows // 2
+
+    def kernel(side_ref, near_ref, one_ref, two_ref):
+        one_ref[...] = side_ref[:, :half, :]
+        two_ref[...] = near_ref[:, half:, :]
+
+    return pl.pallas_call(
+        kernel,
+        in_specs=[pl.BlockSpec(memory_space=pltpu.VMEM)] * 2,
+        out_specs=[pl.BlockSpec(memory_space=pltpu.VMEM)] * 2,
+        out_shape=[shape_of(count, half, columns)] * 2,
+        compiler_params=pltpu.CompilerParams(vmem_limit_bytes=VMEM),
+        cost_estimate=cost(1),
+        name="halve",
+    )(side, near)
+
+
 def prepare(place, shards, w_qkv, w_out, w_up, vectors):
     rows, model = w_out.shape
     half, blocks = rows // 2, w_qkv.shape[1] // LANES
@@ -283,10 +308,10 @@
         in_specs=[pl.BlockSpec(memory_space=pltpu.SMEM)] + [pl.BlockSpec(memory_space=pltpu.VMEM)] * 4,
         out_specs=[pl.BlockSpec(memory_space=pltpu.VMEM)] * 3,
         out_shape=[shape_of(2, half, up_at + wide), shape_of(half, up_at), shape_of(half, wide)],
-        compiler_params=pltpu.CompilerParams(vmem_limit_bytes=40 * 1024 * 1024),
-        cost_estimate=TINY,
+        compiler_params=pltpu.CompilerParams(vmem_limit_bytes=VMEM),
+        cost_estimate=cost(2),
         name="prepare",
-    )(place, w_qkv, w_out, w_up, vectors)
+    )(place, far(w_qkv), far(w_out), far(w_up), vectors)
 
 
 def finish_up(place, shards, own, other):
@@ -307,27 +332,26 @@
         in_specs=[pl.BlockSpec(memory_space=pltpu.SMEM)] + [pl.BlockSpec(memory_space=pltpu.VMEM)] * 2,
         out_specs=pl.BlockSpec(memory_space=pltpu.VMEM),
         out_shape=shape_of(rows, 2 * columns, dtype=f32),
-        cost_estimate=TINY,
+        cost_estimate=cost(2),
         name="finish_up",
     )(place, own, other)
 
 
-def finish_qkv(place, owns, others, out_own, out_other):
-    rows = out_own.shape[0]
-    half = rows // 2
-    columns = sum(own.shape[1] for own in owns)
-    model = 2 * out_own.shape[1]
-    pieces = len(owns)
+def finish_qkv(place, owns, others):
+    rows = owns[0].shape[0]
+    half, pieces = rows // 2, len(owns)
+    columns = owns[-1].shape[1] - LANES
+    third = columns // 3
+    model = 2 * (owns[0].shape[1] - columns - LANES)
 
     def kernel(place_ref, *refs):
         lo = place_ref[3]
         owns_refs, others_refs = refs[:pieces], refs[pieces : 2 * pieces]
-        out_own_ref, out_other_ref, qkv_ref, out_ref = refs[2 * pieces :]
+        qkv_ref, out_ref, sums_ref = refs[2 * pieces :]
         left = lax.broadcasted_iota(jnp.int32, (rows, LANES), 1) < HEAD_DIM
         at = 0
         for j in range(3):
             for own_ref, other_ref in zip(owns_refs, others_refs):
-                third = own_ref.shape[1] // 3
                 for first in range(j * third, (j + 1) * third, LANES):
                     mine = own_ref[:, first : first + LANES].astype(f32)
                     theirs = other_ref[:, first : first + LANES].astype(f32)
@@ -335,37 +359,84 @@
                     qkv_ref[:, at : at + LANES] = jnp.where(left, one, pltpu.roll(two, HEAD_DIM, 1))
                     qkv_ref[:, at + LANES : at + 2 * LANES] = jnp.where(left, pltpu.roll(one, HEAD_DIM, 1), two)
                     at += 2 * LANES
-        mine, theirs = out_own_ref[...].astype(f32), out_other_ref[...].astype(f32)
+        sums = jnp.zeros((rows, LANES), f32)
+        for ref in refs[: 2 * pieces]:
+            sums = sums + ref[:, columns : columns + LANES].astype(f32)
+        sums_ref[...] = sums.T[:8, :]
+        mine, theirs = (ref[:, columns + LANES :].astype(f32) for ref in (owns_refs[0], others_refs[0]))
         for at, value in ((0, jnp.where(lo == 0, mine, theirs)), (half, jnp.where(lo == 0, theirs, mine))):
             out_ref[at : at + half, : model // 2] = value[:half]
             out_ref[at : at + half, model // 2 :] = value[half:]
 
     return pl.pallas_call(
         kernel,
-        in_specs=[pl.BlockSpec(memory_space=pltpu.SMEM)] + [pl.BlockSpec(memory_space=pltpu.VMEM)] * (2 * pieces + 2),
-        out_specs=[pl.BlockSpec(memory_space=pltpu.VMEM)] * 2,
-        out_shape=[shape_of(rows, 2 * columns, dtype=f32), shape_of(rows, model, dtype=f32)],
-        compiler_params=pltpu.CompilerParams(vmem_limit_bytes=40 * 1024 * 1024),
-        cost_estimate=TINY,
+        in_specs=[pl.BlockSpec(memory_space=pltpu.SMEM)] + [pl.BlockSpec(memory_space=pltpu.VMEM)] * (2 * pieces),
+        out_specs=[pl.BlockSpec(memory_space=pltpu.VMEM)] * 3,
+        out_shape=[
+            shape_of(rows, 2 * pieces * columns, dtype=f32),
+            shape_of(rows, model, dtype=f32),
+            shape_of(8, rows, dtype=f32),
+        ],
+        compiler_params=pltpu.CompilerParams(vmem_limit_bytes=VMEM),
+        cost_estimate=cost(2),
         name="finish_qkv",
-    )(place, *owns, *others, out_own, out_other)
+    )(place, *owns, *others)
 
 
 def plus(left, right):
     return (left.astype(f32) + right.astype(f32)).astype(bf16)
 
 
-def cut_again(keep, came, x, h):
-    first, second = plus(keep[0], came[0]), plus(keep[1], came[1])
-    first = first.reshape(second.shape)
-    keep = pick(first, h, 1), pick(second, x, 1)
-    send = pick(first, 1 - h, 1), pick(second, 1 - x, 1)
-    return keep, send
-
-
-def along_z(keep, came, depth, z):
-    both = jnp.stack([plus(keep[0], came[0]), plus(keep[1], came[1])], 1)
-    return pick(both, z, 0), [pick(both, (z + k) % depth, 0) for k in range(1, depth)]
+def fold_one(place, keep, came):
+    depth, top, columns = keep[0].shape
+    low = top // 2
+
+    def kernel(place_ref, keep_one, keep_two, came_one, came_two, kept_ref, send_one, send_two):
+        at_x, at_h = place_ref[1] == 0, place_ref[2] == 0
+        one, two = plus(keep_one[0], came_one[0]), plus(keep_two[0], came_two[0])
+        kept_ref[0, 0] = jnp.where(at_h, one[:low], one[low:])
+        send_one[0] = jnp.where(at_h, one[low:], one[:low])
+        kept_ref[1, 0] = jnp.where(at_x, two[0], two[1])
+        send_two[0] = jnp.where(at_x, two[1], two[0])
+
+    one = pl.BlockSpec((1, top, columns), lambda i: (i, 0, 0))
+    two = pl.BlockSpec((1, 2, low, columns), lambda i: (i, 0, 0, 0))
+    send = pl.BlockSpec((1, low, columns), lambda i: (i, 0, 0))
+    kept, *sends = pl.pallas_call(
+        kernel,
+        grid=(depth,),
+        in_specs=[pl.BlockSpec(memory_space=pltpu.SMEM), one, two, one, two],
+        out_specs=[pl.BlockSpec((2, 1, low, columns), lambda i: (0, i, 0, 0)), send, send],
+        out_shape=[shape_of(2, depth, low, columns)] + [shape_of(depth, low, columns)] * 2,
+        compiler_params=pltpu.CompilerParams(vmem_limit_bytes=VMEM),
+        cost_estimate=cost(1),
+        name="fold_one",
+    )(place, *keep, *came)
+    return kept, sends
+
+
+def fold_two(place, kept, came):
+    _, depth, low, columns = kept.shape
+
+    def kernel(place_ref, kept_ref, came_one, came_two, *refs):
+        *outs, sums = refs
+        for half, came_ref in enumerate((came_one, came_two)):
+            for at in range(depth):
+                sums[at, half] = plus(kept_ref[half, at], came_ref[at])
+        for k, out in enumerate(outs):
+            out[...] = sums[lax.rem(place_ref[0] + k, depth)]
+
+    own, *sends = pl.pallas_call(
+        kernel,
+        in_specs=[pl.BlockSpec(memory_space=pltpu.SMEM)] + [pl.BlockSpec(memory_space=pltpu.VMEM)] * 3,
+        out_specs=[pl.BlockSpec(memory_space=pltpu.VMEM)] * depth,
+        out_shape=[shape_of(2, low, columns)] * depth,
+        scratch_shapes=[pltpu.VMEM((depth, 2, low, columns), bf16)],
+        compiler_params=pltpu.CompilerParams(vmem_limit_bytes=VMEM),
+        cost_estimate=cost(1),
+        name="fold_two",
+    )(place, kept, *came)
+    return own, sends
 
 
 def add_up(own, came):
@@ -383,7 +454,7 @@
     return pl.BlockSpec(shape, lambda i: (0,) * len(shape))
 
 
-def weight_call(name, step, tiles, place, inputs, sets, outs, scratch, copies):
+def weight_call(name, step, tiles, place, inputs, sets, outs, scratch, copies, micros):
     pieces = [piece for held in sets for piece in held]
 
     def kernel(place_ref, *refs):
@@ -404,18 +475,22 @@
         grid=(tiles,),
         in_specs=[pl.BlockSpec(memory_space=pltpu.SMEM)]
         + [spec for _, spec in inputs]
-        + [pl.BlockSpec(memory_space=pl.ANY)] * len(pieces),
+        + [pl.BlockSpec(memory_space=pltpu.HBM)] * len(pieces),
         out_specs=[spec for _, spec in outs],
         out_shape=[shape for shape, _ in outs],
         scratch_shapes=list(scratch) + [pltpu.SemaphoreType.DMA((copies,))],
-        compiler_params=pltpu.CompilerParams(vmem_limit_bytes=56 * 1024 * 1024),
-        cost_estimate=TINY,
+        compiler_params=pltpu.CompilerParams(vmem_limit_bytes=VMEM),
+        cost_estimate=cost(micros),
         name=name,
-    )(place, *[v for v, _ in inputs], *pieces)
+    )(place, *[v for v, _ in inputs], *[far(piece) for piece in pieces])
 
 
 def shape_of(*shape, dtype=bf16):
     return jax.ShapeDtypeStruct(shape, dtype)
+
+
+def far_shape(*shape, dtype=bf16):
+    return pltpu.HBM(shape, dtype)
 
 
 def unit_of(values):
@@ -432,17 +507,9 @@
 
 
 def bell_and_slope(values):
-    size = jnp.abs(values)
-    base = 1.0 + (0.3275911 * math.sqrt(0.5)) * size
-    t = pl.reciprocal(base, approx=True)
-    t = t * (2.0 - base * t)
-    bell = jnp.exp(values * values * -0.5)
-    series = 0.5 * 1.061405429
-    for term in (-1.453152027, 1.421413741, -0.284496736, 0.254829592):
-        series = series * t + 0.5 * term
-    tail = series * t * bell
-    phi = jnp.where(values < 0, tail, 1.0 - tail)
-    return values * phi, phi + values * bell * (1.0 / math.sqrt(2.0 * math.pi))
+    phi = 0.5 + 0.5 * lax.erf(values * math.sqrt(0.5))
+    density = jnp.exp(values * values * -0.5) * (1.0 / math.sqrt(2.0 * math.pi))
+    return values * phi, phi + values * density
 
 
 def outer_whole(left, right):
@@ -458,27 +525,31 @@
         in_specs=[pl.BlockSpec((rows, block), lambda i: (0, i)), whole_block(*right.shape)],
         out_specs=row_block(block, right.shape[1]),
         out_shape=shape_of(across, right.shape[1]),
-        compiler_params=pltpu.CompilerParams(vmem_limit_bytes=56 * 1024 * 1024),
-        cost_estimate=TINY,
+        compiler_params=pltpu.CompilerParams(vmem_limit_bytes=VMEM),
+        cost_estimate=cost(7),
         name="outer_whole",
     )(left, right)
 
 
-def outer(place, depth, left, right, out_pair=None, sums=None):
+def outer(place, depth, left, right, out_pair=None, weight=None, scales=None, piece=0, sums=None):
     rows, own_rows = left.shape[0], left.shape[1] // (2 * depth)
     top, low = own_rows // 2, own_rows // 4
     columns = right.shape[1]
     given = [left, right]
     specs = [pl.BlockSpec((rows, 2 * own_rows), lambda i: (0, i)), whole_block(*right.shape)]
+    total = columns
+    if weight is not None:
+        given += [weight, scales, sums]
+        specs += [pl.BlockSpec((2 * own_rows, part.shape[1]), lambda i: (i, 0)) for part in (weight, scales)]
+        specs.append(pl.BlockSpec((8, 2 * own_rows), lambda i: (0, i)))
+        total += LANES
+        third, width = columns // 3, weight.shape[1] // 3
     if out_pair is not None:
         out_block = out_pair[0].shape[1] // depth
         given += out_pair
         specs += [pl.BlockSpec((rows, out_block), lambda i: (0, i)), whole_block(*out_pair[1].shape)]
         half = out_pair[1].shape[1] // 2
-    if sums is not None:
-        given += sums
-        specs += [pl.BlockSpec((8, 2 * own_rows), lambda i: (0, i))] * 2
-    total = columns + (half if out_pair is not None else 0) + (LANES if sums is not None else 0)
+        total += half
 
     def kernel(place_ref, *refs):
         ins, outs = list(refs[: len(given)]), refs[len(given) :]
@@ -494,17 +565,31 @@
             keep_second[0, :, :, where] = jnp.where(at_h, lower, upper)
             send_second[0, :, :, where] = jnp.where(at_h, upper, lower)
 
-        product = mm_rows(ins.pop(0)[...], ins.pop(0)[...])
+        left_ref, right_ref = ins.pop(0), ins.pop(0)
+        product = mm_rows(left_ref[...], right_ref[...])
         put(0, product.reshape(2, own_rows, columns))
         first = columns
+        if weight is not None:
+            weight_ref, scales_ref, sums_ref = ins.pop(0), ins.pop(0), ins.pop(0)
+            column_sums = jnp.sum(right_ref[...].astype(f32), axis=0, keepdims=True)
+            bias_sum = cross = 0.0
+            for j in range(3):
+                at, to = j * width + piece * third, slice(j * third, (j + 1) * third)
+                part = weight_ref[:, at : at + third].astype(f32)
+                bias_sum = bias_sum + jnp.sum(part * column_sums[:, to], axis=1, keepdims=True)
+                cross = cross + jnp.sum(part * product[:, to], axis=1, keepdims=True)
+            gain, bias = scales_ref[:, 0:1].astype(f32), scales_ref[:, 1:2].astype(f32)
+            gain_sum = (cross - bias * bias_sum) / gain
+            kept = jnp.concatenate(
+                [jnp.zeros((2, 2 * own_rows), f32), sums_ref[0:2, :], jnp.zeros((LANES - 4, 2 * own_rows), f32)], axis=0
+            ).T
+            lane = lax.broadcasted_iota(jnp.int32, kept.shape, 1)
+            kept = jnp.where(lane == 0, gain_sum, jnp.where(lane == 1, bias_sum, kept))
+            put(first, kept.reshape(2, own_rows, LANES))
+            first += LANES
         if out_pair is not None:
             product = mm_rows(ins.pop(0)[...], ins.pop(0)[...]).reshape(2, top, 2 * half)
             put(first, jnp.concatenate([product[:, :, :half], product[:, :, half:]], axis=1))
-            first += half
-        if sums is not None:
-            stacked = jnp.concatenate([ref[0:2, :] for ref in ins], axis=0)
-            stacked = jnp.concatenate([stacked, jnp.zeros((LANES - 4, 2 * own_rows), f32)], axis=0)
-            put(first, stacked.T.reshape(2, own_rows, LANES))
 
     def spec(*block):
         return pl.BlockSpec((1, *block), lambda i: (i,) + (0,) * len(block))
@@ -516,8 +601,8 @@
         in_specs=[pl.BlockSpec(memory_space=pltpu.SMEM)] + specs,
         out_specs=[spec(*first_shape)] * 2 + [spec(*second_shape)] * 2,
         out_shape=[shape_of(depth, *first_shape)] * 2 + [shape_of(depth, *second_shape)] * 2,
-        compiler_params=pltpu.CompilerParams(vmem_limit_bytes=56 * 1024 * 1024),
-        cost_estimate=TINY,
+        compiler_params=pltpu.CompilerParams(vmem_limit_bytes=VMEM),
+        cost_estimate=cost(6),
         name="outer",
     )(place, *given)
     return (made[0], made[2]), (made[1], made[3])
@@ -596,37 +681,38 @@
         first_half, up_half = half[:, : scale_at + LANES], half[:, scale_at + LANES :]
         out_weight = lax.all_gather(out_part, shard_axes, axis=0, tiled=True)
     up_at = first_half.shape[1]
-    down_part = pick(w_down.reshape(group, -1, model), lo, 0)
+    down_rows = inner // shards
+    fine_down = down_rows % 64 == 0
+    down_part = pick(w_down.reshape(group, 2, down_rows // 2, model), lo, 0)
     first_far = [along(first_half, "fz", depth, k) for k in rest]
     side_own = swap(both_own, "fx")
     first_far, side_own, came, up_half = sync(first_far, side_own, came, up_half)
 
-    def last_quarters(side, near):
-        quarter = side.shape[1] // 2
-        return swap(side[:, :quarter], "hi"), swap(near[:, quarter:], "fx")
+    def last_quarters(side_part, near_part):
+        return swap(side_part, "hi"), swap(near_part, "fx")
 
     first_far = jnp.stack(first_far)
     first_side, first_near = swap(first_far, "fx"), swap(first_far, "hi")
+    up_far = [along(up_half, "fz", depth, k) for k in rest]
+    first_side, first_near, up_far, came, down_part = sync(first_side, first_near, up_far, came, down_part)
+
+    cuts, came, tokens, up_far = sync(halve(first_side, first_near), came, tokens, up_far)
+    first_last = last_quarters(*cuts)
+    down_half = pick(down_part, h, 0)
+    if not fine_down:
+        downward = lax.all_gather(down_part.reshape(down_rows, model), shard_axes, axis=0, tiled=True)
     inputs = whole_group(ordered(pick(tokens[:, 0], h, 0), came[0], h, 0), 1).reshape(rows, model)
-    odd = [along(up_half, "fz", depth, k) for k in rest if k % 2]
-    first_side, first_near, inputs, odd, up_half, came = sync(first_side, first_near, inputs, odd, up_half, came)
-
-    first_last = last_quarters(first_side, first_near)
-    even = [along(up_half, "fz", depth, k) for k in rest if k % 2 == 0]
-    grad_result = whole_group(ordered(pick(cotangent[:, 0], h, 0), came[1], h, 0), 1).reshape(rows, model)
-    first_last, even, odd, inputs, grad_result, down_part = sync(
-        first_last, even, odd, inputs, grad_result, down_part
-    )
-    downward = lax.all_gather(down_part, shard_axes, axis=0, tiled=True)
+    up_far = jnp.stack(up_far)
+    first_last, inputs, up_far, came, down_half, down_part = sync(
+        first_last, inputs, up_far, came, down_half, down_part
+    )
     first_set = [both_own, side_own, first_far, first_side, first_near, *first_last]
-    up_far = jnp.stack([odd[k // 2] if k % 2 else even[k // 2 - 1] for k in rest])
 
     segments = pick(segment_ids[:, 0], h, 0)
     seg_col, seg_row = segments[:, None], segments[None, :]
 
     def project(place_ref, given, held, made, scratch, sems):
-        (rows_ref,), (normed_ref, joint_ref, scales_ref, *outs) = given, made
-        weight, columns, *beside = scratch
+        (rows_ref,), (normed_ref, joint_ref, scales_ref, weight, columns, *outs) = given, made
 
         @pl.when(pl.program_id(0) == 0)
         def _():
@@ -635,7 +721,7 @@
                 (scale_at, LANES, below(columns, half_rows)),
             ]
             if fused_out:
-                targets.append((scale_at + LANES, half_model, below(beside[0], half_rows)))
+                targets.append((scale_at + LANES, half_model, below(scratch[0], half_rows)))
             for copy in load(depth, place_ref, held[0], sems, targets):
                 copy.wait()
             scales_ref[...] = columns[...].astype(f32).T[:8, :]
@@ -644,7 +730,7 @@
                     at = shard * own_rows + part * out_rows
                     outs[0][
                         shard * out_rows : (shard + 1) * out_rows, part * half_model : (part + 1) * half_model
-                    ] = beside[0][at : at + out_rows, :]
+                    ] = scratch[0][at : at + out_rows, :]
 
         unit_rows, _ = unit_of(rows_ref[...].astype(f32))
         normed = (unit_rows * scales_ref[0:1, :] + scales_ref[1:2, :]).astype(bf16)
@@ -655,11 +741,10 @@
                 part = part * (1.0 / math.sqrt(HEAD_DIM))
             joint_ref[:, at : at + head_columns] = part.astype(bf16)
 
-    out_shapes, out_scratch = [], []
+    wholes = [(8, model, f32), (model, 3 * head_columns, bf16), (model, LANES, bf16)]
     if fused_out:
-        out_shapes = [(shape_of(head_columns, model), whole_block(head_columns, model))]
-        out_scratch = [pltpu.VMEM((model, half_model), bf16)]
-    normed, joint, scales, *outs = weight_call(
+        wholes.append((head_columns, model, bf16))
+    normed, joint, scales, joint_weight, scale_columns, *outs = weight_call(
         "project",
         project,
         tiles,
@@ -667,13 +752,13 @@
         [(inputs, row_block(tile, model))],
         [first_set],
         [
-            (shape_of(rows, model), row_block(tile, model)),
-            (shape_of(rows, 3 * head_columns), row_block(tile, 3 * head_columns)),
-            (shape_of(8, model, dtype=f32), whole_block(8, model)),
+            (far_shape(rows, model), row_block(tile, model)),
+            (far_shape(rows, 3 * head_columns), row_block(tile, 3 * head_columns)),
         ]
-        + out_shapes,
-        [pltpu.VMEM((model, 3 * head_columns), bf16), pltpu.VMEM((model, LANES), bf16)] + out_scratch,
+        + [(shape_of(*shape, dtype=dtype), whole_block(*shape)) for *shape, dtype in wholes],
+        [pltpu.VMEM((model, half_model), bf16)] if fused_out else [],
         3 * copies,
+        8,
     )
     if fused_out:
         (out_weight,) = outs
@@ -683,12 +768,22 @@
     part_columns = count * LANES
     mixed = [attend(joint, seg_col, seg_row, 0, count)]
     up_side, up_near = swap(up_far, "fx"), swap(up_far, "hi")
-    mixed, joint, up_side, up_near, scales, out_weight = sync(mixed, joint, up_side, up_near, scales, out_weight)
-
-    up_last = last_quarters(up_side, up_near)
+    down_odd = down_even = down_side_own = None
+    if fine_down:
+        down_odd = [along(down_half, "fz", depth, k) for k in rest if k % 2]
+        down_side_own = swap(down_part, "fx")
+    mixed, joint, up_side, up_near, scales, out_weight, came, down_odd, down_side_own, down_half = sync(
+        mixed, joint, up_side, up_near, scales, out_weight, came, down_odd, down_side_own, down_half
+    )
+
+    cuts, joint, came, down_half = sync(halve(up_side, up_near), joint, came, down_half)
+    up_last = last_quarters(*cuts)
     for piece in range(1, pieces):
         mixed.append(attend(joint, seg_col, seg_row, piece * count, count))
-    mixed, up_last, out_weight = sync(mixed, up_last, out_weight)
+    grad_result = whole_group(ordered(pick(cotangent[:, 0], h, 0), came[1], h, 0), 1).reshape(rows, model)
+    if fine_down:
+        down_even = [along(down_half, "fz", depth, k) for k in rest if k % 2 == 0]
+    mixed, up_last, out_weight, grad_result, down_even = sync(mixed, up_last, out_weight, grad_result, down_even)
     up_set = [both_own, side_own, up_far, up_side, up_near, *up_last]
     lses = [lse for _, lse in mixed]
 
@@ -722,8 +817,14 @@
         ],
         [],
         1,
+        3,
     )
     branch_other = other_part(branch)
+
+    if fine_down:
+        down_far = jnp.stack([down_odd[k // 2] if k % 2 else down_even[k // 2 - 1] for k in rest])
+        down_side, down_near = swap(down_far, "fx"), swap(down_far, "hi")
+
     def widen(place_ref, given, held, made, scratch, sems):
         rows_ref, own_ref, other_ref, scales_ref = given
         middle_ref, normed_ref, hidden_ref, slope_ref = made
@@ -759,28 +860,43 @@
         ],
         [up_set],
         [
-            (shape_of(rows, model, dtype=f32), row_block(tile, model)),
-            (shape_of(rows, model), row_block(tile, model)),
-            (shape_of(rows, inner), row_block(tile, inner)),
-            (shape_of(rows, inner), row_block(tile, inner)),
+            (far_shape(rows, model, dtype=f32), row_block(tile, model)),
+            (far_shape(rows, model), row_block(tile, model)),
+            (far_shape(rows, inner), row_block(tile, inner)),
+            (far_shape(rows, inner), row_block(tile, inner)),
         ],
         [pltpu.VMEM((model, inner), bf16)],
         copies,
-    )
-
-    grad_down = outer_whole(hidden, grad_result)
-    hidden, slope, grad_down, normed_two = sync(hidden, slope, grad_down, normed_two)
-    down_own = lax.psum_scatter(grad_down, shard_axes, scatter_dimension=0, tiled=True)
+        13,
+    )
+
+    if fine_down:
+        hidden, slope, normed_two, down_side, down_near = sync(hidden, slope, normed_two, down_side, down_near)
+        cuts, hidden = sync(halve(down_side, down_near), hidden)
+        down_last = last_quarters(*cuts)
+        down_keep, down_send = outer(place, depth, hidden, grad_result)
+        hidden, slope, down_keep, down_send, normed_two, down_last = sync(
+            hidden, slope, down_keep, down_send, normed_two, down_last
+        )
+        down_set = [down_part, down_side_own, down_far, down_side, down_near, *down_last]
+        down_came = swap(down_send[0], "fx"), swap(down_send[1], "hi")
+    else:
+        down_keep = down_came = outer_whole(hidden, grad_result)
 
     def narrow(place_ref, given, held, made, scratch, sems):
-        hidden_ref, grad_ref, slope_ref, down_ref = given
+        hidden_ref, grad_ref, slope_ref, *downs = given
         out_ref, pre_ref, back_ref = made
-        (upward,) = scratch
+        upward = scratch[0]
+        down_ref = scratch[1] if fine_down else downs[0]
 
         @pl.when(pl.program_id(0) == 0)
         def _():
+            started = []
+            if fine_down:
+                targets = [(0, model, below(down_ref, down_rows // 2))]
+                started = load(depth, place_ref, held[1], sems, targets, sem=copies)
             targets = [(0, inner, below(upward, half_rows))]
-            for copy in load(depth, place_ref, held[0], sems, targets, up_at):
+            for copy in started + load(depth, place_ref, held[0], sems, targets, up_at):
                 copy.wait()
 
         for at in range(0, inner, wide):
@@ -795,26 +911,39 @@
         tiles,
         place,
         [
-            (hidden, row_block(tile, inner)),
-            (grad_result, row_block(tile, model)),
-            (slope, row_block(tile, inner)),
-            (downward, whole_block(inner, model)),
+            (far(hidden), row_block(tile, inner)),
+            (far(grad_result), row_block(tile, model)),
+            (far(slope), row_block(tile, inner)),
+        ]
+        + ([] if fine_down else [(far(downward), whole_block(inner, model))]),
+        [up_set, down_set] if fine_down else [up_set],
+        [
+            (far_shape(rows, model), row_block(tile, model)),
+            (far_shape(rows, inner), row_block(tile, inner)),
+            (far_shape(rows, model), row_block(tile, model)),
         ],
-        [up_set],
-        [
-            (shape_of(rows, model), row_block(tile, model)),
-            (shape_of(rows, inner), row_block(tile, inner)),
-            (shape_of(rows, model), row_block(tile, model)),
-        ],
-        [pltpu.VMEM((model, inner), bf16)],
-        copies,
-    )
-    result, grad_pre, back, normed_two = sync(result, grad_pre, back, normed_two)
+        [pltpu.VMEM((model, inner), bf16), pltpu.VMEM((inner, model), bf16)],
+        2 * copies,
+        18,
+    )
+    result, grad_pre, back, normed_two, down_keep, down_came = sync(
+        result, grad_pre, back, normed_two, down_keep, down_came
+    )
 
     back_other = other_part(back)
     result_other = other_own(result)
-    up_keep, up_send = outer(place, depth, normed_two, grad_pre)
-    back, back_other, up_keep, up_send, result_other = sync(back, back_other, up_keep, up_send, result_other)
+    if fine_down:
+        down_kept, down_send = fold_one(place, down_keep, down_came)
+        down_kept, down_send, normed_two, grad_pre = sync(down_kept, down_send, normed_two, grad_pre)
+        down_came = swap(down_send[0], "hi"), swap(down_send[1], "fx")
+    up_keep, up_send = outer(place, depth, far(normed_two), far(grad_pre))
+    back, back_other, up_keep, up_send, result_other, down_came = sync(
+        back, back_other, up_keep, up_send, result_other, down_came
+    )
+    if fine_down:
+        down_sum, down_send = fold_two(place, down_kept, down_came)
+        down_send, back, back_other, up_send = sync(down_send, back, back_other, up_send)
+        down_came = [along(value, "fz", depth, k) for k, value in zip(rest, down_send)]
 
     def between(place_ref, given, held, made, scratch, sems):
         grad_ref, own_ref, other_ref, middle_ref, scales_ref, weight = given
@@ -844,69 +973,77 @@
             (grad_result, row_block(tile, model)),
             (back, row_block(tile, model)),
             (back_other, row_block(tile, model)),
-            (middle, row_block(tile, model)),
+            (far(middle), row_block(tile, model)),
             (scales, whole_block(8, model)),
             (out_weight, whole_block(*out_weight.shape)),
         ],
         [],
         [
-            (shape_of(rows, model, dtype=f32), row_block(tile, model)),
-            (shape_of(rows, model), row_block(tile, model)),
+            (far_shape(rows, model, dtype=f32), row_block(tile, model)),
+            (far_shape(rows, model), row_block(tile, model)),
             (shape_of(rows, head_columns), row_block(tile, head_columns)),
             (shape_of(8, model, dtype=f32), whole_block(8, model)),
         ],
         [],
         1,
+        8,
     )
     grad_joints = [attend_back(joint, grad_attended, lses[0], seg_col, seg_row, 0, count)]
     up_came = swap(up_send[0], "fx"), swap(up_send[1], "hi")
-    grad_joints, grad_attended, grad_branch, up_came = sync(grad_joints, grad_attended, grad_branch, up_came)
-
-    up_keep, up_send = cut_again(up_keep, up_came, x, h)
+    output = (own_chunks(middle) + own_chunks(result).astype(f32) + result_other.astype(f32)).astype(bf16)
+    grad_joints, grad_attended, grad_branch, up_came, output, down_came = sync(
+        grad_joints, grad_attended, grad_branch, up_came, output, down_came
+    )
+
+    def both_halves(value):
+        return ordered(value, swap(value, "hi"), h, 1).reshape(-1, value.shape[2])
+
+    norm_parts = dict(weight=joint_weight, scales=scale_columns)
+    up_kept, up_send = fold_one(place, up_keep, up_came)
+    up_kept, up_send, grad_joints, output = sync(up_kept, up_send, grad_joints, output)
     up_came = swap(up_send[0], "hi"), swap(up_send[1], "fx")
+    if fine_down:
+        down_own = both_halves(add_up(down_sum, down_came))
+    else:
+        down_own = lax.psum(lax.psum_scatter(down_came, shard_axes, scatter_dimension=0, tiled=True), "hi")
     one_keep, one_send = outer(
-        place, depth, normed, grad_joints[0], out_pair=[attended, grad_branch] if fused_out else None
-    )
-    output = (own_chunks(middle) + own_chunks(result).astype(f32) + result_other.astype(f32)).astype(bf16)
-    up_came, one_keep, one_send, grad_attended, output = sync(up_came, one_keep, one_send, grad_attended, output)
-
-    up_own_sum, up_send = along_z(up_keep, up_came, depth, z)
-    up_send = dict(zip(rest, up_send))
+        place,
+        depth,
+        normed,
+        grad_joints[0],
+        out_pair=[attended, grad_branch] if fused_out else None,
+        sums=sums_two,
+        **norm_parts,
+    )
+    up_came, one_keep, one_send, grad_attended, output, down_own = sync(
+        up_came, one_keep, one_send, grad_attended, output, down_own
+    )
+
+    up_sum, up_send = fold_two(place, up_kept, up_came)
+    up_sum, up_send, grad_attended, one_send = sync(up_sum, up_send, grad_attended, one_send)
     for piece in range(1, pieces):
         grad_joints.append(
             attend_back(joint, grad_attended, lses[piece], seg_col, seg_row, piece * count, count)
         )
     one_came = swap(one_send[0], "fx"), swap(one_send[1], "hi")
-    odd = [along(up_send[k], "fz", depth, k) for k in rest if k % 2]
-    output_came = swap(pick(output, 1 - h, 0), "hi")
-    grad_joints, odd, up_send, one_keep, one_came, output_came = sync(
-        grad_joints, odd, up_send, one_keep, one_came, output_came
-    )
-
+    up_came = [along(value, "fz", depth, k) for k, value in zip(rest, up_send)]
+    grad_joints, up_came, one_keep, one_came, up_sum, down_own, output = sync(
+        grad_joints, up_came, one_keep, one_came, up_sum, down_own, output
+    )
+
+    one_kept, one_send = fold_one(place, one_keep, one_came)
+    two_came = None
     if pieces == 2:
-        two_keep, two_send = outer(place, depth, normed, grad_joints[1])
-        two_keep, two_send, grad_joints, one_keep, one_came, up_send = sync(
-            two_keep, two_send, grad_joints, one_keep, one_came, up_send
+        two_keep, two_send = outer(
+            place, depth, normed, grad_joints[1], piece=1, sums=jnp.zeros_like(sums_two), **norm_parts
         )
+        two_send, grad_joints, one_send = sync(two_send, grad_joints, one_send)
         two_came = swap(two_send[0], "fx"), swap(two_send[1], "hi")
-    else:
-        two_keep, two_came = one_keep, one_came
-    one_keep, one_send = cut_again(one_keep, one_came, x, h)
     one_came = swap(one_send[0], "hi"), swap(one_send[1], "fx")
-    even = [along(up_send[k], "fz", depth, k) for k in rest if k % 2 == 0]
 
     def enter(place_ref, given, held, made, scratch, sems):
-        *parts_refs, inputs_ref = given
-        (out_ref, sums_ref), (weight,) = made, scratch
-
-        @pl.when(pl.program_id(0) == 0)
-        def _():
-            sums_ref[...] = jnp.zeros_like(sums_ref)
-            targets = [(0, 3 * head_columns, below(weight, half_rows))]
-            for copy in load(depth, place_ref, held[0], sems, targets):
-                copy.wait()
-
-        unit_rows, _ = unit_of(inputs_ref[...].astype(f32))
+        *parts_refs, weight = given
+        (out_ref,) = made
         grads = jnp.zeros(out_ref.shape, f32)
         for piece, part_ref in enumerate(parts_refs):
             for j in range(3):
@@ -915,81 +1052,65 @@
                     part_ref[:, j * part_columns : (j + 1) * part_columns], weight[:, at : at + part_columns]
                 )
         out_ref[...] = grads.astype(bf16)
-        sums_ref[0:1, :] += jnp.sum(grads * unit_rows, axis=0, keepdims=True)
-        sums_ref[1:2, :] += jnp.sum(grads, axis=0, keepdims=True)
-
-    entered, sums_one = weight_call(
+
+    (entered,) = weight_call(
         "enter",
         enter,
         tiles,
         place,
-        [(value, row_block(tile, 3 * part_columns)) for value in grad_joints] + [(inputs, row_block(tile, model))],
-        [first_set],
-        [
-            (shape_of(rows, model), row_block(tile, model)),
-            (shape_of(8, model, dtype=f32), whole_block(8, model)),
-        ],
-        [pltpu.VMEM((model, 3 * head_columns), bf16)],
-        copies,
-    )
-    sums = jnp.concatenate([sums_one[:2], sums_two[:2]]).reshape(4, depth, 2, own_rows)
-    two_came, one_came, even, entered, sums, down_own = sync(two_came, one_came, even, entered, sums, down_own)
-
-    def both_halves(value):
-        return ordered(value, swap(value, "hi"), h, 1).reshape(own_rows, -1)
-
-    two_keep, two_send = cut_again(two_keep, two_came, x, h)
-    two_came = swap(two_send[0], "hi"), swap(two_send[1], "fx")
-    one_own_sum, one_send = along_z(one_keep, one_came, depth, z)
+        [(value, row_block(tile, 3 * part_columns)) for value in grad_joints]
+        + [(joint_weight, whole_block(*joint_weight.shape))],
+        [],
+        [(shape_of(rows, model), row_block(tile, model))],
+        [],
+        1,
+        14,
+    )
+    two_came, one_came, entered, output, up_sum, up_came, down_own = sync(
+        two_came, one_came, entered, output, up_sum, up_came, down_own
+    )
+
+    if pieces == 2:
+        two_kept, two_send = fold_one(place, two_keep, two_came)
+        two_came = swap(two_send[0], "hi"), swap(two_send[1], "fx")
+    one_sum, one_send = fold_two(place, one_kept, one_came)
     one_came = [along(value, "fz", depth, k) for k, value in zip(rest, one_send)]
+    output_came = swap(pick(output, 1 - h, 0), "hi")
     entered_other = other_own(entered)
-    down_own = plus(down_own, swap(down_own, "hi"))
-    sums = pick(sums, x, 2) + swap(pick(sums, 1 - x, 2), "fx")
-    two_came, one_came, entered_other, sums, odd, even, down_own = sync(
-        two_came, one_came, entered_other, sums, odd, even, down_own
-    )
-
-    two_own_sum, two_send = along_z(two_keep, two_came, depth, z)
-    two_came = [along(value, "fz", depth, k) for k, value in zip(rest, two_send)]
-    up_own = both_halves(add_up(up_own_sum, odd + even))
     grad_normed = own_chunks(entered).astype(f32) + entered_other.astype(f32)
     unit_own, inverse_own = unit_of(own_chunks(inputs).astype(f32))
     grad_tokens = own_chunks(grad_middle) + unit_back(grad_normed * scales[0], unit_own, inverse_own)
+    two_came, one_came, output_came, grad_tokens, up_sum, up_came, down_own = sync(
+        two_came, one_came, output_came, grad_tokens, up_sum, up_came, down_own
+    )
+
+    if pieces == 2:
+        two_sum, two_send = fold_two(place, two_kept, two_came)
+        two_came = [along(value, "fz", depth, k) for k, value in zip(rest, two_send)]
+    up_own = both_halves(add_up(up_sum, up_came))
     grad_came = swap(pick(grad_tokens, 1 - h, 0).astype(bf16), "hi")
-    sums = sums + swap(sums, "hi")
-    two_came, up_own, grad_tokens, grad_came, sums, one_came, down_own = sync(
-        two_came, up_own, grad_tokens, grad_came, sums, one_came, down_own
-    )
-
-    one_own = both_halves(add_up(one_own_sum, one_came))
-    two_own = both_halves(add_up(two_own_sum, two_came))
-    sums_came = [along(pick(sums, (z + k) % depth, 1), "fz", depth, k) for k in rest]
-    sums = pick(sums, z, 1)
-    for piece in sums_came:
-        sums = sums + piece
+    down_all = whole_group(down_own, 0).reshape(-1, model).astype(f32)
+    two_came, grad_tokens, grad_came, one_came, up_own = sync(two_came, grad_tokens, grad_came, one_came, up_own)
+
+    owns = [both_halves(add_up(one_sum, one_came))]
+    if pieces == 2:
+        owns.append(both_halves(add_up(two_sum, two_came)))
     output = ordered(pick(output, h, 0), output_came, h, 0)[:, None]
     grad_tokens = ordered(pick(grad_tokens, h, 0), grad_came.astype(f32), h, 0)[:, None]
-
-    down_all = whole_group(down_own, 0).reshape(-1, model).astype(f32)
-    sums = jnp.sum(whole_group(sums, 0), axis=0)
     if fused_out:
         up_all = finish_up(place, shards, up_own, swap(up_own, "lo"))
-        owns = [value[:, : 3 * part_columns] for value in ((one_own, two_own) if pieces == 2 else (one_own,))]
-        one_other = swap(one_own, "lo")
-        others = [one_other[:, : 3 * part_columns]]
-        if pieces == 2:
-            others.append(swap(two_own, "lo"))
-        out_own, out_other = one_own[:, 3 * part_columns :], one_other[:, 3 * part_columns :]
-        qkv_all, out_all = finish_qkv(place, owns, others, out_own, out_other)
+        qkv_all, out_all, sums = finish_qkv(place, owns, [swap(own, "lo") for own in owns])
     else:
         up_all = whole_group(up_own.reshape(own_rows, shards, -1), 2).reshape(own_rows, -1).astype(f32)
-        qkv_owns = [one_own] + ([two_own] if pieces == 2 else [])
-        qkv_own = jnp.concatenate([value.reshape(own_rows, 3, part_columns) for value in qkv_owns], axis=2)
+        columns = 3 * part_columns
+        qkv_own = jnp.concatenate([own[:, :columns].reshape(own_rows, 3, part_columns) for own in owns], axis=2)
         if split_out:
             qkv_all = whole_group(qkv_own.reshape(own_rows, 3, shards, -1), 3)
         else:
             qkv_all = whole_group(qkv_own, 2)
         qkv_all = qkv_all.reshape(own_rows, -1).astype(f32)
+        sums = sum(own[:, columns : columns + 4].astype(f32) for own in owns)
+        sums = jnp.sum(whole_group(sums, 0), axis=0).T
         grad_out = outer_whole(attended, grad_branch)
         if not split_out:
             empty = jnp.zeros((model, model), bf16)

time: 394 us -> 375 us (0.952)
  waiting for transfers between devices: 92.1 us -> 119 us
  other arithmetic: 34.2 us -> 14.1 us
  between operations: 15.4 us -> 1.99 us
  local copies, waits for them, and re-layouts: 29.2 us -> 18.3 us
  Pallas kernels: 159 us -> 149 us
  starting transfers between devices: 56.9 us -> 66.1 us
    ppermute x18 -> x21, waiting for transfers between devices: 48.7 us -> 67 us  [along(): lax.ppermute(value, axis, [(i, (i + step) % depth) for i in range(depth)])]
    pallas_call x6, Pallas kernels: 75.1 us -> 60.4 us  [weight_call(): pl.pallas_call(kernel, grid=(tiles,), in_specs=[pl.BlockSpec(memory_space...]
    ppermute x41 -> x47, waiting for transfers between devices: 43.4 us -> 52.4 us  [swap(): return lax.ppermute(value, axis, SWAP)]
    convert_element_type x7 -> x0, other arithmetic: 6.43 us -> none  [plus(): return (left.astype(f32) + right.astype(f32)).astype(bf16)]
    ppermute x41 -> x47, starting transfers between devices: 38.8 us -> 43.6 us  [swap(): return lax.ppermute(value, axis, SWAP)]
    another operation x16 -> x18, other arithmetic: 8.05 us -> 3.21 us  [ordered(): return jnp.stack([first, second], axis)]
    slice x10 -> x0, local copies, waits for them, and re-layouts: 4.69 us -> none  [the longest x4 3.12 us: last_quarters(): return (swap(side[:, :quarter], 'hi'), swap(near[:, quarter:], 'fx'))]
    ppermute x18 -> x21, starting transfers between devices: 17.8 us -> 22.4 us  [along(): lax.ppermute(value, axis, [(i, (i + step) % depth) for i in range(depth)])]
  transfers between devices with their start and end apart: 61 -> 68, of which waited for: 18 -> 27; matrix products, arithmetic and copies ran while one was open for 12% -> 5% of each run, Pallas kernels for 35% -> 36%
where the time goes in v4:
time: 375 us; the launch traced here: 369 us
  Pallas kernels  149 us (40%)
  waiting for transfers between devices  119 us (32%)
  starting transfers between devices  66.1 us (18%)
  local copies, waits for them, and re-layouts  18.3 us (5%)
  other arithmetic  14.1 us (4%)
    ppermute x21, waiting for transfers between devices, along(): lax.ppermute(value, axis, [(i, (i + step) % depth) for i in range(depth)])  67 us
    pallas_call x6, Pallas kernels, weight_call(): pl.pallas_call(kernel, grid=(tiles,), in_specs=[pl.BlockSpec(memory_space...  60.4 us
    ppermute x47, waiting for transfers between devices, swap(): return lax.ppermute(value, axis, SWAP)  52.4 us
    ppermute x47, starting transfers between devices, swap(): return lax.ppermute(value, axis, SWAP)  43.6 us
    pallas_call x2, Pallas kernels, attend_back(): pl.pallas_call(functools.partial(attend_back_kernel, spans, tile), grid=(...  27.8 us
    pallas_call x4, Pallas kernels, outer(): pl.pallas_call(kernel, grid=(depth,), in_specs=[pl.BlockSpec(memory_space...  25.1 us
    ppermute x21, starting transfers between devices, along(): lax.ppermute(value, axis, [(i, (i + step) % depth) for i in range(depth)])  22.4 us
    pallas_call x2, Pallas kernels, attend(): pl.pallas_call(functools.partial(attend_kernel, spans, tile), grid=(count...  19.4 us
  transfers between devices with their start and end apart: 68, of which 27 were waited for; matrix products, arithmetic and copies ran while one was open for 5% of the time, Pallas kernels for 36%

profile of v4, /device:TPU:9, one launch (start us, length us, event | category | flops | bytes accessed | tf_op | source)
XLA Modules:
  0.0 368.7 jit_solution(8119799059804589934)
XLA Ops:
  1.5 2.0 prepare.1
  3.5 1.3 collective-permute-start.3
  6.2 1.3 collective-permute-start.4
  7.5 1.3 collective-permute-start
  9.8 1.5 collective-permute-start.2
  11.3 3.2 collective-permute-done
  14.5 16.9 %collective-permute-done.1 = bf16[64,2176]{1,0:T(8,128)(2,1)S(1)} collective-permute-done((bf16[64,2176]{1,0:T(8,128)(2,1)S(1)}, bf16[64,2176]{1,0:T(8,128)(2,1)S(1)}, u32[]{:S(2)}, u32[]{:S(2)}) %collective-permute-start.1) | collective-permute-done | bytes 278560 | tf_op jit(solution)/shard_map/ppermute | solution.py:214
  31.4 3.5 collective-permute-done.2
  37.4 1.5 collective-permute-start.9
  39.7 4.4 %collective-permute-done.7 = bf16[64,2048]{1,0:T(8,128)(2,1)S(1)} collective-permute-done((bf16[64,2048]{1,0:T(8,128)(2,1)S(1)}, bf16[64,2048]{1,0:T(8,128)(2,1)S(1)}, u32[]{:S(2)}, u32[]{:S(2)}) %collective-permute-start.7) | collective-permute-done | bytes 262176 | tf_op jit(solution)/shard_map/ppermute | solution.py:214
  44.1 15.0 %collective-permute-done.8 = bf16[64,2048]{1,0:T(8,128)(2,1)} collective-permute-done((bf16[64,2048]{1,0:T(8,128)(2,1)S(1)}, bf16[64,2048]{1,0:T(8,128)(2,1)}, u32[]{:S(2)}, u32[]{:S(2)}) %collective-permute-start.8) | collective-permute-done | bytes 262176 | tf_op jit(solution)/shard_map/ppermute | solution.py:214
  59.1 1.7 collective-permute-done.9
  63.0 1.3 collective-permute-start.10
  67.6 1.6 select_bitcast_fusion.3
  69.6 4.8 %collective-permute-done.10.refs_6_ = bf16[3,32,2176]{2,1,0:T(8,128)(2,1)S(1)} collective-permute-done((bf16[3,32,2176]{2,1,0:T(8,128)(2,1)}, bf16[3,32,2176]{2,1,0:T(8,128)(2,1)S(1)}, u32[]{:S(2)}, u32[]{:S(2)}) %collective-permute-start.10) | collective-permute-done | bytes 417824 | tf_op jit(solution)/shard_map/ppermute | solution.py:56
  76.8 1.5 collective-permute-start.16
  78.6 10.2 %project.1 = (bf16[1024,1024]{1,0:T(8,128)(2,1)}, bf16[1024,1536]{1,0:T(8,128)(2,1)}, f32[8,1024]{1,0:T(8,128)S(1)}, bf16[1024,1536]{1,0:T(8,128)(2,1)S(1)}, bf1...) custom-call(s32[4]{0:T(128)S(1)} %pad_add_fusion.place_ref, bf16[1024,1024]{1,0:T(8,128)(2,1)S(1)} %bitcast.160, ...), custom_call_target="tpu_custom_call" | custom-call | flops 8800000000 | bytes 1000 | tf_op jit(solution)/shard_map/project/pallas_call | solution.py:473
  88.8 1.7 copy-done.22
  90.5 9.9 %attend.2 = (bf16[1024,256]{1,0:T(8,128)(2,1)S(1)}, f32[1024,256]{1,0:T(8,128)S(1)}) custom-call(bf16[1024,1536]{1,0:T(8,128)(2,1)} %get-tuple-element.315.q_ref.k_ref.v_ref, bf16[1024,1536]{1,0:T(8,128)(2,1)} %get-tuple-element.315.q_ref.k_ref.v_ref, bf16[1024,1536]{1,0:T(8,128)(2,1)} %get-tuple-element.315.q_ref.k_ref.v_ref, s32[1024,1]{1,0:T(8,128)S(1)} %copy.29.seg_col, ...), custom_call_target="tpu_custom_call" | custom-call | flops 8800000000 | bytes 1000 | tf_op jit(solution)/shard_map/attend/pallas_call | solution.py:117
  101.4 2.6 collective-permute-done.17.refs_11_
  105.4 2.3 collective-permute-start.20
  109.5 2.7 collective-permute-start.21
  112.2 9.5 %attend.3 = (bf16[1024,256]{1,0:T(8,128)(2,1)S(1)}, f32[1024,256]{1,0:T(8,128)S(1)}) custom-call(bf16[1024,1536]{1,0:T(8,128)(2,1)} %get-tuple-element.315.q_ref.k_ref.v_ref, bf16[1024,1536]{1,0:T(8,128)(2,1)} %get-tuple-element.315.q_ref.k_ref.v_ref, bf16[1024,1536]{1,0:T(8,128)(2,1)} %get-tuple-element.315.q_ref.k_ref.v_ref, s32[1024,1]{1,0:T(8,128)S(1)} %copy.29.seg_col, ...), custom_call_target="tpu_custom_call" | custom-call | flops 8800000000 | bytes 1000 | tf_op jit(solution)/shard_map/attend/pallas_call | solution.py:117
  122.9 2.4 leave.1
  127.7 2.4 collective-permute-done.22.refs_2_
  130.1 14.0 %widen.1 = (f32[1024,1024]{1,0:T(8,128)}, bf16[1024,1024]{1,0:T(8,128)(2,1)}, bf16[1024,2048]{1,0:T(8,128)(2,1)}, bf16[1024,2048]{1,0:T(8,128)(2,1)}) custom-call(s32[4]{0:T(128)S(1)} %pad_add_fusion.place_ref, bf16[1024,1024]{1,0:T(8,128)(2,1)S(1)} %bitcast.161, bf16[1024,1024]{1,0:T(8,128)(2,1)S(1)} %get-tuple-element.326.refs_1_, ...), custom_call_target="tpu_custom_call" | custom-call | flops 14300000256 | bytes 1000 | tf_op jit(solution)/shard_map/widen/pallas_call | solution.py:473
  144.1 1.5 collective-permute-done.23.side_ref.refs_13_
  147.8 2.2 copy-done.24
  150.0 6.1 %outer.4 = (bf16[4,128,1024]{2,1,0:T(8,128)(2,1)S(1)}, bf16[4,128,1024]{2,1,0:T(8,128)(2,1)S(1)}, bf16[4,2,64,1024]{3,2,1,0:T(8,128)(2,1)S(1)}, bf16[4,2,64,1024]{3,2,1,0:T(8,128)(2,1)S(1)}) custom-call(s32[4]{0:T(128)S(1)} %pad_add_fusion.place_ref, bf16[1024,2048]{1,0:T(8,128)(2,1)S(1)} %copy-done.24, bf16[1024,1024]{1,0:T(8,128)(2,1)S(1)} %bitcast.165), custom_call_target="tpu_custom_call" | custom-call | flops 6600000000 | bytes 1000 | tf_op jit(solution)/shard_map/outer/pallas_call | solution.py:598
  157.6 20.5 %narrow.1 = (bf16[1024,1024]{1,0:T(8,128)(2,1)}, bf16[1024,2048]{1,0:T(8,128)(2,1)}, bf16[1024,1024]{1,0:T(8,128)(2,1)}) custom-call(s32[4]{0:T(128)S(1)} %pad_add_fusion.place_ref, bf16[1024,2048]{1,0:T(8,128)(2,1)} %get-tuple-element.351.refs_0_, bf16[1024,1024]{1,0:T(8,128)(2,1)} %bitcast.166, bf16[1024,2048]{1,0:T(8,128)(2,1)} %get-tuple-element.352.refs_2_, ...), custom_call_target="tpu_custom_call" | custom-call | flops 19800000512 | bytes 1000 | tf_op jit(solution)/shard_map/narrow/pallas_call | solution.py:473
  181.0 2.9 collective-permute-start.29
  183.8 1.4 dynamic-slice_bitcast_fusion.1
  186.9 1.3 fold_one.4
  189.7 7.8 %outer.5 = (bf16[4,64,2048]{2,1,0:T(8,128)(2,1)S(1)}, bf16[4,64,2048]{2,1,0:T(8,128)(2,1)S(1)}, bf16[4,2,32,2048]{3,2,1,0:T(8,128)(2,1)S(1)}, bf16[4,2,32,2048]{3,2,1,0:T(8,128)(2,1)S(1)}) custom-call(s32[4]{0:T(128)S(1)} %pad_add_fusion.place_ref, bf16[1024,1024]{1,0:T(8,128)(2,1)} %get-tuple-element.374.refs_0_, bf16[1024,2048]{1,0:T(8,128)(2,1)} %get-tuple-element.375.refs_1_), custom_call_target="tpu_custom_call" | custom-call | flops 6600000000 | bytes 1000 | tf_op jit(solution)/shard_map/outer/pallas_call | solution.py:598
  197.4 4.2 %collective-permute-done.31.came_one = bf16[4,64,1024]{2,1,0:T(8,128)(2,1)S(1)} collective-permute-done((bf16[4,64,1024]{2,1,0:T(8,128)(2,1)S(1)}, bf16[4,64,1024]{2,1,0:T(8,128)(2,1)S(1)}, u32[]{:S(2)}, u32[]{:S(2)}) %collective-permute-start.31) | collective-permute-done | bytes 524320 | tf_op jit(solution)/shard_map/ppermute | solution.py:56
  204.6 3.8 %collective-permute-start.36 = (bf16[2,64,1024]{2,1,0:T(8,128)(2,1)S(1)}, bf16[2,64,1024]{2,1,0:T(8,128)(2,1)S(1)}, u32[]{:S(2)}, u32[]{:S(2)}) collective-permute-start(bf16[2,64,1024]{2,1,0:T(8,128)(2,1)S(1)} %get-tuple-element.405), channel_id=1, source_target_pairs={{0,4},{2,6},{4,0},{6,2},{1,5},{3,7},{5,1},{7,3},{8,12},{10,14},{12... | collective-permute-start | bytes 786440 | tf_op jit(solution)/shard_map/ppermute | solution.py:214
  208.5 8.6 %between.1 = (f32[1024,1024]{1,0:T(8,128)}, bf16[1024,1024]{1,0:T(8,128)(2,1)}, bf16[1024,512]{1,0:T(8,128)(2,1)S(1)}, f32[8,1024]{1,0:T(8,128)S(1)}) custom-call(s32[4]{0:T(128)S(1)} %pad_add_fusion.place_ref, bf16[1024,1024]{1,0:T(8,128)(2,1)S(1)} %bitcast.167, bf16[1024,1024]{1,0:T(8,128)(2,1)S(1)} %copy-done.14, ...), custom_call_target="tpu_custom_call" | custom-call | flops 8800000000 | bytes 1000 | tf_op jit(solution)/shard_map/between/pallas_call | solution.py:473
  217.2 13.9 %attend_back.2.refs_1_.refs_0_ = bf16[1024,768]{1,0:T(8,128)(2,1)S(1)} custom-call(bf16[1024,1536]{1,0:T(8,128)(2,1)} %get-tuple-element.315.q_ref.k_ref.v_ref, bf16[1024,1536]{1,0:T(8,128)(2,1)} %get-tuple-element.315.q_ref.k_ref.v_ref, bf16[1024,1536]{1,0:T(8,128)(2,1)} %get-tuple-element.315.q_ref.k_ref.v_ref, ...), custom_call_target="tpu_custom_call" | custom-call | flops 13200000000 | bytes 1000 | tf_op jit(solution)/shard_map/attend_back/pallas_call | solution.py:188
  233.1 1.3 fold_one.5
  235.6 6.0 %outer.6 = (bf16[4,64,1408]{2,1,0:T(8,128)(2,1)S(1)}, bf16[4,64,1408]{2,1,0:T(8,128)(2,1)S(1)}, bf16[4,2,32,1408]{3,2,1,0:T(8,128)(2,1)S(1)}, bf16[4,2,32,1408]{3,2,1,0:T(8,128)(2,1)S(1)}) custom-call(s32[4]{0:T(128)S(1)} %pad_add_fusion.place_ref, bf16[1024,1024]{1,0:T(8,128)(2,1)S(1)} %copy-done.25, bf16[1024,768]{1,0:T(8,128)(2,1)S(1)} %attend_back.2.refs_1_.refs_0_, ...), custom_call_target="tpu_custom_call" | custom-call | flops 6600000000 | bytes 1000 | tf_op jit(solution)/shard_map/outer/pallas_call | solution.py:598
  241.8 6.8 %collective-permute-done.38.came_one = bf16[4,32,2048]{2,1,0:T(8,128)(2,1)S(1)} collective-permute-done((bf16[4,32,2048]{2,1,0:T(8,128)(2,1)S(1)}, bf16[4,32,2048]{2,1,0:T(8,128)(2,1)S(1)}, u32[]{:S(2)}, u32[]{:S(2)}) %collective-permute-start.38) | collective-permute-done | bytes 524320 | tf_op jit(solution)/shard_map/ppermute | solution.py:56
  252.6 2.1 collective-permute-start.42
  254.7 13.9 %attend_back.3.refs_1_ = bf16[1024,768]{1,0:T(8,128)(2,1)S(1)} custom-call(bf16[1024,1536]{1,0:T(8,128)(2,1)} %get-tuple-element.315.q_ref.k_ref.v_ref, bf16[1024,1536]{1,0:T(8,128)(2,1)} %get-tuple-element.315.q_ref.k_ref.v_ref, bf16[1024,1536]{1,0:T(8,128)(2,1)} %get-tuple-element.315.q_ref.k_ref.v_ref, bf16[1024,512]{1,0:T(8,128)(2,1)S(1)} %get-tuple-element.442.g_ref, ...), custom_call_target="tpu_custom_call" | custom-call | flops 13200000000 | bytes 1000 | tf_op jit(solution)/shard_map/attend_back/pallas_call | solution.py:188
  268.7 3.8 %collective-permute-done.42 = bf16[2,32,2048]{2,1,0:T(8,128)(2,1)S(1)} collective-permute-done((bf16[2,32,2048]{2,1,0:T(8,128)(2,1)S(1)}, bf16[2,32,2048]{2,1,0:T(8,128)(2,1)S(1)}, u32[]{:S(2)}, u32[]{:S(2)}) %collective-permute-start.42) | collective-permute-done | bytes 262176 | tf_op jit(solution)/shard_map/ppermute | solution.py:214
  272.5 4.7 %collective-permute-done.43 = bf16[2,32,2048]{2,1,0:T(8,128)(2,1)S(1)} collective-permute-done((bf16[2,32,2048]{2,1,0:T(8,128)(2,1)S(1)}, bf16[2,32,2048]{2,1,0:T(8,128)(2,1)S(1)}, u32[]{:S(2)}, u32[]{:S(2)}) %collective-permute-start.43) | collective-permute-done | bytes 262176 | tf_op jit(solution)/shard_map/ppermute | solution.py:214
  277.3 5.2 %outer.7 = (bf16[4,64,896]{2,1,0:T(8,128)(2,1)S(1)}, bf16[4,64,896]{2,1,0:T(8,128)(2,1)S(1)}, bf16[4,2,32,896]{3,2,1,0:T(8,128)(2,1)S(1)}, bf16[4,2,32,896]{3,2,1,0:T(8,128)(2,1)S(1)}) custom-call(s32[4]{0:T(128)S(1)} %pad_add_fusion.place_ref, bf16[1024,1024]{1,0:T(8,128)(2,1)S(1)} %copy-done.25, bf16[1024,768]{1,0:T(8,128)(2,1)S(1)} %attend_back.3.refs_1_, ...), custom_call_target="tpu_custom_call" | custom-call | flops 6600000000 | bytes 1000 | tf_op jit(solution)/shard_map/outer/pallas_call | solution.py:598
  286.6 4.6 %enter.1 = bf16[1024,1024]{1,0:T(8,128)(2,1)S(1)} custom-call(s32[4]{0:T(128)S(1)} %pad_add_fusion.place_ref, bf16[1024,768]{1,0:T(8,128)(2,1)S(1)} %attend_back.2.refs_1_.refs_0_, bf16[1024,768]{1,0:T(8,128)(2,1)S(1)} %attend_back.3.refs_1_, bf16[1024,1536]{1,0:T(8,128)(2,1)S(1)} %copy-done.23), custom_call_target="tpu_custom_call" | custom-call | flops 15399999488 | bytes 1000 | tf_op jit(solution)/shard_map/enter/pallas_call | solution.py:473
  291.2 11.3 %collective-permute-done.48.came_one = bf16[4,32,1408]{2,1,0:T(8,128)(2,1)S(1)} collective-permute-done((bf16[4,32,1408]{2,1,0:T(8,128)(2,1)S(1)}, bf16[4,32,1408]{2,1,0:T(8,128)(2,1)S(1)}, u32[]{:S(2)}, u32[]{:S(2)}) %collective-permute-start.48) | collective-permute-done | bytes 360480 | tf_op jit(solution)/shard_map/ppermute | solution.py:56
  302.7 2.5 collective-permute-start.56
  306.7 1.4 collective-permute-start.54
  314.5 7.8 %collective-permute-done.53 = bf16[2,32,1408]{2,1,0:T(8,128)(2,1)S(1)} collective-permute-done((bf16[2,32,1408]{2,1,0:T(8,128)(2,1)S(1)}, bf16[2,32,1408]{2,1,0:T(8,128)(2,1)S(1)}, u32[]{:S(2)}, u32[]{:S(2)}) %collective-permute-start.53) | collective-permute-done | bytes 180256 | tf_op jit(solution)/shard_map/ppermute | solution.py:214
  322.4 4.5 %collective-permute-done.55 = bf16[256,1024]{1,0:T(8,128)(2,1)S(1)} collective-permute-done((bf16[256,1024]{1,0:T(8,128)(2,1)S(1)}, bf16[256,1024]{1,0:T(8,128)(2,1)S(1)}, u32[]{:S(2)}, u32[]{:S(2)}) %collective-permute-start.55) | collective-permute-done | bytes 524320 | tf_op jit(solution)/shard_map/ppermute | solution.py:56
  326.9 1.5 collective-permute-start.67
  330.8 3.1 collective-permute-start.58
  337.2 1.6 bitcast_convert_fusion
  338.9 2.4 collective-permute-done.58
  341.3 2.1 collective-permute-done.59
  343.4 5.7 %collective-permute-done.60 = bf16[256,1024]{1,0:T(8,128)(2,1)S(1)} collective-permute-done((bf16[256,1024]{1,0:T(8,128)(2,1)S(1)}, bf16[256,1024]{1,0:T(8,128)(2,1)S(1)}, u32[]{:S(2)}, u32[]{:S(2)}) %collective-permute-start.60) | collective-permute-done | bytes 524320 | tf_op jit(solution)/shard_map/ppermute | solution.py:56
  349.2 1.7 collective-permute-start.66
  352.9 2.9 collective-permute-done.63
  357.1 2.5 collective-permute-done.62
  360.6 1.5 maximum_bitcast_fusion
  362.9 2.8 finish_up.1
  365.7 2.2 finish_qkv.1
  (271 shorter events, 65.8 us)
Async XLA Ops:
  3.5 31.4 %collective-permute-start.3 = (bf16[2,64,4224]{2,1,0:T(8,128)(2,1)S(1)}, bf16[2,64,4224]{2,1,0:T(8,128)(2,1)}, u32[]{:S(2)}, u32[]{:S(2)}) collective-permute-start(bf16[2,64,4224]{2,1,0:T(8,128)(2,1)S(1)} %get-tuple-element.269.refs_1_.refs_4_.refs_3_), channel_id=1, source_target_pairs={{0,1},{1,0},{2,3},{3,2},{4,5},{5,4},{6,7},{7,6},{8,9},{9,8},{10,11... | collective-permute-start | bytes 3244040 | tf_op jit(solution)/shard_map/ppermute | solution.py:56
  6.2 28.7 %collective-permute-start.4 = (bf16[2,256,1024]{2,1,0:T(8,128)(2,1)S(1)}, bf16[2,256,1024]{2,1,0:T(8,128)(2,1)S(1)}, u32[]{:S(2)}, u32[]{:S(2)}) collective-permute-start(bf16[2,256,1024]{2,1,0:T(8,128)(2,1)S(1)} %pad_maximum_fusion.2), channel_id=1, source_target_pairs={{0,16},{16,0},{1,17},{17,1},{2,18},{18,2},{3,19},{19,3},{4,20},{20... | collective-permute-start | bytes 3145736 | tf_op jit(solution)/shard_map/ppermute | solution.py:56
  7.5 7.0 %collective-permute-start = (bf16[64,2176]{1,0:T(8,128)(2,1)S(1)}, bf16[64,2176]{1,0:T(8,128)(2,1)S(1)}, u32[]{:S(2)}, u32[]{:S(2)}) collective-permute-start(bf16[64,2176]{1,0:T(8,128)(2,1)S(1)} %get-tuple-element.268), channel_id=1, source_target_pairs={{0,2},{2,4},{4,6},{6,0},{1,3},{3,5},{5,7},{7,1},{8,10},{10,12},{12... | collective-permute-start | bytes 835592 | tf_op jit(solution)/shard_map/ppermute | solution.py:214
  8.8 22.6 %collective-permute-start.1 = (bf16[64,2176]{1,0:T(8,128)(2,1)S(1)}, bf16[64,2176]{1,0:T(8,128)(2,1)S(1)}, u32[]{:S(2)}, u32[]{:S(2)}) collective-permute-start(bf16[64,2176]{1,0:T(8,128)(2,1)S(1)} %get-tuple-element.268), channel_id=1, source_target_pairs={{0,4},{2,6},{4,0},{6,2},{1,5},{3,7},{5,1},{7,3},{8,12},{10,14},{12... | collective-permute-start | bytes 835592 | tf_op jit(solution)/shard_map/ppermute | solution.py:214
  9.8 25.1 %collective-permute-start.2 = (bf16[64,2176]{1,0:T(8,128)(2,1)S(1)}, bf16[64,2176]{1,0:T(8,128)(2,1)S(1)}, u32[]{:S(2)}, u32[]{:S(2)}) collective-permute-start(bf16[64,2176]{1,0:T(8,128)(2,1)S(1)} %get-tuple-element.268), channel_id=1, source_target_pairs={{0,6},{2,0},{4,2},{6,4},{1,7},{3,1},{5,3},{7,5},{8,14},{10,8},{12,... | collective-permute-start | bytes 835592 | tf_op jit(solution)/shard_map/ppermute | solution.py:214
  36.9 24.0 %collective-permute-start.5 = (bf16[3,64,2176]{2,1,0:T(8,128)(2,1)}, bf16[3,64,2176]{2,1,0:T(8,128)(2,1)S(1)}, u32[]{:S(2)}, u32[]{:S(2)}) collective-permute-start(bf16[3,64,2176]{2,1,0:T(8,128)(2,1)} %pad_maximum_fusion.6.refs_3_), channel_id=1, source_target_pairs={{0,1},{1,0},{2,3},{3,2},{4,5},{5,4},{6,7},{7,6},{8,9},{9,8},{10,11... | collective-permute-start | bytes 2506760 | tf_op jit(solution)/shard_map/ppermute | solution.py:56
  37.2 23.7 %collective-permute-start.6 = (bf16[3,64,2176]{2,1,0:T(8,128)(2,1)}, bf16[3,64,2176]{2,1,0:T(8,128)(2,1)S(1)}, u32[]{:S(2)}, u32[]{:S(2)}) collective-permute-start(bf16[3,64,2176]{2,1,0:T(8,128)(2,1)} %pad_maximum_fusion.6.refs_3_), channel_id=1, source_target_pairs={{0,16},{16,0},{1,17},{17,1},{2,18},{18,2},{3,19},{19,3},{4,20},{20... | collective-permute-start | bytes 2506760 | tf_op jit(solution)/shard_map/ppermute | solution.py:56
  37.4 6.7 %collective-permute-start.7 = (bf16[64,2048]{1,0:T(8,128)(2,1)S(1)}, bf16[64,2048]{1,0:T(8,128)(2,1)S(1)}, u32[]{:S(2)}, u32[]{:S(2)}) collective-permute-start(bf16[64,2048]{1,0:T(8,128)(2,1)S(1)} %get-tuple-element.274), channel_id=1, source_target_pairs={{0,2},{2,4},{4,6},{6,0},{1,3},{3,5},{5,7},{7,1},{8,10},{10,12},{12... | collective-permute-start | bytes 786440 | tf_op jit(solution)/shard_map/ppermute | solution.py:214
  37.4 21.7 %collective-permute-start.8 = (bf16[64,2048]{1,0:T(8,128)(2,1)S(1)}, bf16[64,2048]{1,0:T(8,128)(2,1)}, u32[]{:S(2)}, u32[]{:S(2)}) collective-permute-start(bf16[64,2048]{1,0:T(8,128)(2,1)S(1)} %get-tuple-element.274), channel_id=1, source_target_pairs={{0,4},{2,6},{4,0},{6,2},{1,5},{3,7},{5,1},{7,3},{8,12},{10,14},{12... | collective-permute-start | bytes 786440 | tf_op jit(solution)/shard_map/ppermute | solution.py:214
  37.4 23.4 %collective-permute-start.9 = (bf16[64,2048]{1,0:T(8,128)(2,1)S(1)}, bf16[64,2048]{1,0:T(8,128)(2,1)}, u32[]{:S(2)}, u32[]{:S(2)}) collective-permute-start(bf16[64,2048]{1,0:T(8,128)(2,1)S(1)} %get-tuple-element.274), channel_id=1, source_target_pairs={{0,6},{2,0},{4,2},{6,4},{1,7},{3,1},{5,3},{7,5},{8,14},{10,8},{12,... | collective-permute-start | bytes 786440 | tf_op jit(solution)/shard_map/ppermute | solution.py:214
  63.0 11.3 %collective-permute-start.10 = (bf16[3,32,2176]{2,1,0:T(8,128)(2,1)}, bf16[3,32,2176]{2,1,0:T(8,128)(2,1)S(1)}, u32[]{:S(2)}, u32[]{:S(2)}) collective-permute-start(bf16[3,32,2176]{2,1,0:T(8,128)(2,1)} %get-tuple-element.284), channel_id=1, source_target_pairs={{0,16},{16,0},{1,17},{17,1},{2,18},{18,2},{3,19},{19,3},{4,20},{20... | collective-permute-start | bytes 1253384 | tf_op jit(solution)/shard_map/ppermute | solution.py:56
  64.3 10.7 %collective-permute-start.11 = (bf16[3,32,2176]{2,1,0:T(8,128)(2,1)S(1)}, bf16[3,32,2176]{2,1,0:T(8,128)(2,1)S(1)}, u32[]{:S(2)}, u32[]{:S(2)}) collective-permute-start(bf16[3,32,2176]{2,1,0:T(8,128)(2,1)S(1)} %get-tuple-element.285), channel_id=1, source_target_pairs={{0,1},{1,0},{2,3},{3,2},{4,5},{5,4},{6,7},{7,6},{8,9},{9,8},{10,11... | collective-permute-start | bytes 1253384 | tf_op jit(solution)/shard_map/ppermute | solution.py:56
  75.1 29.0 %collective-permute-start.13 = (bf16[3,64,2048]{2,1,0:T(8,128)(2,1)S(1)}, bf16[3,64,2048]{2,1,0:T(8,128)(2,1)S(1)}, u32[]{:S(2)}, u32[]{:S(2)}) collective-permute-start(bf16[3,64,2048]{2,1,0:T(8,128)(2,1)S(1)} %pad_maximum_fusion.7.refs_6_.refs_5_), channel_id=1, source_target_pairs={{0,1},{1,0},{2,3},{3,2},{4,5},{5,4},{6,7},{7,6},{8,9},{9,8},{10,11... | collective-permute-start | bytes 2359304 | tf_op jit(solution)/shard_map/ppermute | solution.py:56
  76.2 27.8 %collective-permute-start.14 = (bf16[3,64,2048]{2,1,0:T(8,128)(2,1)S(1)}, bf16[3,64,2048]{2,1,0:T(8,128)(2,1)S(1)}, u32[]{:S(2)}, u32[]{:S(2)}) collective-permute-start(bf16[3,64,2048]{2,1,0:T(8,128)(2,1)S(1)} %pad_maximum_fusion.7.refs_6_.refs_5_), channel_id=1, source_target_pairs={{0,16},{16,0},{1,17},{17,1},{2,18},{18,2},{3,19},{19,3},{4,20},{20... | collective-permute-start | bytes 2359304 | tf_op jit(solution)/shard_map/ppermute | solution.py:56
  76.8 24.6 %collective-permute-start.15 = (bf16[128,1024]{1,0:T(8,128)(2,1)S(1)}, bf16[128,1024]{1,0:T(8,128)(2,1)S(1)}, u32[]{:S(2)}, u32[]{:S(2)}) collective-permute-start(bf16[128,1024]{1,0:T(8,128)(2,1)S(1)} %dynamic-slice_bitcast_fusion.6), channel_id=1, source_target_pairs={{0,2},{2,4},{4,6},{6,0},{1,3},{3,5},{5,7},{7,1},{8,10},{10,12},{12... | collective-permute-start | bytes 786440 | tf_op jit(solution)/shard_map/ppermute | solution.py:214
  76.8 24.6 %collective-permute-start.16 = (bf16[128,1024]{1,0:T(8,128)(2,1)S(1)}, bf16[128,1024]{1,0:T(8,128)(2,1)S(1)}, u32[]{:S(2)}, u32[]{:S(2)}) collective-permute-start(bf16[128,1024]{1,0:T(8,128)(2,1)S(1)} %dynamic-slice_bitcast_fusion.6), channel_id=1, source_target_pairs={{0,6},{2,0},{4,2},{6,4},{1,7},{3,1},{5,3},{7,5},{8,14},{10,8},{12,... | collective-permute-start | bytes 786440 | tf_op jit(solution)/shard_map/ppermute | solution.py:214
  78.3 25.8 %collective-permute-start.17 = (bf16[2,128,1024]{2,1,0:T(8,128)(2,1)S(1)}, bf16[2,128,1024]{2,1,0:T(8,128)(2,1)S(1)}, u32[]{:S(2)}, u32[]{:S(2)}) collective-permute-start(bf16[2,128,1024]{2,1,0:T(8,128)(2,1)S(1)} %copy-done.36), channel_id=1, source_target_pairs={{0,1},{1,0},{2,3},{3,2},{4,5},{5,4},{6,7},{7,6},{8,9},{9,8},{10,11... | collective-permute-start | bytes 1572872 | tf_op jit(solution)/shard_map/ppermute | solution.py:56
  105.4 16.3 %collective-permute-start.20 = (bf16[2,256,1024]{2,1,0:T(8,128)(2,1)S(1)}, bf16[2,256,1024]{2,1,0:T(8,128)(2,1)S(1)}, u32[]{:S(2)}, u32[]{:S(2)}) collective-permute-start(bf16[2,256,1024]{2,1,0:T(8,128)(2,1)S(1)} %pad_maximum_fusion.4), channel_id=1, source_target_pairs={{0,8},{8,0},{1,9},{9,1},{2,10},{10,2},{3,11},{11,3},{4,12},{12,4},... | collective-permute-start | bytes 3145736 | tf_op jit(solution)/shard_map/ppermute | solution.py:56
  107.7 15.1 %collective-permute-start.18 = (bf16[3,32,2048]{2,1,0:T(8,128)(2,1)S(1)}, bf16[3,32,2048]{2,1,0:T(8,128)(2,1)S(1)}, u32[]{:S(2)}, u32[]{:S(2)}) collective-permute-start(bf16[3,32,2048]{2,1,0:T(8,128)(2,1)S(1)} %get-tuple-element.318), channel_id=1, source_target_pairs={{0,16},{16,0},{1,17},{17,1},{2,18},{18,2},{3,19},{19,3},{4,20},{20... | collective-permute-start | bytes 1179656 | tf_op jit(solution)/shard_map/ppermute | solution.py:56
  108.4 14.6 %collective-permute-start.19 = (bf16[3,32,2048]{2,1,0:T(8,128)(2,1)S(1)}, bf16[3,32,2048]{2,1,0:T(8,128)(2,1)S(1)}, u32[]{:S(2)}, u32[]{:S(2)}) collective-permute-start(bf16[3,32,2048]{2,1,0:T(8,128)(2,1)S(1)} %get-tuple-element.319), channel_id=1, source_target_pairs={{0,1},{1,0},{2,3},{3,2},{4,5},{5,4},{6,7},{7,6},{8,9},{9,8},{10,11... | collective-permute-start | bytes 1179656 | tf_op jit(solution)/shard_map/ppermute | solution.py:56
  109.5 13.4 %collective-permute-start.21 = (bf16[128,1024]{1,0:T(8,128)(2,1)S(1)}, bf16[128,1024]{1,0:T(8,128)(2,1)S(1)}, u32[]{:S(2)}, u32[]{:S(2)}) collective-permute-start(bf16[128,1024]{1,0:T(8,128)(2,1)S(1)} %dynamic-slice_bitcast_fusion.6), channel_id=1, source_target_pairs={{0,4},{2,6},{4,0},{6,2},{1,5},{3,7},{5,1},{7,3},{8,12},{10,14},{12... | collective-permute-start | bytes 786440 | tf_op jit(solution)/shard_map/ppermute | solution.py:214
  126.4 19.2 %collective-permute-start.23 = (bf16[3,128,1024]{2,1,0:T(8,128)(2,1)S(1)}, bf16[3,128,1024]{2,1,0:T(8,128)(2,1)S(1)}, u32[]{:S(2)}, u32[]{:S(2)}) collective-permute-start(bf16[3,128,1024]{2,1,0:T(8,128)(2,1)S(1)} %pad_maximum_fusion.8.refs_12_), channel_id=1, source_target_pairs={{0,1},{1,0},{2,3},{3,2},{4,5},{5,4},{6,7},{7,6},{8,9},{9,8},{10,11... | collective-permute-start | bytes 2359304 | tf_op jit(solution)/shard_map/ppermute | solution.py:56
  126.8 18.9 %collective-permute-start.24 = (bf16[3,128,1024]{2,1,0:T(8,128)(2,1)S(1)}, bf16[3,128,1024]{2,1,0:T(8,128)(2,1)S(1)}, u32[]{:S(2)}, u32[]{:S(2)}) collective-permute-start(bf16[3,128,1024]{2,1,0:T(8,128)(2,1)S(1)} %pad_maximum_fusion.8.refs_12_), channel_id=1, source_target_pairs={{0,16},{16,0},{1,17},{17,1},{2,18},{18,2},{3,19},{19,3},{4,20},{20... | collective-permute-start | bytes 2359304 | tf_op jit(solution)/shard_map/ppermute | solution.py:56
  145.7 10.4 %collective-permute-start.25 = (bf16[3,64,1024]{2,1,0:T(8,128)(2,1)S(1)}, bf16[3,64,1024]{2,1,0:T(8,128)(2,1)S(1)}, u32[]{:S(2)}, u32[]{:S(2)}) collective-permute-start(bf16[3,64,1024]{2,1,0:T(8,128)(2,1)S(1)} %get-tuple-element.349), channel_id=1, source_target_pairs={{0,16},{16,0},{1,17},{17,1},{2,18},{18,2},{3,19},{19,3},{4,20},{20... | collective-permute-start | bytes 1179656 | tf_op jit(solution)/shard_map/ppermute | solution.py:56
  146.7 9.5 %collective-permute-start.26 = (bf16[3,64,1024]{2,1,0:T(8,128)(2,1)S(1)}, bf16[3,64,1024]{2,1,0:T(8,128)(2,1)S(1)}, u32[]{:S(2)}, u32[]{:S(2)}) collective-permute-start(bf16[3,64,1024]{2,1,0:T(8,128)(2,1)S(1)} %get-tuple-element.350), channel_id=1, source_target_pairs={{0,1},{1,0},{2,3},{3,2},{4,5},{5,4},{6,7},{7,6},{8,9},{9,8},{10,11... | collective-permute-start | bytes 1179656 | tf_op jit(solution)/shard_map/ppermute | solution.py:56
  156.2 22.8 %collective-permute-start.27 = (bf16[4,128,1024]{2,1,0:T(8,128)(2,1)S(1)}, bf16[4,128,1024]{2,1,0:T(8,128)(2,1)S(1)}, u32[]{:S(2)}, u32[]{:S(2)}) collective-permute-start(bf16[4,128,1024]{2,1,0:T(8,128)(2,1)S(1)} %get-tuple-element.362), channel_id=1, source_target_pairs={{0,1},{1,0},{2,3},{3,2},{4,5},{5,4},{6,7},{7,6},{8,9},{9,8},{10,11... | collective-permute-start | bytes 3145736 | tf_op jit(solution)/shard_map/ppermute | solution.py:56
  157.0 22.9 %collective-permute-start.28 = (bf16[4,2,64,1024]{3,2,1,0:T(8,128)(2,1)S(1)}, bf16[4,2,64,1024]{3,2,1,0:T(8,128)(2,1)S(1)}, u32[]{:S(2)}, u32[]{:S(2)}) collective-permute-start(bf16[4,2,64,1024]{3,2,1,0:T(8,128)(2,1)S(1)} %get-tuple-element.363), channel_id=1, source_target_pairs={{0,16},{16,0},{1,17},{17,1},{2,18},{18,2},{3,19},{19,3},{4,20},{20... | collective-permute-start | bytes 3145736 | tf_op jit(solution)/shard_map/ppermute | solution.py:56
  181.0 21.0 %collective-permute-start.29 = (bf16[1024,1024]{1,0:T(8,128)(2,1)}, bf16[1024,1024]{1,0:T(8,128)(2,1)}, u32[]{:S(2)}, u32[]{:S(2)}) collective-permute-start(bf16[1024,1024]{1,0:T(8,128)(2,1)} %get-tuple-element.395.refs_1_), channel_id=1, source_target_pairs={{0,8},{8,0},{1,9},{9,1},{2,10},{10,2},{3,11},{11,3},{4,12},{12,4},... | collective-permute-start | bytes 6291464 | tf_op jit(solution)/shard_map/ppermute | solution.py:56
  185.3 16.6 %collective-permute-start.30 = (bf16[2,256,1024]{2,1,0:T(8,128)(2,1)S(1)}, bf16[2,256,1024]{2,1,0:T(8,128)(2,1)S(1)}, u32[]{:S(2)}, u32[]{:S(2)}) collective-permute-start(bf16[2,256,1024]{2,1,0:T(8,128)(2,1)S(1)} %dynamic-slice_bitcast_fusion.1), channel_id=1, source_target_pairs={{0,8},{8,0},{1,9},{9,1},{2,10},{10,2},{3,11},{11,3},{4,12},{12,4},... | collective-permute-start | bytes 3145736 | tf_op jit(solution)/shard_map/ppermute | solution.py:56
  188.3 13.4 %collective-permute-start.31 = (bf16[4,64,1024]{2,1,0:T(8,128)(2,1)S(1)}, bf16[4,64,1024]{2,1,0:T(8,128)(2,1)S(1)}, u32[]{:S(2)}, u32[]{:S(2)}) collective-permute-start(bf16[4,64,1024]{2,1,0:T(8,128)(2,1)S(1)} %get-tuple-element.381), channel_id=1, source_target_pairs={{0,16},{16,0},{1,17},{17,1},{2,18},{18,2},{3,19},{19,3},{4,20},{20... | collective-permute-start | bytes 1572872 | tf_op jit(solution)/shard_map/ppermute | solution.py:56
  188.9 13.0 %collective-permute-start.32 = (bf16[4,64,1024]{2,1,0:T(8,128)(2,1)S(1)}, bf16[4,64,1024]{2,1,0:T(8,128)(2,1)S(1)}, u32[]{:S(2)}, u32[]{:S(2)}) collective-permute-start(bf16[4,64,1024]{2,1,0:T(8,128)(2,1)S(1)} %get-tuple-element.382), channel_id=1, source_target_pairs={{0,1},{1,0},{2,3},{3,2},{4,5},{5,4},{6,7},{7,6},{8,9},{9,8},{10,11... | collective-permute-start | bytes 1572872 | tf_op jit(solution)/shard_map/ppermute | solution.py:56
  202.9 28.8 %collective-permute-start.33 = (bf16[4,64,2048]{2,1,0:T(8,128)(2,1)S(1)}, bf16[4,64,2048]{2,1,0:T(8,128)(2,1)S(1)}, u32[]{:S(2)}, u32[]{:S(2)}) collective-permute-start(bf16[4,64,2048]{2,1,0:T(8,128)(2,1)S(1)} %get-tuple-element.401), channel_id=1, source_target_pairs={{0,1},{1,0},{2,3},{3,2},{4,5},{5,4},{6,7},{7,6},{8,9},{9,8},{10,11... | collective-permute-start | bytes 3145736 | tf_op jit(solution)/shard_map/ppermute | solution.py:56
  203.7 28.0 %collective-permute-start.34 = (bf16[4,2,32,2048]{3,2,1,0:T(8,128)(2,1)S(1)}, bf16[4,2,32,2048]{3,2,1,0:T(8,128)(2,1)S(1)}, u32[]{:S(2)}, u32[]{:S(2)}) collective-permute-start(bf16[4,2,32,2048]{3,2,1,0:T(8,128)(2,1)S(1)} %get-tuple-element.402), channel_id=1, source_target_pairs={{0,16},{16,0},{1,17},{17,1},{2,18},{18,2},{3,19},{19,3},{4,20},{20... | collective-permute-start | bytes 3145736 | tf_op jit(solution)/shard_map/ppermute | solution.py:56
  204.6 27.1 %collective-permute-start.35 = (bf16[2,64,1024]{2,1,0:T(8,128)(2,1)S(1)}, bf16[2,64,1024]{2,1,0:T(8,128)(2,1)S(1)}, u32[]{:S(2)}, u32[]{:S(2)}) collective-permute-start(bf16[2,64,1024]{2,1,0:T(8,128)(2,1)S(1)} %get-tuple-element.404), channel_id=1, source_target_pairs={{0,2},{2,4},{4,6},{6,0},{1,3},{3,5},{5,7},{7,1},{8,10},{10,12},{12... | collective-permute-start | bytes 786440 | tf_op jit(solution)/shard_map/ppermute | solution.py:214
  204.6 27.1 %collective-permute-start.36 = (bf16[2,64,1024]{2,1,0:T(8,128)(2,1)S(1)}, bf16[2,64,1024]{2,1,0:T(8,128)(2,1)S(1)}, u32[]{:S(2)}, u32[]{:S(2)}) collective-permute-start(bf16[2,64,1024]{2,1,0:T(8,128)(2,1)S(1)} %get-tuple-element.405), channel_id=1, source_target_pairs={{0,4},{2,6},{4,0},{6,2},{1,5},{3,7},{5,1},{7,3},{8,12},{10,14},{12... | collective-permute-start | bytes 786440 | tf_op jit(solution)/shard_map/ppermute | solution.py:214
  208.4 23.3 %collective-permute-start.37 = (bf16[2,64,1024]{2,1,0:T(8,128)(2,1)S(1)}, bf16[2,64,1024]{2,1,0:T(8,128)(2,1)S(1)}, u32[]{:S(2)}, u32[]{:S(2)}) collective-permute-start(bf16[2,64,1024]{2,1,0:T(8,128)(2,1)S(1)} %get-tuple-element.406), channel_id=1, source_target_pairs={{0,6},{2,0},{4,2},{6,4},{1,7},{3,1},{5,3},{7,5},{8,14},{10,8},{12,... | collective-permute-start | bytes 786440 | tf_op jit(solution)/shard_map/ppermute | solution.py:214
  231.9 9.7 %collective-permute-start.40 = (bf16[2,64,1024]{2,1,0:T(8,128)(2,1)S(1)}, bf16[2,64,1024]{2,1,0:T(8,128)(2,1)S(1)}, u32[]{:S(2)}, u32[]{:S(2)}) collective-permute-start(bf16[2,64,1024]{2,1,0:T(8,128)(2,1)S(1)} %add_convert_fusion.1), channel_id=1, source_target_pairs={{0,16},{16,0},{1,17},{17,1},{2,18},{18,2},{3,19},{19,3},{4,20},{20... | collective-permute-start | bytes 786440 | tf_op jit(solution)/shard_map/ppermute | solution.py:56
  234.5 14.1 %collective-permute-start.38 = (bf16[4,32,2048]{2,1,0:T(8,128)(2,1)S(1)}, bf16[4,32,2048]{2,1,0:T(8,128)(2,1)S(1)}, u32[]{:S(2)}, u32[]{:S(2)}) collective-permute-start(bf16[4,32,2048]{2,1,0:T(8,128)(2,1)S(1)} %get-tuple-element.416), channel_id=1, source_target_pairs={{0,16},{16,0},{1,17},{17,1},{2,18},{18,2},{3,19},{19,3},{4,20},{20... | collective-permute-start | bytes 1572872 | tf_op jit(solution)/shard_map/ppermute | solution.py:56
  234.9 13.7 %collective-permute-start.39 = (bf16[4,32,2048]{2,1,0:T(8,128)(2,1)S(1)}, bf16[4,32,2048]{2,1,0:T(8,128)(2,1)S(1)}, u32[]{:S(2)}, u32[]{:S(2)}) collective-permute-start(bf16[4,32,2048]{2,1,0:T(8,128)(2,1)S(1)} %get-tuple-element.417), channel_id=1, source_target_pairs={{0,1},{1,0},{2,3},{3,2},{4,5},{5,4},{6,7},{7,6},{8,9},{9,8},{10,11... | collective-permute-start | bytes 1572872 | tf_op jit(solution)/shard_map/ppermute | solution.py:56
  249.6 27.7 %collective-permute-start.44 = (bf16[4,64,1408]{2,1,0:T(8,128)(2,1)S(1)}, bf16[4,64,1408]{2,1,0:T(8,128)(2,1)S(1)}, u32[]{:S(2)}, u32[]{:S(2)}) collective-permute-start(bf16[4,64,1408]{2,1,0:T(8,128)(2,1)S(1)} %get-tuple-element.449), channel_id=1, source_target_pairs={{0,1},{1,0},{2,3},{3,2},{4,5},{5,4},{6,7},{7,6},{8,9},{9,8},{10,11... | collective-permute-start | bytes 2162696 | tf_op jit(solution)/shard_map/ppermute | solution.py:56
  250.4 26.9 %collective-permute-start.45 = (bf16[4,2,32,1408]{3,2,1,0:T(8,128)(2,1)S(1)}, bf16[4,2,32,1408]{3,2,1,0:T(8,128)(2,1)S(1)}, u32[]{:S(2)}, u32[]{:S(2)}) collective-permute-start(bf16[4,2,32,1408]{3,2,1,0:T(8,128)(2,1)S(1)} %get-tuple-element.450), channel_id=1, source_target_pairs={{0,16},{16,0},{1,17},{17,1},{2,18},{18,2},{3,19},{19,3},{4,20},{20... | collective-permute-start | bytes 2162696 | tf_op jit(solution)/shard_map/ppermute | solution.py:56
  251.5 17.2 %collective-permute-start.41 = (bf16[2,32,2048]{2,1,0:T(8,128)(2,1)S(1)}, bf16[2,32,2048]{2,1,0:T(8,128)(2,1)S(1)}, u32[]{:S(2)}, u32[]{:S(2)}) collective-permute-start(bf16[2,32,2048]{2,1,0:T(8,128)(2,1)S(1)} %get-tuple-element.444), channel_id=1, source_target_pairs={{0,2},{2,4},{4,6},{6,0},{1,3},{3,5},{5,7},{7,1},{8,10},{10,12},{12... | collective-permute-start | bytes 786440 | tf_op jit(solution)/shard_map/ppermute | solution.py:214
  252.6 19.9 %collective-permute-start.42 = (bf16[2,32,2048]{2,1,0:T(8,128)(2,1)S(1)}, bf16[2,32,2048]{2,1,0:T(8,128)(2,1)S(1)}, u32[]{:S(2)}, u32[]{:S(2)}) collective-permute-start(bf16[2,32,2048]{2,1,0:T(8,128)(2,1)S(1)} %get-tuple-element.445), channel_id=1, source_target_pairs={{0,4},{2,6},{4,0},{6,2},{1,5},{3,7},{5,1},{7,3},{8,12},{10,14},{12... | collective-permute-start | bytes 786440 | tf_op jit(solution)/shard_map/ppermute | solution.py:214
  254.7 22.5 %collective-permute-start.43 = (bf16[2,32,2048]{2,1,0:T(8,128)(2,1)S(1)}, bf16[2,32,2048]{2,1,0:T(8,128)(2,1)S(1)}, u32[]{:S(2)}, u32[]{:S(2)}) collective-permute-start(bf16[2,32,2048]{2,1,0:T(8,128)(2,1)S(1)} %get-tuple-element.446), channel_id=1, source_target_pairs={{0,6},{2,0},{4,2},{6,4},{1,7},{3,1},{5,3},{7,5},{8,14},{10,8},{12,... | collective-permute-start | bytes 786440 | tf_op jit(solution)/shard_map/ppermute | solution.py:214
  283.6 19.0 %collective-permute-start.46 = (bf16[4,64,896]{2,1,0:T(8,128)(2,1)S(1)}, bf16[4,64,896]{2,1,0:T(8,128)(2,1)S(1)}, u32[]{:S(2)}, u32[]{:S(2)}) collective-permute-start(bf16[4,64,896]{2,1,0:T(8,128)(2,1)S(1)} %get-tuple-element.464), channel_id=1, source_target_pairs={{0,1},{1,0},{2,3},{3,2},{4,5},{5,4},{6,7},{7,6},{8,9},{9,8},{10,11... | collective-permute-start | bytes 1376264 | tf_op jit(solution)/shard_map/ppermute | solution.py:56
  284.3 18.3 %collective-permute-start.47 = (bf16[4,2,32,896]{3,2,1,0:T(8,128)(2,1)S(1)}, bf16[4,2,32,896]{3,2,1,0:T(8,128)(2,1)S(1)}, u32[]{:S(2)}, u32[]{:S(2)}) collective-permute-start(bf16[4,2,32,896]{3,2,1,0:T(8,128)(2,1)S(1)} %get-tuple-element.465), channel_id=1, source_target_pairs={{0,16},{16,0},{1,17},{17,1},{2,18},{18,2},{3,19},{19,3},{4,20},{20... | collective-permute-start | bytes 1376264 | tf_op jit(solution)/shard_map/ppermute | solution.py:56
  284.6 17.9 %collective-permute-start.48 = (bf16[4,32,1408]{2,1,0:T(8,128)(2,1)S(1)}, bf16[4,32,1408]{2,1,0:T(8,128)(2,1)S(1)}, u32[]{:S(2)}, u32[]{:S(2)}) collective-permute-start(bf16[4,32,1408]{2,1,0:T(8,128)(2,1)S(1)} %get-tuple-element.466), channel_id=1, source_target_pairs={{0,16},{16,0},{1,17},{17,1},{2,18},{18,2},{3,19},{19,3},{4,20},{20... | collective-permute-start | bytes 1081352 | tf_op jit(solution)/shard_map/ppermute | solution.py:56
  285.8 16.8 %collective-permute-start.49 = (bf16[4,32,1408]{2,1,0:T(8,128)(2,1)S(1)}, bf16[4,32,1408]{2,1,0:T(8,128)(2,1)S(1)}, u32[]{:S(2)}, u32[]{:S(2)}) collective-permute-start(bf16[4,32,1408]{2,1,0:T(8,128)(2,1)S(1)} %get-tuple-element.467), channel_id=1, source_target_pairs={{0,1},{1,0},{2,3},{3,2},{4,5},{5,4},{6,7},{7,6},{8,9},{9,8},{10,11... | collective-permute-start | bytes 1081352 | tf_op jit(solution)/shard_map/ppermute | solution.py:56
  302.7 6.8 %collective-permute-start.56 = (bf16[2,256,1024]{2,1,0:T(8,128)(2,1)S(1)}, bf16[2,256,1024]{2,1,0:T(8,128)(2,1)S(1)}, u32[]{:S(2)}, u32[]{:S(2)}) collective-permute-start(bf16[2,256,1024]{2,1,0:T(8,128)(2,1)S(1)} %dynamic-slice_bitcast_fusion), channel_id=1, source_target_pairs={{0,8},{8,0},{1,9},{9,1},{2,10},{10,2},{3,11},{11,3},{4,12},{12,4},... | collective-permute-start | bytes 3145736 | tf_op jit(solution)/shard_map/ppermute | solution.py:56
  306.6 6.2 %collective-permute-start.52 = (bf16[2,32,1408]{2,1,0:T(8,128)(2,1)S(1)}, bf16[2,32,1408]{2,1,0:T(8,128)(2,1)S(1)}, u32[]{:S(2)}, u32[]{:S(2)}) collective-permute-start(bf16[2,32,1408]{2,1,0:T(8,128)(2,1)S(1)} %get-tuple-element.486), channel_id=1, source_target_pairs={{0,2},{2,4},{4,6},{6,0},{1,3},{3,5},{5,7},{7,1},{8,10},{10,12},{12... | collective-permute-start | bytes 540680 | tf_op jit(solution)/shard_map/ppermute | solution.py:214
  306.6 15.7 %collective-permute-start.53 = (bf16[2,32,1408]{2,1,0:T(8,128)(2,1)S(1)}, bf16[2,32,1408]{2,1,0:T(8,128)(2,1)S(1)}, u32[]{:S(2)}, u32[]{:S(2)}) collective-permute-start(bf16[2,32,1408]{2,1,0:T(8,128)(2,1)S(1)} %get-tuple-element.487), channel_id=1, source_target_pairs={{0,4},{2,6},{4,0},{6,2},{1,5},{3,7},{5,1},{7,3},{8,12},{10,14},{12... | collective-permute-start | bytes 540680 | tf_op jit(solution)/shard_map/ppermute | solution.py:214
  306.7 15.7 %collective-permute-start.54 = (bf16[2,32,1408]{2,1,0:T(8,128)(2,1)S(1)}, bf16[2,32,1408]{2,1,0:T(8,128)(2,1)S(1)}, u32[]{:S(2)}, u32[]{:S(2)}) collective-permute-start(bf16[2,32,1408]{2,1,0:T(8,128)(2,1)S(1)} %get-tuple-element.488), channel_id=1, source_target_pairs={{0,6},{2,0},{4,2},{6,4},{1,7},{3,1},{5,3},{7,5},{8,14},{10,8},{12,... | collective-permute-start | bytes 540680 | tf_op jit(solution)/shard_map/ppermute | solution.py:214
  309.1 13.3 %collective-permute-start.50 = (bf16[4,32,896]{2,1,0:T(8,128)(2,1)S(1)}, bf16[4,32,896]{2,1,0:T(8,128)(2,1)S(1)}, u32[]{:S(2)}, u32[]{:S(2)}) collective-permute-start(bf16[4,32,896]{2,1,0:T(8,128)(2,1)S(1)} %get-tuple-element.481), channel_id=1, source_target_pairs={{0,16},{16,0},{1,17},{17,1},{2,18},{18,2},{3,19},{19,3},{4,20},{20... | collective-permute-start | bytes 688136 | tf_op jit(solution)/shard_map/ppermute | solution.py:56
  309.5 17.4 %collective-permute-start.55 = (bf16[256,1024]{1,0:T(8,128)(2,1)S(1)}, bf16[256,1024]{1,0:T(8,128)(2,1)S(1)}, u32[]{:S(2)}, u32[]{:S(2)}) collective-permute-start(bf16[256,1024]{1,0:T(8,128)(2,1)S(1)} %dynamic-slice_bitcast_fusion.2), channel_id=1, source_target_pairs={{0,16},{16,0},{1,17},{17,1},{2,18},{18,2},{3,19},{19,3},{4,20},{20... | collective-permute-start | bytes 1572872 | tf_op jit(solution)/shard_map/ppermute | solution.py:56
  312.8 9.6 %collective-permute-start.51 = (bf16[4,32,896]{2,1,0:T(8,128)(2,1)S(1)}, bf16[4,32,896]{2,1,0:T(8,128)(2,1)S(1)}, u32[]{:S(2)}, u32[]{:S(2)}) collective-permute-start(bf16[4,32,896]{2,1,0:T(8,128)(2,1)S(1)} %get-tuple-element.482), channel_id=1, source_target_pairs={{0,1},{1,0},{2,3},{3,2},{4,5},{5,4},{6,7},{7,6},{8,9},{9,8},{10,11... | collective-permute-start | bytes 688136 | tf_op jit(solution)/shard_map/ppermute | solution.py:56
  326.9 10.1 %collective-permute-start.67 = (bf16[256,1024]{1,0:T(8,128)(2,1)S(1)}, bf16[256,1024]{1,0:T(8,128)(2,1)S(1)}, u32[]{:S(2)}, u32[]{:S(2)}) collective-permute-start(bf16[256,1024]{1,0:T(8,128)(2,1)S(1)} %bitcast.172), channel_id=1, source_target_pairs={{0,8},{8,0},{1,9},{9,1},{2,10},{10,2},{3,11},{11,3},{4,12},{12,4},... | collective-permute-start | bytes 1572872 | tf_op jit(solution)/shard_map/ppermute | solution.py:56
  328.5 8.0 %collective-permute-start.61 = (bf16[2,32,2048]{2,1,0:T(8,128)(2,1)S(1)}, bf16[2,32,2048]{2,1,0:T(8,128)(2,1)S(1)}, u32[]{:S(2)}, u32[]{:S(2)}) collective-permute-start(bf16[2,32,2048]{2,1,0:T(8,128)(2,1)S(1)} %add_convert_fusion), channel_id=1, source_target_pairs={{0,16},{16,0},{1,17},{17,1},{2,18},{18,2},{3,19},{19,3},{4,20},{20... | collective-permute-start | bytes 786440 | tf_op jit(solution)/shard_map/ppermute | solution.py:56
  329.6 9.2 %collective-permute-start.57 = (bf16[2,32,896]{2,1,0:T(8,128)(2,1)S(1)}, bf16[2,32,896]{2,1,0:T(8,128)(2,1)S(1)}, u32[]{:S(2)}, u32[]{:S(2)}) collective-permute-start(bf16[2,32,896]{2,1,0:T(8,128)(2,1)S(1)} %get-tuple-element.500), channel_id=1, source_target_pairs={{0,2},{2,4},{4,6},{6,0},{1,3},{3,5},{5,7},{7,1},{8,10},{10,12},{12... | collective-permute-start | bytes 344072 | tf_op jit(solution)/shard_map/ppermute | solution.py:214
  330.8 10.5 %collective-permute-start.58 = (bf16[2,32,896]{2,1,0:T(8,128)(2,1)S(1)}, bf16[2,32,896]{2,1,0:T(8,128)(2,1)S(1)}, u32[]{:S(2)}, u32[]{:S(2)}) collective-permute-start(bf16[2,32,896]{2,1,0:T(8,128)(2,1)S(1)} %get-tuple-element.501), channel_id=1, source_target_pairs={{0,4},{2,6},{4,0},{6,2},{1,5},{3,7},{5,1},{7,3},{8,12},{10,14},{12... | collective-permute-start | bytes 344072 | tf_op jit(solution)/shard_map/ppermute | solution.py:214
  333.9 9.5 %collective-permute-start.59 = (bf16[2,32,896]{2,1,0:T(8,128)(2,1)S(1)}, bf16[2,32,896]{2,1,0:T(8,128)(2,1)S(1)}, u32[]{:S(2)}, u32[]{:S(2)}) collective-permute-start(bf16[2,32,896]{2,1,0:T(8,128)(2,1)S(1)} %get-tuple-element.502), channel_id=1, source_target_pairs={{0,6},{2,0},{4,2},{6,4},{1,7},{3,1},{5,3},{7,5},{8,14},{10,8},{12,... | collective-permute-start | bytes 344072 | tf_op jit(solution)/shard_map/ppermute | solution.py:214
  336.5 12.7 %collective-permute-start.60 = (bf16[256,1024]{1,0:T(8,128)(2,1)S(1)}, bf16[256,1024]{1,0:T(8,128)(2,1)S(1)}, u32[]{:S(2)}, u32[]{:S(2)}) collective-permute-start(bf16[256,1024]{1,0:T(8,128)(2,1)S(1)} %fusion.15), channel_id=1, source_target_pairs={{0,16},{16,0},{1,17},{17,1},{2,18},{18,2},{3,19},{19,3},{4,20},{20... | collective-permute-start | bytes 1572872 | tf_op jit(solution)/shard_map/ppermute | solution.py:56
  349.2 12.9 %collective-permute-start.66 = (bf16[128,2048]{1,0:T(8,128)(2,1)S(1)}, bf16[128,2048]{1,0:T(8,128)(2,1)S(1)}, u32[]{:S(2)}, u32[]{:S(2)}) collective-permute-start(bf16[128,2048]{1,0:T(8,128)(2,1)S(1)} %bitcast.178), channel_id=1, source_target_pairs={{0,8},{8,0},{1,9},{9,1},{2,10},{10,2},{3,11},{11,3},{4,12},{12,4},... | collective-permute-start | bytes 1572872 | tf_op jit(solution)/shard_map/ppermute | solution.py:56
  351.4 8.2 %collective-permute-start.62 = (bf16[2,32,1408]{2,1,0:T(8,128)(2,1)S(1)}, bf16[2,32,1408]{2,1,0:T(8,128)(2,1)S(1)}, u32[]{:S(2)}, u32[]{:S(2)}) collective-permute-start(bf16[2,32,1408]{2,1,0:T(8,128)(2,1)S(1)} %add_convert_fusion.2), channel_id=1, source_target_pairs={{0,16},{16,0},{1,17},{17,1},{2,18},{18,2},{3,19},{19,3},{4,20},{20... | collective-permute-start | bytes 540680 | tf_op jit(solution)/shard_map/ppermute | solution.py:56
  355.9 9.8 %collective-permute-start.65 = (bf16[128,896]{1,0:T(8,128)(2,1)S(1)}, bf16[128,896]{1,0:T(8,128)(2,1)S(1)}, u32[]{:S(2)}, u32[]{:S(2)}) collective-permute-start(bf16[128,896]{1,0:T(8,128)(2,1)S(1)} %bitcast.170), channel_id=1, source_target_pairs={{0,8},{8,0},{1,9},{9,1},{2,10},{10,2},{3,11},{11,3},{4,12},{12,4},... | collective-permute-start | bytes 688136 | tf_op jit(solution)/shard_map/ppermute | solution.py:56
  (60 other events, 820.6 us)

commit v5 on v4

--- a/solution.py
+++ b/solution.py
@@ -13,7 +13,7 @@
 DOC_MOST = 512
 TILE = 256
 LANES = 128
-VMEM = 30 * 1024 * 1024
+VMEM = 26 * 1024 * 1024
 epsilon = 1e-05
 SWAP = [(0, 1), (1, 0)]
 f32 = jnp.float32
@@ -81,27 +81,52 @@
         bias[i, :, :width] = jnp.where(allowed, 0.0, -1e30).astype(f32)
 
 
+def pipelined(count, first, second, third):
+    current, waiting = first(0), None
+    for block in range(count):
+        following = first(block + 1) if block + 1 < count else None
+        middle = second(block, current)
+        if waiting is not None:
+            third(*waiting)
+        waiting = (block, current, middle)
+        current = following
+    third(*waiting)
+
+
+def own_half(left, head, rows):
+    return jnp.where(left if head == 0 else ~left, rows, jnp.zeros_like(rows))
+
+
 def attend_kernel(spans, tile, q_ref, k_ref, v_ref, seg_col, seg_row, out_ref, lse_ref, bias):
     @pl.when(pl.program_id(0) == 0)
     def _():
         fill_bias(bias, seg_col, seg_row, spans, tile)
 
     left = lax.broadcasted_iota(jnp.int32, (tile, LANES), 1) < HEAD_DIM
-    for i, (start, low, high) in enumerate(spans):
-        rows = slice(start, start + tile)
-        queries = q_ref[rows, :]
-        keys, values = k_ref[low:high, :], v_ref[low:high, :]
-        mixed, logs = [], []
-        for half in (left, ~left):
-            scores = mm_cols(jnp.where(half, queries, jnp.zeros_like(queries)), keys)
-            scores = scores + bias[i, :, : high - low]
-            top = jnp.max(scores, axis=-1, keepdims=True)
-            powers = jnp.exp(scores - top)
-            total = jnp.sum(powers, axis=-1, keepdims=True)
-            mixed.append(mm((powers * (1.0 / total)).astype(bf16), values))
-            logs.append(top + jnp.log(total))
-        out_ref[rows, :] = jnp.where(left, mixed[0], mixed[1]).astype(bf16)
-        lse_ref[rows, :] = jnp.where(left, logs[0], logs[1])
+    done = {}
+
+    def scores(block):
+        (start, low, high), head = spans[block // 2], block % 2
+        return mm_cols(own_half(left, head, q_ref[start : start + tile, :]), k_ref[low:high, :])
+
+    def softmax(block, values):
+        _, low, high = spans[block // 2]
+        values = values + bias[block // 2, :, : high - low]
+        top = jnp.max(values, axis=-1, keepdims=True)
+        powers = jnp.exp(values - top)
+        total = jnp.sum(powers, axis=-1, keepdims=True)
+        return powers.astype(bf16), total, top + jnp.log(total)
+
+    def mix(block, _, held):
+        (start, low, high), head = spans[block // 2], block % 2
+        powers, total, logs = held
+        done[head] = mm(powers, v_ref[low:high, :]) * (1.0 / total), logs
+        if head == 1:
+            rows = slice(start, start + tile)
+            out_ref[rows, :] = jnp.where(left, done[0][0], done[1][0]).astype(bf16)
+            lse_ref[rows, :] = jnp.where(left, done[0][1], done[1][1])
+
+    pipelined(2 * len(spans), scores, softmax, mix)
 
 
 def attend(joint, seg_col, seg_row, begin, count):
@@ -139,41 +164,44 @@
 def attend_back_kernel(
     spans, tile, q_ref, k_ref, v_ref, g_ref, lse_ref, seg_col, seg_row, out_ref, bias, keys_sum, values_sum
 ):
-    @pl.when((pl.program_id(0) == 0) & (pl.program_id(1) == 0))
+    @pl.when(pl.program_id(0) == 0)
     def _():
         fill_bias(bias, seg_col, seg_row, spans, tile)
 
-    @pl.when(pl.program_id(1) == 0)
-    def _():
-        keys_sum[...] = jnp.zeros_like(keys_sum)
-        values_sum[...] = jnp.zeros_like(values_sum)
-        left = lax.broadcasted_iota(jnp.int32, (tile, LANES), 1) < HEAD_DIM
-        for i, (start, low, high) in enumerate(spans):
-            rows = slice(start, start + tile)
-            queries, grads = q_ref[rows, :], g_ref[rows, :]
-            keys, values = k_ref[low:high, :], v_ref[low:high, :]
-            parts = []
-            for half, lane in ((left, 0), (~left, HEAD_DIM)):
-                own_queries = jnp.where(half, queries, jnp.zeros_like(queries))
-                own_grads = jnp.where(half, grads, jnp.zeros_like(grads))
-                scores = mm_cols(own_queries, keys) + bias[i, :, : high - low]
-                probs = jnp.exp(scores - lse_ref[rows, lane : lane + 1])
-                grad_probs = mm_cols(own_grads, values)
-                inner = jnp.sum(probs * grad_probs, axis=-1, keepdims=True)
-                grad_scores = (probs * (grad_probs - inner)).astype(bf16)
-                parts.append(mm(grad_scores, keys))
-                keys_sum[low:high, :] += mm_rows(grad_scores, own_queries)
-                values_sum[low:high, :] += mm_rows(probs.astype(bf16), own_grads)
-            grad_queries = jnp.where(left, parts[0], parts[1]).astype(bf16)
-            out_ref[rows, :] = grad_queries * jnp.asarray(1.0 / math.sqrt(HEAD_DIM), bf16)
-
-    @pl.when(pl.program_id(1) == 1)
-    def _():
-        out_ref[...] = keys_sum[...].astype(bf16)
-
-    @pl.when(pl.program_id(1) == 2)
-    def _():
-        out_ref[...] = values_sum[...].astype(bf16)
+    keys_sum[...] = jnp.zeros_like(keys_sum)
+    values_sum[...] = jnp.zeros_like(values_sum)
+    left = lax.broadcasted_iota(jnp.int32, (tile, LANES), 1) < HEAD_DIM
+    done = {}
+
+    def products(block):
+        (start, low, high), head = spans[block // 2], block % 2
+        rows = slice(start, start + tile)
+        queries, grads = own_half(left, head, q_ref[rows, :]), own_half(left, head, g_ref[rows, :])
+        return queries, grads, mm_cols(queries, k_ref[low:high, :]), mm_cols(grads, v_ref[low:high, :])
+
+    def softmax_back(block, held):
+        (start, low, high), lane = spans[block // 2], block % 2 * HEAD_DIM
+        _, _, scores, grad_probs = held
+        logs = lse_ref[start : start + tile, lane : lane + 1]
+        probs = jnp.exp(scores + bias[block // 2, :, : high - low] - logs)
+        both = probs * grad_probs
+        inner = jnp.sum(both, axis=-1, keepdims=True)
+        return (both - probs * inner).astype(bf16), probs.astype(bf16)
+
+    def gather_up(block, held, middle):
+        (start, low, high), head = spans[block // 2], block % 2
+        queries, grads, _, _ = held
+        grad_scores, probs = middle
+        done[head] = mm(grad_scores, k_ref[low:high, :])
+        keys_sum[low:high, :] += mm_rows(grad_scores, queries)
+        values_sum[low:high, :] += mm_rows(probs, grads)
+        if head == 1:
+            grad_queries = jnp.where(left, done[0], done[1]).astype(bf16)
+            out_ref[0, start : start + tile, :] = grad_queries * jnp.asarray(1.0 / math.sqrt(HEAD_DIM), bf16)
+
+    pipelined(2 * len(spans), products, softmax_back, gather_up)
+    out_ref[1] = keys_sum[...].astype(bf16)
+    out_ref[2] = values_sum[...].astype(bf16)
 
 
 def attend_back(joint, grads, lse, seg_col, seg_row, begin, count):
@@ -183,22 +211,22 @@
     widest = max(high - low for _, low, high in spans)
 
     def part(which):
-        return pl.BlockSpec((rows, LANES), lambda p, j: (0, which * pairs + begin + p))
+        return pl.BlockSpec((rows, LANES), lambda p: (0, which * pairs + begin + p))
 
     return pl.pallas_call(
         functools.partial(attend_back_kernel, spans, tile),
-        grid=(count, 3),
+        grid=(count,),
         in_specs=[
             part(0),
             part(1),
             part(2),
             part(0),
-            pl.BlockSpec((rows, LANES), lambda p, j: (0, p)),
-            pl.BlockSpec((rows, 1), lambda p, j: (0, 0)),
-            pl.BlockSpec((1, rows), lambda p, j: (0, 0)),
+            pl.BlockSpec((rows, LANES), lambda p: (0, p)),
+            pl.BlockSpec((rows, 1), lambda p: (0, 0)),
+            pl.BlockSpec((1, rows), lambda p: (0, 0)),
         ],
-        out_specs=pl.BlockSpec((rows, LANES), lambda p, j: (0, j * count + p)),
-        out_shape=jax.ShapeDtypeStruct((rows, 3 * count * LANES), bf16),
+        out_specs=pl.BlockSpec((3, rows, LANES), lambda p: (0, 0, p)),
+        out_shape=jax.ShapeDtypeStruct((3, rows, count * LANES), bf16),
         scratch_shapes=[
             pltpu.VMEM((len(spans), tile, widest), f32),
             pltpu.VMEM((rows, LANES), f32),
@@ -208,6 +236,14 @@
         cost_estimate=cost(6 * count),
         name="attend_back",
     )(far(joint), far(joint), far(joint), grads, lse, seg_col, seg_row)
+
+
+def shape_of(*shape, dtype=bf16):
+    return jax.ShapeDtypeStruct(shape, dtype)
+
+
+def far_shape(*shape, dtype=bf16):
+    return pltpu.HBM(shape, dtype)
 
 
 def along(value, axis, depth, step):
@@ -337,10 +373,9 @@
     )(place, own, other)
 
 
-def finish_qkv(place, owns, others):
+def finish_qkv(place, columns, owns, others):
     rows = owns[0].shape[0]
     half, pieces = rows // 2, len(owns)
-    columns = owns[-1].shape[1] - LANES
     third = columns // 3
     model = 2 * (owns[0].shape[1] - columns - LANES)
 
@@ -387,7 +422,7 @@
     return (left.astype(f32) + right.astype(f32)).astype(bf16)
 
 
-def fold_one(place, keep, came):
+def fold_one(place, keep, came, shape=shape_of):
     depth, top, columns = keep[0].shape
     low = top // 2
 
@@ -407,7 +442,7 @@
         grid=(depth,),
         in_specs=[pl.BlockSpec(memory_space=pltpu.SMEM), one, two, one, two],
         out_specs=[pl.BlockSpec((2, 1, low, columns), lambda i: (0, i, 0, 0)), send, send],
-        out_shape=[shape_of(2, depth, low, columns)] + [shape_of(depth, low, columns)] * 2,
+        out_shape=[shape(2, depth, low, columns)] + [shape(depth, low, columns)] * 2,
         compiler_params=pltpu.CompilerParams(vmem_limit_bytes=VMEM),
         cost_estimate=cost(1),
         name="fold_one",
@@ -485,14 +520,6 @@
     )(place, *[v for v, _ in inputs], *[far(piece) for piece in pieces])
 
 
-def shape_of(*shape, dtype=bf16):
-    return jax.ShapeDtypeStruct(shape, dtype)
-
-
-def far_shape(*shape, dtype=bf16):
-    return pltpu.HBM(shape, dtype)
-
-
 def unit_of(values):
     centred = values - jnp.mean(values, axis=-1, keepdims=True)
     variance = jnp.mean(centred * centred, axis=-1, keepdims=True)
@@ -534,7 +561,9 @@
 def outer(place, depth, left, right, out_pair=None, weight=None, scales=None, piece=0, sums=None):
     rows, own_rows = left.shape[0], left.shape[1] // (2 * depth)
     top, low = own_rows // 2, own_rows // 4
-    columns = right.shape[1]
+    parts = right.shape[0] if right.ndim == 3 else 1
+    third = right.shape[-1]
+    columns = parts * third
     given = [left, right]
     specs = [pl.BlockSpec((rows, 2 * own_rows), lambda i: (0, i)), whole_block(*right.shape)]
     total = columns
@@ -543,7 +572,7 @@
         specs += [pl.BlockSpec((2 * own_rows, part.shape[1]), lambda i: (i, 0)) for part in (weight, scales)]
         specs.append(pl.BlockSpec((8, 2 * own_rows), lambda i: (0, i)))
         total += LANES
-        third, width = columns // 3, weight.shape[1] // 3
+        width = weight.shape[1] // 3
     if out_pair is not None:
         out_block = out_pair[0].shape[1] // depth
         given += out_pair
@@ -566,18 +595,20 @@
             send_second[0, :, :, where] = jnp.where(at_h, upper, lower)
 
         left_ref, right_ref = ins.pop(0), ins.pop(0)
-        product = mm_rows(left_ref[...], right_ref[...])
-        put(0, product.reshape(2, own_rows, columns))
+        rights = [right_ref.at[j] for j in range(parts)] if parts > 1 else [right_ref]
+        products = [mm_rows(left_ref[...], ref[...]) for ref in rights]
+        for j, product in enumerate(products):
+            put(j * third, product.reshape(2, own_rows, third))
         first = columns
         if weight is not None:
             weight_ref, scales_ref, sums_ref = ins.pop(0), ins.pop(0), ins.pop(0)
-            column_sums = jnp.sum(right_ref[...].astype(f32), axis=0, keepdims=True)
             bias_sum = cross = 0.0
-            for j in range(3):
-                at, to = j * width + piece * third, slice(j * third, (j + 1) * third)
+            for j, product in enumerate(products):
+                at = j * width + piece * third
                 part = weight_ref[:, at : at + third].astype(f32)
-                bias_sum = bias_sum + jnp.sum(part * column_sums[:, to], axis=1, keepdims=True)
-                cross = cross + jnp.sum(part * product[:, to], axis=1, keepdims=True)
+                column_sums = jnp.sum(rights[j][...].astype(f32), axis=0, keepdims=True)
+                bias_sum = bias_sum + jnp.sum(part * column_sums, axis=1, keepdims=True)
+                cross = cross + jnp.sum(part * product, axis=1, keepdims=True)
             gain, bias = scales_ref[:, 0:1].astype(f32), scales_ref[:, 1:2].astype(f32)
             gain_sum = (cross - bias * bias_sum) / gain
             kept = jnp.concatenate(
@@ -640,6 +671,8 @@
     wide = min(512, inner)
     shard_axes = ("fz", "fx")
 
+    rest = range(1, depth)
+
     def whole_group(value, axis):
         if group == 2:
             return ordered(value, swap(value, "lo"), lo, axis)
@@ -659,10 +692,12 @@
             return swap(pick(parts, 1 - lo, 1), "lo")
         return plus(lax.psum_scatter(parts, "lo", scatter_dimension=1), -pick(parts, lo, 1))
 
+    def hop(values, parity):
+        return [along(value, "fz", depth, k) for k, value in zip(rest, values) if k % 2 == parity]
+
     fused_out = split_out and group == 2
     out_rows, half_model = own_rows // group, model // 2
     place = jnp.stack([z, x, h, lo]).astype(jnp.int32)
-    rest = range(1, depth)
     came = swap(jnp.stack([pick(tokens[:, 0], 1 - h, 0), pick(cotangent[:, 0], 1 - h, 0)]), "hi")
     vectors = jnp.stack([norm1_gain, norm1_bias, norm2_gain, norm2_bias])
     if fused_out:
@@ -785,7 +820,7 @@
         down_even = [along(down_half, "fz", depth, k) for k in rest if k % 2 == 0]
     mixed, up_last, out_weight, grad_result, down_even = sync(mixed, up_last, out_weight, grad_result, down_even)
     up_set = [both_own, side_own, up_far, up_side, up_near, *up_last]
-    lses = [lse for _, lse in mixed]
+    lse = mixed[0][1] if pieces == 1 else jnp.concatenate([part for _, part in mixed], axis=1)
 
     def leave(place_ref, given, held, made, scratch, sems):
         *parts_refs, weight = given
@@ -874,7 +909,7 @@
         hidden, slope, normed_two, down_side, down_near = sync(hidden, slope, normed_two, down_side, down_near)
         cuts, hidden = sync(halve(down_side, down_near), hidden)
         down_last = last_quarters(*cuts)
-        down_keep, down_send = outer(place, depth, hidden, grad_result)
+        down_keep, down_send = outer(place, depth, far(hidden), grad_result)
         hidden, slope, down_keep, down_send, normed_two, down_last = sync(
             hidden, slope, down_keep, down_send, normed_two, down_last
         )
@@ -882,6 +917,7 @@
         down_came = swap(down_send[0], "fx"), swap(down_send[1], "hi")
     else:
         down_keep = down_came = outer_whole(hidden, grad_result)
+        down_send = None
 
     def narrow(place_ref, given, held, made, scratch, sems):
         hidden_ref, grad_ref, slope_ref, *downs = given
@@ -926,24 +962,26 @@
         2 * copies,
         18,
     )
-    result, grad_pre, back, normed_two, down_keep, down_came = sync(
-        result, grad_pre, back, normed_two, down_keep, down_came
+    down_kept = None
+    if fine_down:
+        down_kept, down_send = fold_one(place, down_keep, down_came, far_shape)
+    result, grad_pre, back, normed_two, down_kept, down_send, down_came = sync(
+        result, grad_pre, back, normed_two, down_kept, down_send, down_came
     )
 
     back_other = other_part(back)
     result_other = other_own(result)
     if fine_down:
-        down_kept, down_send = fold_one(place, down_keep, down_came)
-        down_kept, down_send, normed_two, grad_pre = sync(down_kept, down_send, normed_two, grad_pre)
         down_came = swap(down_send[0], "hi"), swap(down_send[1], "fx")
     up_keep, up_send = outer(place, depth, far(normed_two), far(grad_pre))
-    back, back_other, up_keep, up_send, result_other, down_came = sync(
-        back, back_other, up_keep, up_send, result_other, down_came
+    output = (own_chunks(middle) + own_chunks(result).astype(f32) + result_other.astype(f32)).astype(bf16)
+    back, back_other, up_keep, up_send, down_came, output = sync(
+        back, back_other, up_keep, up_send, down_came, output
     )
     if fine_down:
         down_sum, down_send = fold_two(place, down_kept, down_came)
         down_send, back, back_other, up_send = sync(down_send, back, back_other, up_send)
-        down_came = [along(value, "fz", depth, k) for k, value in zip(rest, down_send)]
+        down_came = hop(down_send, 1)
 
     def between(place_ref, given, held, made, scratch, sems):
         grad_ref, own_ref, other_ref, middle_ref, scales_ref, weight = given
@@ -988,69 +1026,53 @@
         1,
         8,
     )
-    grad_joints = [attend_back(joint, grad_attended, lses[0], seg_col, seg_row, 0, count)]
+    if fine_down:
+        grad_attended, down_came, down_send = sync(grad_attended, down_came, down_send)
+        down_came = down_came + hop(down_send, 0)
+    grad_joint = attend_back(joint, grad_attended, lse, seg_col, seg_row, 0, pairs)
     up_came = swap(up_send[0], "fx"), swap(up_send[1], "hi")
-    output = (own_chunks(middle) + own_chunks(result).astype(f32) + result_other.astype(f32)).astype(bf16)
-    grad_joints, grad_attended, grad_branch, up_came, output, down_came = sync(
-        grad_joints, grad_attended, grad_branch, up_came, output, down_came
+    output_came = swap(pick(output, 1 - h, 0), "hi")
+    if fine_down:
+        down_came = add_up(down_sum, down_came)
+    grad_joint, grad_branch, up_came, output_came, down_came = sync(
+        grad_joint, grad_branch, up_came, output_came, down_came
     )
 
     def both_halves(value):
         return ordered(value, swap(value, "hi"), h, 1).reshape(-1, value.shape[2])
 
-    norm_parts = dict(weight=joint_weight, scales=scale_columns)
     up_kept, up_send = fold_one(place, up_keep, up_came)
-    up_kept, up_send, grad_joints, output = sync(up_kept, up_send, grad_joints, output)
+    up_kept, up_send, grad_joint = sync(up_kept, up_send, grad_joint)
     up_came = swap(up_send[0], "hi"), swap(up_send[1], "fx")
     if fine_down:
-        down_own = both_halves(add_up(down_sum, down_came))
+        down_own = both_halves(down_came)
     else:
         down_own = lax.psum(lax.psum_scatter(down_came, shard_axes, scatter_dimension=0, tiled=True), "hi")
-    one_keep, one_send = outer(
+    last_keep, last_send = outer(
         place,
         depth,
         normed,
-        grad_joints[0],
+        grad_joint,
         out_pair=[attended, grad_branch] if fused_out else None,
+        weight=joint_weight,
+        scales=scale_columns,
         sums=sums_two,
-        **norm_parts,
-    )
-    up_came, one_keep, one_send, grad_attended, output, down_own = sync(
-        up_came, one_keep, one_send, grad_attended, output, down_own
+    )
+    up_came, last_keep, last_send, down_own, grad_joint = sync(
+        up_came, last_keep, last_send, down_own, grad_joint
     )
 
     up_sum, up_send = fold_two(place, up_kept, up_came)
-    up_sum, up_send, grad_attended, one_send = sync(up_sum, up_send, grad_attended, one_send)
-    for piece in range(1, pieces):
-        grad_joints.append(
-            attend_back(joint, grad_attended, lses[piece], seg_col, seg_row, piece * count, count)
-        )
-    one_came = swap(one_send[0], "fx"), swap(one_send[1], "hi")
+    up_sum, up_send, last_send, grad_joint = sync(up_sum, up_send, last_send, grad_joint)
+    last_came = swap(last_send[0], "fx"), swap(last_send[1], "hi")
     up_came = [along(value, "fz", depth, k) for k, value in zip(rest, up_send)]
-    grad_joints, up_came, one_keep, one_came, up_sum, down_own, output = sync(
-        grad_joints, up_came, one_keep, one_came, up_sum, down_own, output
-    )
-
-    one_kept, one_send = fold_one(place, one_keep, one_came)
-    two_came = None
-    if pieces == 2:
-        two_keep, two_send = outer(
-            place, depth, normed, grad_joints[1], piece=1, sums=jnp.zeros_like(sums_two), **norm_parts
-        )
-        two_send, grad_joints, one_send = sync(two_send, grad_joints, one_send)
-        two_came = swap(two_send[0], "fx"), swap(two_send[1], "hi")
-    one_came = swap(one_send[0], "hi"), swap(one_send[1], "fx")
 
     def enter(place_ref, given, held, made, scratch, sems):
-        *parts_refs, weight = given
+        part_ref, weight = given
         (out_ref,) = made
         grads = jnp.zeros(out_ref.shape, f32)
-        for piece, part_ref in enumerate(parts_refs):
-            for j in range(3):
-                at = j * head_columns + piece * part_columns
-                grads = grads + mm_cols(
-                    part_ref[:, j * part_columns : (j + 1) * part_columns], weight[:, at : at + part_columns]
-                )
+        for j in range(3):
+            grads = grads + mm_cols(part_ref[j], weight[:, j * head_columns : (j + 1) * head_columns])
         out_ref[...] = grads.astype(bf16)
 
     (entered,) = weight_call(
@@ -1058,59 +1080,58 @@
         enter,
         tiles,
         place,
-        [(value, row_block(tile, 3 * part_columns)) for value in grad_joints]
-        + [(joint_weight, whole_block(*joint_weight.shape))],
+        [
+            (grad_joint, pl.BlockSpec((3, tile, head_columns), lambda i: (0, i, 0))),
+            (joint_weight, whole_block(*joint_weight.shape)),
+        ],
         [],
         [(shape_of(rows, model), row_block(tile, model))],
         [],
         1,
         14,
     )
-    two_came, one_came, entered, output, up_sum, up_came, down_own = sync(
-        two_came, one_came, entered, output, up_sum, up_came, down_own
-    )
-
-    if pieces == 2:
-        two_kept, two_send = fold_one(place, two_keep, two_came)
-        two_came = swap(two_send[0], "hi"), swap(two_send[1], "fx")
-    one_sum, one_send = fold_two(place, one_kept, one_came)
-    one_came = [along(value, "fz", depth, k) for k, value in zip(rest, one_send)]
-    output_came = swap(pick(output, 1 - h, 0), "hi")
+    output = ordered(pick(output, h, 0), output_came, h, 0)[:, None]
+    last_came, entered, up_sum, up_came, down_own, output = sync(
+        last_came, entered, up_sum, up_came, down_own, output
+    )
+
+    last_kept, last_send = fold_one(place, last_keep, last_came)
+    up_own = add_up(up_sum, up_came)
+    last_kept, last_send, entered, up_own, down_own = sync(last_kept, last_send, entered, up_own, down_own)
+    last_came = swap(last_send[0], "hi"), swap(last_send[1], "fx")
     entered_other = other_own(entered)
     grad_normed = own_chunks(entered).astype(f32) + entered_other.astype(f32)
     unit_own, inverse_own = unit_of(own_chunks(inputs).astype(f32))
     grad_tokens = own_chunks(grad_middle) + unit_back(grad_normed * scales[0], unit_own, inverse_own)
-    two_came, one_came, output_came, grad_tokens, up_sum, up_came, down_own = sync(
-        two_came, one_came, output_came, grad_tokens, up_sum, up_came, down_own
-    )
-
-    if pieces == 2:
-        two_sum, two_send = fold_two(place, two_kept, two_came)
-        two_came = [along(value, "fz", depth, k) for k, value in zip(rest, two_send)]
-    up_own = both_halves(add_up(up_sum, up_came))
-    grad_came = swap(pick(grad_tokens, 1 - h, 0).astype(bf16), "hi")
+    grad_sent = pick(grad_tokens, 1 - h, 0).astype(bf16)
+    last_came, grad_tokens, grad_sent, up_own, down_own = sync(last_came, grad_tokens, grad_sent, up_own, down_own)
+
+    last_sum, last_send = fold_two(place, last_kept, last_came)
+    last_came = [along(value, "fz", depth, k) for k, value in zip(rest, last_send)]
+    grad_came = swap(grad_sent, "hi")
+    up_own = both_halves(up_own)
     down_all = whole_group(down_own, 0).reshape(-1, model).astype(f32)
-    two_came, grad_tokens, grad_came, one_came, up_own = sync(two_came, grad_tokens, grad_came, one_came, up_own)
-
-    owns = [both_halves(add_up(one_sum, one_came))]
-    if pieces == 2:
-        owns.append(both_halves(add_up(two_sum, two_came)))
-    output = ordered(pick(output, h, 0), output_came, h, 0)[:, None]
+    up_all = None
+    if fused_out:
+        up_all = finish_up(place, shards, up_own, swap(up_own, "lo"))
+    last_came, grad_came, grad_tokens, up_own, up_all, down_all = sync(
+        last_came, grad_came, grad_tokens, up_own, up_all, down_all
+    )
+
+    last_own = both_halves(add_up(last_sum, last_came))
     grad_tokens = ordered(pick(grad_tokens, h, 0), grad_came.astype(f32), h, 0)[:, None]
     if fused_out:
-        up_all = finish_up(place, shards, up_own, swap(up_own, "lo"))
-        qkv_all, out_all, sums = finish_qkv(place, owns, [swap(own, "lo") for own in owns])
+        qkv_all, out_all, sums = finish_qkv(place, 3 * head_columns, [last_own], [swap(last_own, "lo")])
     else:
         up_all = whole_group(up_own.reshape(own_rows, shards, -1), 2).reshape(own_rows, -1).astype(f32)
-        columns = 3 * part_columns
-        qkv_own = jnp.concatenate([own[:, :columns].reshape(own_rows, 3, part_columns) for own in owns], axis=2)
+        columns = 3 * head_columns
+        qkv_own = last_own[:, :columns]
         if split_out:
             qkv_all = whole_group(qkv_own.reshape(own_rows, 3, shards, -1), 3)
         else:
-            qkv_all = whole_group(qkv_own, 2)
+            qkv_all = whole_group(qkv_own.reshape(own_rows, 3, -1), 2)
         qkv_all = qkv_all.reshape(own_rows, -1).astype(f32)
-        sums = sum(own[:, columns : columns + 4].astype(f32) for own in owns)
-        sums = jnp.sum(whole_group(sums, 0), axis=0).T
+        sums = jnp.sum(whole_group(last_own[:, columns : columns + 4].astype(f32), 0), axis=0).T
         grad_out = outer_whole(attended, grad_branch)
         if not split_out:
             empty = jnp.zeros((model, model), bf16)

time: 375 us -> 353 us (0.941)
  Pallas kernels: 149 us -> 132 us
  waiting for transfers between devices: 119 us -> 130 us
  starting transfers between devices: 66.1 us -> 57.3 us
  local copies, waits for them, and re-layouts: 18.3 us -> 12.5 us
    ppermute x21 -> x18, waiting for transfers between devices: 67 us -> 83.3 us  [along(): lax.ppermute(value, axis, [(i, (i + step) % depth) for i in range(depth)])]
    pallas_call x2 -> x1, Pallas kernels: 27.8 us -> 18.8 us  [attend_back(): pl.pallas_call(functools.partial(attend_back_kernel, spans, tile), grid=(...]
    unnamed x112 -> x100, local copies, waits for them, and re-layouts: 12.5 us -> 5.15 us
    pallas_call x2, Pallas kernels: 19.4 us -> 12.4 us  [attend(): pl.pallas_call(functools.partial(attend_kernel, spans, tile), grid=(count...]
    ppermute x47 -> x41, waiting for transfers between devices: 52.4 us -> 47 us  [swap(): return lax.ppermute(value, axis, SWAP)]
    ppermute x47 -> x41, starting transfers between devices: 43.6 us -> 38.3 us  [swap(): return lax.ppermute(value, axis, SWAP)]
    ppermute x21 -> x18, starting transfers between devices: 22.4 us -> 19.1 us  [along(): lax.ppermute(value, axis, [(i, (i + step) % depth) for i in range(depth)])]
    pallas_call x4 -> x3, Pallas kernels: 25.1 us -> 23.6 us  [outer(): pl.pallas_call(kernel, grid=(depth,), in_specs=[pl.BlockSpec(memory_space...]
  transfers between devices with their start and end apart: 68 -> 59, of which waited for: 27 -> 30; matrix products, arithmetic and copies ran while one was open for 5% -> 5% of each run, Pallas kernels for 36% -> 34%
where the time goes in v5:
time: 353 us; the launch traced here: 350 us
  Pallas kernels  132 us (37%)
  waiting for transfers between devices  130 us (37%)
  starting transfers between devices  57.3 us (16%)
  other arithmetic  15.8 us (4%)
  local copies, waits for them, and re-layouts  12.5 us (4%)
    ppermute x18, waiting for transfers between devices, along(): lax.ppermute(value, axis, [(i, (i + step) % depth) for i in range(depth)])  83.3 us
    pallas_call x6, Pallas kernels, weight_call(): pl.pallas_call(kernel, grid=(tiles,), in_specs=[pl.BlockSpec(memory_space...  61 us
    ppermute x41, waiting for transfers between devices, swap(): return lax.ppermute(value, axis, SWAP)  47 us
    ppermute x41, starting transfers between devices, swap(): return lax.ppermute(value, axis, SWAP)  38.3 us
    pallas_call x3, Pallas kernels, outer(): pl.pallas_call(kernel, grid=(depth,), in_specs=[pl.BlockSpec(memory_space...  23.6 us
    ppermute x18, starting transfers between devices, along(): lax.ppermute(value, axis, [(i, (i + step) % depth) for i in range(depth)])  19.1 us
    pallas_call x1, Pallas kernels, attend_back(): pl.pallas_call(functools.partial(attend_back_kernel, spans, tile), grid=(...  18.8 us
    pallas_call x2, Pallas kernels, attend(): pl.pallas_call(functools.partial(attend_kernel, spans, tile), grid=(count...  12.4 us
  transfers between devices with their start and end apart: 59, of which 30 were waited for; matrix products, arithmetic and copies ran while one was open for 5% of the time, Pallas kernels for 34%

profile of v5, /device:TPU:9, one launch (start us, length us, event | category | flops | bytes accessed | tf_op | source)
XLA Modules:
  0.0 349.8 jit_solution(5417293767575718136)
XLA Ops:
  1.5 2.0 prepare.1
  3.5 1.3 collective-permute-start.3
  4.8 1.3 dynamic-slice_bitcast_fusion.4
  6.2 1.3 collective-permute-start.4
  7.5 1.3 collective-permute-start
  9.8 1.5 collective-permute-start.2
  11.3 3.2 collective-permute-done
  14.5 16.9 %collective-permute-done.1 = bf16[64,2176]{1,0:T(8,128)(2,1)S(1)} collective-permute-done((bf16[64,2176]{1,0:T(8,128)(2,1)S(1)}, bf16[64,2176]{1,0:T(8,128)(2,1)S(1)}, u32[]{:S(2)}, u32[]{:S(2)}) %collective-permute-start.1) | collective-permute-done | bytes 278560 | tf_op jit(solution)/shard_map/ppermute | solution.py:250
  31.4 3.5 collective-permute-done.2
  37.4 1.5 collective-permute-start.9
  39.7 4.5 %collective-permute-done.7 = bf16[64,2048]{1,0:T(8,128)(2,1)} collective-permute-done((bf16[64,2048]{1,0:T(8,128)(2,1)S(1)}, bf16[64,2048]{1,0:T(8,128)(2,1)}, u32[]{:S(2)}, u32[]{:S(2)}) %collective-permute-start.7) | collective-permute-done | bytes 262176 | tf_op jit(solution)/shard_map/ppermute | solution.py:250
  44.2 14.9 %collective-permute-done.8 = bf16[64,2048]{1,0:T(8,128)(2,1)} collective-permute-done((bf16[64,2048]{1,0:T(8,128)(2,1)S(1)}, bf16[64,2048]{1,0:T(8,128)(2,1)}, u32[]{:S(2)}, u32[]{:S(2)}) %collective-permute-start.8) | collective-permute-done | bytes 262176 | tf_op jit(solution)/shard_map/ppermute | solution.py:250
  59.1 1.7 collective-permute-done.9
  64.0 1.3 collective-permute-start.10
  67.3 1.2 pad_maximum_fusion.8.refs_6_.refs_5_
  68.6 1.6 select_bitcast_fusion.3
  70.6 4.8 %collective-permute-done.10.refs_6_ = bf16[3,32,2176]{2,1,0:T(8,128)(2,1)S(1)} collective-permute-done((bf16[3,32,2176]{2,1,0:T(8,128)(2,1)}, bf16[3,32,2176]{2,1,0:T(8,128)(2,1)S(1)}, u32[]{:S(2)}, u32[]{:S(2)}) %collective-permute-start.10) | collective-permute-done | bytes 417824 | tf_op jit(solution)/shard_map/ppermute | solution.py:56
  77.8 2.0 collective-permute-start.16
  80.2 10.2 %project.1 = (bf16[1024,1024]{1,0:T(8,128)(2,1)}, bf16[1024,1536]{1,0:T(8,128)(2,1)}, f32[8,1024]{1,0:T(8,128)S(1)}, bf16[1024,1536]{1,0:T(8,128)(2,1)S(1)}, bf1...) custom-call(s32[4]{0:T(128)S(1)} %pad_add_fusion.place_ref, bf16[1024,1024]{1,0:T(8,128)(2,1)S(1)} %bitcast.155, ...), custom_call_target="tpu_custom_call" | custom-call | flops 8800000000 | bytes 1000 | tf_op jit(solution)/shard_map/project/pallas_call | solution.py:508
  90.4 6.5 %attend.2 = (bf16[1024,256]{1,0:T(8,128)(2,1)S(1)}, f32[1024,256]{1,0:T(8,128)S(1)}) custom-call(bf16[1024,1536]{1,0:T(8,128)(2,1)} %get-tuple-element.274.q_ref.k_ref.v_ref, bf16[1024,1536]{1,0:T(8,128)(2,1)} %get-tuple-element.274.q_ref.k_ref.v_ref, bf16[1024,1536]{1,0:T(8,128)(2,1)} %get-tuple-element.274.q_ref.k_ref.v_ref, s32[1024,1]{1,0:T(8,128)S(1)} %copy-done.6, ...), custom_call_target="tpu_custom_call" | custom-call | flops 8800000000 | bytes 1000 | tf_op jit(solution)/shard_map/attend/pallas_call | solution.py:142
  97.0 8.4 %collective-permute-done.17.refs_11_ = bf16[2,128,1024]{2,1,0:T(8,128)(2,1)S(1)} collective-permute-done((bf16[2,128,1024]{2,1,0:T(8,128)(2,1)S(1)}, bf16[2,128,1024]{2,1,0:T(8,128)(2,1)S(1)}, u32[]{:S(2)}, u32[]{:S(2)}) %collective-permute-start.17) | collective-permute-done | bytes 524320 | tf_op jit(solution)/shard_map/ppermute | solution.py:56
  106.8 2.2 collective-permute-start.20
  110.5 2.6 collective-permute-start.21
  113.1 5.8 %attend.3 = (bf16[1024,256]{1,0:T(8,128)(2,1)S(1)}, f32[1024,256]{1,0:T(8,128)S(1)}) custom-call(bf16[1024,1536]{1,0:T(8,128)(2,1)} %get-tuple-element.274.q_ref.k_ref.v_ref, bf16[1024,1536]{1,0:T(8,128)(2,1)} %get-tuple-element.274.q_ref.k_ref.v_ref, bf16[1024,1536]{1,0:T(8,128)(2,1)} %get-tuple-element.274.q_ref.k_ref.v_ref, s32[1024,1]{1,0:T(8,128)S(1)} %copy-done.6, ...), custom_call_target="tpu_custom_call" | custom-call | flops 8800000000 | bytes 1000 | tf_op jit(solution)/shard_map/attend/pallas_call | solution.py:142
  120.2 2.1 collective-permute-done.21
  122.3 2.4 leave.1
  127.8 2.2 collective-permute-done.22.refs_2_
  129.9 13.9 %widen.1 = (f32[1024,1024]{1,0:T(8,128)}, bf16[1024,1024]{1,0:T(8,128)(2,1)}, bf16[1024,2048]{1,0:T(8,128)(2,1)}, bf16[1024,2048]{1,0:T(8,128)(2,1)}) custom-call(s32[4]{0:T(128)S(1)} %pad_add_fusion.place_ref, bf16[1024,1024]{1,0:T(8,128)(2,1)S(1)} %bitcast.156, bf16[1024,1024]{1,0:T(8,128)(2,1)S(1)} %get-tuple-element.285.refs_1_, ...), custom_call_target="tpu_custom_call" | custom-call | flops 14300000256 | bytes 1000 | tf_op jit(solution)/shard_map/widen/pallas_call | solution.py:508
  143.8 1.7 collective-permute-done.23.side_ref.refs_13_
  147.8 6.6 %outer.3 = (bf16[4,128,1024]{2,1,0:T(8,128)(2,1)S(1)}, bf16[4,128,1024]{2,1,0:T(8,128)(2,1)S(1)}, bf16[4,2,64,1024]{3,2,1,0:T(8,128)(2,1)S(1)}, bf16[4,2,64,1024]{3,2,1,0:T(8,128)(2,1)S(1)}) custom-call(s32[4]{0:T(128)S(1)} %pad_add_fusion.place_ref, bf16[1024,2048]{1,0:T(8,128)(2,1)} %get-tuple-element.310.refs_0_, bf16[1024,1024]{1,0:T(8,128)(2,1)S(1)} %bitcast.160), custom_call_target="tpu_custom_call" | custom-call | flops 6600000000 | bytes 1000 | tf_op jit(solution)/shard_map/outer/pallas_call | solution.py:629
  157.4 20.7 %narrow.1 = (bf16[1024,1024]{1,0:T(8,128)(2,1)}, bf16[1024,2048]{1,0:T(8,128)(2,1)}, bf16[1024,1024]{1,0:T(8,128)(2,1)}) custom-call(s32[4]{0:T(128)S(1)} %pad_add_fusion.place_ref, bf16[1024,2048]{1,0:T(8,128)(2,1)} %get-tuple-element.310.refs_0_, bf16[1024,1024]{1,0:T(8,128)(2,1)} %bitcast.161, bf16[1024,2048]{1,0:T(8,128)(2,1)} %get-tuple-element.311.refs_2_, ...), custom_call_target="tpu_custom_call" | custom-call | flops 19800000512 | bytes 1000 | tf_op jit(solution)/shard_map/narrow/pallas_call | solution.py:508
  179.1 2.6 fold_one.3
  181.7 3.5 %collective-permute-start.29 = (bf16[1024,1024]{1,0:T(8,128)(2,1)}, bf16[1024,1024]{1,0:T(8,128)(2,1)}, u32[]{:S(2)}, u32[]{:S(2)}) collective-permute-start(bf16[1024,1024]{1,0:T(8,128)(2,1)} %get-tuple-element.349.refs_1_), channel_id=1, source_target_pairs={{0,8},{8,0},{1,9},{9,1},{2,10},{10,2},{3,11},{11,3},{4,12},{12,4},... | collective-permute-start | bytes 6291464 | tf_op jit(solution)/shard_map/ppermute | solution.py:56
  185.3 1.4 dynamic-slice_bitcast_fusion.1
  188.5 8.0 %outer.4 = (bf16[4,64,2048]{2,1,0:T(8,128)(2,1)S(1)}, bf16[4,64,2048]{2,1,0:T(8,128)(2,1)S(1)}, bf16[4,2,32,2048]{3,2,1,0:T(8,128)(2,1)S(1)}, bf16[4,2,32,2048]{3,2,1,0:T(8,128)(2,1)S(1)}) custom-call(s32[4]{0:T(128)S(1)} %pad_add_fusion.place_ref, bf16[1024,1024]{1,0:T(8,128)(2,1)} %get-tuple-element.327.refs_0_, bf16[1024,2048]{1,0:T(8,128)(2,1)} %get-tuple-element.328.refs_1_), custom_call_target="tpu_custom_call" | custom-call | flops 6600000000 | bytes 1000 | tf_op jit(solution)/shard_map/outer/pallas_call | solution.py:629
  197.0 4.2 %collective-permute-done.30.came_one = bf16[4,64,1024]{2,1,0:T(8,128)(2,1)S(1)} collective-permute-done((bf16[4,64,1024]{2,1,0:T(8,128)(2,1)S(1)}, bf16[4,64,1024]{2,1,0:T(8,128)(2,1)S(1)}, u32[]{:S(2)}, u32[]{:S(2)}) %collective-permute-start.30) | collective-permute-done | bytes 524320 | tf_op jit(solution)/shard_map/ppermute | solution.py:56
  202.4 1.5 collective-permute-start.34
  205.8 8.8 %between.1 = (f32[1024,1024]{1,0:T(8,128)}, bf16[1024,1024]{1,0:T(8,128)(2,1)}, bf16[1024,512]{1,0:T(8,128)(2,1)S(1)}, f32[8,1024]{1,0:T(8,128)S(1)}) custom-call(s32[4]{0:T(128)S(1)} %pad_add_fusion.place_ref, bf16[1024,1024]{1,0:T(8,128)(2,1)S(1)} %bitcast.162, bf16[1024,1024]{1,0:T(8,128)(2,1)} %get-tuple-element.349.refs_1_, ...), custom_call_target="tpu_custom_call" | custom-call | flops 8800000000 | bytes 1000 | tf_op jit(solution)/shard_map/between/pallas_call | solution.py:508
  214.6 3.3 collective-permute-done.34
  217.9 18.8 %attend_back.1.refs_1_.refs_0_ = bf16[3,1024,512]{2,1,0:T(8,128)(2,1)S(1)} custom-call(bf16[1024,1536]{1,0:T(8,128)(2,1)} %get-tuple-element.274.q_ref.k_ref.v_ref, bf16[1024,1536]{1,0:T(8,128)(2,1)} %get-tuple-element.274.q_ref.k_ref.v_ref, bf16[1024,1536]{1,0:T(8,128)(2,1)} %get-tuple-element.274.q_ref.k_ref.v_ref, ...), custom_call_target="tpu_custom_call" | custom-call | flops 26400000000 | bytes 1000 | tf_op jit(solution)/shard_map/attend_back/pallas_call | solution.py:216
  239.3 1.3 fold_one.4
  242.2 9.1 %outer.5 = (bf16[4,64,2176]{2,1,0:T(8,128)(2,1)S(1)}, bf16[4,64,2176]{2,1,0:T(8,128)(2,1)S(1)}, bf16[4,2,32,2176]{3,2,1,0:T(8,128)(2,1)S(1)}, bf16[4,2,32,2176]{3,2,1,0:T(8,128)(2,1)S(1)}) custom-call(s32[4]{0:T(128)S(1)} %pad_add_fusion.place_ref, bf16[1024,1024]{1,0:T(8,128)(2,1)S(1)} %copy-done.20, bf16[3,1024,512]{2,1,0:T(8,128)(2,1)S(1)} %attend_back.1.refs_1_.refs_0_, ...), custom_call_target="tpu_custom_call" | custom-call | flops 6600000000 | bytes 1000 | tf_op jit(solution)/shard_map/outer/pallas_call | solution.py:629
  252.6 1.8 collective-permute-done.39.came_one
  255.4 1.2 collective-permute-start.42
  257.6 2.5 collective-permute-start.44
  260.1 2.6 collective-permute-start.45
  262.7 5.1 %enter.1 = bf16[1024,1024]{1,0:T(8,128)(2,1)S(1)} custom-call(s32[4]{0:T(128)S(1)} %pad_add_fusion.place_ref, bf16[3,1024,512]{2,1,0:T(8,128)(2,1)S(1)} %attend_back.1.refs_1_.refs_0_, bf16[1024,1536]{1,0:T(8,128)(2,1)S(1)} %copy-done.19), custom_call_target="tpu_custom_call" | custom-call | flops 15399999488 | bytes 1000 | tf_op jit(solution)/shard_map/enter/pallas_call | solution.py:508
  267.8 12.1 %collective-permute-done.45 = bf16[2,32,2048]{2,1,0:T(8,128)(2,1)S(1)} collective-permute-done((bf16[2,32,2048]{2,1,0:T(8,128)(2,1)S(1)}, bf16[2,32,2048]{2,1,0:T(8,128)(2,1)S(1)}, u32[]{:S(2)}, u32[]{:S(2)}) %collective-permute-start.45) | collective-permute-done | bytes 262176 | tf_op jit(solution)/shard_map/ppermute | solution.py:250
  279.9 4.6 %collective-permute-done.46 = bf16[2,32,2048]{2,1,0:T(8,128)(2,1)S(1)} collective-permute-done((bf16[2,32,2048]{2,1,0:T(8,128)(2,1)S(1)}, bf16[2,32,2048]{2,1,0:T(8,128)(2,1)S(1)}, u32[]{:S(2)}, u32[]{:S(2)}) %collective-permute-start.46) | collective-permute-done | bytes 262176 | tf_op jit(solution)/shard_map/ppermute | solution.py:250
  284.7 1.4 fold_one.5
  286.2 1.5 collective-permute-start.49
  292.7 9.9 %collective-permute-done.47.came_one = bf16[4,32,2176]{2,1,0:T(8,128)(2,1)S(1)} collective-permute-done((bf16[4,32,2176]{2,1,0:T(8,128)(2,1)S(1)}, bf16[4,32,2176]{2,1,0:T(8,128)(2,1)S(1)}, u32[]{:S(2)}, u32[]{:S(2)}) %collective-permute-start.47) | collective-permute-done | bytes 557088 | tf_op jit(solution)/shard_map/ppermute | solution.py:56
  303.8 1.4 collective-permute-start.56
  306.3 2.6 collective-permute-start.51
  310.7 2.4 collective-permute-start.55
  313.2 1.6 bitcast_convert_fusion
  314.9 2.7 finish_up.1
  317.6 12.7 %collective-permute-done.51 = bf16[2,32,2176]{2,1,0:T(8,128)(2,1)} collective-permute-done((bf16[2,32,2176]{2,1,0:T(8,128)(2,1)S(1)}, bf16[2,32,2176]{2,1,0:T(8,128)(2,1)}, u32[]{:S(2)}, u32[]{:S(2)}) %collective-permute-start.51) | collective-permute-done | bytes 278560 | tf_op jit(solution)/shard_map/ppermute | solution.py:250
  330.3 3.8 %collective-permute-done.52 = bf16[2,32,2176]{2,1,0:T(8,128)(2,1)} collective-permute-done((bf16[2,32,2176]{2,1,0:T(8,128)(2,1)S(1)}, bf16[2,32,2176]{2,1,0:T(8,128)(2,1)}, u32[]{:S(2)}, u32[]{:S(2)}) %collective-permute-start.52) | collective-permute-done | bytes 278560 | tf_op jit(solution)/shard_map/ppermute | solution.py:250
  334.1 1.3 add_convert_fusion
  335.5 7.7 %collective-permute-done.57 = bf16[2,32,2176]{2,1,0:T(8,128)(2,1)S(1)} collective-permute-done((bf16[2,32,2176]{2,1,0:T(8,128)(2,1)S(1)}, bf16[2,32,2176]{2,1,0:T(8,128)(2,1)S(1)}, u32[]{:S(2)}, u32[]{:S(2)}) %collective-permute-start.57) | collective-permute-done | bytes 278560 | tf_op jit(solution)/shard_map/ppermute | solution.py:56
  343.4 1.4 collective-permute-start.58
  345.1 1.6 maximum_bitcast_fusion
  346.7 2.3 finish_qkv.1
  (233 shorter events, 50.4 us)
Async XLA Ops:
  0.6 38.2 %copy-start = (bf16[512,1024]{1,0:T(8,128)(2,1)S(1)}, bf16[512,1024]{1,0:T(8,128)(2,1)}, u32[]{:S(2)}) copy-start(bf16[512,1024]{1,0:T(8,128)(2,1)} %param.20) | copy-start | bytes 3145732
  0.7 304.5 %copy-start.8 = (s32[4]{0:T(128)}, s32[4]{0:T(128)S(1)}, u32[]{:S(2)}) copy-start(s32[4]{0:T(128)S(1)} %pad_add_fusion.place_ref) | copy-start | bytes 52
  3.5 31.4 %collective-permute-start.3 = (bf16[2,64,4224]{2,1,0:T(8,128)(2,1)S(1)}, bf16[2,64,4224]{2,1,0:T(8,128)(2,1)}, u32[]{:S(2)}, u32[]{:S(2)}) collective-permute-start(bf16[2,64,4224]{2,1,0:T(8,128)(2,1)S(1)} %get-tuple-element.229.refs_1_.refs_4_.refs_3_), channel_id=1, source_target_pairs={{0,1},{1,0},{2,3},{3,2},{4,5},{5,4},{6,7},{7,6},{8,9},{9,8},{10,11... | collective-permute-start | bytes 3244040 | tf_op jit(solution)/shard_map/ppermute | solution.py:56
  6.2 28.7 %collective-permute-start.4 = (bf16[2,256,1024]{2,1,0:T(8,128)(2,1)S(1)}, bf16[2,256,1024]{2,1,0:T(8,128)(2,1)S(1)}, u32[]{:S(2)}, u32[]{:S(2)}) collective-permute-start(bf16[2,256,1024]{2,1,0:T(8,128)(2,1)S(1)} %pad_maximum_fusion.3), channel_id=1, source_target_pairs={{0,16},{16,0},{1,17},{17,1},{2,18},{18,2},{3,19},{19,3},{4,20},{20... | collective-permute-start | bytes 3145736 | tf_op jit(solution)/shard_map/ppermute | solution.py:56
  7.5 7.0 %collective-permute-start = (bf16[64,2176]{1,0:T(8,128)(2,1)S(1)}, bf16[64,2176]{1,0:T(8,128)(2,1)S(1)}, u32[]{:S(2)}, u32[]{:S(2)}) collective-permute-start(bf16[64,2176]{1,0:T(8,128)(2,1)S(1)} %get-tuple-element.228), channel_id=1, source_target_pairs={{0,2},{2,4},{4,6},{6,0},{1,3},{3,5},{5,7},{7,1},{8,10},{10,12},{12... | collective-permute-start | bytes 835592 | tf_op jit(solution)/shard_map/ppermute | solution.py:250
  8.8 22.6 %collective-permute-start.1 = (bf16[64,2176]{1,0:T(8,128)(2,1)S(1)}, bf16[64,2176]{1,0:T(8,128)(2,1)S(1)}, u32[]{:S(2)}, u32[]{:S(2)}) collective-permute-start(bf16[64,2176]{1,0:T(8,128)(2,1)S(1)} %get-tuple-element.228), channel_id=1, source_target_pairs={{0,4},{2,6},{4,0},{6,2},{1,5},{3,7},{5,1},{7,3},{8,12},{10,14},{12... | collective-permute-start | bytes 835592 | tf_op jit(solution)/shard_map/ppermute | solution.py:250
  9.8 25.1 %collective-permute-start.2 = (bf16[64,2176]{1,0:T(8,128)(2,1)S(1)}, bf16[64,2176]{1,0:T(8,128)(2,1)S(1)}, u32[]{:S(2)}, u32[]{:S(2)}) collective-permute-start(bf16[64,2176]{1,0:T(8,128)(2,1)S(1)} %get-tuple-element.228), channel_id=1, source_target_pairs={{0,6},{2,0},{4,2},{6,4},{1,7},{3,1},{5,3},{7,5},{8,14},{10,8},{12,... | collective-permute-start | bytes 835592 | tf_op jit(solution)/shard_map/ppermute | solution.py:250
  36.9 24.0 %collective-permute-start.5 = (bf16[3,64,2176]{2,1,0:T(8,128)(2,1)}, bf16[3,64,2176]{2,1,0:T(8,128)(2,1)S(1)}, u32[]{:S(2)}, u32[]{:S(2)}) collective-permute-start(bf16[3,64,2176]{2,1,0:T(8,128)(2,1)} %pad_maximum_fusion.7.refs_3_), channel_id=1, source_target_pairs={{0,1},{1,0},{2,3},{3,2},{4,5},{5,4},{6,7},{7,6},{8,9},{9,8},{10,11... | collective-permute-start | bytes 2506760 | tf_op jit(solution)/shard_map/ppermute | solution.py:56
  37.2 23.7 %collective-permute-start.6 = (bf16[3,64,2176]{2,1,0:T(8,128)(2,1)}, bf16[3,64,2176]{2,1,0:T(8,128)(2,1)S(1)}, u32[]{:S(2)}, u32[]{:S(2)}) collective-permute-start(bf16[3,64,2176]{2,1,0:T(8,128)(2,1)} %pad_maximum_fusion.7.refs_3_), channel_id=1, source_target_pairs={{0,16},{16,0},{1,17},{17,1},{2,18},{18,2},{3,19},{19,3},{4,20},{20... | collective-permute-start | bytes 2506760 | tf_op jit(solution)/shard_map/ppermute | solution.py:56
  37.4 6.9 %collective-permute-start.7 = (bf16[64,2048]{1,0:T(8,128)(2,1)S(1)}, bf16[64,2048]{1,0:T(8,128)(2,1)}, u32[]{:S(2)}, u32[]{:S(2)}) collective-permute-start(bf16[64,2048]{1,0:T(8,128)(2,1)S(1)} %get-tuple-element.234), channel_id=1, source_target_pairs={{0,2},{2,4},{4,6},{6,0},{1,3},{3,5},{5,7},{7,1},{8,10},{10,12},{12... | collective-permute-start | bytes 786440 | tf_op jit(solution)/shard_map/ppermute | solution.py:250
  37.4 21.7 %collective-permute-start.8 = (bf16[64,2048]{1,0:T(8,128)(2,1)S(1)}, bf16[64,2048]{1,0:T(8,128)(2,1)}, u32[]{:S(2)}, u32[]{:S(2)}) collective-permute-start(bf16[64,2048]{1,0:T(8,128)(2,1)S(1)} %get-tuple-element.234), channel_id=1, source_target_pairs={{0,4},{2,6},{4,0},{6,2},{1,5},{3,7},{5,1},{7,3},{8,12},{10,14},{12... | collective-permute-start | bytes 786440 | tf_op jit(solution)/shard_map/ppermute | solution.py:250
  37.4 23.4 %collective-permute-start.9 = (bf16[64,2048]{1,0:T(8,128)(2,1)S(1)}, bf16[64,2048]{1,0:T(8,128)(2,1)}, u32[]{:S(2)}, u32[]{:S(2)}) collective-permute-start(bf16[64,2048]{1,0:T(8,128)(2,1)S(1)} %get-tuple-element.234), channel_id=1, source_target_pairs={{0,6},{2,0},{4,2},{6,4},{1,7},{3,1},{5,3},{7,5},{8,14},{10,8},{12,... | collective-permute-start | bytes 786440 | tf_op jit(solution)/shard_map/ppermute | solution.py:250
  62.4 6.2 %collective-permute-start.12 = (bf16[2,256,1024]{2,1,0:T(8,128)(2,1)S(1)}, bf16[2,256,1024]{2,1,0:T(8,128)(2,1)}, u32[]{:S(2)}, u32[]{:S(2)}) collective-permute-start(bf16[2,256,1024]{2,1,0:T(8,128)(2,1)S(1)} %pad_maximum_fusion.4), channel_id=1, source_target_pairs={{0,8},{8,0},{1,9},{9,1},{2,10},{10,2},{3,11},{11,3},{4,12},{12,4},... | collective-permute-start | bytes 3145736 | tf_op jit(solution)/shard_map/ppermute | solution.py:56
  64.0 11.4 %collective-permute-start.10 = (bf16[3,32,2176]{2,1,0:T(8,128)(2,1)}, bf16[3,32,2176]{2,1,0:T(8,128)(2,1)S(1)}, u32[]{:S(2)}, u32[]{:S(2)}) collective-permute-start(bf16[3,32,2176]{2,1,0:T(8,128)(2,1)} %get-tuple-element.244), channel_id=1, source_target_pairs={{0,16},{16,0},{1,17},{17,1},{2,18},{18,2},{3,19},{19,3},{4,20},{20... | collective-permute-start | bytes 1253384 | tf_op jit(solution)/shard_map/ppermute | solution.py:56
  65.3 11.1 %collective-permute-start.11 = (bf16[3,32,2176]{2,1,0:T(8,128)(2,1)}, bf16[3,32,2176]{2,1,0:T(8,128)(2,1)S(1)}, u32[]{:S(2)}, u32[]{:S(2)}) collective-permute-start(bf16[3,32,2176]{2,1,0:T(8,128)(2,1)} %get-tuple-element.245), channel_id=1, source_target_pairs={{0,1},{1,0},{2,3},{3,2},{4,5},{5,4},{6,7},{7,6},{8,9},{9,8},{10,11... | collective-permute-start | bytes 1253384 | tf_op jit(solution)/shard_map/ppermute | solution.py:56
  76.3 29.1 %collective-permute-start.13 = (bf16[3,64,2048]{2,1,0:T(8,128)(2,1)S(1)}, bf16[3,64,2048]{2,1,0:T(8,128)(2,1)S(1)}, u32[]{:S(2)}, u32[]{:S(2)}) collective-permute-start(bf16[3,64,2048]{2,1,0:T(8,128)(2,1)S(1)} %pad_maximum_fusion.8.refs_6_.refs_5_), channel_id=1, source_target_pairs={{0,1},{1,0},{2,3},{3,2},{4,5},{5,4},{6,7},{7,6},{8,9},{9,8},{10,11... | collective-permute-start | bytes 2359304 | tf_op jit(solution)/shard_map/ppermute | solution.py:56
  77.4 28.0 %collective-permute-start.14 = (bf16[3,64,2048]{2,1,0:T(8,128)(2,1)S(1)}, bf16[3,64,2048]{2,1,0:T(8,128)(2,1)S(1)}, u32[]{:S(2)}, u32[]{:S(2)}) collective-permute-start(bf16[3,64,2048]{2,1,0:T(8,128)(2,1)S(1)} %pad_maximum_fusion.8.refs_6_.refs_5_), channel_id=1, source_target_pairs={{0,16},{16,0},{1,17},{17,1},{2,18},{18,2},{3,19},{19,3},{4,20},{20... | collective-permute-start | bytes 2359304 | tf_op jit(solution)/shard_map/ppermute | solution.py:56
  77.8 19.1 %collective-permute-start.15 = (bf16[128,1024]{1,0:T(8,128)(2,1)S(1)}, bf16[128,1024]{1,0:T(8,128)(2,1)S(1)}, u32[]{:S(2)}, u32[]{:S(2)}) collective-permute-start(bf16[128,1024]{1,0:T(8,128)(2,1)S(1)} %dynamic-slice_bitcast_fusion.6), channel_id=1, source_target_pairs={{0,2},{2,4},{4,6},{6,0},{1,3},{3,5},{5,7},{7,1},{8,10},{10,12},{12... | collective-permute-start | bytes 786440 | tf_op jit(solution)/shard_map/ppermute | solution.py:250
  77.8 19.1 %collective-permute-start.16 = (bf16[128,1024]{1,0:T(8,128)(2,1)S(1)}, bf16[128,1024]{1,0:T(8,128)(2,1)S(1)}, u32[]{:S(2)}, u32[]{:S(2)}) collective-permute-start(bf16[128,1024]{1,0:T(8,128)(2,1)S(1)} %dynamic-slice_bitcast_fusion.6), channel_id=1, source_target_pairs={{0,6},{2,0},{4,2},{6,4},{1,7},{3,1},{5,3},{7,5},{8,14},{10,8},{12,... | collective-permute-start | bytes 786440 | tf_op jit(solution)/shard_map/ppermute | solution.py:250
  79.8 25.6 %collective-permute-start.17 = (bf16[2,128,1024]{2,1,0:T(8,128)(2,1)S(1)}, bf16[2,128,1024]{2,1,0:T(8,128)(2,1)S(1)}, u32[]{:S(2)}, u32[]{:S(2)}) collective-permute-start(bf16[2,128,1024]{2,1,0:T(8,128)(2,1)S(1)} %copy-done.29), channel_id=1, source_target_pairs={{0,1},{1,0},{2,3},{3,2},{4,5},{5,4},{6,7},{7,6},{8,9},{9,8},{10,11... | collective-permute-start | bytes 1572872 | tf_op jit(solution)/shard_map/ppermute | solution.py:56
  90.4 31.9 %copy-start.22 = (bf16[512,1024]{1,0:T(8,128)(2,1)}, bf16[512,1024]{1,0:T(8,128)(2,1)S(1)}, u32[]{:S(2)}) copy-start(bf16[512,1024]{1,0:T(8,128)(2,1)S(1)} %get-tuple-element.284.refs_2_.refs_5_) | copy-start | bytes 3145732
  106.8 12.2 %collective-permute-start.20 = (bf16[2,256,1024]{2,1,0:T(8,128)(2,1)S(1)}, bf16[2,256,1024]{2,1,0:T(8,128)(2,1)S(1)}, u32[]{:S(2)}, u32[]{:S(2)}) collective-permute-start(bf16[2,256,1024]{2,1,0:T(8,128)(2,1)S(1)} %pad_maximum_fusion.5), channel_id=1, source_target_pairs={{0,8},{8,0},{1,9},{9,1},{2,10},{10,2},{3,11},{11,3},{4,12},{12,4},... | collective-permute-start | bytes 3145736 | tf_op jit(solution)/shard_map/ppermute | solution.py:56
  109.0 13.2 %collective-permute-start.18 = (bf16[3,32,2048]{2,1,0:T(8,128)(2,1)S(1)}, bf16[3,32,2048]{2,1,0:T(8,128)(2,1)S(1)}, u32[]{:S(2)}, u32[]{:S(2)}) collective-permute-start(bf16[3,32,2048]{2,1,0:T(8,128)(2,1)S(1)} %get-tuple-element.277), channel_id=1, source_target_pairs={{0,16},{16,0},{1,17},{17,1},{2,18},{18,2},{3,19},{19,3},{4,20},{20... | collective-permute-start | bytes 1179656 | tf_op jit(solution)/shard_map/ppermute | solution.py:56
  109.4 12.8 %collective-permute-start.19 = (bf16[3,32,2048]{2,1,0:T(8,128)(2,1)S(1)}, bf16[3,32,2048]{2,1,0:T(8,128)(2,1)S(1)}, u32[]{:S(2)}, u32[]{:S(2)}) collective-permute-start(bf16[3,32,2048]{2,1,0:T(8,128)(2,1)S(1)} %get-tuple-element.278), channel_id=1, source_target_pairs={{0,1},{1,0},{2,3},{3,2},{4,5},{5,4},{6,7},{7,6},{8,9},{9,8},{10,11... | collective-permute-start | bytes 1179656 | tf_op jit(solution)/shard_map/ppermute | solution.py:56
  110.5 11.7 %collective-permute-start.21 = (bf16[128,1024]{1,0:T(8,128)(2,1)S(1)}, bf16[128,1024]{1,0:T(8,128)(2,1)S(1)}, u32[]{:S(2)}, u32[]{:S(2)}) collective-permute-start(bf16[128,1024]{1,0:T(8,128)(2,1)S(1)} %dynamic-slice_bitcast_fusion.6), channel_id=1, source_target_pairs={{0,4},{2,6},{4,0},{6,2},{1,5},{3,7},{5,1},{7,3},{8,12},{10,14},{12... | collective-permute-start | bytes 786440 | tf_op jit(solution)/shard_map/ppermute | solution.py:250
  120.2 27.7 %copy-start.2 = (bf16[2,2,256,1024]{3,2,1,0:T(8,128)(2,1)}, bf16[2,2,256,1024]{3,2,1,0:T(8,128)(2,1)S(1)}, u32[]{:S(2)}) copy-start(bf16[2,2,256,1024]{3,2,1,0:T(8,128)(2,1)S(1)} %pad_maximum_fusion.1) | copy-start | bytes 6291460
  125.7 4.3 %collective-permute-start.22 = (bf16[1024,1024]{1,0:T(8,128)(2,1)S(1)}, bf16[1024,1024]{1,0:T(8,128)(2,1)S(1)}, u32[]{:S(2)}, u32[]{:S(2)}) collective-permute-start(bf16[1024,1024]{1,0:T(8,128)(2,1)S(1)} %get-tuple-element.285.refs_1_), channel_id=1, source_target_pairs={{0,8},{8,0},{1,9},{9,1},{2,10},{10,2},{3,11},{11,3},{4,12},{12,4},... | collective-permute-start | bytes 6291464 | tf_op jit(solution)/shard_map/ppermute | solution.py:56
  126.3 19.2 %collective-permute-start.23 = (bf16[3,128,1024]{2,1,0:T(8,128)(2,1)S(1)}, bf16[3,128,1024]{2,1,0:T(8,128)(2,1)S(1)}, u32[]{:S(2)}, u32[]{:S(2)}) collective-permute-start(bf16[3,128,1024]{2,1,0:T(8,128)(2,1)S(1)} %pad_maximum_fusion.9.refs_12_), channel_id=1, source_target_pairs={{0,1},{1,0},{2,3},{3,2},{4,5},{5,4},{6,7},{7,6},{8,9},{9,8},{10,11... | collective-permute-start | bytes 2359304 | tf_op jit(solution)/shard_map/ppermute | solution.py:56
  126.7 18.8 %collective-permute-start.24 = (bf16[3,128,1024]{2,1,0:T(8,128)(2,1)S(1)}, bf16[3,128,1024]{2,1,0:T(8,128)(2,1)S(1)}, u32[]{:S(2)}, u32[]{:S(2)}) collective-permute-start(bf16[3,128,1024]{2,1,0:T(8,128)(2,1)S(1)} %pad_maximum_fusion.9.refs_12_), channel_id=1, source_target_pairs={{0,16},{16,0},{1,17},{17,1},{2,18},{18,2},{3,19},{19,3},{4,20},{20... | collective-permute-start | bytes 2359304 | tf_op jit(solution)/shard_map/ppermute | solution.py:56
  145.6 9.6 %collective-permute-start.25 = (bf16[3,64,1024]{2,1,0:T(8,128)(2,1)S(1)}, bf16[3,64,1024]{2,1,0:T(8,128)(2,1)S(1)}, u32[]{:S(2)}, u32[]{:S(2)}) collective-permute-start(bf16[3,64,1024]{2,1,0:T(8,128)(2,1)S(1)} %get-tuple-element.308), channel_id=1, source_target_pairs={{0,16},{16,0},{1,17},{17,1},{2,18},{18,2},{3,19},{19,3},{4,20},{20... | collective-permute-start | bytes 1179656 | tf_op jit(solution)/shard_map/ppermute | solution.py:56
  146.7 9.2 %collective-permute-start.26 = (bf16[3,64,1024]{2,1,0:T(8,128)(2,1)S(1)}, bf16[3,64,1024]{2,1,0:T(8,128)(2,1)S(1)}, u32[]{:S(2)}, u32[]{:S(2)}) collective-permute-start(bf16[3,64,1024]{2,1,0:T(8,128)(2,1)S(1)} %get-tuple-element.309), channel_id=1, source_target_pairs={{0,1},{1,0},{2,3},{3,2},{4,5},{5,4},{6,7},{7,6},{8,9},{9,8},{10,11... | collective-permute-start | bytes 1179656 | tf_op jit(solution)/shard_map/ppermute | solution.py:56
  155.9 22.3 %collective-permute-start.27 = (bf16[4,128,1024]{2,1,0:T(8,128)(2,1)S(1)}, bf16[4,128,1024]{2,1,0:T(8,128)(2,1)S(1)}, u32[]{:S(2)}, u32[]{:S(2)}) collective-permute-start(bf16[4,128,1024]{2,1,0:T(8,128)(2,1)S(1)} %get-tuple-element.321), channel_id=1, source_target_pairs={{0,1},{1,0},{2,3},{3,2},{4,5},{5,4},{6,7},{7,6},{8,9},{9,8},{10,11... | collective-permute-start | bytes 3145736 | tf_op jit(solution)/shard_map/ppermute | solution.py:56
  157.0 22.1 %collective-permute-start.28 = (bf16[4,2,64,1024]{3,2,1,0:T(8,128)(2,1)S(1)}, bf16[4,2,64,1024]{3,2,1,0:T(8,128)(2,1)S(1)}, u32[]{:S(2)}, u32[]{:S(2)}) collective-permute-start(bf16[4,2,64,1024]{3,2,1,0:T(8,128)(2,1)S(1)} %get-tuple-element.322), channel_id=1, source_target_pairs={{0,16},{16,0},{1,17},{17,1},{2,18},{18,2},{3,19},{19,3},{4,20},{20... | collective-permute-start | bytes 3145736 | tf_op jit(solution)/shard_map/ppermute | solution.py:56
  181.7 19.6 %collective-permute-start.29 = (bf16[1024,1024]{1,0:T(8,128)(2,1)}, bf16[1024,1024]{1,0:T(8,128)(2,1)}, u32[]{:S(2)}, u32[]{:S(2)}) collective-permute-start(bf16[1024,1024]{1,0:T(8,128)(2,1)} %get-tuple-element.349.refs_1_), channel_id=1, source_target_pairs={{0,8},{8,0},{1,9},{9,1},{2,10},{10,2},{3,11},{11,3},{4,12},{12,4},... | collective-permute-start | bytes 6291464 | tf_op jit(solution)/shard_map/ppermute | solution.py:56
  186.7 9.8 %collective-permute-start.32 = (bf16[2,256,1024]{2,1,0:T(8,128)(2,1)S(1)}, bf16[2,256,1024]{2,1,0:T(8,128)(2,1)S(1)}, u32[]{:S(2)}, u32[]{:S(2)}) collective-permute-start(bf16[2,256,1024]{2,1,0:T(8,128)(2,1)S(1)} %dynamic-slice_bitcast_fusion.1), channel_id=1, source_target_pairs={{0,8},{8,0},{1,9},{9,1},{2,10},{10,2},{3,11},{11,3},{4,12},{12,4},... | collective-permute-start | bytes 3145736 | tf_op jit(solution)/shard_map/ppermute | solution.py:56
  187.7 13.6 %collective-permute-start.30 = (bf16[4,64,1024]{2,1,0:T(8,128)(2,1)S(1)}, bf16[4,64,1024]{2,1,0:T(8,128)(2,1)S(1)}, u32[]{:S(2)}, u32[]{:S(2)}) collective-permute-start(bf16[4,64,1024]{2,1,0:T(8,128)(2,1)S(1)} %copy-done.43), channel_id=1, source_target_pairs={{0,16},{16,0},{1,17},{17,1},{2,18},{18,2},{3,19},{19,3},{4,20},{20... | collective-permute-start | bytes 1572872 | tf_op jit(solution)/shard_map/ppermute | solution.py:56
  188.1 13.2 %collective-permute-start.31 = (bf16[4,64,1024]{2,1,0:T(8,128)(2,1)S(1)}, bf16[4,64,1024]{2,1,0:T(8,128)(2,1)S(1)}, u32[]{:S(2)}, u32[]{:S(2)}) collective-permute-start(bf16[4,64,1024]{2,1,0:T(8,128)(2,1)S(1)} %copy-done.42), channel_id=1, source_target_pairs={{0,1},{1,0},{2,3},{3,2},{4,5},{5,4},{6,7},{7,6},{8,9},{9,8},{10,11... | collective-permute-start | bytes 1572872 | tf_op jit(solution)/shard_map/ppermute | solution.py:56
  202.4 12.2 %collective-permute-start.33 = (bf16[2,64,1024]{2,1,0:T(8,128)(2,1)S(1)}, bf16[2,64,1024]{2,1,0:T(8,128)(2,1)S(1)}, u32[]{:S(2)}, u32[]{:S(2)}) collective-permute-start(bf16[2,64,1024]{2,1,0:T(8,128)(2,1)S(1)} %get-tuple-element.352), channel_id=1, source_target_pairs={{0,2},{2,4},{4,6},{6,0},{1,3},{3,5},{5,7},{7,1},{8,10},{10,12},{12... | collective-permute-start | bytes 786440 | tf_op jit(solution)/shard_map/ppermute | solution.py:250
  202.4 15.5 %collective-permute-start.34 = (bf16[2,64,1024]{2,1,0:T(8,128)(2,1)S(1)}, bf16[2,64,1024]{2,1,0:T(8,128)(2,1)S(1)}, u32[]{:S(2)}, u32[]{:S(2)}) collective-permute-start(bf16[2,64,1024]{2,1,0:T(8,128)(2,1)S(1)} %get-tuple-element.353), channel_id=1, source_target_pairs={{0,6},{2,0},{4,2},{6,4},{1,7},{3,1},{5,3},{7,5},{8,14},{10,8},{12,... | collective-permute-start | bytes 786440 | tf_op jit(solution)/shard_map/ppermute | solution.py:250
  203.9 34.3 %collective-permute-start.35 = (bf16[4,64,2048]{2,1,0:T(8,128)(2,1)S(1)}, bf16[4,64,2048]{2,1,0:T(8,128)(2,1)S(1)}, u32[]{:S(2)}, u32[]{:S(2)}) collective-permute-start(bf16[4,64,2048]{2,1,0:T(8,128)(2,1)S(1)} %get-tuple-element.359), channel_id=1, source_target_pairs={{0,1},{1,0},{2,3},{3,2},{4,5},{5,4},{6,7},{7,6},{8,9},{9,8},{10,11... | collective-permute-start | bytes 3145736 | tf_op jit(solution)/shard_map/ppermute | solution.py:56
  204.2 34.0 %collective-permute-start.36 = (bf16[4,2,32,2048]{3,2,1,0:T(8,128)(2,1)S(1)}, bf16[4,2,32,2048]{3,2,1,0:T(8,128)(2,1)S(1)}, u32[]{:S(2)}, u32[]{:S(2)}) collective-permute-start(bf16[4,2,32,2048]{3,2,1,0:T(8,128)(2,1)S(1)} %get-tuple-element.360), channel_id=1, source_target_pairs={{0,16},{16,0},{1,17},{17,1},{2,18},{18,2},{3,19},{19,3},{4,20},{20... | collective-permute-start | bytes 3145736 | tf_op jit(solution)/shard_map/ppermute | solution.py:56
  205.3 32.8 %collective-permute-start.37 = (bf16[256,1024]{1,0:T(8,128)(2,1)S(1)}, bf16[256,1024]{1,0:T(8,128)(2,1)S(1)}, u32[]{:S(2)}, u32[]{:S(2)}) collective-permute-start(bf16[256,1024]{1,0:T(8,128)(2,1)S(1)} %dynamic-slice_bitcast_fusion.2), channel_id=1, source_target_pairs={{0,16},{16,0},{1,17},{17,1},{2,18},{18,2},{3,19},{19,3},{4,20},{20... | collective-permute-start | bytes 1572872 | tf_op jit(solution)/shard_map/ppermute | solution.py:56
  217.9 18.9 %collective-permute-start.38 = (bf16[2,64,1024]{2,1,0:T(8,128)(2,1)S(1)}, bf16[2,64,1024]{2,1,0:T(8,128)(2,1)S(1)}, u32[]{:S(2)}, u32[]{:S(2)}) collective-permute-start(bf16[2,64,1024]{2,1,0:T(8,128)(2,1)S(1)} %get-tuple-element.365), channel_id=1, source_target_pairs={{0,4},{2,6},{4,0},{6,2},{1,5},{3,7},{5,1},{7,3},{8,12},{10,14},{12... | collective-permute-start | bytes 786440 | tf_op jit(solution)/shard_map/ppermute | solution.py:250
  217.9 24.3 %copy-start.20 = (bf16[1024,1024]{1,0:T(8,128)(2,1)S(1)}, bf16[1024,1024]{1,0:T(8,128)(2,1)}, u32[]{:S(2)}) copy-start(bf16[1024,1024]{1,0:T(8,128)(2,1)} %get-tuple-element.375.refs_0_) | copy-start | bytes 6291460
  238.2 14.3 %collective-permute-start.41 = (bf16[2,64,1024]{2,1,0:T(8,128)(2,1)S(1)}, bf16[2,64,1024]{2,1,0:T(8,128)(2,1)S(1)}, u32[]{:S(2)}, u32[]{:S(2)}) collective-permute-start(bf16[2,64,1024]{2,1,0:T(8,128)(2,1)S(1)} %add_convert_fusion.2), channel_id=1, source_target_pairs={{0,16},{16,0},{1,17},{17,1},{2,18},{18,2},{3,19},{19,3},{4,20},{20... | collective-permute-start | bytes 786440 | tf_op jit(solution)/shard_map/ppermute | solution.py:56
  240.6 13.8 %collective-permute-start.39 = (bf16[4,32,2048]{2,1,0:T(8,128)(2,1)S(1)}, bf16[4,32,2048]{2,1,0:T(8,128)(2,1)S(1)}, u32[]{:S(2)}, u32[]{:S(2)}) collective-permute-start(bf16[4,32,2048]{2,1,0:T(8,128)(2,1)S(1)} %get-tuple-element.373), channel_id=1, source_target_pairs={{0,16},{16,0},{1,17},{17,1},{2,18},{18,2},{3,19},{19,3},{4,20},{20... | collective-permute-start | bytes 1572872 | tf_op jit(solution)/shard_map/ppermute | solution.py:56
  241.1 13.3 %collective-permute-start.40 = (bf16[4,32,2048]{2,1,0:T(8,128)(2,1)S(1)}, bf16[4,32,2048]{2,1,0:T(8,128)(2,1)S(1)}, u32[]{:S(2)}, u32[]{:S(2)}) collective-permute-start(bf16[4,32,2048]{2,1,0:T(8,128)(2,1)S(1)} %get-tuple-element.374), channel_id=1, source_target_pairs={{0,1},{1,0},{2,3},{3,2},{4,5},{5,4},{6,7},{7,6},{8,9},{9,8},{10,11... | collective-permute-start | bytes 1572872 | tf_op jit(solution)/shard_map/ppermute | solution.py:56
  255.4 29.2 %collective-permute-start.42 = (bf16[4,64,2176]{2,1,0:T(8,128)(2,1)S(1)}, bf16[4,64,2176]{2,1,0:T(8,128)(2,1)S(1)}, u32[]{:S(2)}, u32[]{:S(2)}) collective-permute-start(bf16[4,64,2176]{2,1,0:T(8,128)(2,1)S(1)} %get-tuple-element.396), channel_id=1, source_target_pairs={{0,1},{1,0},{2,3},{3,2},{4,5},{5,4},{6,7},{7,6},{8,9},{9,8},{10,11... | collective-permute-start | bytes 3342344 | tf_op jit(solution)/shard_map/ppermute | solution.py:56
  256.6 28.0 %collective-permute-start.43 = (bf16[4,2,32,2176]{3,2,1,0:T(8,128)(2,1)S(1)}, bf16[4,2,32,2176]{3,2,1,0:T(8,128)(2,1)S(1)}, u32[]{:S(2)}, u32[]{:S(2)}) collective-permute-start(bf16[4,2,32,2176]{3,2,1,0:T(8,128)(2,1)S(1)} %get-tuple-element.397), channel_id=1, source_target_pairs={{0,16},{16,0},{1,17},{17,1},{2,18},{18,2},{3,19},{19,3},{4,20},{20... | collective-permute-start | bytes 3342344 | tf_op jit(solution)/shard_map/ppermute | solution.py:56
  257.6 10.1 %collective-permute-start.44 = (bf16[2,32,2048]{2,1,0:T(8,128)(2,1)S(1)}, bf16[2,32,2048]{2,1,0:T(8,128)(2,1)S(1)}, u32[]{:S(2)}, u32[]{:S(2)}) collective-permute-start(bf16[2,32,2048]{2,1,0:T(8,128)(2,1)S(1)} %get-tuple-element.400), channel_id=1, source_target_pairs={{0,2},{2,4},{4,6},{6,0},{1,3},{3,5},{5,7},{7,1},{8,10},{10,12},{12... | collective-permute-start | bytes 786440 | tf_op jit(solution)/shard_map/ppermute | solution.py:250
  260.1 19.8 %collective-permute-start.45 = (bf16[2,32,2048]{2,1,0:T(8,128)(2,1)S(1)}, bf16[2,32,2048]{2,1,0:T(8,128)(2,1)S(1)}, u32[]{:S(2)}, u32[]{:S(2)}) collective-permute-start(bf16[2,32,2048]{2,1,0:T(8,128)(2,1)S(1)} %get-tuple-element.401), channel_id=1, source_target_pairs={{0,4},{2,6},{4,0},{6,2},{1,5},{3,7},{5,1},{7,3},{8,12},{10,14},{12... | collective-permute-start | bytes 786440 | tf_op jit(solution)/shard_map/ppermute | solution.py:250
  262.7 21.8 %collective-permute-start.46 = (bf16[2,32,2048]{2,1,0:T(8,128)(2,1)S(1)}, bf16[2,32,2048]{2,1,0:T(8,128)(2,1)S(1)}, u32[]{:S(2)}, u32[]{:S(2)}) collective-permute-start(bf16[2,32,2048]{2,1,0:T(8,128)(2,1)S(1)} %get-tuple-element.402), channel_id=1, source_target_pairs={{0,6},{2,0},{4,2},{6,4},{1,7},{3,1},{5,3},{7,5},{8,14},{10,8},{12,... | collective-permute-start | bytes 786440 | tf_op jit(solution)/shard_map/ppermute | solution.py:250
  286.2 3.8 %collective-permute-start.49 = (bf16[2,256,1024]{2,1,0:T(8,128)(2,1)S(1)}, bf16[2,256,1024]{2,1,0:T(8,128)(2,1)S(1)}, u32[]{:S(2)}, u32[]{:S(2)}) collective-permute-start(bf16[2,256,1024]{2,1,0:T(8,128)(2,1)S(1)} %dynamic-slice_bitcast_fusion), channel_id=1, source_target_pairs={{0,8},{8,0},{1,9},{9,1},{2,10},{10,2},{3,11},{11,3},{4,12},{12,4},... | collective-permute-start | bytes 3145736 | tf_op jit(solution)/shard_map/ppermute | solution.py:56
  288.4 14.3 %collective-permute-start.47 = (bf16[4,32,2176]{2,1,0:T(8,128)(2,1)S(1)}, bf16[4,32,2176]{2,1,0:T(8,128)(2,1)S(1)}, u32[]{:S(2)}, u32[]{:S(2)}) collective-permute-start(bf16[4,32,2176]{2,1,0:T(8,128)(2,1)S(1)} %get-tuple-element.420), channel_id=1, source_target_pairs={{0,16},{16,0},{1,17},{17,1},{2,18},{18,2},{3,19},{19,3},{4,20},{20... | collective-permute-start | bytes 1671176 | tf_op jit(solution)/shard_map/ppermute | solution.py:56
  288.8 13.9 %collective-permute-start.48 = (bf16[4,32,2176]{2,1,0:T(8,128)(2,1)S(1)}, bf16[4,32,2176]{2,1,0:T(8,128)(2,1)S(1)}, u32[]{:S(2)}, u32[]{:S(2)}) collective-permute-start(bf16[4,32,2176]{2,1,0:T(8,128)(2,1)S(1)} %get-tuple-element.421), channel_id=1, source_target_pairs={{0,1},{1,0},{2,3},{3,2},{4,5},{5,4},{6,7},{7,6},{8,9},{9,8},{10,11... | collective-permute-start | bytes 1671176 | tf_op jit(solution)/shard_map/ppermute | solution.py:56
  302.7 6.7 %collective-permute-start.54 = (bf16[2,32,2048]{2,1,0:T(8,128)(2,1)S(1)}, bf16[2,32,2048]{2,1,0:T(8,128)(2,1)S(1)}, u32[]{:S(2)}, u32[]{:S(2)}) collective-permute-start(bf16[2,32,2048]{2,1,0:T(8,128)(2,1)S(1)} %add_convert_fusion.1), channel_id=1, source_target_pairs={{0,16},{16,0},{1,17},{17,1},{2,18},{18,2},{3,19},{19,3},{4,20},{20... | collective-permute-start | bytes 786440 | tf_op jit(solution)/shard_map/ppermute | solution.py:56
  303.8 6.8 %collective-permute-start.56 = (bf16[256,1024]{1,0:T(8,128)(2,1)S(1)}, bf16[256,1024]{1,0:T(8,128)(2,1)S(1)}, u32[]{:S(2)}, u32[]{:S(2)}) collective-permute-start(bf16[256,1024]{1,0:T(8,128)(2,1)S(1)} %bitcast.165), channel_id=1, source_target_pairs={{0,8},{8,0},{1,9},{9,1},{2,10},{10,2},{3,11},{11,3},{4,12},{12,4},... | collective-permute-start | bytes 1572872 | tf_op jit(solution)/shard_map/ppermute | solution.py:56
  306.2 11.4 %collective-permute-start.50 = (bf16[2,32,2176]{2,1,0:T(8,128)(2,1)S(1)}, bf16[2,32,2176]{2,1,0:T(8,128)(2,1)S(1)}, u32[]{:S(2)}, u32[]{:S(2)}) collective-permute-start(bf16[2,32,2176]{2,1,0:T(8,128)(2,1)S(1)} %get-tuple-element.428), channel_id=1, source_target_pairs={{0,2},{2,4},{4,6},{6,0},{1,3},{3,5},{5,7},{7,1},{8,10},{10,12},{12... | collective-permute-start | bytes 835592 | tf_op jit(solution)/shard_map/ppermute | solution.py:250
  306.3 24.0 %collective-permute-start.51 = (bf16[2,32,2176]{2,1,0:T(8,128)(2,1)S(1)}, bf16[2,32,2176]{2,1,0:T(8,128)(2,1)}, u32[]{:S(2)}, u32[]{:S(2)}) collective-permute-start(bf16[2,32,2176]{2,1,0:T(8,128)(2,1)S(1)} %get-tuple-element.429), channel_id=1, source_target_pairs={{0,4},{2,6},{4,0},{6,2},{1,5},{3,7},{5,1},{7,3},{8,12},{10,14},{12... | collective-permute-start | bytes 835592 | tf_op jit(solution)/shard_map/ppermute | solution.py:250
  308.9 25.2 %collective-permute-start.52 = (bf16[2,32,2176]{2,1,0:T(8,128)(2,1)S(1)}, bf16[2,32,2176]{2,1,0:T(8,128)(2,1)}, u32[]{:S(2)}, u32[]{:S(2)}) collective-permute-start(bf16[2,32,2176]{2,1,0:T(8,128)(2,1)S(1)} %get-tuple-element.430), channel_id=1, source_target_pairs={{0,6},{2,0},{4,2},{6,4},{1,7},{3,1},{5,3},{7,5},{8,14},{10,8},{12,... | collective-permute-start | bytes 835592 | tf_op jit(solution)/shard_map/ppermute | solution.py:250
  309.4 24.6 %collective-permute-start.53 = (bf16[256,1024]{1,0:T(8,128)(2,1)}, bf16[256,1024]{1,0:T(8,128)(2,1)S(1)}, u32[]{:S(2)}, u32[]{:S(2)}) collective-permute-start(bf16[256,1024]{1,0:T(8,128)(2,1)} %fusion.15), channel_id=1, source_target_pairs={{0,16},{16,0},{1,17},{17,1},{2,18},{18,2},{3,19},{19,3},{4,20},{20... | collective-permute-start | bytes 1572872 | tf_op jit(solution)/shard_map/ppermute | solution.py:56
  310.7 4.2 %collective-permute-start.55 = (bf16[128,2048]{1,0:T(8,128)(2,1)S(1)}, bf16[128,2048]{1,0:T(8,128)(2,1)}, u32[]{:S(2)}, u32[]{:S(2)}) collective-permute-start(bf16[128,2048]{1,0:T(8,128)(2,1)S(1)} %bitcast.171), channel_id=1, source_target_pairs={{0,8},{8,0},{1,9},{9,1},{2,10},{10,2},{3,11},{11,3},{4,12},{12,4},... | collective-permute-start | bytes 1572872 | tf_op jit(solution)/shard_map/ppermute | solution.py:56
  335.4 7.8 %collective-permute-start.57 = (bf16[2,32,2176]{2,1,0:T(8,128)(2,1)S(1)}, bf16[2,32,2176]{2,1,0:T(8,128)(2,1)S(1)}, u32[]{:S(2)}, u32[]{:S(2)}) collective-permute-start(bf16[2,32,2176]{2,1,0:T(8,128)(2,1)S(1)} %add_convert_fusion), channel_id=1, source_target_pairs={{0,16},{16,0},{1,17},{17,1},{2,18},{18,2},{3,19},{19,3},{4,20},{20... | collective-permute-start | bytes 835592 | tf_op jit(solution)/shard_map/ppermute | solution.py:56
  343.4 3.3 collective-permute-start.58
  (45 other events, 283.9 us)

commit v6 on v5

--- a/solution.py
+++ b/solution.py
@@ -152,7 +152,7 @@
         out_specs=[out, out],
         out_shape=[
             jax.ShapeDtypeStruct((rows, count * LANES), bf16),
-            jax.ShapeDtypeStruct((rows, count * LANES), f32),
+            pltpu.HBM((rows, count * LANES), f32),
         ],
         scratch_shapes=[pltpu.VMEM((len(spans), tile, widest), f32)],
         compiler_params=pltpu.CompilerParams(vmem_limit_bytes=VMEM),
@@ -235,7 +235,7 @@
         compiler_params=pltpu.CompilerParams(vmem_limit_bytes=VMEM),
         cost_estimate=cost(6 * count),
         name="attend_back",
-    )(far(joint), far(joint), far(joint), grads, lse, seg_col, seg_row)
+    )(far(joint), far(joint), far(joint), grads, far(lse), seg_col, seg_row)
 
 
 def shape_of(*shape, dtype=bf16):
@@ -303,7 +303,7 @@
         compiler_params=pltpu.CompilerParams(vmem_limit_bytes=VMEM),
         cost_estimate=cost(1),
         name="halve",
-    )(side, near)
+    )(far(side), far(near))
 
 
 def prepare(place, shards, w_qkv, w_out, w_up, vectors):
@@ -790,7 +790,7 @@
             (far_shape(rows, model), row_block(tile, model)),
             (far_shape(rows, 3 * head_columns), row_block(tile, 3 * head_columns)),
         ]
-        + [(shape_of(*shape, dtype=dtype), whole_block(*shape)) for *shape, dtype in wholes],
+        + [(far_shape(*shape, dtype=dtype), whole_block(*shape)) for *shape, dtype in wholes],
         [pltpu.VMEM((model, half_model), bf16)] if fused_out else [],
         3 * copies,
         8,
@@ -848,7 +848,7 @@
         [],
         [
             (shape_of(rows, model), row_block(tile, model)),
-            (shape_of(rows, head_columns), row_block(tile, head_columns)),
+            (far_shape(rows, head_columns), row_block(tile, head_columns)),
         ],
         [],
         1,
@@ -873,7 +873,7 @@
 
         added = own_ref[...].astype(f32) + other_ref[...].astype(f32)
         middle = rows_ref[...].astype(f32) + added
-        middle_ref[...] = middle
+        middle_ref[...] = middle.astype(bf16)
         unit_rows, _ = unit_of(middle)
         normed = (unit_rows * scales_ref[2:3, :] + scales_ref[3:4, :]).astype(bf16)
         normed_ref[...] = normed
@@ -895,7 +895,7 @@
         ],
         [up_set],
         [
-            (far_shape(rows, model, dtype=f32), row_block(tile, model)),
+            (far_shape(rows, model), row_block(tile, model)),
             (far_shape(rows, model), row_block(tile, model)),
             (far_shape(rows, inner), row_block(tile, inner)),
             (far_shape(rows, inner), row_block(tile, inner)),
@@ -906,7 +906,9 @@
     )
 
     if fine_down:
-        hidden, slope, normed_two, down_side, down_near = sync(hidden, slope, normed_two, down_side, down_near)
+        hidden, slope, normed_two, down_side, down_near, lse = sync(
+            hidden, slope, normed_two, down_side, down_near, lse
+        )
         cuts, hidden = sync(halve(down_side, down_near), hidden)
         down_last = last_quarters(*cuts)
         down_keep, down_send = outer(place, depth, far(hidden), grad_result)
@@ -919,9 +921,11 @@
         down_keep = down_came = outer_whole(hidden, grad_result)
         down_send = None
 
+    by_chunk = group == 2 and tile == chunk
+
     def narrow(place_ref, given, held, made, scratch, sems):
         hidden_ref, grad_ref, slope_ref, *downs = given
-        out_ref, pre_ref, back_ref = made
+        *out_refs, pre_ref, back_ref = made
         upward = scratch[0]
         down_ref = scratch[1] if fine_down else downs[0]
 
@@ -939,9 +943,21 @@
             grad = mm_cols(grad_ref[...], down_ref[at : at + wide, :])
             pre_ref[:, at : at + wide] = (grad * slope_ref[:, at : at + wide].astype(f32)).astype(bf16)
         back_ref[...] = mm_cols(pre_ref[...], upward[...]).astype(bf16)
-        out_ref[...] = mm(hidden_ref[...], down_ref[...]).astype(bf16)
-
-    result, grad_pre, back = weight_call(
+        out = mm(hidden_ref[...], down_ref[...]).astype(bf16)
+        if by_chunk:
+            own = lax.rem(pl.program_id(0), 2) == place_ref[3]
+
+            @pl.when(own)
+            def _():
+                out_refs[0][0] = out
+
+            @pl.when(~own)
+            def _():
+                out_refs[1][0] = out
+        else:
+            out_refs[0][...] = out
+
+    *results, grad_pre, back = weight_call(
         "narrow",
         narrow,
         tiles,
@@ -953,8 +969,15 @@
         ]
         + ([] if fine_down else [(far(downward), whole_block(inner, model))]),
         [up_set, down_set] if fine_down else [up_set],
-        [
-            (far_shape(rows, model), row_block(tile, model)),
+        (
+            [
+                (shape(micro, chunk, model), pl.BlockSpec((1, chunk, model), lambda i: (i // 2, 0, 0)))
+                for shape in (far_shape, shape_of)
+            ]
+            if by_chunk
+            else [(far_shape(rows, model), row_block(tile, model))]
+        )
+        + [
             (far_shape(rows, inner), row_block(tile, inner)),
             (far_shape(rows, model), row_block(tile, model)),
         ],
@@ -965,16 +988,19 @@
     down_kept = None
     if fine_down:
         down_kept, down_send = fold_one(place, down_keep, down_came, far_shape)
-    result, grad_pre, back, normed_two, down_kept, down_send, down_came = sync(
-        result, grad_pre, back, normed_two, down_kept, down_send, down_came
+    results, grad_pre, back, normed_two, down_kept, down_send, down_came = sync(
+        results, grad_pre, back, normed_two, down_kept, down_send, down_came
     )
 
     back_other = other_part(back)
-    result_other = other_own(result)
+    if by_chunk:
+        result, result_other = results[0], swap(results[1], "lo")
+    else:
+        result, result_other = own_chunks(results[0]), other_own(results[0])
     if fine_down:
         down_came = swap(down_send[0], "hi"), swap(down_send[1], "fx")
     up_keep, up_send = outer(place, depth, far(normed_two), far(grad_pre))
-    output = (own_chunks(middle) + own_chunks(result).astype(f32) + result_other.astype(f32)).astype(bf16)
+    output = (own_chunks(middle).astype(f32) + result.astype(f32) + result_other.astype(f32)).astype(bf16)
     back, back_other, up_keep, up_send, down_came, output = sync(
         back, back_other, up_keep, up_send, down_came, output
     )
@@ -985,24 +1011,23 @@
 
     def between(place_ref, given, held, made, scratch, sems):
         grad_ref, own_ref, other_ref, middle_ref, scales_ref, weight = given
-        middle_grad_ref, branch_ref, attended_ref, sums_ref = made
+        branch_ref, attended_ref, sums_ref = made
 
         @pl.when(pl.program_id(0) == 0)
         def _():
             sums_ref[...] = jnp.zeros_like(sums_ref)
 
-        unit_rows, inverse = unit_of(middle_ref[...])
+        unit_rows, inverse = unit_of(middle_ref[...].astype(f32))
         own_back = own_ref[...].astype(f32)
         back_rows = own_back + other_ref[...].astype(f32)
         sums_ref[0:1, :] += jnp.sum(own_back * unit_rows, axis=0, keepdims=True)
         sums_ref[1:2, :] += jnp.sum(own_back, axis=0, keepdims=True)
         grads = grad_ref[...].astype(f32) + unit_back(back_rows * scales_ref[2:3, :], unit_rows, inverse)
-        middle_grad_ref[...] = grads
         low = grads.astype(bf16)
         branch_ref[...] = low
         attended_ref[...] = mm_cols(low, own_out(weight, place_ref)).astype(bf16)
 
-    grad_middle, grad_branch, grad_attended, sums_two = weight_call(
+    grad_branch, grad_attended, sums_two = weight_call(
         "between",
         between,
         tiles,
@@ -1017,7 +1042,6 @@
         ],
         [],
         [
-            (far_shape(rows, model, dtype=f32), row_block(tile, model)),
             (far_shape(rows, model), row_block(tile, model)),
             (shape_of(rows, head_columns), row_block(tile, head_columns)),
             (shape_of(8, model, dtype=f32), whole_block(8, model)),
@@ -1102,7 +1126,7 @@
     entered_other = other_own(entered)
     grad_normed = own_chunks(entered).astype(f32) + entered_other.astype(f32)
     unit_own, inverse_own = unit_of(own_chunks(inputs).astype(f32))
-    grad_tokens = own_chunks(grad_middle) + unit_back(grad_normed * scales[0], unit_own, inverse_own)
+    grad_tokens = own_chunks(grad_branch).astype(f32) + unit_back(grad_normed * scales[0], unit_own, inverse_own)
     grad_sent = pick(grad_tokens, 1 - h, 0).astype(bf16)
     last_came, grad_tokens, grad_sent, up_own, down_own = sync(last_came, grad_tokens, grad_sent, up_own, down_own)
 
@@ -1120,6 +1144,7 @@
 
     last_own = both_halves(add_up(last_sum, last_came))
     grad_tokens = ordered(pick(grad_tokens, h, 0), grad_came.astype(f32), h, 0)[:, None]
+    last_own, grad_tokens = sync(last_own, grad_tokens)
     if fused_out:
         qkv_all, out_all, sums = finish_qkv(place, 3 * head_columns, [last_own], [swap(last_own, "lo")])
     else:

time: 353 us -> 353 us (level)
  local copies, waits for them, and re-layouts: 12.5 us -> 6.91 us
  Pallas kernels: 132 us -> 137 us
  other arithmetic: 15.8 us -> 20.2 us
  waiting for transfers between devices: 130 us -> 126 us
    ppermute x41, waiting for transfers between devices: 47 us -> 42.1 us  [swap(): return lax.ppermute(value, axis, SWAP)]
  transfers between devices with their start and end apart: 59 -> 59, of which waited for: 30 -> 29; matrix products, arithmetic and copies ran while one was open for 5% -> 5% of each run, Pallas kernels for 34% -> 34%
where the time goes in v6:
time: 353 us; the launch traced here: 349 us
  Pallas kernels  137 us (39%)
  waiting for transfers between devices  126 us (36%)
  starting transfers between devices  57.6 us (16%)
  other arithmetic  20.2 us (6%)
  local copies, waits for them, and re-layouts  6.91 us (2%)
    ppermute x18, waiting for transfers between devices, along(): lax.ppermute(value, axis, [(i, (i + step) % depth) for i in range(depth)])  83.9 us
    pallas_call x6, Pallas kernels, weight_call(): pl.pallas_call(kernel, grid=(tiles,), in_specs=[pl.BlockSpec(memory_space...  61.9 us
    ppermute x41, waiting for transfers between devices, swap(): return lax.ppermute(value, axis, SWAP)  42.1 us
    ppermute x41, starting transfers between devices, swap(): return lax.ppermute(value, axis, SWAP)  38 us
    pallas_call x3, Pallas kernels, outer(): pl.pallas_call(kernel, grid=(depth,), in_specs=[pl.BlockSpec(memory_space...  23.2 us
    ppermute x18, starting transfers between devices, along(): lax.ppermute(value, axis, [(i, (i + step) % depth) for i in range(depth)])  19.5 us
    pallas_call x1, Pallas kernels, attend_back(): pl.pallas_call(functools.partial(attend_back_kernel, spans, tile), grid=(...  18.9 us
    pallas_call x2, Pallas kernels, attend(): pl.pallas_call(functools.partial(attend_kernel, spans, tile), grid=(count...  13.1 us
  transfers between devices with their start and end apart: 59, of which 29 were waited for; matrix products, arithmetic and copies ran while one was open for 5% of the time, Pallas kernels for 34%

profile of v6, /device:TPU:9, one launch (start us, length us, event | category | flops | bytes accessed | tf_op | source)
XLA Modules:
  0.0 349.3 jit_solution(5108644683654565049)
XLA Ops:
  1.5 2.0 prepare.1
  6.2 1.3 collective-permute-start.4
  7.5 1.3 collective-permute-start
  9.8 1.5 collective-permute-start.2
  11.3 3.2 collective-permute-done
  14.5 16.9 %collective-permute-done.1 = bf16[64,2176]{1,0:T(8,128)(2,1)S(1)} collective-permute-done((bf16[64,2176]{1,0:T(8,128)(2,1)S(1)}, bf16[64,2176]{1,0:T(8,128)(2,1)S(1)}, u32[]{:S(2)}, u32[]{:S(2)}) %collective-permute-start.1) | collective-permute-done | bytes 278560 | tf_op jit(solution)/shard_map/ppermute | solution.py:250
  31.4 3.5 collective-permute-done.2
  37.4 1.5 collective-permute-start.9
  38.9 5.3 %collective-permute-done.7 = bf16[64,2048]{1,0:T(8,128)(2,1)S(1)} collective-permute-done((bf16[64,2048]{1,0:T(8,128)(2,1)S(1)}, bf16[64,2048]{1,0:T(8,128)(2,1)S(1)}, u32[]{:S(2)}, u32[]{:S(2)}) %collective-permute-start.7) | collective-permute-done | bytes 262176 | tf_op jit(solution)/shard_map/ppermute | solution.py:250
  44.2 14.9 %collective-permute-done.8 = bf16[64,2048]{1,0:T(8,128)(2,1)S(1)} collective-permute-done((bf16[64,2048]{1,0:T(8,128)(2,1)S(1)}, bf16[64,2048]{1,0:T(8,128)(2,1)S(1)}, u32[]{:S(2)}, u32[]{:S(2)}) %collective-permute-start.8) | collective-permute-done | bytes 262176 | tf_op jit(solution)/shard_map/ppermute | solution.py:250
  59.1 1.7 collective-permute-done.9
  60.8 1.5 halve.3
  64.4 1.3 collective-permute-start.10
  67.9 1.6 select_bitcast_fusion.3
  70.0 5.7 %collective-permute-done.10.refs_6_ = bf16[3,32,2176]{2,1,0:T(8,128)(2,1)S(1)} collective-permute-done((bf16[3,32,2176]{2,1,0:T(8,128)(2,1)S(1)}, bf16[3,32,2176]{2,1,0:T(8,128)(2,1)S(1)}, u32[]{:S(2)}, u32[]{:S(2)}) %collective-permute-start.10) | collective-permute-done | bytes 417824 | tf_op jit(solution)/shard_map/ppermute | solution.py:56
  78.2 2.0 collective-permute-start.16
  80.5 10.6 %project.1 = (bf16[1024,1024]{1,0:T(8,128)(2,1)}, bf16[1024,1536]{1,0:T(8,128)(2,1)}, f32[8,1024]{1,0:T(8,128)}, bf16[1024,1536]{1,0:T(8,128)(2,1)}, bf16[1024,1...) custom-call(s32[4]{0:T(128)S(1)} %pad_add_fusion.place_ref, bf16[1024,1024]{1,0:T(8,128)(2,1)S(1)} %bitcast.156, ...), custom_call_target="tpu_custom_call" | custom-call | flops 8800000000 | bytes 1000 | tf_op jit(solution)/shard_map/project/pallas_call | solution.py:508
  91.1 6.5 %attend.2 = (bf16[1024,256]{1,0:T(8,128)(2,1)S(1)}, f32[1024,256]{1,0:T(8,128)}) custom-call(bf16[1024,1536]{1,0:T(8,128)(2,1)} %get-tuple-element.278.q_ref.k_ref.v_ref, bf16[1024,1536]{1,0:T(8,128)(2,1)} %get-tuple-element.278.q_ref.k_ref.v_ref, bf16[1024,1536]{1,0:T(8,128)(2,1)} %get-tuple-element.278.q_ref.k_ref.v_ref, s32[1024,1]{1,0:T(8,128)S(1)} %copy.29.seg_col, ...), custom_call_target="tpu_custom_call" | custom-call | flops 8800000000 | bytes 1000 | tf_op jit(solution)/shard_map/attend/pallas_call | solution.py:142
  97.6 8.2 %collective-permute-done.17.refs_11_ = bf16[2,128,1024]{2,1,0:T(8,128)(2,1)S(1)} collective-permute-done((bf16[2,128,1024]{2,1,0:T(8,128)(2,1)S(1)}, bf16[2,128,1024]{2,1,0:T(8,128)(2,1)S(1)}, u32[]{:S(2)}, u32[]{:S(2)}) %collective-permute-start.17) | collective-permute-done | bytes 524320 | tf_op jit(solution)/shard_map/ppermute | solution.py:56
  107.0 1.4 halve.4
  108.6 2.1 collective-permute-start.20
  112.3 3.1 collective-permute-start.21
  115.4 6.5 %attend.3 = (bf16[1024,256]{1,0:T(8,128)(2,1)S(1)}, f32[1024,256]{1,0:T(8,128)}) custom-call(bf16[1024,1536]{1,0:T(8,128)(2,1)} %get-tuple-element.278.q_ref.k_ref.v_ref, bf16[1024,1536]{1,0:T(8,128)(2,1)} %get-tuple-element.278.q_ref.k_ref.v_ref, bf16[1024,1536]{1,0:T(8,128)(2,1)} %get-tuple-element.278.q_ref.k_ref.v_ref, s32[1024,1]{1,0:T(8,128)S(1)} %copy.29.seg_col, ...), custom_call_target="tpu_custom_call" | custom-call | flops 8800000000 | bytes 1000 | tf_op jit(solution)/shard_map/attend/pallas_call | solution.py:142
  122.3 1.5 collective-permute-done.21
  123.8 3.2 leave.1
  129.3 1.6 pad_maximum_fusion.2.lse_ref
  131.5 13.8 %widen.1 = (bf16[1024,1024]{1,0:T(8,128)(2,1)}, bf16[1024,1024]{1,0:T(8,128)(2,1)}, bf16[1024,2048]{1,0:T(8,128)(2,1)}, bf16[1024,2048]{1,0:T(8,128)(2,1)}) custom-call(s32[4]{0:T(128)S(1)} %pad_add_fusion.place_ref, bf16[1024,1024]{1,0:T(8,128)(2,1)S(1)} %bitcast.157, bf16[1024,1024]{1,0:T(8,128)(2,1)S(1)} %get-tuple-element.289.refs_1_, ...), custom_call_target="tpu_custom_call" | custom-call | flops 14300000256 | bytes 1000 | tf_op jit(solution)/shard_map/widen/pallas_call | solution.py:508
  145.3 1.8 collective-permute-done.23.side_ref.refs_13_
  148.2 1.4 halve.5
  151.7 6.6 %outer.3 = (bf16[4,128,1024]{2,1,0:T(8,128)(2,1)S(1)}, bf16[4,128,1024]{2,1,0:T(8,128)(2,1)S(1)}, bf16[4,2,64,1024]{3,2,1,0:T(8,128)(2,1)S(1)}, bf16[4,2,64,1024]{3,2,1,0:T(8,128)(2,1)S(1)}) custom-call(s32[4]{0:T(128)S(1)} %pad_add_fusion.place_ref, bf16[1024,2048]{1,0:T(8,128)(2,1)} %get-tuple-element.316.refs_0_, bf16[1024,1024]{1,0:T(8,128)(2,1)S(1)} %bitcast.161), custom_call_target="tpu_custom_call" | custom-call | flops 6600000000 | bytes 1000 | tf_op jit(solution)/shard_map/outer/pallas_call | solution.py:629
  161.3 21.7 %narrow.1 = (bf16[2,256,1024]{2,1,0:T(8,128)(2,1)}, bf16[2,256,1024]{2,1,0:T(8,128)(2,1)}, bf16[1024,2048]{1,0:T(8,128)(2,1)}, bf16[1024,1024]{1,0:T(8,128)(2,1)}) custom-call(s32[4]{0:T(128)S(1)} %pad_add_fusion.place_ref, bf16[1024,2048]{1,0:T(8,128)(2,1)} %get-tuple-element.316.refs_0_, bf16[1024,1024]{1,0:T(8,128)(2,1)} %bitcast.162, ...), custom_call_target="tpu_custom_call" | custom-call | flops 19800000512 | bytes 1000 | tf_op jit(solution)/shard_map/narrow/pallas_call | solution.py:508
  183.0 2.7 fold_one.3
  185.7 3.5 collective-permute-start.29
  190.4 7.6 %outer.4 = (bf16[4,64,2048]{2,1,0:T(8,128)(2,1)S(1)}, bf16[4,64,2048]{2,1,0:T(8,128)(2,1)S(1)}, bf16[4,2,32,2048]{3,2,1,0:T(8,128)(2,1)S(1)}, bf16[4,2,32,2048]{3,2,1,0:T(8,128)(2,1)S(1)}) custom-call(s32[4]{0:T(128)S(1)} %pad_add_fusion.place_ref, bf16[1024,1024]{1,0:T(8,128)(2,1)} %get-tuple-element.334.refs_0_, bf16[1024,2048]{1,0:T(8,128)(2,1)} %get-tuple-element.335.refs_1_), custom_call_target="tpu_custom_call" | custom-call | flops 6600000000 | bytes 1000 | tf_op jit(solution)/shard_map/outer/pallas_call | solution.py:629
  198.1 1.9 fusion.12
  200.0 2.3 collective-permute-done.30.came_one
  203.6 1.5 collective-permute-start.34
  207.3 7.6 %between.1 = (bf16[1024,1024]{1,0:T(8,128)(2,1)}, bf16[1024,512]{1,0:T(8,128)(2,1)S(1)}, f32[8,1024]{1,0:T(8,128)S(1)}) custom-call(s32[4]{0:T(128)S(1)} %pad_add_fusion.place_ref, bf16[1024,1024]{1,0:T(8,128)(2,1)S(1)} %bitcast.163, bf16[1024,1024]{1,0:T(8,128)(2,1)} %get-tuple-element.357.refs_1_, bf16[1024,1024]{1,0:T(8,128)(2,1)} %collective-permute-done.29.refs_2_, ...), custom_call_target="tpu_custom_call" | custom-call | flops 8800000000 | bytes 1000 | tf_op jit(solution)/shard_map/between/pallas_call | solution.py:508
  214.9 4.0 %collective-permute-done.34 = bf16[2,64,1024]{2,1,0:T(8,128)(2,1)S(1)} collective-permute-done((bf16[2,64,1024]{2,1,0:T(8,128)(2,1)S(1)}, bf16[2,64,1024]{2,1,0:T(8,128)(2,1)S(1)}, u32[]{:S(2)}, u32[]{:S(2)}) %collective-permute-start.34) | collective-permute-done | bytes 262176 | tf_op jit(solution)/shard_map/ppermute | solution.py:250
  218.9 18.9 %attend_back.1.refs_1_.refs_0_ = bf16[3,1024,512]{2,1,0:T(8,128)(2,1)S(1)} custom-call(bf16[1024,1536]{1,0:T(8,128)(2,1)} %get-tuple-element.278.q_ref.k_ref.v_ref, bf16[1024,1536]{1,0:T(8,128)(2,1)} %get-tuple-element.278.q_ref.k_ref.v_ref, bf16[1024,1536]{1,0:T(8,128)(2,1)} %get-tuple-element.278.q_ref.k_ref.v_ref, ...), custom_call_target="tpu_custom_call" | custom-call | flops 26400000000 | bytes 1000 | tf_op jit(solution)/shard_map/attend_back/pallas_call | solution.py:216
  240.3 1.3 fold_one.4
  242.8 9.0 %outer.5 = (bf16[4,64,2176]{2,1,0:T(8,128)(2,1)S(1)}, bf16[4,64,2176]{2,1,0:T(8,128)(2,1)S(1)}, bf16[4,2,32,2176]{3,2,1,0:T(8,128)(2,1)S(1)}, bf16[4,2,32,2176]{3,2,1,0:T(8,128)(2,1)S(1)}) custom-call(s32[4]{0:T(128)S(1)} %pad_add_fusion.place_ref, bf16[1024,1024]{1,0:T(8,128)(2,1)S(1)} %copy-done.11, bf16[3,1024,512]{2,1,0:T(8,128)(2,1)S(1)} %attend_back.1.refs_1_.refs_0_, ...), custom_call_target="tpu_custom_call" | custom-call | flops 6600000000 | bytes 1000 | tf_op jit(solution)/shard_map/outer/pallas_call | solution.py:629
  253.1 2.0 collective-permute-done.39.came_one
  257.8 2.1 collective-permute-start.44
  259.9 2.9 collective-permute-start.45
  262.8 5.1 %enter.1 = bf16[1024,1024]{1,0:T(8,128)(2,1)S(1)} custom-call(s32[4]{0:T(128)S(1)} %pad_add_fusion.place_ref, bf16[3,1024,512]{2,1,0:T(8,128)(2,1)S(1)} %attend_back.1.refs_1_.refs_0_, bf16[1024,1536]{1,0:T(8,128)(2,1)S(1)} %copy-done.10), custom_call_target="tpu_custom_call" | custom-call | flops 15399999488 | bytes 1000 | tf_op jit(solution)/shard_map/enter/pallas_call | solution.py:508
  267.9 11.7 %collective-permute-done.45 = bf16[2,32,2048]{2,1,0:T(8,128)(2,1)S(1)} collective-permute-done((bf16[2,32,2048]{2,1,0:T(8,128)(2,1)S(1)}, bf16[2,32,2048]{2,1,0:T(8,128)(2,1)S(1)}, u32[]{:S(2)}, u32[]{:S(2)}) %collective-permute-start.45) | collective-permute-done | bytes 262176 | tf_op jit(solution)/shard_map/ppermute | solution.py:250
  279.5 5.1 %collective-permute-done.46 = bf16[2,32,2048]{2,1,0:T(8,128)(2,1)S(1)} collective-permute-done((bf16[2,32,2048]{2,1,0:T(8,128)(2,1)S(1)}, bf16[2,32,2048]{2,1,0:T(8,128)(2,1)S(1)}, u32[]{:S(2)}, u32[]{:S(2)}) %collective-permute-start.46) | collective-permute-done | bytes 262176 | tf_op jit(solution)/shard_map/ppermute | solution.py:250
  284.8 1.4 fold_one.5
  286.3 1.5 collective-permute-start.49
  292.9 9.9 %collective-permute-done.47.came_one = bf16[4,32,2176]{2,1,0:T(8,128)(2,1)S(1)} collective-permute-done((bf16[4,32,2176]{2,1,0:T(8,128)(2,1)S(1)}, bf16[4,32,2176]{2,1,0:T(8,128)(2,1)S(1)}, u32[]{:S(2)}, u32[]{:S(2)}) %collective-permute-start.47) | collective-permute-done | bytes 557088 | tf_op jit(solution)/shard_map/ppermute | solution.py:56
  303.9 1.4 collective-permute-start.56
  306.4 2.7 collective-permute-start.51
  310.7 2.4 collective-permute-start.55
  313.4 1.6 bitcast_convert_fusion
  315.0 2.9 finish_up.1
  317.9 12.5 %collective-permute-done.51 = bf16[2,32,2176]{2,1,0:T(8,128)(2,1)} collective-permute-done((bf16[2,32,2176]{2,1,0:T(8,128)(2,1)S(1)}, bf16[2,32,2176]{2,1,0:T(8,128)(2,1)}, u32[]{:S(2)}, u32[]{:S(2)}) %collective-permute-start.51) | collective-permute-done | bytes 278560 | tf_op jit(solution)/shard_map/ppermute | solution.py:250
  330.4 3.7 %collective-permute-done.52 = bf16[2,32,2176]{2,1,0:T(8,128)(2,1)} collective-permute-done((bf16[2,32,2176]{2,1,0:T(8,128)(2,1)S(1)}, bf16[2,32,2176]{2,1,0:T(8,128)(2,1)}, u32[]{:S(2)}, u32[]{:S(2)}) %collective-permute-start.52) | collective-permute-done | bytes 278560 | tf_op jit(solution)/shard_map/ppermute | solution.py:250
  335.5 1.3 fusion.14
  336.8 1.5 maximum_bitcast_fusion
  338.2 4.8 %collective-permute-done.57 = bf16[2,32,2176]{2,1,0:T(8,128)(2,1)S(1)} collective-permute-done((bf16[2,32,2176]{2,1,0:T(8,128)(2,1)S(1)}, bf16[2,32,2176]{2,1,0:T(8,128)(2,1)S(1)}, u32[]{:S(2)}, u32[]{:S(2)}) %collective-permute-start.57) | collective-permute-done | bytes 278560 | tf_op jit(solution)/shard_map/ppermute | solution.py:56
  343.2 1.5 collective-permute-start.58
  344.7 1.6 collective-permute-done.58.refs_1_
  346.3 2.3 finish_qkv.1
  (228 shorter events, 50.6 us)
Async XLA Ops:
  0.6 38.2 %copy-start = (bf16[512,1024]{1,0:T(8,128)(2,1)S(1)}, bf16[512,1024]{1,0:T(8,128)(2,1)}, u32[]{:S(2)}) copy-start(bf16[512,1024]{1,0:T(8,128)(2,1)} %param.20) | copy-start | bytes 3145732
  0.7 304.6 %copy-start.5 = (s32[4]{0:T(128)}, s32[4]{0:T(128)S(1)}, u32[]{:S(2)}) copy-start(s32[4]{0:T(128)S(1)} %pad_add_fusion.place_ref) | copy-start | bytes 52
  3.5 31.4 %collective-permute-start.3 = (bf16[2,64,4224]{2,1,0:T(8,128)(2,1)S(1)}, bf16[2,64,4224]{2,1,0:T(8,128)(2,1)}, u32[]{:S(2)}, u32[]{:S(2)}) collective-permute-start(bf16[2,64,4224]{2,1,0:T(8,128)(2,1)S(1)} %get-tuple-element.233.refs_1_.refs_4_.refs_3_), channel_id=1, source_target_pairs={{0,1},{1,0},{2,3},{3,2},{4,5},{5,4},{6,7},{7,6},{8,9},{9,8},{10,11... | collective-permute-start | bytes 3244040 | tf_op jit(solution)/shard_map/ppermute | solution.py:56
  6.2 28.7 %collective-permute-start.4 = (bf16[2,256,1024]{2,1,0:T(8,128)(2,1)S(1)}, bf16[2,256,1024]{2,1,0:T(8,128)(2,1)S(1)}, u32[]{:S(2)}, u32[]{:S(2)}) collective-permute-start(bf16[2,256,1024]{2,1,0:T(8,128)(2,1)S(1)} %pad_maximum_fusion.3), channel_id=1, source_target_pairs={{0,16},{16,0},{1,17},{17,1},{2,18},{18,2},{3,19},{19,3},{4,20},{20... | collective-permute-start | bytes 3145736 | tf_op jit(solution)/shard_map/ppermute | solution.py:56
  7.5 7.0 %collective-permute-start = (bf16[64,2176]{1,0:T(8,128)(2,1)S(1)}, bf16[64,2176]{1,0:T(8,128)(2,1)S(1)}, u32[]{:S(2)}, u32[]{:S(2)}) collective-permute-start(bf16[64,2176]{1,0:T(8,128)(2,1)S(1)} %get-tuple-element.232), channel_id=1, source_target_pairs={{0,2},{2,4},{4,6},{6,0},{1,3},{3,5},{5,7},{7,1},{8,10},{10,12},{12... | collective-permute-start | bytes 835592 | tf_op jit(solution)/shard_map/ppermute | solution.py:250
  8.8 22.6 %collective-permute-start.1 = (bf16[64,2176]{1,0:T(8,128)(2,1)S(1)}, bf16[64,2176]{1,0:T(8,128)(2,1)S(1)}, u32[]{:S(2)}, u32[]{:S(2)}) collective-permute-start(bf16[64,2176]{1,0:T(8,128)(2,1)S(1)} %get-tuple-element.232), channel_id=1, source_target_pairs={{0,4},{2,6},{4,0},{6,2},{1,5},{3,7},{5,1},{7,3},{8,12},{10,14},{12... | collective-permute-start | bytes 835592 | tf_op jit(solution)/shard_map/ppermute | solution.py:250
  9.8 25.1 %collective-permute-start.2 = (bf16[64,2176]{1,0:T(8,128)(2,1)S(1)}, bf16[64,2176]{1,0:T(8,128)(2,1)S(1)}, u32[]{:S(2)}, u32[]{:S(2)}) collective-permute-start(bf16[64,2176]{1,0:T(8,128)(2,1)S(1)} %get-tuple-element.232), channel_id=1, source_target_pairs={{0,6},{2,0},{4,2},{6,4},{1,7},{3,1},{5,3},{7,5},{8,14},{10,8},{12,... | collective-permute-start | bytes 835592 | tf_op jit(solution)/shard_map/ppermute | solution.py:250
  36.9 24.0 %collective-permute-start.5 = (bf16[3,64,2176]{2,1,0:T(8,128)(2,1)}, bf16[3,64,2176]{2,1,0:T(8,128)(2,1)}, u32[]{:S(2)}, u32[]{:S(2)}) collective-permute-start(bf16[3,64,2176]{2,1,0:T(8,128)(2,1)} %pad_maximum_fusion.7.refs_3_), channel_id=1, source_target_pairs={{0,1},{1,0},{2,3},{3,2},{4,5},{5,4},{6,7},{7,6},{8,9},{9,8},{10,11... | collective-permute-start | bytes 2506760 | tf_op jit(solution)/shard_map/ppermute | solution.py:56
  37.2 23.7 %collective-permute-start.6 = (bf16[3,64,2176]{2,1,0:T(8,128)(2,1)}, bf16[3,64,2176]{2,1,0:T(8,128)(2,1)}, u32[]{:S(2)}, u32[]{:S(2)}) collective-permute-start(bf16[3,64,2176]{2,1,0:T(8,128)(2,1)} %pad_maximum_fusion.7.refs_3_), channel_id=1, source_target_pairs={{0,16},{16,0},{1,17},{17,1},{2,18},{18,2},{3,19},{19,3},{4,20},{20... | collective-permute-start | bytes 2506760 | tf_op jit(solution)/shard_map/ppermute | solution.py:56
  37.4 6.9 %collective-permute-start.7 = (bf16[64,2048]{1,0:T(8,128)(2,1)S(1)}, bf16[64,2048]{1,0:T(8,128)(2,1)S(1)}, u32[]{:S(2)}, u32[]{:S(2)}) collective-permute-start(bf16[64,2048]{1,0:T(8,128)(2,1)S(1)} %get-tuple-element.238), channel_id=1, source_target_pairs={{0,2},{2,4},{4,6},{6,0},{1,3},{3,5},{5,7},{7,1},{8,10},{10,12},{12... | collective-permute-start | bytes 786440 | tf_op jit(solution)/shard_map/ppermute | solution.py:250
  37.4 21.7 %collective-permute-start.8 = (bf16[64,2048]{1,0:T(8,128)(2,1)S(1)}, bf16[64,2048]{1,0:T(8,128)(2,1)S(1)}, u32[]{:S(2)}, u32[]{:S(2)}) collective-permute-start(bf16[64,2048]{1,0:T(8,128)(2,1)S(1)} %get-tuple-element.238), channel_id=1, source_target_pairs={{0,4},{2,6},{4,0},{6,2},{1,5},{3,7},{5,1},{7,3},{8,12},{10,14},{12... | collective-permute-start | bytes 786440 | tf_op jit(solution)/shard_map/ppermute | solution.py:250
  37.4 23.4 %collective-permute-start.9 = (bf16[64,2048]{1,0:T(8,128)(2,1)S(1)}, bf16[64,2048]{1,0:T(8,128)(2,1)}, u32[]{:S(2)}, u32[]{:S(2)}) collective-permute-start(bf16[64,2048]{1,0:T(8,128)(2,1)S(1)} %get-tuple-element.238), channel_id=1, source_target_pairs={{0,6},{2,0},{4,2},{6,4},{1,7},{3,1},{5,3},{7,5},{8,14},{10,8},{12,... | collective-permute-start | bytes 786440 | tf_op jit(solution)/shard_map/ppermute | solution.py:250
  38.9 27.9 %copy-start.18 = (bf16[2,128,1024]{2,1,0:T(8,128)(2,1)}, bf16[2,128,1024]{2,1,0:T(8,128)(2,1)S(1)}, u32[]{:S(2)}) copy-start(bf16[2,128,1024]{2,1,0:T(8,128)(2,1)S(1)} %dynamic-slice_bitcast_fusion.2.refs_10_) | copy-start | bytes 1572868
  63.5 4.4 %collective-permute-start.12 = (bf16[2,256,1024]{2,1,0:T(8,128)(2,1)}, bf16[2,256,1024]{2,1,0:T(8,128)(2,1)}, u32[]{:S(2)}, u32[]{:S(2)}) collective-permute-start(bf16[2,256,1024]{2,1,0:T(8,128)(2,1)} %pad_maximum_fusion.4), channel_id=1, source_target_pairs={{0,8},{8,0},{1,9},{9,1},{2,10},{10,2},{3,11},{11,3},{4,12},{12,4},... | collective-permute-start | bytes 3145736 | tf_op jit(solution)/shard_map/ppermute | solution.py:56
  64.4 11.3 %collective-permute-start.10 = (bf16[3,32,2176]{2,1,0:T(8,128)(2,1)S(1)}, bf16[3,32,2176]{2,1,0:T(8,128)(2,1)S(1)}, u32[]{:S(2)}, u32[]{:S(2)}) collective-permute-start(bf16[3,32,2176]{2,1,0:T(8,128)(2,1)S(1)} %get-tuple-element.248), channel_id=1, source_target_pairs={{0,16},{16,0},{1,17},{17,1},{2,18},{18,2},{3,19},{19,3},{4,20},{20... | collective-permute-start | bytes 1253384 | tf_op jit(solution)/shard_map/ppermute | solution.py:56
  65.7 11.0 %collective-permute-start.11 = (bf16[3,32,2176]{2,1,0:T(8,128)(2,1)S(1)}, bf16[3,32,2176]{2,1,0:T(8,128)(2,1)S(1)}, u32[]{:S(2)}, u32[]{:S(2)}) collective-permute-start(bf16[3,32,2176]{2,1,0:T(8,128)(2,1)S(1)} %get-tuple-element.249), channel_id=1, source_target_pairs={{0,1},{1,0},{2,3},{3,2},{4,5},{5,4},{6,7},{7,6},{8,9},{9,8},{10,11... | collective-permute-start | bytes 1253384 | tf_op jit(solution)/shard_map/ppermute | solution.py:56
  76.6 29.2 %collective-permute-start.13 = (bf16[3,64,2048]{2,1,0:T(8,128)(2,1)S(1)}, bf16[3,64,2048]{2,1,0:T(8,128)(2,1)S(1)}, u32[]{:S(2)}, u32[]{:S(2)}) collective-permute-start(bf16[3,64,2048]{2,1,0:T(8,128)(2,1)S(1)} %pad_maximum_fusion.8.refs_6_.refs_5_), channel_id=1, source_target_pairs={{0,1},{1,0},{2,3},{3,2},{4,5},{5,4},{6,7},{7,6},{8,9},{9,8},{10,11... | collective-permute-start | bytes 2359304 | tf_op jit(solution)/shard_map/ppermute | solution.py:56
  77.8 28.0 %collective-permute-start.14 = (bf16[3,64,2048]{2,1,0:T(8,128)(2,1)S(1)}, bf16[3,64,2048]{2,1,0:T(8,128)(2,1)S(1)}, u32[]{:S(2)}, u32[]{:S(2)}) collective-permute-start(bf16[3,64,2048]{2,1,0:T(8,128)(2,1)S(1)} %pad_maximum_fusion.8.refs_6_.refs_5_), channel_id=1, source_target_pairs={{0,16},{16,0},{1,17},{17,1},{2,18},{18,2},{3,19},{19,3},{4,20},{20... | collective-permute-start | bytes 2359304 | tf_op jit(solution)/shard_map/ppermute | solution.py:56
  78.2 19.4 %collective-permute-start.15 = (bf16[128,1024]{1,0:T(8,128)(2,1)S(1)}, bf16[128,1024]{1,0:T(8,128)(2,1)S(1)}, u32[]{:S(2)}, u32[]{:S(2)}) collective-permute-start(bf16[128,1024]{1,0:T(8,128)(2,1)S(1)} %dynamic-slice_bitcast_fusion.5), channel_id=1, source_target_pairs={{0,2},{2,4},{4,6},{6,0},{1,3},{3,5},{5,7},{7,1},{8,10},{10,12},{12... | collective-permute-start | bytes 786440 | tf_op jit(solution)/shard_map/ppermute | solution.py:250
  78.2 19.4 %collective-permute-start.16 = (bf16[128,1024]{1,0:T(8,128)(2,1)S(1)}, bf16[128,1024]{1,0:T(8,128)(2,1)S(1)}, u32[]{:S(2)}, u32[]{:S(2)}) collective-permute-start(bf16[128,1024]{1,0:T(8,128)(2,1)S(1)} %dynamic-slice_bitcast_fusion.5), channel_id=1, source_target_pairs={{0,6},{2,0},{4,2},{6,4},{1,7},{3,1},{5,3},{7,5},{8,14},{10,8},{12,... | collective-permute-start | bytes 786440 | tf_op jit(solution)/shard_map/ppermute | solution.py:250
  80.2 25.6 %collective-permute-start.17 = (bf16[2,128,1024]{2,1,0:T(8,128)(2,1)S(1)}, bf16[2,128,1024]{2,1,0:T(8,128)(2,1)S(1)}, u32[]{:S(2)}, u32[]{:S(2)}) collective-permute-start(bf16[2,128,1024]{2,1,0:T(8,128)(2,1)S(1)} %copy-done.19), channel_id=1, source_target_pairs={{0,1},{1,0},{2,3},{3,2},{4,5},{5,4},{6,7},{7,6},{8,9},{9,8},{10,11... | collective-permute-start | bytes 1572872 | tf_op jit(solution)/shard_map/ppermute | solution.py:56
  108.6 13.3 %collective-permute-start.20 = (bf16[2,256,1024]{2,1,0:T(8,128)(2,1)S(1)}, bf16[2,256,1024]{2,1,0:T(8,128)(2,1)S(1)}, u32[]{:S(2)}, u32[]{:S(2)}) collective-permute-start(bf16[2,256,1024]{2,1,0:T(8,128)(2,1)S(1)} %pad_maximum_fusion.5), channel_id=1, source_target_pairs={{0,8},{8,0},{1,9},{9,1},{2,10},{10,2},{3,11},{11,3},{4,12},{12,4},... | collective-permute-start | bytes 3145736 | tf_op jit(solution)/shard_map/ppermute | solution.py:56
  110.7 13.0 %collective-permute-start.18 = (bf16[3,32,2048]{2,1,0:T(8,128)(2,1)S(1)}, bf16[3,32,2048]{2,1,0:T(8,128)(2,1)S(1)}, u32[]{:S(2)}, u32[]{:S(2)}) collective-permute-start(bf16[3,32,2048]{2,1,0:T(8,128)(2,1)S(1)} %get-tuple-element.281), channel_id=1, source_target_pairs={{0,16},{16,0},{1,17},{17,1},{2,18},{18,2},{3,19},{19,3},{4,20},{20... | collective-permute-start | bytes 1179656 | tf_op jit(solution)/shard_map/ppermute | solution.py:56
  111.1 12.7 %collective-permute-start.19 = (bf16[3,32,2048]{2,1,0:T(8,128)(2,1)S(1)}, bf16[3,32,2048]{2,1,0:T(8,128)(2,1)S(1)}, u32[]{:S(2)}, u32[]{:S(2)}) collective-permute-start(bf16[3,32,2048]{2,1,0:T(8,128)(2,1)S(1)} %get-tuple-element.282), channel_id=1, source_target_pairs={{0,1},{1,0},{2,3},{3,2},{4,5},{5,4},{6,7},{7,6},{8,9},{9,8},{10,11... | collective-permute-start | bytes 1179656 | tf_op jit(solution)/shard_map/ppermute | solution.py:56
  112.3 11.5 %collective-permute-start.21 = (bf16[128,1024]{1,0:T(8,128)(2,1)S(1)}, bf16[128,1024]{1,0:T(8,128)(2,1)S(1)}, u32[]{:S(2)}, u32[]{:S(2)}) collective-permute-start(bf16[128,1024]{1,0:T(8,128)(2,1)S(1)} %dynamic-slice_bitcast_fusion.5), channel_id=1, source_target_pairs={{0,4},{2,6},{4,0},{6,2},{1,5},{3,7},{5,1},{7,3},{8,12},{10,14},{12... | collective-permute-start | bytes 786440 | tf_op jit(solution)/shard_map/ppermute | solution.py:250
  122.3 29.4 %copy-start.2 = (bf16[2,2,256,1024]{3,2,1,0:T(8,128)(2,1)}, bf16[2,2,256,1024]{3,2,1,0:T(8,128)(2,1)S(1)}, u32[]{:S(2)}) copy-start(bf16[2,2,256,1024]{3,2,1,0:T(8,128)(2,1)S(1)} %pad_maximum_fusion.1) | copy-start | bytes 6291460
  127.1 4.4 %collective-permute-start.22 = (bf16[1024,1024]{1,0:T(8,128)(2,1)S(1)}, bf16[1024,1024]{1,0:T(8,128)(2,1)S(1)}, u32[]{:S(2)}, u32[]{:S(2)}) collective-permute-start(bf16[1024,1024]{1,0:T(8,128)(2,1)S(1)} %get-tuple-element.289.refs_1_), channel_id=1, source_target_pairs={{0,8},{8,0},{1,9},{9,1},{2,10},{10,2},{3,11},{11,3},{4,12},{12,4},... | collective-permute-start | bytes 6291464 | tf_op jit(solution)/shard_map/ppermute | solution.py:56
  127.8 19.2 %collective-permute-start.23 = (bf16[3,128,1024]{2,1,0:T(8,128)(2,1)S(1)}, bf16[3,128,1024]{2,1,0:T(8,128)(2,1)S(1)}, u32[]{:S(2)}, u32[]{:S(2)}) collective-permute-start(bf16[3,128,1024]{2,1,0:T(8,128)(2,1)S(1)} %pad_maximum_fusion.9.refs_12_), channel_id=1, source_target_pairs={{0,1},{1,0},{2,3},{3,2},{4,5},{5,4},{6,7},{7,6},{8,9},{9,8},{10,11... | collective-permute-start | bytes 2359304 | tf_op jit(solution)/shard_map/ppermute | solution.py:56
  128.2 18.9 %collective-permute-start.24 = (bf16[3,128,1024]{2,1,0:T(8,128)(2,1)S(1)}, bf16[3,128,1024]{2,1,0:T(8,128)(2,1)S(1)}, u32[]{:S(2)}, u32[]{:S(2)}) collective-permute-start(bf16[3,128,1024]{2,1,0:T(8,128)(2,1)S(1)} %pad_maximum_fusion.9.refs_12_), channel_id=1, source_target_pairs={{0,16},{16,0},{1,17},{17,1},{2,18},{18,2},{3,19},{19,3},{4,20},{20... | collective-permute-start | bytes 2359304 | tf_op jit(solution)/shard_map/ppermute | solution.py:56
  149.6 9.9 %collective-permute-start.25 = (bf16[3,64,1024]{2,1,0:T(8,128)(2,1)S(1)}, bf16[3,64,1024]{2,1,0:T(8,128)(2,1)S(1)}, u32[]{:S(2)}, u32[]{:S(2)}) collective-permute-start(bf16[3,64,1024]{2,1,0:T(8,128)(2,1)S(1)} %get-tuple-element.314), channel_id=1, source_target_pairs={{0,16},{16,0},{1,17},{17,1},{2,18},{18,2},{3,19},{19,3},{4,20},{20... | collective-permute-start | bytes 1179656 | tf_op jit(solution)/shard_map/ppermute | solution.py:56
  150.8 9.5 %collective-permute-start.26 = (bf16[3,64,1024]{2,1,0:T(8,128)(2,1)S(1)}, bf16[3,64,1024]{2,1,0:T(8,128)(2,1)S(1)}, u32[]{:S(2)}, u32[]{:S(2)}) collective-permute-start(bf16[3,64,1024]{2,1,0:T(8,128)(2,1)S(1)} %get-tuple-element.315), channel_id=1, source_target_pairs={{0,1},{1,0},{2,3},{3,2},{4,5},{5,4},{6,7},{7,6},{8,9},{9,8},{10,11... | collective-permute-start | bytes 1179656 | tf_op jit(solution)/shard_map/ppermute | solution.py:56
  160.3 22.7 %collective-permute-start.27 = (bf16[4,128,1024]{2,1,0:T(8,128)(2,1)S(1)}, bf16[4,128,1024]{2,1,0:T(8,128)(2,1)S(1)}, u32[]{:S(2)}, u32[]{:S(2)}) collective-permute-start(bf16[4,128,1024]{2,1,0:T(8,128)(2,1)S(1)} %get-tuple-element.328), channel_id=1, source_target_pairs={{0,1},{1,0},{2,3},{3,2},{4,5},{5,4},{6,7},{7,6},{8,9},{9,8},{10,11... | collective-permute-start | bytes 3145736 | tf_op jit(solution)/shard_map/ppermute | solution.py:56
  160.9 22.1 %collective-permute-start.28 = (bf16[4,2,64,1024]{3,2,1,0:T(8,128)(2,1)S(1)}, bf16[4,2,64,1024]{3,2,1,0:T(8,128)(2,1)S(1)}, u32[]{:S(2)}, u32[]{:S(2)}) collective-permute-start(bf16[4,2,64,1024]{3,2,1,0:T(8,128)(2,1)S(1)} %get-tuple-element.329), channel_id=1, source_target_pairs={{0,16},{16,0},{1,17},{17,1},{2,18},{18,2},{3,19},{19,3},{4,20},{20... | collective-permute-start | bytes 3145736 | tf_op jit(solution)/shard_map/ppermute | solution.py:56
  185.7 16.8 %collective-permute-start.29 = (bf16[1024,1024]{1,0:T(8,128)(2,1)}, bf16[1024,1024]{1,0:T(8,128)(2,1)}, u32[]{:S(2)}, u32[]{:S(2)}) collective-permute-start(bf16[1024,1024]{1,0:T(8,128)(2,1)} %get-tuple-element.357.refs_1_), channel_id=1, source_target_pairs={{0,8},{8,0},{1,9},{9,1},{2,10},{10,2},{3,11},{11,3},{4,12},{12,4},... | collective-permute-start | bytes 6291464 | tf_op jit(solution)/shard_map/ppermute | solution.py:56
  189.1 8.9 %collective-permute-start.32 = (bf16[2,256,1024]{2,1,0:T(8,128)(2,1)}, bf16[2,256,1024]{2,1,0:T(8,128)(2,1)}, u32[]{:S(2)}, u32[]{:S(2)}) collective-permute-start(bf16[2,256,1024]{2,1,0:T(8,128)(2,1)} %get-tuple-element.344), channel_id=1, source_target_pairs={{0,8},{8,0},{1,9},{9,1},{2,10},{10,2},{3,11},{11,3},{4,12},{12,4},... | collective-permute-start | bytes 3145736 | tf_op jit(solution)/shard_map/ppermute | solution.py:56
  189.1 13.2 %collective-permute-start.30 = (bf16[4,64,1024]{2,1,0:T(8,128)(2,1)}, bf16[4,64,1024]{2,1,0:T(8,128)(2,1)S(1)}, u32[]{:S(2)}, u32[]{:S(2)}) collective-permute-start(bf16[4,64,1024]{2,1,0:T(8,128)(2,1)} %get-tuple-element.340), channel_id=1, source_target_pairs={{0,16},{16,0},{1,17},{17,1},{2,18},{18,2},{3,19},{19,3},{4,20},{20... | collective-permute-start | bytes 1572872 | tf_op jit(solution)/shard_map/ppermute | solution.py:56
  189.6 12.9 %collective-permute-start.31 = (bf16[4,64,1024]{2,1,0:T(8,128)(2,1)}, bf16[4,64,1024]{2,1,0:T(8,128)(2,1)S(1)}, u32[]{:S(2)}, u32[]{:S(2)}) collective-permute-start(bf16[4,64,1024]{2,1,0:T(8,128)(2,1)} %get-tuple-element.341), channel_id=1, source_target_pairs={{0,1},{1,0},{2,3},{3,2},{4,5},{5,4},{6,7},{7,6},{8,9},{9,8},{10,11... | collective-permute-start | bytes 1572872 | tf_op jit(solution)/shard_map/ppermute | solution.py:56
  203.5 11.4 %collective-permute-start.33 = (bf16[2,64,1024]{2,1,0:T(8,128)(2,1)S(1)}, bf16[2,64,1024]{2,1,0:T(8,128)(2,1)S(1)}, u32[]{:S(2)}, u32[]{:S(2)}) collective-permute-start(bf16[2,64,1024]{2,1,0:T(8,128)(2,1)S(1)} %get-tuple-element.360), channel_id=1, source_target_pairs={{0,2},{2,4},{4,6},{6,0},{1,3},{3,5},{5,7},{7,1},{8,10},{10,12},{12... | collective-permute-start | bytes 786440 | tf_op jit(solution)/shard_map/ppermute | solution.py:250
  203.6 15.4 %collective-permute-start.34 = (bf16[2,64,1024]{2,1,0:T(8,128)(2,1)S(1)}, bf16[2,64,1024]{2,1,0:T(8,128)(2,1)S(1)}, u32[]{:S(2)}, u32[]{:S(2)}) collective-permute-start(bf16[2,64,1024]{2,1,0:T(8,128)(2,1)S(1)} %get-tuple-element.361), channel_id=1, source_target_pairs={{0,6},{2,0},{4,2},{6,4},{1,7},{3,1},{5,3},{7,5},{8,14},{10,8},{12,... | collective-permute-start | bytes 786440 | tf_op jit(solution)/shard_map/ppermute | solution.py:250
  205.0 34.1 %collective-permute-start.35 = (bf16[4,64,2048]{2,1,0:T(8,128)(2,1)S(1)}, bf16[4,64,2048]{2,1,0:T(8,128)(2,1)S(1)}, u32[]{:S(2)}, u32[]{:S(2)}) collective-permute-start(bf16[4,64,2048]{2,1,0:T(8,128)(2,1)S(1)} %get-tuple-element.366), channel_id=1, source_target_pairs={{0,1},{1,0},{2,3},{3,2},{4,5},{5,4},{6,7},{7,6},{8,9},{9,8},{10,11... | collective-permute-start | bytes 3145736 | tf_op jit(solution)/shard_map/ppermute | solution.py:56
  205.7 33.4 %collective-permute-start.36 = (bf16[4,2,32,2048]{3,2,1,0:T(8,128)(2,1)S(1)}, bf16[4,2,32,2048]{3,2,1,0:T(8,128)(2,1)S(1)}, u32[]{:S(2)}, u32[]{:S(2)}) collective-permute-start(bf16[4,2,32,2048]{3,2,1,0:T(8,128)(2,1)S(1)} %get-tuple-element.367), channel_id=1, source_target_pairs={{0,16},{16,0},{1,17},{17,1},{2,18},{18,2},{3,19},{19,3},{4,20},{20... | collective-permute-start | bytes 3145736 | tf_op jit(solution)/shard_map/ppermute | solution.py:56
  206.8 32.3 %collective-permute-start.37 = (bf16[256,1024]{1,0:T(8,128)(2,1)S(1)}, bf16[256,1024]{1,0:T(8,128)(2,1)S(1)}, u32[]{:S(2)}, u32[]{:S(2)}) collective-permute-start(bf16[256,1024]{1,0:T(8,128)(2,1)S(1)} %dynamic-slice_bitcast_fusion.1), channel_id=1, source_target_pairs={{0,16},{16,0},{1,17},{17,1},{2,18},{18,2},{3,19},{19,3},{4,20},{20... | collective-permute-start | bytes 1572872 | tf_op jit(solution)/shard_map/ppermute | solution.py:56
  218.9 18.9 %collective-permute-start.38 = (bf16[2,64,1024]{2,1,0:T(8,128)(2,1)S(1)}, bf16[2,64,1024]{2,1,0:T(8,128)(2,1)S(1)}, u32[]{:S(2)}, u32[]{:S(2)}) collective-permute-start(bf16[2,64,1024]{2,1,0:T(8,128)(2,1)S(1)} %get-tuple-element.372), channel_id=1, source_target_pairs={{0,4},{2,6},{4,0},{6,2},{1,5},{3,7},{5,1},{7,3},{8,12},{10,14},{12... | collective-permute-start | bytes 786440 | tf_op jit(solution)/shard_map/ppermute | solution.py:250
  218.9 23.9 %copy-start.15 = (bf16[1024,128]{1,0:T(8,128)(2,1)S(1)}, bf16[1024,128]{1,0:T(8,128)(2,1)}, u32[]{:S(2)}) copy-start(bf16[1024,128]{1,0:T(8,128)(2,1)} %get-tuple-element.385.refs_3_) | copy-start | bytes 786436
  239.1 13.9 %collective-permute-start.41 = (bf16[2,64,1024]{2,1,0:T(8,128)(2,1)S(1)}, bf16[2,64,1024]{2,1,0:T(8,128)(2,1)S(1)}, u32[]{:S(2)}, u32[]{:S(2)}) collective-permute-start(bf16[2,64,1024]{2,1,0:T(8,128)(2,1)S(1)} %add_convert_fusion.2), channel_id=1, source_target_pairs={{0,16},{16,0},{1,17},{17,1},{2,18},{18,2},{3,19},{19,3},{4,20},{20... | collective-permute-start | bytes 786440 | tf_op jit(solution)/shard_map/ppermute | solution.py:56
  241.6 13.5 %collective-permute-start.39 = (bf16[4,32,2048]{2,1,0:T(8,128)(2,1)S(1)}, bf16[4,32,2048]{2,1,0:T(8,128)(2,1)S(1)}, u32[]{:S(2)}, u32[]{:S(2)}) collective-permute-start(bf16[4,32,2048]{2,1,0:T(8,128)(2,1)S(1)} %get-tuple-element.380), channel_id=1, source_target_pairs={{0,16},{16,0},{1,17},{17,1},{2,18},{18,2},{3,19},{19,3},{4,20},{20... | collective-permute-start | bytes 1572872 | tf_op jit(solution)/shard_map/ppermute | solution.py:56
  242.1 13.0 %collective-permute-start.40 = (bf16[4,32,2048]{2,1,0:T(8,128)(2,1)S(1)}, bf16[4,32,2048]{2,1,0:T(8,128)(2,1)S(1)}, u32[]{:S(2)}, u32[]{:S(2)}) collective-permute-start(bf16[4,32,2048]{2,1,0:T(8,128)(2,1)S(1)} %get-tuple-element.381), channel_id=1, source_target_pairs={{0,1},{1,0},{2,3},{3,2},{4,5},{5,4},{6,7},{7,6},{8,9},{9,8},{10,11... | collective-permute-start | bytes 1572872 | tf_op jit(solution)/shard_map/ppermute | solution.py:56
  256.1 28.5 %collective-permute-start.42 = (bf16[4,64,2176]{2,1,0:T(8,128)(2,1)S(1)}, bf16[4,64,2176]{2,1,0:T(8,128)(2,1)S(1)}, u32[]{:S(2)}, u32[]{:S(2)}) collective-permute-start(bf16[4,64,2176]{2,1,0:T(8,128)(2,1)S(1)} %get-tuple-element.403), channel_id=1, source_target_pairs={{0,1},{1,0},{2,3},{3,2},{4,5},{5,4},{6,7},{7,6},{8,9},{9,8},{10,11... | collective-permute-start | bytes 3342344 | tf_op jit(solution)/shard_map/ppermute | solution.py:56
  256.9 27.7 %collective-permute-start.43 = (bf16[4,2,32,2176]{3,2,1,0:T(8,128)(2,1)S(1)}, bf16[4,2,32,2176]{3,2,1,0:T(8,128)(2,1)S(1)}, u32[]{:S(2)}, u32[]{:S(2)}) collective-permute-start(bf16[4,2,32,2176]{3,2,1,0:T(8,128)(2,1)S(1)} %get-tuple-element.404), channel_id=1, source_target_pairs={{0,16},{16,0},{1,17},{17,1},{2,18},{18,2},{3,19},{19,3},{4,20},{20... | collective-permute-start | bytes 3342344 | tf_op jit(solution)/shard_map/ppermute | solution.py:56
  257.8 10.0 %collective-permute-start.44 = (bf16[2,32,2048]{2,1,0:T(8,128)(2,1)S(1)}, bf16[2,32,2048]{2,1,0:T(8,128)(2,1)S(1)}, u32[]{:S(2)}, u32[]{:S(2)}) collective-permute-start(bf16[2,32,2048]{2,1,0:T(8,128)(2,1)S(1)} %get-tuple-element.407), channel_id=1, source_target_pairs={{0,2},{2,4},{4,6},{6,0},{1,3},{3,5},{5,7},{7,1},{8,10},{10,12},{12... | collective-permute-start | bytes 786440 | tf_op jit(solution)/shard_map/ppermute | solution.py:250
  259.9 19.6 %collective-permute-start.45 = (bf16[2,32,2048]{2,1,0:T(8,128)(2,1)S(1)}, bf16[2,32,2048]{2,1,0:T(8,128)(2,1)S(1)}, u32[]{:S(2)}, u32[]{:S(2)}) collective-permute-start(bf16[2,32,2048]{2,1,0:T(8,128)(2,1)S(1)} %get-tuple-element.408), channel_id=1, source_target_pairs={{0,4},{2,6},{4,0},{6,2},{1,5},{3,7},{5,1},{7,3},{8,12},{10,14},{12... | collective-permute-start | bytes 786440 | tf_op jit(solution)/shard_map/ppermute | solution.py:250
  262.8 21.8 %collective-permute-start.46 = (bf16[2,32,2048]{2,1,0:T(8,128)(2,1)S(1)}, bf16[2,32,2048]{2,1,0:T(8,128)(2,1)S(1)}, u32[]{:S(2)}, u32[]{:S(2)}) collective-permute-start(bf16[2,32,2048]{2,1,0:T(8,128)(2,1)S(1)} %get-tuple-element.409), channel_id=1, source_target_pairs={{0,6},{2,0},{4,2},{6,4},{1,7},{3,1},{5,3},{7,5},{8,14},{10,8},{12,... | collective-permute-start | bytes 786440 | tf_op jit(solution)/shard_map/ppermute | solution.py:250
  286.3 3.8 %collective-permute-start.49 = (bf16[2,256,1024]{2,1,0:T(8,128)(2,1)S(1)}, bf16[2,256,1024]{2,1,0:T(8,128)(2,1)S(1)}, u32[]{:S(2)}, u32[]{:S(2)}) collective-permute-start(bf16[2,256,1024]{2,1,0:T(8,128)(2,1)S(1)} %dynamic-slice_bitcast_fusion), channel_id=1, source_target_pairs={{0,8},{8,0},{1,9},{9,1},{2,10},{10,2},{3,11},{11,3},{4,12},{12,4},... | collective-permute-start | bytes 3145736 | tf_op jit(solution)/shard_map/ppermute | solution.py:56
  288.4 14.3 %collective-permute-start.47 = (bf16[4,32,2176]{2,1,0:T(8,128)(2,1)S(1)}, bf16[4,32,2176]{2,1,0:T(8,128)(2,1)S(1)}, u32[]{:S(2)}, u32[]{:S(2)}) collective-permute-start(bf16[4,32,2176]{2,1,0:T(8,128)(2,1)S(1)} %get-tuple-element.427), channel_id=1, source_target_pairs={{0,16},{16,0},{1,17},{17,1},{2,18},{18,2},{3,19},{19,3},{4,20},{20... | collective-permute-start | bytes 1671176 | tf_op jit(solution)/shard_map/ppermute | solution.py:56
  289.0 13.9 %collective-permute-start.48 = (bf16[4,32,2176]{2,1,0:T(8,128)(2,1)S(1)}, bf16[4,32,2176]{2,1,0:T(8,128)(2,1)S(1)}, u32[]{:S(2)}, u32[]{:S(2)}) collective-permute-start(bf16[4,32,2176]{2,1,0:T(8,128)(2,1)S(1)} %get-tuple-element.428), channel_id=1, source_target_pairs={{0,1},{1,0},{2,3},{3,2},{4,5},{5,4},{6,7},{7,6},{8,9},{9,8},{10,11... | collective-permute-start | bytes 1671176 | tf_op jit(solution)/shard_map/ppermute | solution.py:56
  302.9 6.7 %collective-permute-start.54 = (bf16[2,32,2048]{2,1,0:T(8,128)(2,1)S(1)}, bf16[2,32,2048]{2,1,0:T(8,128)(2,1)S(1)}, u32[]{:S(2)}, u32[]{:S(2)}) collective-permute-start(bf16[2,32,2048]{2,1,0:T(8,128)(2,1)S(1)} %add_convert_fusion.1), channel_id=1, source_target_pairs={{0,16},{16,0},{1,17},{17,1},{2,18},{18,2},{3,19},{19,3},{4,20},{20... | collective-permute-start | bytes 786440 | tf_op jit(solution)/shard_map/ppermute | solution.py:56
  303.9 6.8 %collective-permute-start.56 = (bf16[256,1024]{1,0:T(8,128)(2,1)S(1)}, bf16[256,1024]{1,0:T(8,128)(2,1)S(1)}, u32[]{:S(2)}, u32[]{:S(2)}) collective-permute-start(bf16[256,1024]{1,0:T(8,128)(2,1)S(1)} %bitcast.167), channel_id=1, source_target_pairs={{0,8},{8,0},{1,9},{9,1},{2,10},{10,2},{3,11},{11,3},{4,12},{12,4},... | collective-permute-start | bytes 1572872 | tf_op jit(solution)/shard_map/ppermute | solution.py:56
  306.3 11.6 %collective-permute-start.50 = (bf16[2,32,2176]{2,1,0:T(8,128)(2,1)S(1)}, bf16[2,32,2176]{2,1,0:T(8,128)(2,1)S(1)}, u32[]{:S(2)}, u32[]{:S(2)}) collective-permute-start(bf16[2,32,2176]{2,1,0:T(8,128)(2,1)S(1)} %get-tuple-element.435), channel_id=1, source_target_pairs={{0,2},{2,4},{4,6},{6,0},{1,3},{3,5},{5,7},{7,1},{8,10},{10,12},{12... | collective-permute-start | bytes 835592 | tf_op jit(solution)/shard_map/ppermute | solution.py:250
  306.4 24.1 %collective-permute-start.51 = (bf16[2,32,2176]{2,1,0:T(8,128)(2,1)S(1)}, bf16[2,32,2176]{2,1,0:T(8,128)(2,1)}, u32[]{:S(2)}, u32[]{:S(2)}) collective-permute-start(bf16[2,32,2176]{2,1,0:T(8,128)(2,1)S(1)} %get-tuple-element.436), channel_id=1, source_target_pairs={{0,4},{2,6},{4,0},{6,2},{1,5},{3,7},{5,1},{7,3},{8,12},{10,14},{12... | collective-permute-start | bytes 835592 | tf_op jit(solution)/shard_map/ppermute | solution.py:250
  309.1 25.0 %collective-permute-start.52 = (bf16[2,32,2176]{2,1,0:T(8,128)(2,1)S(1)}, bf16[2,32,2176]{2,1,0:T(8,128)(2,1)}, u32[]{:S(2)}, u32[]{:S(2)}) collective-permute-start(bf16[2,32,2176]{2,1,0:T(8,128)(2,1)S(1)} %get-tuple-element.437), channel_id=1, source_target_pairs={{0,6},{2,0},{4,2},{6,4},{1,7},{3,1},{5,3},{7,5},{8,14},{10,8},{12,... | collective-permute-start | bytes 835592 | tf_op jit(solution)/shard_map/ppermute | solution.py:250
  309.6 24.5 %collective-permute-start.53 = (bf16[256,1024]{1,0:T(8,128)(2,1)}, bf16[256,1024]{1,0:T(8,128)(2,1)}, u32[]{:S(2)}, u32[]{:S(2)}) collective-permute-start(bf16[256,1024]{1,0:T(8,128)(2,1)} %fusion.16), channel_id=1, source_target_pairs={{0,16},{16,0},{1,17},{17,1},{2,18},{18,2},{3,19},{19,3},{4,20},{20... | collective-permute-start | bytes 1572872 | tf_op jit(solution)/shard_map/ppermute | solution.py:56
  310.7 4.3 %collective-permute-start.55 = (bf16[128,2048]{1,0:T(8,128)(2,1)S(1)}, bf16[128,2048]{1,0:T(8,128)(2,1)}, u32[]{:S(2)}, u32[]{:S(2)}) collective-permute-start(bf16[128,2048]{1,0:T(8,128)(2,1)S(1)} %bitcast.170), channel_id=1, source_target_pairs={{0,8},{8,0},{1,9},{9,1},{2,10},{10,2},{3,11},{11,3},{4,12},{12,4},... | collective-permute-start | bytes 1572872 | tf_op jit(solution)/shard_map/ppermute | solution.py:56
  335.3 7.7 %collective-permute-start.57 = (bf16[2,32,2176]{2,1,0:T(8,128)(2,1)S(1)}, bf16[2,32,2176]{2,1,0:T(8,128)(2,1)S(1)}, u32[]{:S(2)}, u32[]{:S(2)}) collective-permute-start(bf16[2,32,2176]{2,1,0:T(8,128)(2,1)S(1)} %add_convert_fusion), channel_id=1, source_target_pairs={{0,16},{16,0},{1,17},{17,1},{2,18},{18,2},{3,19},{19,3},{4,20},{20... | collective-permute-start | bytes 835592 | tf_op jit(solution)/shard_map/ppermute | solution.py:56
  343.2 3.1 collective-permute-start.58
  (43 other events, 314.2 us)

commit v7 on v6

--- a/solution.py
+++ b/solution.py
@@ -233,7 +233,7 @@
             pltpu.VMEM((rows, LANES), f32),
         ],
         compiler_params=pltpu.CompilerParams(vmem_limit_bytes=VMEM),
-        cost_estimate=cost(6 * count),
+        cost_estimate=cost(0.5 * count),
         name="attend_back",
     )(far(joint), far(joint), far(joint), grads, far(lse), seg_col, seg_row)
 
@@ -1000,14 +1000,7 @@
     if fine_down:
         down_came = swap(down_send[0], "hi"), swap(down_send[1], "fx")
     up_keep, up_send = outer(place, depth, far(normed_two), far(grad_pre))
-    output = (own_chunks(middle).astype(f32) + result.astype(f32) + result_other.astype(f32)).astype(bf16)
-    back, back_other, up_keep, up_send, down_came, output = sync(
-        back, back_other, up_keep, up_send, down_came, output
-    )
-    if fine_down:
-        down_sum, down_send = fold_two(place, down_kept, down_came)
-        down_send, back, back_other, up_send = sync(down_send, back, back_other, up_send)
-        down_came = hop(down_send, 1)
+    back, back_other, up_keep, up_send, result_other = sync(back, back_other, up_keep, up_send, result_other)
 
     def between(place_ref, given, held, made, scratch, sems):
         grad_ref, own_ref, other_ref, middle_ref, scales_ref, weight = given
@@ -1050,16 +1043,16 @@
         1,
         8,
     )
+    up_came = swap(up_send[0], "fx"), swap(up_send[1], "hi")
+    down_sum = None
     if fine_down:
-        grad_attended, down_came, down_send = sync(grad_attended, down_came, down_send)
-        down_came = down_came + hop(down_send, 0)
+        grad_attended, down_came, down_kept = sync(grad_attended, down_came, down_kept)
+        down_sum, down_send = fold_two(place, down_kept, down_came)
+        grad_attended, down_send = sync(grad_attended, down_send)
+        down_came = [along(value, "fz", depth, k) for k, value in zip(rest, down_send)]
     grad_joint = attend_back(joint, grad_attended, lse, seg_col, seg_row, 0, pairs)
-    up_came = swap(up_send[0], "fx"), swap(up_send[1], "hi")
-    output_came = swap(pick(output, 1 - h, 0), "hi")
-    if fine_down:
-        down_came = add_up(down_sum, down_came)
-    grad_joint, grad_branch, up_came, output_came, down_came = sync(
-        grad_joint, grad_branch, up_came, output_came, down_came
+    grad_joint, grad_branch, up_came, result_other, down_came, down_sum = sync(
+        grad_joint, grad_branch, up_came, result_other, down_came, down_sum
     )
 
     def both_halves(value):
@@ -1069,7 +1062,7 @@
     up_kept, up_send, grad_joint = sync(up_kept, up_send, grad_joint)
     up_came = swap(up_send[0], "hi"), swap(up_send[1], "fx")
     if fine_down:
-        down_own = both_halves(down_came)
+        down_own = both_halves(add_up(down_sum, down_came))
     else:
         down_own = lax.psum(lax.psum_scatter(down_came, shard_axes, scatter_dimension=0, tiled=True), "hi")
     last_keep, last_send = outer(
@@ -1082,8 +1075,8 @@
         scales=scale_columns,
         sums=sums_two,
     )
-    up_came, last_keep, last_send, down_own, grad_joint = sync(
-        up_came, last_keep, last_send, down_own, grad_joint
+    up_came, last_keep, last_send, down_own, grad_joint, result_other = sync(
+        up_came, last_keep, last_send, down_own, grad_joint, result_other
     )
 
     up_sum, up_send = fold_two(place, up_kept, up_came)
@@ -1114,7 +1107,7 @@
         1,
         14,
     )
-    output = ordered(pick(output, h, 0), output_came, h, 0)[:, None]
+    output = (own_chunks(middle).astype(f32) + result.astype(f32) + result_other.astype(f32)).astype(bf16)
     last_came, entered, up_sum, up_came, down_own, output = sync(
         last_came, entered, up_sum, up_came, down_own, output
     )
@@ -1123,28 +1116,32 @@
     up_own = add_up(up_sum, up_came)
     last_kept, last_send, entered, up_own, down_own = sync(last_kept, last_send, entered, up_own, down_own)
     last_came = swap(last_send[0], "hi"), swap(last_send[1], "fx")
+    up_own = both_halves(up_own)
+    down_all = whole_group(down_own, 0).reshape(-1, model).astype(f32)
     entered_other = other_own(entered)
     grad_normed = own_chunks(entered).astype(f32) + entered_other.astype(f32)
     unit_own, inverse_own = unit_of(own_chunks(inputs).astype(f32))
     grad_tokens = own_chunks(grad_branch).astype(f32) + unit_back(grad_normed * scales[0], unit_own, inverse_own)
     grad_sent = pick(grad_tokens, 1 - h, 0).astype(bf16)
-    last_came, grad_tokens, grad_sent, up_own, down_own = sync(last_came, grad_tokens, grad_sent, up_own, down_own)
+    last_came, grad_tokens, grad_sent, up_own, down_all, output = sync(
+        last_came, grad_tokens, grad_sent, up_own, down_all, output
+    )
 
     last_sum, last_send = fold_two(place, last_kept, last_came)
     last_came = [along(value, "fz", depth, k) for k, value in zip(rest, last_send)]
     grad_came = swap(grad_sent, "hi")
-    up_own = both_halves(up_own)
-    down_all = whole_group(down_own, 0).reshape(-1, model).astype(f32)
+    output_came = swap(pick(output, 1 - h, 0), "hi")
     up_all = None
     if fused_out:
         up_all = finish_up(place, shards, up_own, swap(up_own, "lo"))
-    last_came, grad_came, grad_tokens, up_own, up_all, down_all = sync(
-        last_came, grad_came, grad_tokens, up_own, up_all, down_all
+    last_came, grad_came, grad_tokens, up_own, up_all, output_came = sync(
+        last_came, grad_came, grad_tokens, up_own, up_all, output_came
     )
 
     last_own = both_halves(add_up(last_sum, last_came))
+    output = ordered(pick(output, h, 0), output_came, h, 0)[:, None]
     grad_tokens = ordered(pick(grad_tokens, h, 0), grad_came.astype(f32), h, 0)[:, None]
-    last_own, grad_tokens = sync(last_own, grad_tokens)
+    last_own, grad_tokens, output = sync(last_own, grad_tokens, output)
     if fused_out:
         qkv_all, out_all, sums = finish_qkv(place, 3 * head_columns, [last_own], [swap(last_own, "lo")])
     else:

time: 353 us -> 351 us (level)
  waiting for transfers between devices: 126 us -> 122 us
  transfers between devices with their start and end apart: 59 -> 59, of which waited for: 29 -> 26; matrix products, arithmetic and copies ran while one was open for 5% -> 5% of each run, Pallas kernels for 34% -> 35%
where the time goes in v7:
time: 351 us; the launch traced here: 347 us
  Pallas kernels  137 us (39%)
  waiting for transfers between devices  122 us (35%)
  starting transfers between devices  56.8 us (16%)
  other arithmetic  20.2 us (6%)
  local copies, waits for them, and re-layouts  8.54 us (2%)
    ppermute x18, waiting for transfers between devices, along(): lax.ppermute(value, axis, [(i, (i + step) % depth) for i in range(depth)])  83.7 us
    pallas_call x6, Pallas kernels, weight_call(): pl.pallas_call(kernel, grid=(tiles,), in_specs=[pl.BlockSpec(memory_space...  61.8 us
    ppermute x41, starting transfers between devices, swap(): return lax.ppermute(value, axis, SWAP)  39 us
    ppermute x41, waiting for transfers between devices, swap(): return lax.ppermute(value, axis, SWAP)  38.7 us
    pallas_call x3, Pallas kernels, outer(): pl.pallas_call(kernel, grid=(depth,), in_specs=[pl.BlockSpec(memory_space...  23.2 us
    pallas_call x1, Pallas kernels, attend_back(): pl.pallas_call(functools.partial(attend_back_kernel, spans, tile), grid=(...  19.1 us
    ppermute x18, starting transfers between devices, along(): lax.ppermute(value, axis, [(i, (i + step) % depth) for i in range(depth)])  17.8 us
    pallas_call x2, Pallas kernels, attend(): pl.pallas_call(functools.partial(attend_kernel, spans, tile), grid=(count...  13.1 us
  transfers between devices with their start and end apart: 59, of which 26 were waited for; matrix products, arithmetic and copies ran while one was open for 5% of the time, Pallas kernels for 35%

profile of v7, /device:TPU:9, one launch (start us, length us, event | category | flops | bytes accessed | tf_op | source)
XLA Modules:
  0.0 346.6 jit_solution(1325744471118748266)
XLA Ops:
  1.5 2.0 prepare.1
  3.5 1.3 collective-permute-start.3
  6.2 1.3 collective-permute-start.4
  7.5 1.3 collective-permute-start
  9.8 1.5 collective-permute-start.2
  11.3 3.2 collective-permute-done
  14.5 16.9 %collective-permute-done.1 = bf16[64,2176]{1,0:T(8,128)(2,1)S(1)} collective-permute-done((bf16[64,2176]{1,0:T(8,128)(2,1)S(1)}, bf16[64,2176]{1,0:T(8,128)(2,1)S(1)}, u32[]{:S(2)}, u32[]{:S(2)}) %collective-permute-start.1) | collective-permute-done | bytes 278560 | tf_op jit(solution)/shard_map/ppermute | solution.py:250
  31.4 3.5 collective-permute-done.2
  37.4 1.5 collective-permute-start.9
  38.9 5.3 %collective-permute-done.7 = bf16[64,2048]{1,0:T(8,128)(2,1)S(1)} collective-permute-done((bf16[64,2048]{1,0:T(8,128)(2,1)S(1)}, bf16[64,2048]{1,0:T(8,128)(2,1)S(1)}, u32[]{:S(2)}, u32[]{:S(2)}) %collective-permute-start.7) | collective-permute-done | bytes 262176 | tf_op jit(solution)/shard_map/ppermute | solution.py:250
  44.2 14.9 %collective-permute-done.8 = bf16[64,2048]{1,0:T(8,128)(2,1)S(1)} collective-permute-done((bf16[64,2048]{1,0:T(8,128)(2,1)S(1)}, bf16[64,2048]{1,0:T(8,128)(2,1)S(1)}, u32[]{:S(2)}, u32[]{:S(2)}) %collective-permute-start.8) | collective-permute-done | bytes 262176 | tf_op jit(solution)/shard_map/ppermute | solution.py:250
  59.1 1.7 collective-permute-done.9
  60.8 1.5 halve.3
  64.4 1.3 collective-permute-start.10
  67.9 1.6 select_bitcast_fusion.3
  70.0 5.7 %collective-permute-done.10.refs_6_ = bf16[3,32,2176]{2,1,0:T(8,128)(2,1)S(1)} collective-permute-done((bf16[3,32,2176]{2,1,0:T(8,128)(2,1)S(1)}, bf16[3,32,2176]{2,1,0:T(8,128)(2,1)S(1)}, u32[]{:S(2)}, u32[]{:S(2)}) %collective-permute-start.10) | collective-permute-done | bytes 417824 | tf_op jit(solution)/shard_map/ppermute | solution.py:56
  78.2 2.0 collective-permute-start.16
  80.5 10.6 %project.1 = (bf16[1024,1024]{1,0:T(8,128)(2,1)}, bf16[1024,1536]{1,0:T(8,128)(2,1)}, f32[8,1024]{1,0:T(8,128)}, bf16[1024,1536]{1,0:T(8,128)(2,1)}, bf16[1024,1...) custom-call(s32[4]{0:T(128)S(1)} %pad_add_fusion.place_ref, bf16[1024,1024]{1,0:T(8,128)(2,1)S(1)} %bitcast.156, ...), custom_call_target="tpu_custom_call" | custom-call | flops 8800000000 | bytes 1000 | tf_op jit(solution)/shard_map/project/pallas_call | solution.py:508
  91.1 6.5 %attend.2 = (bf16[1024,256]{1,0:T(8,128)(2,1)S(1)}, f32[1024,256]{1,0:T(8,128)}) custom-call(bf16[1024,1536]{1,0:T(8,128)(2,1)} %get-tuple-element.279.q_ref.k_ref.v_ref, bf16[1024,1536]{1,0:T(8,128)(2,1)} %get-tuple-element.279.q_ref.k_ref.v_ref, bf16[1024,1536]{1,0:T(8,128)(2,1)} %get-tuple-element.279.q_ref.k_ref.v_ref, s32[1024,1]{1,0:T(8,128)S(1)} %copy.29.seg_col, ...), custom_call_target="tpu_custom_call" | custom-call | flops 8800000000 | bytes 1000 | tf_op jit(solution)/shard_map/attend/pallas_call | solution.py:142
  97.6 8.2 %collective-permute-done.17.refs_11_ = bf16[2,128,1024]{2,1,0:T(8,128)(2,1)S(1)} collective-permute-done((bf16[2,128,1024]{2,1,0:T(8,128)(2,1)S(1)}, bf16[2,128,1024]{2,1,0:T(8,128)(2,1)S(1)}, u32[]{:S(2)}, u32[]{:S(2)}) %collective-permute-start.17) | collective-permute-done | bytes 524320 | tf_op jit(solution)/shard_map/ppermute | solution.py:56
  107.0 1.4 halve.4
  108.6 2.1 collective-permute-start.20
  112.3 3.1 collective-permute-start.21
  115.4 6.5 %attend.3 = (bf16[1024,256]{1,0:T(8,128)(2,1)S(1)}, f32[1024,256]{1,0:T(8,128)}) custom-call(bf16[1024,1536]{1,0:T(8,128)(2,1)} %get-tuple-element.279.q_ref.k_ref.v_ref, bf16[1024,1536]{1,0:T(8,128)(2,1)} %get-tuple-element.279.q_ref.k_ref.v_ref, bf16[1024,1536]{1,0:T(8,128)(2,1)} %get-tuple-element.279.q_ref.k_ref.v_ref, s32[1024,1]{1,0:T(8,128)S(1)} %copy.29.seg_col, ...), custom_call_target="tpu_custom_call" | custom-call | flops 8800000000 | bytes 1000 | tf_op jit(solution)/shard_map/attend/pallas_call | solution.py:142
  122.3 1.5 collective-permute-done.21
  123.8 3.2 leave.1
  129.3 1.6 pad_maximum_fusion.2.lse_ref
  131.5 13.8 %widen.1 = (bf16[1024,1024]{1,0:T(8,128)(2,1)}, bf16[1024,1024]{1,0:T(8,128)(2,1)}, bf16[1024,2048]{1,0:T(8,128)(2,1)}, bf16[1024,2048]{1,0:T(8,128)(2,1)}) custom-call(s32[4]{0:T(128)S(1)} %pad_add_fusion.place_ref, bf16[1024,1024]{1,0:T(8,128)(2,1)S(1)} %bitcast.157, bf16[1024,1024]{1,0:T(8,128)(2,1)S(1)} %get-tuple-element.290.refs_1_, ...), custom_call_target="tpu_custom_call" | custom-call | flops 14300000256 | bytes 1000 | tf_op jit(solution)/shard_map/widen/pallas_call | solution.py:508
  145.3 1.8 collective-permute-done.23.side_ref.refs_13_
  148.2 1.4 halve.5
  151.7 6.6 %outer.3 = (bf16[4,128,1024]{2,1,0:T(8,128)(2,1)S(1)}, bf16[4,128,1024]{2,1,0:T(8,128)(2,1)S(1)}, bf16[4,2,64,1024]{3,2,1,0:T(8,128)(2,1)S(1)}, bf16[4,2,64,1024]{3,2,1,0:T(8,128)(2,1)S(1)}) custom-call(s32[4]{0:T(128)S(1)} %pad_add_fusion.place_ref, bf16[1024,2048]{1,0:T(8,128)(2,1)} %get-tuple-element.317.refs_0_, bf16[1024,1024]{1,0:T(8,128)(2,1)S(1)} %bitcast.161), custom_call_target="tpu_custom_call" | custom-call | flops 6600000000 | bytes 1000 | tf_op jit(solution)/shard_map/outer/pallas_call | solution.py:629
  161.3 21.7 %narrow.1 = (bf16[2,256,1024]{2,1,0:T(8,128)(2,1)}, bf16[2,256,1024]{2,1,0:T(8,128)(2,1)}, bf16[1024,2048]{1,0:T(8,128)(2,1)}, bf16[1024,1024]{1,0:T(8,128)(2,1)}) custom-call(s32[4]{0:T(128)S(1)} %pad_add_fusion.place_ref, bf16[1024,2048]{1,0:T(8,128)(2,1)} %get-tuple-element.317.refs_0_, bf16[1024,1024]{1,0:T(8,128)(2,1)} %bitcast.162, ...), custom_call_target="tpu_custom_call" | custom-call | flops 19800000512 | bytes 1000 | tf_op jit(solution)/shard_map/narrow/pallas_call | solution.py:508
  183.0 2.7 fold_one.3
  185.6 3.5 collective-permute-start.29
  190.7 7.6 %outer.4 = (bf16[4,64,2048]{2,1,0:T(8,128)(2,1)S(1)}, bf16[4,64,2048]{2,1,0:T(8,128)(2,1)S(1)}, bf16[4,2,32,2048]{3,2,1,0:T(8,128)(2,1)S(1)}, bf16[4,2,32,2048]{3,2,1,0:T(8,128)(2,1)S(1)}) custom-call(s32[4]{0:T(128)S(1)} %pad_add_fusion.place_ref, bf16[1024,1024]{1,0:T(8,128)(2,1)} %get-tuple-element.335.refs_0_, bf16[1024,2048]{1,0:T(8,128)(2,1)} %get-tuple-element.336.refs_1_), custom_call_target="tpu_custom_call" | custom-call | flops 6600000000 | bytes 1000 | tf_op jit(solution)/shard_map/outer/pallas_call | solution.py:629
  200.1 7.5 %between.1 = (bf16[1024,1024]{1,0:T(8,128)(2,1)}, bf16[1024,512]{1,0:T(8,128)(2,1)S(1)}, f32[8,1024]{1,0:T(8,128)S(1)}) custom-call(s32[4]{0:T(128)S(1)} %pad_add_fusion.place_ref, bf16[1024,1024]{1,0:T(8,128)(2,1)S(1)} %bitcast.163, bf16[1024,1024]{1,0:T(8,128)(2,1)} %get-tuple-element.344.refs_1_, bf16[1024,1024]{1,0:T(8,128)(2,1)} %collective-permute-done.29.refs_2_, ...), custom_call_target="tpu_custom_call" | custom-call | flops 8800000000 | bytes 1000 | tf_op jit(solution)/shard_map/between/pallas_call | solution.py:508
  208.6 3.1 collective-permute-start.36
  211.7 1.4 collective-permute-start.37
  213.5 19.1 %attend_back.1.refs_1_.refs_0_ = bf16[3,1024,512]{2,1,0:T(8,128)(2,1)S(1)} custom-call(bf16[1024,1536]{1,0:T(8,128)(2,1)} %get-tuple-element.279.q_ref.k_ref.v_ref, bf16[1024,1536]{1,0:T(8,128)(2,1)} %get-tuple-element.279.q_ref.k_ref.v_ref, bf16[1024,1536]{1,0:T(8,128)(2,1)} %get-tuple-element.279.q_ref.k_ref.v_ref, ...), custom_call_target="tpu_custom_call" | custom-call | flops 2200000000 | bytes 1000 | tf_op jit(solution)/shard_map/attend_back/pallas_call | solution.py:216
  232.7 2.6 collective-permute-done.37
  236.1 1.3 fold_one.4
  239.3 9.0 %outer.5 = (bf16[4,64,2176]{2,1,0:T(8,128)(2,1)S(1)}, bf16[4,64,2176]{2,1,0:T(8,128)(2,1)S(1)}, bf16[4,2,32,2176]{3,2,1,0:T(8,128)(2,1)S(1)}, bf16[4,2,32,2176]{3,2,1,0:T(8,128)(2,1)S(1)}) custom-call(s32[4]{0:T(128)S(1)} %pad_add_fusion.place_ref, bf16[1024,1024]{1,0:T(8,128)(2,1)S(1)} %copy-done.11, bf16[3,1024,512]{2,1,0:T(8,128)(2,1)S(1)} %attend_back.1.refs_1_.refs_0_, ...), custom_call_target="tpu_custom_call" | custom-call | flops 6600000000 | bytes 1000 | tf_op jit(solution)/shard_map/outer/pallas_call | solution.py:629
  248.5 5.7 %collective-permute-done.38.came_one = bf16[4,32,2048]{2,1,0:T(8,128)(2,1)S(1)} collective-permute-done((bf16[4,32,2048]{2,1,0:T(8,128)(2,1)S(1)}, bf16[4,32,2048]{2,1,0:T(8,128)(2,1)S(1)}, u32[]{:S(2)}, u32[]{:S(2)}) %collective-permute-start.38) | collective-permute-done | bytes 524320 | tf_op jit(solution)/shard_map/ppermute | solution.py:56
  256.5 1.5 collective-permute-start.45
  257.9 5.1 %enter.1 = bf16[1024,1024]{1,0:T(8,128)(2,1)S(1)} custom-call(s32[4]{0:T(128)S(1)} %pad_add_fusion.place_ref, bf16[3,1024,512]{2,1,0:T(8,128)(2,1)S(1)} %attend_back.1.refs_1_.refs_0_, bf16[1024,1536]{1,0:T(8,128)(2,1)S(1)} %copy-done.10), custom_call_target="tpu_custom_call" | custom-call | flops 15399999488 | bytes 1000 | tf_op jit(solution)/shard_map/enter/pallas_call | solution.py:508
  263.0 1.9 fusion.12
  264.9 12.4 %collective-permute-done.44 = bf16[2,32,2048]{2,1,0:T(8,128)(2,1)S(1)} collective-permute-done((bf16[2,32,2048]{2,1,0:T(8,128)(2,1)S(1)}, bf16[2,32,2048]{2,1,0:T(8,128)(2,1)S(1)}, u32[]{:S(2)}, u32[]{:S(2)}) %collective-permute-start.44) | collective-permute-done | bytes 262176 | tf_op jit(solution)/shard_map/ppermute | solution.py:250
  277.3 1.8 collective-permute-done.45
  280.7 1.4 fold_one.5
  282.5 2.9 collective-permute-start.50
  287.7 1.6 bitcast_convert_fusion
  292.2 8.0 %collective-permute-done.46.came_one = bf16[4,32,2176]{2,1,0:T(8,128)(2,1)S(1)} collective-permute-done((bf16[4,32,2176]{2,1,0:T(8,128)(2,1)S(1)}, bf16[4,32,2176]{2,1,0:T(8,128)(2,1)S(1)}, u32[]{:S(2)}, u32[]{:S(2)}) %collective-permute-start.46) | collective-permute-done | bytes 557088 | tf_op jit(solution)/shard_map/ppermute | solution.py:56
  300.2 2.8 collective-permute-start.55
  307.2 1.4 collective-permute-start.53
  308.6 2.7 finish_up.1
  311.3 2.7 collective-permute-done.51
  314.1 15.9 %collective-permute-done.52 = bf16[2,32,2176]{2,1,0:T(8,128)(2,1)S(1)} collective-permute-done((bf16[2,32,2176]{2,1,0:T(8,128)(2,1)S(1)}, bf16[2,32,2176]{2,1,0:T(8,128)(2,1)S(1)}, u32[]{:S(2)}, u32[]{:S(2)}) %collective-permute-start.52) | collective-permute-done | bytes 278560 | tf_op jit(solution)/shard_map/ppermute | solution.py:250
  330.0 1.3 collective-permute-done.53
  333.7 1.4 fusion.14
  336.2 1.6 maximum_bitcast_fusion
  337.7 2.6 collective-permute-done.57
  340.6 1.4 collective-permute-start.58
  342.0 1.6 collective-permute-done.58.refs_1_
  343.6 2.3 finish_qkv.1
  (234 shorter events, 50.8 us)
Async XLA Ops:
  0.6 38.2 %copy-start = (bf16[512,1024]{1,0:T(8,128)(2,1)S(1)}, bf16[512,1024]{1,0:T(8,128)(2,1)}, u32[]{:S(2)}) copy-start(bf16[512,1024]{1,0:T(8,128)(2,1)} %param.20) | copy-start | bytes 3145732
  0.7 304.6 %copy-start.5 = (s32[4]{0:T(128)}, s32[4]{0:T(128)S(1)}, u32[]{:S(2)}) copy-start(s32[4]{0:T(128)S(1)} %pad_add_fusion.place_ref) | copy-start | bytes 52
  3.5 31.4 %collective-permute-start.3 = (bf16[2,64,4224]{2,1,0:T(8,128)(2,1)S(1)}, bf16[2,64,4224]{2,1,0:T(8,128)(2,1)}, u32[]{:S(2)}, u32[]{:S(2)}) collective-permute-start(bf16[2,64,4224]{2,1,0:T(8,128)(2,1)S(1)} %get-tuple-element.234.refs_1_.refs_4_.refs_3_), channel_id=1, source_target_pairs={{0,1},{1,0},{2,3},{3,2},{4,5},{5,4},{6,7},{7,6},{8,9},{9,8},{10,11... | collective-permute-start | bytes 3244040 | tf_op jit(solution)/shard_map/ppermute | solution.py:56
  6.2 28.7 %collective-permute-start.4 = (bf16[2,256,1024]{2,1,0:T(8,128)(2,1)S(1)}, bf16[2,256,1024]{2,1,0:T(8,128)(2,1)S(1)}, u32[]{:S(2)}, u32[]{:S(2)}) collective-permute-start(bf16[2,256,1024]{2,1,0:T(8,128)(2,1)S(1)} %pad_maximum_fusion.3), channel_id=1, source_target_pairs={{0,16},{16,0},{1,17},{17,1},{2,18},{18,2},{3,19},{19,3},{4,20},{20... | collective-permute-start | bytes 3145736 | tf_op jit(solution)/shard_map/ppermute | solution.py:56
  7.5 7.0 %collective-permute-start = (bf16[64,2176]{1,0:T(8,128)(2,1)S(1)}, bf16[64,2176]{1,0:T(8,128)(2,1)S(1)}, u32[]{:S(2)}, u32[]{:S(2)}) collective-permute-start(bf16[64,2176]{1,0:T(8,128)(2,1)S(1)} %get-tuple-element.233), channel_id=1, source_target_pairs={{0,2},{2,4},{4,6},{6,0},{1,3},{3,5},{5,7},{7,1},{8,10},{10,12},{12... | collective-permute-start | bytes 835592 | tf_op jit(solution)/shard_map/ppermute | solution.py:250
  8.8 22.6 %collective-permute-start.1 = (bf16[64,2176]{1,0:T(8,128)(2,1)S(1)}, bf16[64,2176]{1,0:T(8,128)(2,1)S(1)}, u32[]{:S(2)}, u32[]{:S(2)}) collective-permute-start(bf16[64,2176]{1,0:T(8,128)(2,1)S(1)} %get-tuple-element.233), channel_id=1, source_target_pairs={{0,4},{2,6},{4,0},{6,2},{1,5},{3,7},{5,1},{7,3},{8,12},{10,14},{12... | collective-permute-start | bytes 835592 | tf_op jit(solution)/shard_map/ppermute | solution.py:250
  9.8 25.1 %collective-permute-start.2 = (bf16[64,2176]{1,0:T(8,128)(2,1)S(1)}, bf16[64,2176]{1,0:T(8,128)(2,1)S(1)}, u32[]{:S(2)}, u32[]{:S(2)}) collective-permute-start(bf16[64,2176]{1,0:T(8,128)(2,1)S(1)} %get-tuple-element.233), channel_id=1, source_target_pairs={{0,6},{2,0},{4,2},{6,4},{1,7},{3,1},{5,3},{7,5},{8,14},{10,8},{12,... | collective-permute-start | bytes 835592 | tf_op jit(solution)/shard_map/ppermute | solution.py:250
  36.9 24.0 %collective-permute-start.5 = (bf16[3,64,2176]{2,1,0:T(8,128)(2,1)}, bf16[3,64,2176]{2,1,0:T(8,128)(2,1)}, u32[]{:S(2)}, u32[]{:S(2)}) collective-permute-start(bf16[3,64,2176]{2,1,0:T(8,128)(2,1)} %pad_maximum_fusion.7.refs_3_), channel_id=1, source_target_pairs={{0,1},{1,0},{2,3},{3,2},{4,5},{5,4},{6,7},{7,6},{8,9},{9,8},{10,11... | collective-permute-start | bytes 2506760 | tf_op jit(solution)/shard_map/ppermute | solution.py:56
  37.2 23.7 %collective-permute-start.6 = (bf16[3,64,2176]{2,1,0:T(8,128)(2,1)}, bf16[3,64,2176]{2,1,0:T(8,128)(2,1)}, u32[]{:S(2)}, u32[]{:S(2)}) collective-permute-start(bf16[3,64,2176]{2,1,0:T(8,128)(2,1)} %pad_maximum_fusion.7.refs_3_), channel_id=1, source_target_pairs={{0,16},{16,0},{1,17},{17,1},{2,18},{18,2},{3,19},{19,3},{4,20},{20... | collective-permute-start | bytes 2506760 | tf_op jit(solution)/shard_map/ppermute | solution.py:56
  37.4 6.9 %collective-permute-start.7 = (bf16[64,2048]{1,0:T(8,128)(2,1)S(1)}, bf16[64,2048]{1,0:T(8,128)(2,1)S(1)}, u32[]{:S(2)}, u32[]{:S(2)}) collective-permute-start(bf16[64,2048]{1,0:T(8,128)(2,1)S(1)} %get-tuple-element.239), channel_id=1, source_target_pairs={{0,2},{2,4},{4,6},{6,0},{1,3},{3,5},{5,7},{7,1},{8,10},{10,12},{12... | collective-permute-start | bytes 786440 | tf_op jit(solution)/shard_map/ppermute | solution.py:250
  37.4 21.7 %collective-permute-start.8 = (bf16[64,2048]{1,0:T(8,128)(2,1)S(1)}, bf16[64,2048]{1,0:T(8,128)(2,1)S(1)}, u32[]{:S(2)}, u32[]{:S(2)}) collective-permute-start(bf16[64,2048]{1,0:T(8,128)(2,1)S(1)} %get-tuple-element.239), channel_id=1, source_target_pairs={{0,4},{2,6},{4,0},{6,2},{1,5},{3,7},{5,1},{7,3},{8,12},{10,14},{12... | collective-permute-start | bytes 786440 | tf_op jit(solution)/shard_map/ppermute | solution.py:250
  37.4 23.4 %collective-permute-start.9 = (bf16[64,2048]{1,0:T(8,128)(2,1)S(1)}, bf16[64,2048]{1,0:T(8,128)(2,1)}, u32[]{:S(2)}, u32[]{:S(2)}) collective-permute-start(bf16[64,2048]{1,0:T(8,128)(2,1)S(1)} %get-tuple-element.239), channel_id=1, source_target_pairs={{0,6},{2,0},{4,2},{6,4},{1,7},{3,1},{5,3},{7,5},{8,14},{10,8},{12,... | collective-permute-start | bytes 786440 | tf_op jit(solution)/shard_map/ppermute | solution.py:250
  38.9 27.9 %copy-start.20 = (bf16[2,128,1024]{2,1,0:T(8,128)(2,1)}, bf16[2,128,1024]{2,1,0:T(8,128)(2,1)S(1)}, u32[]{:S(2)}) copy-start(bf16[2,128,1024]{2,1,0:T(8,128)(2,1)S(1)} %dynamic-slice_bitcast_fusion.2.refs_10_) | copy-start | bytes 1572868
  63.5 4.4 %collective-permute-start.12 = (bf16[2,256,1024]{2,1,0:T(8,128)(2,1)}, bf16[2,256,1024]{2,1,0:T(8,128)(2,1)}, u32[]{:S(2)}, u32[]{:S(2)}) collective-permute-start(bf16[2,256,1024]{2,1,0:T(8,128)(2,1)} %pad_maximum_fusion.4), channel_id=1, source_target_pairs={{0,8},{8,0},{1,9},{9,1},{2,10},{10,2},{3,11},{11,3},{4,12},{12,4},... | collective-permute-start | bytes 3145736 | tf_op jit(solution)/shard_map/ppermute | solution.py:56
  64.4 11.3 %collective-permute-start.10 = (bf16[3,32,2176]{2,1,0:T(8,128)(2,1)S(1)}, bf16[3,32,2176]{2,1,0:T(8,128)(2,1)S(1)}, u32[]{:S(2)}, u32[]{:S(2)}) collective-permute-start(bf16[3,32,2176]{2,1,0:T(8,128)(2,1)S(1)} %get-tuple-element.249), channel_id=1, source_target_pairs={{0,16},{16,0},{1,17},{17,1},{2,18},{18,2},{3,19},{19,3},{4,20},{20... | collective-permute-start | bytes 1253384 | tf_op jit(solution)/shard_map/ppermute | solution.py:56
  65.7 11.0 %collective-permute-start.11 = (bf16[3,32,2176]{2,1,0:T(8,128)(2,1)S(1)}, bf16[3,32,2176]{2,1,0:T(8,128)(2,1)S(1)}, u32[]{:S(2)}, u32[]{:S(2)}) collective-permute-start(bf16[3,32,2176]{2,1,0:T(8,128)(2,1)S(1)} %get-tuple-element.250), channel_id=1, source_target_pairs={{0,1},{1,0},{2,3},{3,2},{4,5},{5,4},{6,7},{7,6},{8,9},{9,8},{10,11... | collective-permute-start | bytes 1253384 | tf_op jit(solution)/shard_map/ppermute | solution.py:56
  76.6 29.2 %collective-permute-start.13 = (bf16[3,64,2048]{2,1,0:T(8,128)(2,1)S(1)}, bf16[3,64,2048]{2,1,0:T(8,128)(2,1)S(1)}, u32[]{:S(2)}, u32[]{:S(2)}) collective-permute-start(bf16[3,64,2048]{2,1,0:T(8,128)(2,1)S(1)} %pad_maximum_fusion.8.refs_6_.refs_5_), channel_id=1, source_target_pairs={{0,1},{1,0},{2,3},{3,2},{4,5},{5,4},{6,7},{7,6},{8,9},{9,8},{10,11... | collective-permute-start | bytes 2359304 | tf_op jit(solution)/shard_map/ppermute | solution.py:56
  77.8 28.0 %collective-permute-start.14 = (bf16[3,64,2048]{2,1,0:T(8,128)(2,1)S(1)}, bf16[3,64,2048]{2,1,0:T(8,128)(2,1)S(1)}, u32[]{:S(2)}, u32[]{:S(2)}) collective-permute-start(bf16[3,64,2048]{2,1,0:T(8,128)(2,1)S(1)} %pad_maximum_fusion.8.refs_6_.refs_5_), channel_id=1, source_target_pairs={{0,16},{16,0},{1,17},{17,1},{2,18},{18,2},{3,19},{19,3},{4,20},{20... | collective-permute-start | bytes 2359304 | tf_op jit(solution)/shard_map/ppermute | solution.py:56
  78.2 19.4 %collective-permute-start.15 = (bf16[128,1024]{1,0:T(8,128)(2,1)S(1)}, bf16[128,1024]{1,0:T(8,128)(2,1)S(1)}, u32[]{:S(2)}, u32[]{:S(2)}) collective-permute-start(bf16[128,1024]{1,0:T(8,128)(2,1)S(1)} %dynamic-slice_bitcast_fusion.5), channel_id=1, source_target_pairs={{0,2},{2,4},{4,6},{6,0},{1,3},{3,5},{5,7},{7,1},{8,10},{10,12},{12... | collective-permute-start | bytes 786440 | tf_op jit(solution)/shard_map/ppermute | solution.py:250
  78.2 19.4 %collective-permute-start.16 = (bf16[128,1024]{1,0:T(8,128)(2,1)S(1)}, bf16[128,1024]{1,0:T(8,128)(2,1)S(1)}, u32[]{:S(2)}, u32[]{:S(2)}) collective-permute-start(bf16[128,1024]{1,0:T(8,128)(2,1)S(1)} %dynamic-slice_bitcast_fusion.5), channel_id=1, source_target_pairs={{0,6},{2,0},{4,2},{6,4},{1,7},{3,1},{5,3},{7,5},{8,14},{10,8},{12,... | collective-permute-start | bytes 786440 | tf_op jit(solution)/shard_map/ppermute | solution.py:250
  80.2 25.6 %collective-permute-start.17 = (bf16[2,128,1024]{2,1,0:T(8,128)(2,1)S(1)}, bf16[2,128,1024]{2,1,0:T(8,128)(2,1)S(1)}, u32[]{:S(2)}, u32[]{:S(2)}) collective-permute-start(bf16[2,128,1024]{2,1,0:T(8,128)(2,1)S(1)} %copy-done.21), channel_id=1, source_target_pairs={{0,1},{1,0},{2,3},{3,2},{4,5},{5,4},{6,7},{7,6},{8,9},{9,8},{10,11... | collective-permute-start | bytes 1572872 | tf_op jit(solution)/shard_map/ppermute | solution.py:56
  108.6 13.3 %collective-permute-start.20 = (bf16[2,256,1024]{2,1,0:T(8,128)(2,1)S(1)}, bf16[2,256,1024]{2,1,0:T(8,128)(2,1)S(1)}, u32[]{:S(2)}, u32[]{:S(2)}) collective-permute-start(bf16[2,256,1024]{2,1,0:T(8,128)(2,1)S(1)} %pad_maximum_fusion.5), channel_id=1, source_target_pairs={{0,8},{8,0},{1,9},{9,1},{2,10},{10,2},{3,11},{11,3},{4,12},{12,4},... | collective-permute-start | bytes 3145736 | tf_op jit(solution)/shard_map/ppermute | solution.py:56
  110.7 13.0 %collective-permute-start.18 = (bf16[3,32,2048]{2,1,0:T(8,128)(2,1)S(1)}, bf16[3,32,2048]{2,1,0:T(8,128)(2,1)S(1)}, u32[]{:S(2)}, u32[]{:S(2)}) collective-permute-start(bf16[3,32,2048]{2,1,0:T(8,128)(2,1)S(1)} %get-tuple-element.282), channel_id=1, source_target_pairs={{0,16},{16,0},{1,17},{17,1},{2,18},{18,2},{3,19},{19,3},{4,20},{20... | collective-permute-start | bytes 1179656 | tf_op jit(solution)/shard_map/ppermute | solution.py:56
  111.1 12.7 %collective-permute-start.19 = (bf16[3,32,2048]{2,1,0:T(8,128)(2,1)S(1)}, bf16[3,32,2048]{2,1,0:T(8,128)(2,1)S(1)}, u32[]{:S(2)}, u32[]{:S(2)}) collective-permute-start(bf16[3,32,2048]{2,1,0:T(8,128)(2,1)S(1)} %get-tuple-element.283), channel_id=1, source_target_pairs={{0,1},{1,0},{2,3},{3,2},{4,5},{5,4},{6,7},{7,6},{8,9},{9,8},{10,11... | collective-permute-start | bytes 1179656 | tf_op jit(solution)/shard_map/ppermute | solution.py:56
  112.3 11.5 %collective-permute-start.21 = (bf16[128,1024]{1,0:T(8,128)(2,1)S(1)}, bf16[128,1024]{1,0:T(8,128)(2,1)S(1)}, u32[]{:S(2)}, u32[]{:S(2)}) collective-permute-start(bf16[128,1024]{1,0:T(8,128)(2,1)S(1)} %dynamic-slice_bitcast_fusion.5), channel_id=1, source_target_pairs={{0,4},{2,6},{4,0},{6,2},{1,5},{3,7},{5,1},{7,3},{8,12},{10,14},{12... | collective-permute-start | bytes 786440 | tf_op jit(solution)/shard_map/ppermute | solution.py:250
  122.3 29.4 %copy-start.2 = (bf16[2,2,256,1024]{3,2,1,0:T(8,128)(2,1)}, bf16[2,2,256,1024]{3,2,1,0:T(8,128)(2,1)S(1)}, u32[]{:S(2)}) copy-start(bf16[2,2,256,1024]{3,2,1,0:T(8,128)(2,1)S(1)} %pad_maximum_fusion.1) | copy-start | bytes 6291460
  127.1 4.4 %collective-permute-start.22 = (bf16[1024,1024]{1,0:T(8,128)(2,1)S(1)}, bf16[1024,1024]{1,0:T(8,128)(2,1)S(1)}, u32[]{:S(2)}, u32[]{:S(2)}) collective-permute-start(bf16[1024,1024]{1,0:T(8,128)(2,1)S(1)} %get-tuple-element.290.refs_1_), channel_id=1, source_target_pairs={{0,8},{8,0},{1,9},{9,1},{2,10},{10,2},{3,11},{11,3},{4,12},{12,4},... | collective-permute-start | bytes 6291464 | tf_op jit(solution)/shard_map/ppermute | solution.py:56
  127.8 19.2 %collective-permute-start.23 = (bf16[3,128,1024]{2,1,0:T(8,128)(2,1)S(1)}, bf16[3,128,1024]{2,1,0:T(8,128)(2,1)S(1)}, u32[]{:S(2)}, u32[]{:S(2)}) collective-permute-start(bf16[3,128,1024]{2,1,0:T(8,128)(2,1)S(1)} %pad_maximum_fusion.9.refs_12_), channel_id=1, source_target_pairs={{0,1},{1,0},{2,3},{3,2},{4,5},{5,4},{6,7},{7,6},{8,9},{9,8},{10,11... | collective-permute-start | bytes 2359304 | tf_op jit(solution)/shard_map/ppermute | solution.py:56
  128.2 18.9 %collective-permute-start.24 = (bf16[3,128,1024]{2,1,0:T(8,128)(2,1)S(1)}, bf16[3,128,1024]{2,1,0:T(8,128)(2,1)S(1)}, u32[]{:S(2)}, u32[]{:S(2)}) collective-permute-start(bf16[3,128,1024]{2,1,0:T(8,128)(2,1)S(1)} %pad_maximum_fusion.9.refs_12_), channel_id=1, source_target_pairs={{0,16},{16,0},{1,17},{17,1},{2,18},{18,2},{3,19},{19,3},{4,20},{20... | collective-permute-start | bytes 2359304 | tf_op jit(solution)/shard_map/ppermute | solution.py:56
  149.6 9.9 %collective-permute-start.25 = (bf16[3,64,1024]{2,1,0:T(8,128)(2,1)S(1)}, bf16[3,64,1024]{2,1,0:T(8,128)(2,1)S(1)}, u32[]{:S(2)}, u32[]{:S(2)}) collective-permute-start(bf16[3,64,1024]{2,1,0:T(8,128)(2,1)S(1)} %get-tuple-element.315), channel_id=1, source_target_pairs={{0,16},{16,0},{1,17},{17,1},{2,18},{18,2},{3,19},{19,3},{4,20},{20... | collective-permute-start | bytes 1179656 | tf_op jit(solution)/shard_map/ppermute | solution.py:56
  150.8 9.5 %collective-permute-start.26 = (bf16[3,64,1024]{2,1,0:T(8,128)(2,1)S(1)}, bf16[3,64,1024]{2,1,0:T(8,128)(2,1)S(1)}, u32[]{:S(2)}, u32[]{:S(2)}) collective-permute-start(bf16[3,64,1024]{2,1,0:T(8,128)(2,1)S(1)} %get-tuple-element.316), channel_id=1, source_target_pairs={{0,1},{1,0},{2,3},{3,2},{4,5},{5,4},{6,7},{7,6},{8,9},{9,8},{10,11... | collective-permute-start | bytes 1179656 | tf_op jit(solution)/shard_map/ppermute | solution.py:56
  160.3 22.7 %collective-permute-start.27 = (bf16[4,128,1024]{2,1,0:T(8,128)(2,1)S(1)}, bf16[4,128,1024]{2,1,0:T(8,128)(2,1)S(1)}, u32[]{:S(2)}, u32[]{:S(2)}) collective-permute-start(bf16[4,128,1024]{2,1,0:T(8,128)(2,1)S(1)} %get-tuple-element.329), channel_id=1, source_target_pairs={{0,1},{1,0},{2,3},{3,2},{4,5},{5,4},{6,7},{7,6},{8,9},{9,8},{10,11... | collective-permute-start | bytes 3145736 | tf_op jit(solution)/shard_map/ppermute | solution.py:56
  160.9 22.1 %collective-permute-start.28 = (bf16[4,2,64,1024]{3,2,1,0:T(8,128)(2,1)S(1)}, bf16[4,2,64,1024]{3,2,1,0:T(8,128)(2,1)S(1)}, u32[]{:S(2)}, u32[]{:S(2)}) collective-permute-start(bf16[4,2,64,1024]{3,2,1,0:T(8,128)(2,1)S(1)} %get-tuple-element.330), channel_id=1, source_target_pairs={{0,16},{16,0},{1,17},{17,1},{2,18},{18,2},{3,19},{19,3},{4,20},{20... | collective-permute-start | bytes 3145736 | tf_op jit(solution)/shard_map/ppermute | solution.py:56
  185.6 12.7 %collective-permute-start.29 = (bf16[1024,1024]{1,0:T(8,128)(2,1)}, bf16[1024,1024]{1,0:T(8,128)(2,1)}, u32[]{:S(2)}, u32[]{:S(2)}) collective-permute-start(bf16[1024,1024]{1,0:T(8,128)(2,1)} %get-tuple-element.344.refs_1_), channel_id=1, source_target_pairs={{0,8},{8,0},{1,9},{9,1},{2,10},{10,2},{3,11},{11,3},{4,12},{12,4},... | collective-permute-start | bytes 6291464 | tf_op jit(solution)/shard_map/ppermute | solution.py:56
  189.1 9.2 %collective-permute-start.30 = (bf16[2,256,1024]{2,1,0:T(8,128)(2,1)}, bf16[2,256,1024]{2,1,0:T(8,128)(2,1)}, u32[]{:S(2)}, u32[]{:S(2)}) collective-permute-start(bf16[2,256,1024]{2,1,0:T(8,128)(2,1)} %get-tuple-element.341), channel_id=1, source_target_pairs={{0,8},{8,0},{1,9},{9,1},{2,10},{10,2},{3,11},{11,3},{4,12},{12,4},... | collective-permute-start | bytes 3145736 | tf_op jit(solution)/shard_map/ppermute | solution.py:56
  189.3 18.3 %collective-permute-start.31 = (bf16[4,64,1024]{2,1,0:T(8,128)(2,1)}, bf16[4,64,1024]{2,1,0:T(8,128)(2,1)S(1)}, u32[]{:S(2)}, u32[]{:S(2)}) collective-permute-start(bf16[4,64,1024]{2,1,0:T(8,128)(2,1)} %get-tuple-element.348), channel_id=1, source_target_pairs={{0,16},{16,0},{1,17},{17,1},{2,18},{18,2},{3,19},{19,3},{4,20},{20... | collective-permute-start | bytes 1572872 | tf_op jit(solution)/shard_map/ppermute | solution.py:56
  189.9 17.7 %collective-permute-start.32 = (bf16[4,64,1024]{2,1,0:T(8,128)(2,1)}, bf16[4,64,1024]{2,1,0:T(8,128)(2,1)S(1)}, u32[]{:S(2)}, u32[]{:S(2)}) collective-permute-start(bf16[4,64,1024]{2,1,0:T(8,128)(2,1)} %get-tuple-element.349), channel_id=1, source_target_pairs={{0,1},{1,0},{2,3},{3,2},{4,5},{5,4},{6,7},{7,6},{8,9},{9,8},{10,11... | collective-permute-start | bytes 1572872 | tf_op jit(solution)/shard_map/ppermute | solution.py:56
  198.3 37.0 %collective-permute-start.33 = (bf16[4,64,2048]{2,1,0:T(8,128)(2,1)S(1)}, bf16[4,64,2048]{2,1,0:T(8,128)(2,1)S(1)}, u32[]{:S(2)}, u32[]{:S(2)}) collective-permute-start(bf16[4,64,2048]{2,1,0:T(8,128)(2,1)S(1)} %get-tuple-element.361), channel_id=1, source_target_pairs={{0,1},{1,0},{2,3},{3,2},{4,5},{5,4},{6,7},{7,6},{8,9},{9,8},{10,11... | collective-permute-start | bytes 3145736 | tf_op jit(solution)/shard_map/ppermute | solution.py:56
  199.1 36.2 %collective-permute-start.34 = (bf16[4,2,32,2048]{3,2,1,0:T(8,128)(2,1)S(1)}, bf16[4,2,32,2048]{3,2,1,0:T(8,128)(2,1)S(1)}, u32[]{:S(2)}, u32[]{:S(2)}) collective-permute-start(bf16[4,2,32,2048]{3,2,1,0:T(8,128)(2,1)S(1)} %get-tuple-element.362), channel_id=1, source_target_pairs={{0,16},{16,0},{1,17},{17,1},{2,18},{18,2},{3,19},{19,3},{4,20},{20... | collective-permute-start | bytes 3145736 | tf_op jit(solution)/shard_map/ppermute | solution.py:56
  208.6 24.1 %collective-permute-start.35 = (bf16[2,64,1024]{2,1,0:T(8,128)(2,1)S(1)}, bf16[2,64,1024]{2,1,0:T(8,128)(2,1)S(1)}, u32[]{:S(2)}, u32[]{:S(2)}) collective-permute-start(bf16[2,64,1024]{2,1,0:T(8,128)(2,1)S(1)} %get-tuple-element.364), channel_id=1, source_target_pairs={{0,2},{2,4},{4,6},{6,0},{1,3},{3,5},{5,7},{7,1},{8,10},{10,12},{12... | collective-permute-start | bytes 786440 | tf_op jit(solution)/shard_map/ppermute | solution.py:250
  208.6 24.0 %collective-permute-start.36 = (bf16[2,64,1024]{2,1,0:T(8,128)(2,1)S(1)}, bf16[2,64,1024]{2,1,0:T(8,128)(2,1)S(1)}, u32[]{:S(2)}, u32[]{:S(2)}) collective-permute-start(bf16[2,64,1024]{2,1,0:T(8,128)(2,1)S(1)} %get-tuple-element.365), channel_id=1, source_target_pairs={{0,4},{2,6},{4,0},{6,2},{1,5},{3,7},{5,1},{7,3},{8,12},{10,14},{12... | collective-permute-start | bytes 786440 | tf_op jit(solution)/shard_map/ppermute | solution.py:250
  211.7 23.6 %collective-permute-start.37 = (bf16[2,64,1024]{2,1,0:T(8,128)(2,1)S(1)}, bf16[2,64,1024]{2,1,0:T(8,128)(2,1)S(1)}, u32[]{:S(2)}, u32[]{:S(2)}) collective-permute-start(bf16[2,64,1024]{2,1,0:T(8,128)(2,1)S(1)} %get-tuple-element.366), channel_id=1, source_target_pairs={{0,6},{2,0},{4,2},{6,4},{1,7},{3,1},{5,3},{7,5},{8,14},{10,8},{12,... | collective-permute-start | bytes 786440 | tf_op jit(solution)/shard_map/ppermute | solution.py:250
  235.5 12.8 %collective-permute-start.40 = (bf16[2,64,1024]{2,1,0:T(8,128)(2,1)S(1)}, bf16[2,64,1024]{2,1,0:T(8,128)(2,1)S(1)}, u32[]{:S(2)}, u32[]{:S(2)}) collective-permute-start(bf16[2,64,1024]{2,1,0:T(8,128)(2,1)S(1)} %add_convert_fusion.2), channel_id=1, source_target_pairs={{0,16},{16,0},{1,17},{17,1},{2,18},{18,2},{3,19},{19,3},{4,20},{20... | collective-permute-start | bytes 786440 | tf_op jit(solution)/shard_map/ppermute | solution.py:56
  237.4 16.8 %collective-permute-start.38 = (bf16[4,32,2048]{2,1,0:T(8,128)(2,1)S(1)}, bf16[4,32,2048]{2,1,0:T(8,128)(2,1)S(1)}, u32[]{:S(2)}, u32[]{:S(2)}) collective-permute-start(bf16[4,32,2048]{2,1,0:T(8,128)(2,1)S(1)} %get-tuple-element.374), channel_id=1, source_target_pairs={{0,16},{16,0},{1,17},{17,1},{2,18},{18,2},{3,19},{19,3},{4,20},{20... | collective-permute-start | bytes 1572872 | tf_op jit(solution)/shard_map/ppermute | solution.py:56
  238.4 15.8 %collective-permute-start.39 = (bf16[4,32,2048]{2,1,0:T(8,128)(2,1)S(1)}, bf16[4,32,2048]{2,1,0:T(8,128)(2,1)S(1)}, u32[]{:S(2)}, u32[]{:S(2)}) collective-permute-start(bf16[4,32,2048]{2,1,0:T(8,128)(2,1)S(1)} %get-tuple-element.375), channel_id=1, source_target_pairs={{0,1},{1,0},{2,3},{3,2},{4,5},{5,4},{6,7},{7,6},{8,9},{9,8},{10,11... | collective-permute-start | bytes 1572872 | tf_op jit(solution)/shard_map/ppermute | solution.py:56
  255.2 24.8 %collective-permute-start.41 = (bf16[4,64,2176]{2,1,0:T(8,128)(2,1)S(1)}, bf16[4,64,2176]{2,1,0:T(8,128)(2,1)S(1)}, u32[]{:S(2)}, u32[]{:S(2)}) collective-permute-start(bf16[4,64,2176]{2,1,0:T(8,128)(2,1)S(1)} %get-tuple-element.404), channel_id=1, source_target_pairs={{0,1},{1,0},{2,3},{3,2},{4,5},{5,4},{6,7},{7,6},{8,9},{9,8},{10,11... | collective-permute-start | bytes 3342344 | tf_op jit(solution)/shard_map/ppermute | solution.py:56
  256.1 24.4 %collective-permute-start.42 = (bf16[4,2,32,2176]{3,2,1,0:T(8,128)(2,1)S(1)}, bf16[4,2,32,2176]{3,2,1,0:T(8,128)(2,1)S(1)}, u32[]{:S(2)}, u32[]{:S(2)}) collective-permute-start(bf16[4,2,32,2176]{3,2,1,0:T(8,128)(2,1)S(1)} %get-tuple-element.405), channel_id=1, source_target_pairs={{0,16},{16,0},{1,17},{17,1},{2,18},{18,2},{3,19},{19,3},{4,20},{20... | collective-permute-start | bytes 3342344 | tf_op jit(solution)/shard_map/ppermute | solution.py:56
  256.5 8.4 %collective-permute-start.43 = (bf16[2,32,2048]{2,1,0:T(8,128)(2,1)S(1)}, bf16[2,32,2048]{2,1,0:T(8,128)(2,1)S(1)}, u32[]{:S(2)}, u32[]{:S(2)}) collective-permute-start(bf16[2,32,2048]{2,1,0:T(8,128)(2,1)S(1)} %get-tuple-element.408), channel_id=1, source_target_pairs={{0,2},{2,4},{4,6},{6,0},{1,3},{3,5},{5,7},{7,1},{8,10},{10,12},{12... | collective-permute-start | bytes 786440 | tf_op jit(solution)/shard_map/ppermute | solution.py:250
  256.5 20.8 %collective-permute-start.44 = (bf16[2,32,2048]{2,1,0:T(8,128)(2,1)S(1)}, bf16[2,32,2048]{2,1,0:T(8,128)(2,1)S(1)}, u32[]{:S(2)}, u32[]{:S(2)}) collective-permute-start(bf16[2,32,2048]{2,1,0:T(8,128)(2,1)S(1)} %get-tuple-element.409), channel_id=1, source_target_pairs={{0,4},{2,6},{4,0},{6,2},{1,5},{3,7},{5,1},{7,3},{8,12},{10,14},{12... | collective-permute-start | bytes 786440 | tf_op jit(solution)/shard_map/ppermute | solution.py:250
  256.5 22.6 %collective-permute-start.45 = (bf16[2,32,2048]{2,1,0:T(8,128)(2,1)S(1)}, bf16[2,32,2048]{2,1,0:T(8,128)(2,1)S(1)}, u32[]{:S(2)}, u32[]{:S(2)}) collective-permute-start(bf16[2,32,2048]{2,1,0:T(8,128)(2,1)S(1)} %get-tuple-element.410), channel_id=1, source_target_pairs={{0,6},{2,0},{4,2},{6,4},{1,7},{3,1},{5,3},{7,5},{8,14},{10,8},{12,... | collective-permute-start | bytes 786440 | tf_op jit(solution)/shard_map/ppermute | solution.py:250
  264.9 38.1 %copy-start.18 = (bf16[2,256,1024]{2,1,0:T(8,128)(2,1)}, bf16[2,256,1024]{2,1,0:T(8,128)(2,1)S(1)}, u32[]{:S(2)}) copy-start(bf16[2,256,1024]{2,1,0:T(8,128)(2,1)S(1)} %fusion.12) | copy-start | bytes 3145732
  282.1 5.3 %collective-permute-start.49 = (bf16[2,32,2048]{2,1,0:T(8,128)(2,1)S(1)}, bf16[2,32,2048]{2,1,0:T(8,128)(2,1)S(1)}, u32[]{:S(2)}, u32[]{:S(2)}) collective-permute-start(bf16[2,32,2048]{2,1,0:T(8,128)(2,1)S(1)} %add_convert_fusion.1), channel_id=1, source_target_pairs={{0,16},{16,0},{1,17},{17,1},{2,18},{18,2},{3,19},{19,3},{4,20},{20... | collective-permute-start | bytes 786440 | tf_op jit(solution)/shard_map/ppermute | solution.py:56
  282.5 5.0 %collective-permute-start.50 = (bf16[256,1024]{1,0:T(8,128)(2,1)S(1)}, bf16[256,1024]{1,0:T(8,128)(2,1)S(1)}, u32[]{:S(2)}, u32[]{:S(2)}) collective-permute-start(bf16[256,1024]{1,0:T(8,128)(2,1)S(1)} %bitcast.167), channel_id=1, source_target_pairs={{0,8},{8,0},{1,9},{9,1},{2,10},{10,2},{3,11},{11,3},{4,12},{12,4},... | collective-permute-start | bytes 1572872 | tf_op jit(solution)/shard_map/ppermute | solution.py:56
  285.5 3.9 %collective-permute-start.48 = (bf16[2,256,1024]{2,1,0:T(8,128)(2,1)S(1)}, bf16[2,256,1024]{2,1,0:T(8,128)(2,1)S(1)}, u32[]{:S(2)}, u32[]{:S(2)}) collective-permute-start(bf16[2,256,1024]{2,1,0:T(8,128)(2,1)S(1)} %dynamic-slice_bitcast_fusion), channel_id=1, source_target_pairs={{0,8},{8,0},{1,9},{9,1},{2,10},{10,2},{3,11},{11,3},{4,12},{12,4},... | collective-permute-start | bytes 3145736 | tf_op jit(solution)/shard_map/ppermute | solution.py:56
  285.6 14.6 %collective-permute-start.46 = (bf16[4,32,2176]{2,1,0:T(8,128)(2,1)S(1)}, bf16[4,32,2176]{2,1,0:T(8,128)(2,1)S(1)}, u32[]{:S(2)}, u32[]{:S(2)}) collective-permute-start(bf16[4,32,2176]{2,1,0:T(8,128)(2,1)S(1)} %get-tuple-element.426), channel_id=1, source_target_pairs={{0,16},{16,0},{1,17},{17,1},{2,18},{18,2},{3,19},{19,3},{4,20},{20... | collective-permute-start | bytes 1671176 | tf_op jit(solution)/shard_map/ppermute | solution.py:56
  286.7 13.5 %collective-permute-start.47 = (bf16[4,32,2176]{2,1,0:T(8,128)(2,1)S(1)}, bf16[4,32,2176]{2,1,0:T(8,128)(2,1)S(1)}, u32[]{:S(2)}, u32[]{:S(2)}) collective-permute-start(bf16[4,32,2176]{2,1,0:T(8,128)(2,1)S(1)} %get-tuple-element.427), channel_id=1, source_target_pairs={{0,1},{1,0},{2,3},{3,2},{4,5},{5,4},{6,7},{7,6},{8,9},{9,8},{10,11... | collective-permute-start | bytes 1671176 | tf_op jit(solution)/shard_map/ppermute | solution.py:56
  300.2 6.2 %collective-permute-start.55 = (bf16[128,2048]{1,0:T(8,128)(2,1)S(1)}, bf16[128,2048]{1,0:T(8,128)(2,1)S(1)}, u32[]{:S(2)}, u32[]{:S(2)}) collective-permute-start(bf16[128,2048]{1,0:T(8,128)(2,1)S(1)} %bitcast.170), channel_id=1, source_target_pairs={{0,8},{8,0},{1,9},{9,1},{2,10},{10,2},{3,11},{11,3},{4,12},{12,4},... | collective-permute-start | bytes 1572872 | tf_op jit(solution)/shard_map/ppermute | solution.py:56
  303.8 27.5 %collective-permute-start.56 = (bf16[256,1024]{1,0:T(8,128)(2,1)}, bf16[256,1024]{1,0:T(8,128)(2,1)}, u32[]{:S(2)}, u32[]{:S(2)}) collective-permute-start(bf16[256,1024]{1,0:T(8,128)(2,1)} %dynamic-slice_bitcast_fusion.1), channel_id=1, source_target_pairs={{0,16},{16,0},{1,17},{17,1},{2,18},{18,2},{3,19},{19,3},{4,20},{20... | collective-permute-start | bytes 1572872 | tf_op jit(solution)/shard_map/ppermute | solution.py:56
  304.2 27.1 %collective-permute-start.54 = (bf16[256,1024]{1,0:T(8,128)(2,1)}, bf16[256,1024]{1,0:T(8,128)(2,1)}, u32[]{:S(2)}, u32[]{:S(2)}) collective-permute-start(bf16[256,1024]{1,0:T(8,128)(2,1)} %fusion.16), channel_id=1, source_target_pairs={{0,16},{16,0},{1,17},{17,1},{2,18},{18,2},{3,19},{19,3},{4,20},{20... | collective-permute-start | bytes 1572872 | tf_op jit(solution)/shard_map/ppermute | solution.py:56
  306.3 7.8 %collective-permute-start.51 = (bf16[2,32,2176]{2,1,0:T(8,128)(2,1)S(1)}, bf16[2,32,2176]{2,1,0:T(8,128)(2,1)S(1)}, u32[]{:S(2)}, u32[]{:S(2)}) collective-permute-start(bf16[2,32,2176]{2,1,0:T(8,128)(2,1)S(1)} %get-tuple-element.435), channel_id=1, source_target_pairs={{0,2},{2,4},{4,6},{6,0},{1,3},{3,5},{5,7},{7,1},{8,10},{10,12},{12... | collective-permute-start | bytes 835592 | tf_op jit(solution)/shard_map/ppermute | solution.py:250
  306.3 23.6 %collective-permute-start.52 = (bf16[2,32,2176]{2,1,0:T(8,128)(2,1)S(1)}, bf16[2,32,2176]{2,1,0:T(8,128)(2,1)S(1)}, u32[]{:S(2)}, u32[]{:S(2)}) collective-permute-start(bf16[2,32,2176]{2,1,0:T(8,128)(2,1)S(1)} %get-tuple-element.436), channel_id=1, source_target_pairs={{0,4},{2,6},{4,0},{6,2},{1,5},{3,7},{5,1},{7,3},{8,12},{10,14},{12... | collective-permute-start | bytes 835592 | tf_op jit(solution)/shard_map/ppermute | solution.py:250
  307.2 24.1 %collective-permute-start.53 = (bf16[2,32,2176]{2,1,0:T(8,128)(2,1)S(1)}, bf16[2,32,2176]{2,1,0:T(8,128)(2,1)S(1)}, u32[]{:S(2)}, u32[]{:S(2)}) collective-permute-start(bf16[2,32,2176]{2,1,0:T(8,128)(2,1)S(1)} %get-tuple-element.437), channel_id=1, source_target_pairs={{0,6},{2,0},{4,2},{6,4},{1,7},{3,1},{5,3},{7,5},{8,14},{10,8},{12,... | collective-permute-start | bytes 835592 | tf_op jit(solution)/shard_map/ppermute | solution.py:250
  332.6 7.8 %collective-permute-start.57 = (bf16[2,32,2176]{2,1,0:T(8,128)(2,1)S(1)}, bf16[2,32,2176]{2,1,0:T(8,128)(2,1)S(1)}, u32[]{:S(2)}, u32[]{:S(2)}) collective-permute-start(bf16[2,32,2176]{2,1,0:T(8,128)(2,1)S(1)} %add_convert_fusion), channel_id=1, source_target_pairs={{0,16},{16,0},{1,17},{17,1},{2,18},{18,2},{3,19},{19,3},{4,20},{20... | collective-permute-start | bytes 835592 | tf_op jit(solution)/shard_map/ppermute | solution.py:56
  340.6 3.0 collective-permute-start.58
  (46 other events, 368.1 us)

commit v8 on v7

--- a/solution.py
+++ b/solution.py
@@ -81,15 +81,16 @@
         bias[i, :, :width] = jnp.where(allowed, 0.0, -1e30).astype(f32)
 
 
-def pipelined(count, first, second, third):
-    current, waiting = first(0), None
+def pipelined(count, first, second, third, lead=1):
+    ready, waiting = [first(block) for block in range(min(lead, count))], None
     for block in range(count):
-        following = first(block + 1) if block + 1 < count else None
+        if block + lead < count:
+            ready.append(first(block + lead))
+        current = ready.pop(0)
         middle = second(block, current)
         if waiting is not None:
             third(*waiting)
         waiting = (block, current, middle)
-        current = following
     third(*waiting)
 
 
@@ -199,7 +200,7 @@
             grad_queries = jnp.where(left, done[0], done[1]).astype(bf16)
             out_ref[0, start : start + tile, :] = grad_queries * jnp.asarray(1.0 / math.sqrt(HEAD_DIM), bf16)
 
-    pipelined(2 * len(spans), products, softmax_back, gather_up)
+    pipelined(2 * len(spans), products, softmax_back, gather_up, lead=2)
     out_ref[1] = keys_sum[...].astype(bf16)
     out_ref[2] = values_sum[...].astype(bf16)
 

time: 351 us -> 351 us (level)
  transfers between devices with their start and end apart: 59 -> 59, of which waited for: 26 -> 26; matrix products, arithmetic and copies ran while one was open for 5% -> 5% of each run, Pallas kernels for 35% -> 34%
where the time goes in v8:
time: 351 us; the launch traced here: 347 us
  Pallas kernels  136 us (39%)
  waiting for transfers between devices  123 us (35%)
  starting transfers between devices  56.8 us (16%)
  other arithmetic  20.2 us (6%)
  local copies, waits for them, and re-layouts  8.54 us (2%)
    ppermute x18, waiting for transfers between devices, along(): lax.ppermute(value, axis, [(i, (i + step) % depth) for i in range(depth)])  83.7 us
    pallas_call x6, Pallas kernels, weight_call(): pl.pallas_call(kernel, grid=(tiles,), in_specs=[pl.BlockSpec(memory_space...  61.8 us
    ppermute x41, waiting for transfers between devices, swap(): return lax.ppermute(value, axis, SWAP)  39.7 us
    ppermute x41, starting transfers between devices, swap(): return lax.ppermute(value, axis, SWAP)  39 us
    pallas_call x3, Pallas kernels, outer(): pl.pallas_call(kernel, grid=(depth,), in_specs=[pl.BlockSpec(memory_space...  23.2 us
    pallas_call x1, Pallas kernels, attend_back(): pl.pallas_call(functools.partial(attend_back_kernel, spans, tile), grid=(...  18.1 us
    ppermute x18, starting transfers between devices, along(): lax.ppermute(value, axis, [(i, (i + step) % depth) for i in range(depth)])  17.8 us
    pallas_call x2, Pallas kernels, attend(): pl.pallas_call(functools.partial(attend_kernel, spans, tile), grid=(count...  13.1 us
  transfers between devices with their start and end apart: 59, of which 26 were waited for; matrix products, arithmetic and copies ran while one was open for 5% of the time, Pallas kernels for 34%

profile of v8, /device:TPU:9, one launch (start us, length us, event | category | flops | bytes accessed | tf_op | source)
XLA Modules:
  0.0 346.6 jit_solution(11136616883446290111)
XLA Ops:
  1.5 2.0 prepare.1
  3.5 1.3 collective-permute-start.3
  6.2 1.3 collective-permute-start.4
  7.5 1.3 collective-permute-start
  9.8 1.5 collective-permute-start.2
  11.3 3.2 collective-permute-done
  14.5 16.9 %collective-permute-done.1 = bf16[64,2176]{1,0:T(8,128)(2,1)S(1)} collective-permute-done((bf16[64,2176]{1,0:T(8,128)(2,1)S(1)}, bf16[64,2176]{1,0:T(8,128)(2,1)S(1)}, u32[]{:S(2)}, u32[]{:S(2)}) %collective-permute-start.1) | collective-permute-done | bytes 278560 | tf_op jit(solution)/shard_map/ppermute | solution.py:251
  31.4 3.5 collective-permute-done.2
  37.4 1.5 collective-permute-start.9
  38.9 5.3 %collective-permute-done.7 = bf16[64,2048]{1,0:T(8,128)(2,1)S(1)} collective-permute-done((bf16[64,2048]{1,0:T(8,128)(2,1)S(1)}, bf16[64,2048]{1,0:T(8,128)(2,1)S(1)}, u32[]{:S(2)}, u32[]{:S(2)}) %collective-permute-start.7) | collective-permute-done | bytes 262176 | tf_op jit(solution)/shard_map/ppermute | solution.py:251
  44.2 14.9 %collective-permute-done.8 = bf16[64,2048]{1,0:T(8,128)(2,1)S(1)} collective-permute-done((bf16[64,2048]{1,0:T(8,128)(2,1)S(1)}, bf16[64,2048]{1,0:T(8,128)(2,1)S(1)}, u32[]{:S(2)}, u32[]{:S(2)}) %collective-permute-start.8) | collective-permute-done | bytes 262176 | tf_op jit(solution)/shard_map/ppermute | solution.py:251
  59.1 1.7 collective-permute-done.9
  60.8 1.5 halve.3
  64.4 1.3 collective-permute-start.10
  67.9 1.6 select_bitcast_fusion.3
  70.0 5.7 %collective-permute-done.10.refs_6_ = bf16[3,32,2176]{2,1,0:T(8,128)(2,1)S(1)} collective-permute-done((bf16[3,32,2176]{2,1,0:T(8,128)(2,1)S(1)}, bf16[3,32,2176]{2,1,0:T(8,128)(2,1)S(1)}, u32[]{:S(2)}, u32[]{:S(2)}) %collective-permute-start.10) | collective-permute-done | bytes 417824 | tf_op jit(solution)/shard_map/ppermute | solution.py:56
  78.2 2.0 collective-permute-start.16
  80.5 10.6 %project.1 = (bf16[1024,1024]{1,0:T(8,128)(2,1)}, bf16[1024,1536]{1,0:T(8,128)(2,1)}, f32[8,1024]{1,0:T(8,128)}, bf16[1024,1536]{1,0:T(8,128)(2,1)}, bf16[1024,1...) custom-call(s32[4]{0:T(128)S(1)} %pad_add_fusion.place_ref, bf16[1024,1024]{1,0:T(8,128)(2,1)S(1)} %bitcast.156, ...), custom_call_target="tpu_custom_call" | custom-call | flops 8800000000 | bytes 1000 | tf_op jit(solution)/shard_map/project/pallas_call | solution.py:509
  91.1 6.5 %attend.2 = (bf16[1024,256]{1,0:T(8,128)(2,1)S(1)}, f32[1024,256]{1,0:T(8,128)}) custom-call(bf16[1024,1536]{1,0:T(8,128)(2,1)} %get-tuple-element.279.q_ref.k_ref.v_ref, bf16[1024,1536]{1,0:T(8,128)(2,1)} %get-tuple-element.279.q_ref.k_ref.v_ref, bf16[1024,1536]{1,0:T(8,128)(2,1)} %get-tuple-element.279.q_ref.k_ref.v_ref, s32[1024,1]{1,0:T(8,128)S(1)} %copy.29.seg_col, ...), custom_call_target="tpu_custom_call" | custom-call | flops 8800000000 | bytes 1000 | tf_op jit(solution)/shard_map/attend/pallas_call | solution.py:143
  97.6 8.2 %collective-permute-done.17.refs_11_ = bf16[2,128,1024]{2,1,0:T(8,128)(2,1)S(1)} collective-permute-done((bf16[2,128,1024]{2,1,0:T(8,128)(2,1)S(1)}, bf16[2,128,1024]{2,1,0:T(8,128)(2,1)S(1)}, u32[]{:S(2)}, u32[]{:S(2)}) %collective-permute-start.17) | collective-permute-done | bytes 524320 | tf_op jit(solution)/shard_map/ppermute | solution.py:56
  107.0 1.4 halve.4
  108.6 2.1 collective-permute-start.20
  112.3 3.1 collective-permute-start.21
  115.4 6.5 %attend.3 = (bf16[1024,256]{1,0:T(8,128)(2,1)S(1)}, f32[1024,256]{1,0:T(8,128)}) custom-call(bf16[1024,1536]{1,0:T(8,128)(2,1)} %get-tuple-element.279.q_ref.k_ref.v_ref, bf16[1024,1536]{1,0:T(8,128)(2,1)} %get-tuple-element.279.q_ref.k_ref.v_ref, bf16[1024,1536]{1,0:T(8,128)(2,1)} %get-tuple-element.279.q_ref.k_ref.v_ref, s32[1024,1]{1,0:T(8,128)S(1)} %copy.29.seg_col, ...), custom_call_target="tpu_custom_call" | custom-call | flops 8800000000 | bytes 1000 | tf_op jit(solution)/shard_map/attend/pallas_call | solution.py:143
  122.3 1.5 collective-permute-done.21
  123.8 3.2 leave.1
  129.3 1.6 pad_maximum_fusion.2.lse_ref
  131.5 13.8 %widen.1 = (bf16[1024,1024]{1,0:T(8,128)(2,1)}, bf16[1024,1024]{1,0:T(8,128)(2,1)}, bf16[1024,2048]{1,0:T(8,128)(2,1)}, bf16[1024,2048]{1,0:T(8,128)(2,1)}) custom-call(s32[4]{0:T(128)S(1)} %pad_add_fusion.place_ref, bf16[1024,1024]{1,0:T(8,128)(2,1)S(1)} %bitcast.157, bf16[1024,1024]{1,0:T(8,128)(2,1)S(1)} %get-tuple-element.290.refs_1_, ...), custom_call_target="tpu_custom_call" | custom-call | flops 14300000256 | bytes 1000 | tf_op jit(solution)/shard_map/widen/pallas_call | solution.py:509
  145.3 1.8 collective-permute-done.23.side_ref.refs_13_
  148.2 1.4 halve.5
  151.7 6.6 %outer.3 = (bf16[4,128,1024]{2,1,0:T(8,128)(2,1)S(1)}, bf16[4,128,1024]{2,1,0:T(8,128)(2,1)S(1)}, bf16[4,2,64,1024]{3,2,1,0:T(8,128)(2,1)S(1)}, bf16[4,2,64,1024]{3,2,1,0:T(8,128)(2,1)S(1)}) custom-call(s32[4]{0:T(128)S(1)} %pad_add_fusion.place_ref, bf16[1024,2048]{1,0:T(8,128)(2,1)} %get-tuple-element.317.refs_0_, bf16[1024,1024]{1,0:T(8,128)(2,1)S(1)} %bitcast.161), custom_call_target="tpu_custom_call" | custom-call | flops 6600000000 | bytes 1000 | tf_op jit(solution)/shard_map/outer/pallas_call | solution.py:630
  161.3 21.7 %narrow.1 = (bf16[2,256,1024]{2,1,0:T(8,128)(2,1)}, bf16[2,256,1024]{2,1,0:T(8,128)(2,1)}, bf16[1024,2048]{1,0:T(8,128)(2,1)}, bf16[1024,1024]{1,0:T(8,128)(2,1)}) custom-call(s32[4]{0:T(128)S(1)} %pad_add_fusion.place_ref, bf16[1024,2048]{1,0:T(8,128)(2,1)} %get-tuple-element.317.refs_0_, bf16[1024,1024]{1,0:T(8,128)(2,1)} %bitcast.162, ...), custom_call_target="tpu_custom_call" | custom-call | flops 19800000512 | bytes 1000 | tf_op jit(solution)/shard_map/narrow/pallas_call | solution.py:509
  183.0 2.7 fold_one.3
  185.6 3.5 collective-permute-start.29
  190.7 7.6 %outer.4 = (bf16[4,64,2048]{2,1,0:T(8,128)(2,1)S(1)}, bf16[4,64,2048]{2,1,0:T(8,128)(2,1)S(1)}, bf16[4,2,32,2048]{3,2,1,0:T(8,128)(2,1)S(1)}, bf16[4,2,32,2048]{3,2,1,0:T(8,128)(2,1)S(1)}) custom-call(s32[4]{0:T(128)S(1)} %pad_add_fusion.place_ref, bf16[1024,1024]{1,0:T(8,128)(2,1)} %get-tuple-element.335.refs_0_, bf16[1024,2048]{1,0:T(8,128)(2,1)} %get-tuple-element.336.refs_1_), custom_call_target="tpu_custom_call" | custom-call | flops 6600000000 | bytes 1000 | tf_op jit(solution)/shard_map/outer/pallas_call | solution.py:630
  200.1 7.5 %between.1 = (bf16[1024,1024]{1,0:T(8,128)(2,1)}, bf16[1024,512]{1,0:T(8,128)(2,1)S(1)}, f32[8,1024]{1,0:T(8,128)S(1)}) custom-call(s32[4]{0:T(128)S(1)} %pad_add_fusion.place_ref, bf16[1024,1024]{1,0:T(8,128)(2,1)S(1)} %bitcast.163, bf16[1024,1024]{1,0:T(8,128)(2,1)} %get-tuple-element.344.refs_1_, bf16[1024,1024]{1,0:T(8,128)(2,1)} %collective-permute-done.29.refs_2_, ...), custom_call_target="tpu_custom_call" | custom-call | flops 8800000000 | bytes 1000 | tf_op jit(solution)/shard_map/between/pallas_call | solution.py:509
  208.6 3.1 collective-permute-start.36
  211.7 1.4 collective-permute-start.37
  213.5 18.1 %attend_back.1.refs_1_.refs_0_ = bf16[3,1024,512]{2,1,0:T(8,128)(2,1)S(1)} custom-call(bf16[1024,1536]{1,0:T(8,128)(2,1)} %get-tuple-element.279.q_ref.k_ref.v_ref, bf16[1024,1536]{1,0:T(8,128)(2,1)} %get-tuple-element.279.q_ref.k_ref.v_ref, bf16[1024,1536]{1,0:T(8,128)(2,1)} %get-tuple-element.279.q_ref.k_ref.v_ref, ...), custom_call_target="tpu_custom_call" | custom-call | flops 2200000000 | bytes 1000 | tf_op jit(solution)/shard_map/attend_back/pallas_call | solution.py:217
  231.6 3.7 %collective-permute-done.37 = bf16[2,64,1024]{2,1,0:T(8,128)(2,1)S(1)} collective-permute-done((bf16[2,64,1024]{2,1,0:T(8,128)(2,1)S(1)}, bf16[2,64,1024]{2,1,0:T(8,128)(2,1)S(1)}, u32[]{:S(2)}, u32[]{:S(2)}) %collective-permute-start.37) | collective-permute-done | bytes 262176 | tf_op jit(solution)/shard_map/ppermute | solution.py:251
  236.1 1.3 fold_one.4
  239.3 9.0 %outer.5 = (bf16[4,64,2176]{2,1,0:T(8,128)(2,1)S(1)}, bf16[4,64,2176]{2,1,0:T(8,128)(2,1)S(1)}, bf16[4,2,32,2176]{3,2,1,0:T(8,128)(2,1)S(1)}, bf16[4,2,32,2176]{3,2,1,0:T(8,128)(2,1)S(1)}) custom-call(s32[4]{0:T(128)S(1)} %pad_add_fusion.place_ref, bf16[1024,1024]{1,0:T(8,128)(2,1)S(1)} %copy-done.11, bf16[3,1024,512]{2,1,0:T(8,128)(2,1)S(1)} %attend_back.1.refs_1_.refs_0_, ...), custom_call_target="tpu_custom_call" | custom-call | flops 6600000000 | bytes 1000 | tf_op jit(solution)/shard_map/outer/pallas_call | solution.py:630
  248.5 5.7 %collective-permute-done.38.came_one = bf16[4,32,2048]{2,1,0:T(8,128)(2,1)S(1)} collective-permute-done((bf16[4,32,2048]{2,1,0:T(8,128)(2,1)S(1)}, bf16[4,32,2048]{2,1,0:T(8,128)(2,1)S(1)}, u32[]{:S(2)}, u32[]{:S(2)}) %collective-permute-start.38) | collective-permute-done | bytes 524320 | tf_op jit(solution)/shard_map/ppermute | solution.py:56
  256.5 1.5 collective-permute-start.45
  257.9 5.1 %enter.1 = bf16[1024,1024]{1,0:T(8,128)(2,1)S(1)} custom-call(s32[4]{0:T(128)S(1)} %pad_add_fusion.place_ref, bf16[3,1024,512]{2,1,0:T(8,128)(2,1)S(1)} %attend_back.1.refs_1_.refs_0_, bf16[1024,1536]{1,0:T(8,128)(2,1)S(1)} %copy-done.10), custom_call_target="tpu_custom_call" | custom-call | flops 15399999488 | bytes 1000 | tf_op jit(solution)/shard_map/enter/pallas_call | solution.py:509
  263.0 1.9 fusion.12
  264.9 12.4 %collective-permute-done.44 = bf16[2,32,2048]{2,1,0:T(8,128)(2,1)S(1)} collective-permute-done((bf16[2,32,2048]{2,1,0:T(8,128)(2,1)S(1)}, bf16[2,32,2048]{2,1,0:T(8,128)(2,1)S(1)}, u32[]{:S(2)}, u32[]{:S(2)}) %collective-permute-start.44) | collective-permute-done | bytes 262176 | tf_op jit(solution)/shard_map/ppermute | solution.py:251
  278.1 1.9 collective-permute-done.41.came_one
  280.7 1.4 fold_one.5
  282.5 2.9 collective-permute-start.50
  287.7 1.6 bitcast_convert_fusion
  292.2 8.0 %collective-permute-done.46.came_one = bf16[4,32,2176]{2,1,0:T(8,128)(2,1)S(1)} collective-permute-done((bf16[4,32,2176]{2,1,0:T(8,128)(2,1)S(1)}, bf16[4,32,2176]{2,1,0:T(8,128)(2,1)S(1)}, u32[]{:S(2)}, u32[]{:S(2)}) %collective-permute-start.46) | collective-permute-done | bytes 557088 | tf_op jit(solution)/shard_map/ppermute | solution.py:56
  300.2 2.8 collective-permute-start.55
  307.2 1.4 collective-permute-start.53
  308.6 2.7 finish_up.1
  311.3 2.7 collective-permute-done.51
  314.1 15.9 %collective-permute-done.52 = bf16[2,32,2176]{2,1,0:T(8,128)(2,1)S(1)} collective-permute-done((bf16[2,32,2176]{2,1,0:T(8,128)(2,1)S(1)}, bf16[2,32,2176]{2,1,0:T(8,128)(2,1)S(1)}, u32[]{:S(2)}, u32[]{:S(2)}) %collective-permute-start.52) | collective-permute-done | bytes 278560 | tf_op jit(solution)/shard_map/ppermute | solution.py:251
  330.0 1.3 collective-permute-done.53
  333.7 1.4 fusion.14
  336.2 1.6 maximum_bitcast_fusion
  337.7 2.6 collective-permute-done.57
  340.6 1.4 collective-permute-start.58
  342.0 1.6 collective-permute-done.58.refs_1_
  343.6 2.3 finish_qkv.1
  (234 shorter events, 50.6 us)
Async XLA Ops:
  0.6 38.2 %copy-start = (bf16[512,1024]{1,0:T(8,128)(2,1)S(1)}, bf16[512,1024]{1,0:T(8,128)(2,1)}, u32[]{:S(2)}) copy-start(bf16[512,1024]{1,0:T(8,128)(2,1)} %param.20) | copy-start | bytes 3145732
  0.7 304.6 %copy-start.5 = (s32[4]{0:T(128)}, s32[4]{0:T(128)S(1)}, u32[]{:S(2)}) copy-start(s32[4]{0:T(128)S(1)} %pad_add_fusion.place_ref) | copy-start | bytes 52
  3.5 31.4 %collective-permute-start.3 = (bf16[2,64,4224]{2,1,0:T(8,128)(2,1)S(1)}, bf16[2,64,4224]{2,1,0:T(8,128)(2,1)}, u32[]{:S(2)}, u32[]{:S(2)}) collective-permute-start(bf16[2,64,4224]{2,1,0:T(8,128)(2,1)S(1)} %get-tuple-element.234.refs_1_.refs_4_.refs_3_), channel_id=1, source_target_pairs={{0,1},{1,0},{2,3},{3,2},{4,5},{5,4},{6,7},{7,6},{8,9},{9,8},{10,11... | collective-permute-start | bytes 3244040 | tf_op jit(solution)/shard_map/ppermute | solution.py:56
  6.2 28.7 %collective-permute-start.4 = (bf16[2,256,1024]{2,1,0:T(8,128)(2,1)S(1)}, bf16[2,256,1024]{2,1,0:T(8,128)(2,1)S(1)}, u32[]{:S(2)}, u32[]{:S(2)}) collective-permute-start(bf16[2,256,1024]{2,1,0:T(8,128)(2,1)S(1)} %pad_maximum_fusion.3), channel_id=1, source_target_pairs={{0,16},{16,0},{1,17},{17,1},{2,18},{18,2},{3,19},{19,3},{4,20},{20... | collective-permute-start | bytes 3145736 | tf_op jit(solution)/shard_map/ppermute | solution.py:56
  7.5 7.0 %collective-permute-start = (bf16[64,2176]{1,0:T(8,128)(2,1)S(1)}, bf16[64,2176]{1,0:T(8,128)(2,1)S(1)}, u32[]{:S(2)}, u32[]{:S(2)}) collective-permute-start(bf16[64,2176]{1,0:T(8,128)(2,1)S(1)} %get-tuple-element.233), channel_id=1, source_target_pairs={{0,2},{2,4},{4,6},{6,0},{1,3},{3,5},{5,7},{7,1},{8,10},{10,12},{12... | collective-permute-start | bytes 835592 | tf_op jit(solution)/shard_map/ppermute | solution.py:251
  8.8 22.6 %collective-permute-start.1 = (bf16[64,2176]{1,0:T(8,128)(2,1)S(1)}, bf16[64,2176]{1,0:T(8,128)(2,1)S(1)}, u32[]{:S(2)}, u32[]{:S(2)}) collective-permute-start(bf16[64,2176]{1,0:T(8,128)(2,1)S(1)} %get-tuple-element.233), channel_id=1, source_target_pairs={{0,4},{2,6},{4,0},{6,2},{1,5},{3,7},{5,1},{7,3},{8,12},{10,14},{12... | collective-permute-start | bytes 835592 | tf_op jit(solution)/shard_map/ppermute | solution.py:251
  9.8 25.1 %collective-permute-start.2 = (bf16[64,2176]{1,0:T(8,128)(2,1)S(1)}, bf16[64,2176]{1,0:T(8,128)(2,1)S(1)}, u32[]{:S(2)}, u32[]{:S(2)}) collective-permute-start(bf16[64,2176]{1,0:T(8,128)(2,1)S(1)} %get-tuple-element.233), channel_id=1, source_target_pairs={{0,6},{2,0},{4,2},{6,4},{1,7},{3,1},{5,3},{7,5},{8,14},{10,8},{12,... | collective-permute-start | bytes 835592 | tf_op jit(solution)/shard_map/ppermute | solution.py:251
  36.9 24.0 %collective-permute-start.5 = (bf16[3,64,2176]{2,1,0:T(8,128)(2,1)}, bf16[3,64,2176]{2,1,0:T(8,128)(2,1)}, u32[]{:S(2)}, u32[]{:S(2)}) collective-permute-start(bf16[3,64,2176]{2,1,0:T(8,128)(2,1)} %pad_maximum_fusion.7.refs_3_), channel_id=1, source_target_pairs={{0,1},{1,0},{2,3},{3,2},{4,5},{5,4},{6,7},{7,6},{8,9},{9,8},{10,11... | collective-permute-start | bytes 2506760 | tf_op jit(solution)/shard_map/ppermute | solution.py:56
  37.2 23.7 %collective-permute-start.6 = (bf16[3,64,2176]{2,1,0:T(8,128)(2,1)}, bf16[3,64,2176]{2,1,0:T(8,128)(2,1)}, u32[]{:S(2)}, u32[]{:S(2)}) collective-permute-start(bf16[3,64,2176]{2,1,0:T(8,128)(2,1)} %pad_maximum_fusion.7.refs_3_), channel_id=1, source_target_pairs={{0,16},{16,0},{1,17},{17,1},{2,18},{18,2},{3,19},{19,3},{4,20},{20... | collective-permute-start | bytes 2506760 | tf_op jit(solution)/shard_map/ppermute | solution.py:56
  37.4 6.9 %collective-permute-start.7 = (bf16[64,2048]{1,0:T(8,128)(2,1)S(1)}, bf16[64,2048]{1,0:T(8,128)(2,1)S(1)}, u32[]{:S(2)}, u32[]{:S(2)}) collective-permute-start(bf16[64,2048]{1,0:T(8,128)(2,1)S(1)} %get-tuple-element.239), channel_id=1, source_target_pairs={{0,2},{2,4},{4,6},{6,0},{1,3},{3,5},{5,7},{7,1},{8,10},{10,12},{12... | collective-permute-start | bytes 786440 | tf_op jit(solution)/shard_map/ppermute | solution.py:251
  37.4 21.7 %collective-permute-start.8 = (bf16[64,2048]{1,0:T(8,128)(2,1)S(1)}, bf16[64,2048]{1,0:T(8,128)(2,1)S(1)}, u32[]{:S(2)}, u32[]{:S(2)}) collective-permute-start(bf16[64,2048]{1,0:T(8,128)(2,1)S(1)} %get-tuple-element.239), channel_id=1, source_target_pairs={{0,4},{2,6},{4,0},{6,2},{1,5},{3,7},{5,1},{7,3},{8,12},{10,14},{12... | collective-permute-start | bytes 786440 | tf_op jit(solution)/shard_map/ppermute | solution.py:251
  37.4 23.4 %collective-permute-start.9 = (bf16[64,2048]{1,0:T(8,128)(2,1)S(1)}, bf16[64,2048]{1,0:T(8,128)(2,1)}, u32[]{:S(2)}, u32[]{:S(2)}) collective-permute-start(bf16[64,2048]{1,0:T(8,128)(2,1)S(1)} %get-tuple-element.239), channel_id=1, source_target_pairs={{0,6},{2,0},{4,2},{6,4},{1,7},{3,1},{5,3},{7,5},{8,14},{10,8},{12,... | collective-permute-start | bytes 786440 | tf_op jit(solution)/shard_map/ppermute | solution.py:251
  38.9 27.9 %copy-start.20 = (bf16[2,128,1024]{2,1,0:T(8,128)(2,1)}, bf16[2,128,1024]{2,1,0:T(8,128)(2,1)S(1)}, u32[]{:S(2)}) copy-start(bf16[2,128,1024]{2,1,0:T(8,128)(2,1)S(1)} %dynamic-slice_bitcast_fusion.2.refs_10_) | copy-start | bytes 1572868
  63.5 4.4 %collective-permute-start.12 = (bf16[2,256,1024]{2,1,0:T(8,128)(2,1)}, bf16[2,256,1024]{2,1,0:T(8,128)(2,1)}, u32[]{:S(2)}, u32[]{:S(2)}) collective-permute-start(bf16[2,256,1024]{2,1,0:T(8,128)(2,1)} %pad_maximum_fusion.4), channel_id=1, source_target_pairs={{0,8},{8,0},{1,9},{9,1},{2,10},{10,2},{3,11},{11,3},{4,12},{12,4},... | collective-permute-start | bytes 3145736 | tf_op jit(solution)/shard_map/ppermute | solution.py:56
  64.4 11.3 %collective-permute-start.10 = (bf16[3,32,2176]{2,1,0:T(8,128)(2,1)S(1)}, bf16[3,32,2176]{2,1,0:T(8,128)(2,1)S(1)}, u32[]{:S(2)}, u32[]{:S(2)}) collective-permute-start(bf16[3,32,2176]{2,1,0:T(8,128)(2,1)S(1)} %get-tuple-element.249), channel_id=1, source_target_pairs={{0,16},{16,0},{1,17},{17,1},{2,18},{18,2},{3,19},{19,3},{4,20},{20... | collective-permute-start | bytes 1253384 | tf_op jit(solution)/shard_map/ppermute | solution.py:56
  65.7 11.0 %collective-permute-start.11 = (bf16[3,32,2176]{2,1,0:T(8,128)(2,1)S(1)}, bf16[3,32,2176]{2,1,0:T(8,128)(2,1)S(1)}, u32[]{:S(2)}, u32[]{:S(2)}) collective-permute-start(bf16[3,32,2176]{2,1,0:T(8,128)(2,1)S(1)} %get-tuple-element.250), channel_id=1, source_target_pairs={{0,1},{1,0},{2,3},{3,2},{4,5},{5,4},{6,7},{7,6},{8,9},{9,8},{10,11... | collective-permute-start | bytes 1253384 | tf_op jit(solution)/shard_map/ppermute | solution.py:56
  76.6 29.2 %collective-permute-start.13 = (bf16[3,64,2048]{2,1,0:T(8,128)(2,1)S(1)}, bf16[3,64,2048]{2,1,0:T(8,128)(2,1)S(1)}, u32[]{:S(2)}, u32[]{:S(2)}) collective-permute-start(bf16[3,64,2048]{2,1,0:T(8,128)(2,1)S(1)} %pad_maximum_fusion.8.refs_6_.refs_5_), channel_id=1, source_target_pairs={{0,1},{1,0},{2,3},{3,2},{4,5},{5,4},{6,7},{7,6},{8,9},{9,8},{10,11... | collective-permute-start | bytes 2359304 | tf_op jit(solution)/shard_map/ppermute | solution.py:56
  77.8 28.0 %collective-permute-start.14 = (bf16[3,64,2048]{2,1,0:T(8,128)(2,1)S(1)}, bf16[3,64,2048]{2,1,0:T(8,128)(2,1)S(1)}, u32[]{:S(2)}, u32[]{:S(2)}) collective-permute-start(bf16[3,64,2048]{2,1,0:T(8,128)(2,1)S(1)} %pad_maximum_fusion.8.refs_6_.refs_5_), channel_id=1, source_target_pairs={{0,16},{16,0},{1,17},{17,1},{2,18},{18,2},{3,19},{19,3},{4,20},{20... | collective-permute-start | bytes 2359304 | tf_op jit(solution)/shard_map/ppermute | solution.py:56
  78.2 19.4 %collective-permute-start.15 = (bf16[128,1024]{1,0:T(8,128)(2,1)S(1)}, bf16[128,1024]{1,0:T(8,128)(2,1)S(1)}, u32[]{:S(2)}, u32[]{:S(2)}) collective-permute-start(bf16[128,1024]{1,0:T(8,128)(2,1)S(1)} %dynamic-slice_bitcast_fusion.5), channel_id=1, source_target_pairs={{0,2},{2,4},{4,6},{6,0},{1,3},{3,5},{5,7},{7,1},{8,10},{10,12},{12... | collective-permute-start | bytes 786440 | tf_op jit(solution)/shard_map/ppermute | solution.py:251
  78.2 19.4 %collective-permute-start.16 = (bf16[128,1024]{1,0:T(8,128)(2,1)S(1)}, bf16[128,1024]{1,0:T(8,128)(2,1)S(1)}, u32[]{:S(2)}, u32[]{:S(2)}) collective-permute-start(bf16[128,1024]{1,0:T(8,128)(2,1)S(1)} %dynamic-slice_bitcast_fusion.5), channel_id=1, source_target_pairs={{0,6},{2,0},{4,2},{6,4},{1,7},{3,1},{5,3},{7,5},{8,14},{10,8},{12,... | collective-permute-start | bytes 786440 | tf_op jit(solution)/shard_map/ppermute | solution.py:251
  80.2 25.6 %collective-permute-start.17 = (bf16[2,128,1024]{2,1,0:T(8,128)(2,1)S(1)}, bf16[2,128,1024]{2,1,0:T(8,128)(2,1)S(1)}, u32[]{:S(2)}, u32[]{:S(2)}) collective-permute-start(bf16[2,128,1024]{2,1,0:T(8,128)(2,1)S(1)} %copy-done.21), channel_id=1, source_target_pairs={{0,1},{1,0},{2,3},{3,2},{4,5},{5,4},{6,7},{7,6},{8,9},{9,8},{10,11... | collective-permute-start | bytes 1572872 | tf_op jit(solution)/shard_map/ppermute | solution.py:56
  108.6 13.3 %collective-permute-start.20 = (bf16[2,256,1024]{2,1,0:T(8,128)(2,1)S(1)}, bf16[2,256,1024]{2,1,0:T(8,128)(2,1)S(1)}, u32[]{:S(2)}, u32[]{:S(2)}) collective-permute-start(bf16[2,256,1024]{2,1,0:T(8,128)(2,1)S(1)} %pad_maximum_fusion.5), channel_id=1, source_target_pairs={{0,8},{8,0},{1,9},{9,1},{2,10},{10,2},{3,11},{11,3},{4,12},{12,4},... | collective-permute-start | bytes 3145736 | tf_op jit(solution)/shard_map/ppermute | solution.py:56
  110.7 13.0 %collective-permute-start.18 = (bf16[3,32,2048]{2,1,0:T(8,128)(2,1)S(1)}, bf16[3,32,2048]{2,1,0:T(8,128)(2,1)S(1)}, u32[]{:S(2)}, u32[]{:S(2)}) collective-permute-start(bf16[3,32,2048]{2,1,0:T(8,128)(2,1)S(1)} %get-tuple-element.282), channel_id=1, source_target_pairs={{0,16},{16,0},{1,17},{17,1},{2,18},{18,2},{3,19},{19,3},{4,20},{20... | collective-permute-start | bytes 1179656 | tf_op jit(solution)/shard_map/ppermute | solution.py:56
  111.1 12.7 %collective-permute-start.19 = (bf16[3,32,2048]{2,1,0:T(8,128)(2,1)S(1)}, bf16[3,32,2048]{2,1,0:T(8,128)(2,1)S(1)}, u32[]{:S(2)}, u32[]{:S(2)}) collective-permute-start(bf16[3,32,2048]{2,1,0:T(8,128)(2,1)S(1)} %get-tuple-element.283), channel_id=1, source_target_pairs={{0,1},{1,0},{2,3},{3,2},{4,5},{5,4},{6,7},{7,6},{8,9},{9,8},{10,11... | collective-permute-start | bytes 1179656 | tf_op jit(solution)/shard_map/ppermute | solution.py:56
  112.3 11.5 %collective-permute-start.21 = (bf16[128,1024]{1,0:T(8,128)(2,1)S(1)}, bf16[128,1024]{1,0:T(8,128)(2,1)S(1)}, u32[]{:S(2)}, u32[]{:S(2)}) collective-permute-start(bf16[128,1024]{1,0:T(8,128)(2,1)S(1)} %dynamic-slice_bitcast_fusion.5), channel_id=1, source_target_pairs={{0,4},{2,6},{4,0},{6,2},{1,5},{3,7},{5,1},{7,3},{8,12},{10,14},{12... | collective-permute-start | bytes 786440 | tf_op jit(solution)/shard_map/ppermute | solution.py:251
  122.3 29.4 %copy-start.2 = (bf16[2,2,256,1024]{3,2,1,0:T(8,128)(2,1)}, bf16[2,2,256,1024]{3,2,1,0:T(8,128)(2,1)S(1)}, u32[]{:S(2)}) copy-start(bf16[2,2,256,1024]{3,2,1,0:T(8,128)(2,1)S(1)} %pad_maximum_fusion.1) | copy-start | bytes 6291460
  127.1 4.4 %collective-permute-start.22 = (bf16[1024,1024]{1,0:T(8,128)(2,1)S(1)}, bf16[1024,1024]{1,0:T(8,128)(2,1)S(1)}, u32[]{:S(2)}, u32[]{:S(2)}) collective-permute-start(bf16[1024,1024]{1,0:T(8,128)(2,1)S(1)} %get-tuple-element.290.refs_1_), channel_id=1, source_target_pairs={{0,8},{8,0},{1,9},{9,1},{2,10},{10,2},{3,11},{11,3},{4,12},{12,4},... | collective-permute-start | bytes 6291464 | tf_op jit(solution)/shard_map/ppermute | solution.py:56
  127.8 19.2 %collective-permute-start.23 = (bf16[3,128,1024]{2,1,0:T(8,128)(2,1)S(1)}, bf16[3,128,1024]{2,1,0:T(8,128)(2,1)S(1)}, u32[]{:S(2)}, u32[]{:S(2)}) collective-permute-start(bf16[3,128,1024]{2,1,0:T(8,128)(2,1)S(1)} %pad_maximum_fusion.9.refs_12_), channel_id=1, source_target_pairs={{0,1},{1,0},{2,3},{3,2},{4,5},{5,4},{6,7},{7,6},{8,9},{9,8},{10,11... | collective-permute-start | bytes 2359304 | tf_op jit(solution)/shard_map/ppermute | solution.py:56
  128.2 18.9 %collective-permute-start.24 = (bf16[3,128,1024]{2,1,0:T(8,128)(2,1)S(1)}, bf16[3,128,1024]{2,1,0:T(8,128)(2,1)S(1)}, u32[]{:S(2)}, u32[]{:S(2)}) collective-permute-start(bf16[3,128,1024]{2,1,0:T(8,128)(2,1)S(1)} %pad_maximum_fusion.9.refs_12_), channel_id=1, source_target_pairs={{0,16},{16,0},{1,17},{17,1},{2,18},{18,2},{3,19},{19,3},{4,20},{20... | collective-permute-start | bytes 2359304 | tf_op jit(solution)/shard_map/ppermute | solution.py:56
  149.6 9.9 %collective-permute-start.25 = (bf16[3,64,1024]{2,1,0:T(8,128)(2,1)S(1)}, bf16[3,64,1024]{2,1,0:T(8,128)(2,1)S(1)}, u32[]{:S(2)}, u32[]{:S(2)}) collective-permute-start(bf16[3,64,1024]{2,1,0:T(8,128)(2,1)S(1)} %get-tuple-element.315), channel_id=1, source_target_pairs={{0,16},{16,0},{1,17},{17,1},{2,18},{18,2},{3,19},{19,3},{4,20},{20... | collective-permute-start | bytes 1179656 | tf_op jit(solution)/shard_map/ppermute | solution.py:56
  150.8 9.5 %collective-permute-start.26 = (bf16[3,64,1024]{2,1,0:T(8,128)(2,1)S(1)}, bf16[3,64,1024]{2,1,0:T(8,128)(2,1)S(1)}, u32[]{:S(2)}, u32[]{:S(2)}) collective-permute-start(bf16[3,64,1024]{2,1,0:T(8,128)(2,1)S(1)} %get-tuple-element.316), channel_id=1, source_target_pairs={{0,1},{1,0},{2,3},{3,2},{4,5},{5,4},{6,7},{7,6},{8,9},{9,8},{10,11... | collective-permute-start | bytes 1179656 | tf_op jit(solution)/shard_map/ppermute | solution.py:56
  160.3 22.7 %collective-permute-start.27 = (bf16[4,128,1024]{2,1,0:T(8,128)(2,1)S(1)}, bf16[4,128,1024]{2,1,0:T(8,128)(2,1)S(1)}, u32[]{:S(2)}, u32[]{:S(2)}) collective-permute-start(bf16[4,128,1024]{2,1,0:T(8,128)(2,1)S(1)} %get-tuple-element.329), channel_id=1, source_target_pairs={{0,1},{1,0},{2,3},{3,2},{4,5},{5,4},{6,7},{7,6},{8,9},{9,8},{10,11... | collective-permute-start | bytes 3145736 | tf_op jit(solution)/shard_map/ppermute | solution.py:56
  160.9 22.1 %collective-permute-start.28 = (bf16[4,2,64,1024]{3,2,1,0:T(8,128)(2,1)S(1)}, bf16[4,2,64,1024]{3,2,1,0:T(8,128)(2,1)S(1)}, u32[]{:S(2)}, u32[]{:S(2)}) collective-permute-start(bf16[4,2,64,1024]{3,2,1,0:T(8,128)(2,1)S(1)} %get-tuple-element.330), channel_id=1, source_target_pairs={{0,16},{16,0},{1,17},{17,1},{2,18},{18,2},{3,19},{19,3},{4,20},{20... | collective-permute-start | bytes 3145736 | tf_op jit(solution)/shard_map/ppermute | solution.py:56
  185.6 12.7 %collective-permute-start.29 = (bf16[1024,1024]{1,0:T(8,128)(2,1)}, bf16[1024,1024]{1,0:T(8,128)(2,1)}, u32[]{:S(2)}, u32[]{:S(2)}) collective-permute-start(bf16[1024,1024]{1,0:T(8,128)(2,1)} %get-tuple-element.344.refs_1_), channel_id=1, source_target_pairs={{0,8},{8,0},{1,9},{9,1},{2,10},{10,2},{3,11},{11,3},{4,12},{12,4},... | collective-permute-start | bytes 6291464 | tf_op jit(solution)/shard_map/ppermute | solution.py:56
  189.1 9.2 %collective-permute-start.30 = (bf16[2,256,1024]{2,1,0:T(8,128)(2,1)}, bf16[2,256,1024]{2,1,0:T(8,128)(2,1)}, u32[]{:S(2)}, u32[]{:S(2)}) collective-permute-start(bf16[2,256,1024]{2,1,0:T(8,128)(2,1)} %get-tuple-element.341), channel_id=1, source_target_pairs={{0,8},{8,0},{1,9},{9,1},{2,10},{10,2},{3,11},{11,3},{4,12},{12,4},... | collective-permute-start | bytes 3145736 | tf_op jit(solution)/shard_map/ppermute | solution.py:56
  189.3 18.3 %collective-permute-start.31 = (bf16[4,64,1024]{2,1,0:T(8,128)(2,1)}, bf16[4,64,1024]{2,1,0:T(8,128)(2,1)S(1)}, u32[]{:S(2)}, u32[]{:S(2)}) collective-permute-start(bf16[4,64,1024]{2,1,0:T(8,128)(2,1)} %get-tuple-element.348), channel_id=1, source_target_pairs={{0,16},{16,0},{1,17},{17,1},{2,18},{18,2},{3,19},{19,3},{4,20},{20... | collective-permute-start | bytes 1572872 | tf_op jit(solution)/shard_map/ppermute | solution.py:56
  189.9 17.7 %collective-permute-start.32 = (bf16[4,64,1024]{2,1,0:T(8,128)(2,1)}, bf16[4,64,1024]{2,1,0:T(8,128)(2,1)S(1)}, u32[]{:S(2)}, u32[]{:S(2)}) collective-permute-start(bf16[4,64,1024]{2,1,0:T(8,128)(2,1)} %get-tuple-element.349), channel_id=1, source_target_pairs={{0,1},{1,0},{2,3},{3,2},{4,5},{5,4},{6,7},{7,6},{8,9},{9,8},{10,11... | collective-permute-start | bytes 1572872 | tf_op jit(solution)/shard_map/ppermute | solution.py:56
  198.3 37.0 %collective-permute-start.33 = (bf16[4,64,2048]{2,1,0:T(8,128)(2,1)S(1)}, bf16[4,64,2048]{2,1,0:T(8,128)(2,1)S(1)}, u32[]{:S(2)}, u32[]{:S(2)}) collective-permute-start(bf16[4,64,2048]{2,1,0:T(8,128)(2,1)S(1)} %get-tuple-element.361), channel_id=1, source_target_pairs={{0,1},{1,0},{2,3},{3,2},{4,5},{5,4},{6,7},{7,6},{8,9},{9,8},{10,11... | collective-permute-start | bytes 3145736 | tf_op jit(solution)/shard_map/ppermute | solution.py:56
  199.1 36.2 %collective-permute-start.34 = (bf16[4,2,32,2048]{3,2,1,0:T(8,128)(2,1)S(1)}, bf16[4,2,32,2048]{3,2,1,0:T(8,128)(2,1)S(1)}, u32[]{:S(2)}, u32[]{:S(2)}) collective-permute-start(bf16[4,2,32,2048]{3,2,1,0:T(8,128)(2,1)S(1)} %get-tuple-element.362), channel_id=1, source_target_pairs={{0,16},{16,0},{1,17},{17,1},{2,18},{18,2},{3,19},{19,3},{4,20},{20... | collective-permute-start | bytes 3145736 | tf_op jit(solution)/shard_map/ppermute | solution.py:56
  208.6 23.0 %collective-permute-start.35 = (bf16[2,64,1024]{2,1,0:T(8,128)(2,1)S(1)}, bf16[2,64,1024]{2,1,0:T(8,128)(2,1)S(1)}, u32[]{:S(2)}, u32[]{:S(2)}) collective-permute-start(bf16[2,64,1024]{2,1,0:T(8,128)(2,1)S(1)} %get-tuple-element.364), channel_id=1, source_target_pairs={{0,2},{2,4},{4,6},{6,0},{1,3},{3,5},{5,7},{7,1},{8,10},{10,12},{12... | collective-permute-start | bytes 786440 | tf_op jit(solution)/shard_map/ppermute | solution.py:251
  208.6 23.0 %collective-permute-start.36 = (bf16[2,64,1024]{2,1,0:T(8,128)(2,1)S(1)}, bf16[2,64,1024]{2,1,0:T(8,128)(2,1)S(1)}, u32[]{:S(2)}, u32[]{:S(2)}) collective-permute-start(bf16[2,64,1024]{2,1,0:T(8,128)(2,1)S(1)} %get-tuple-element.365), channel_id=1, source_target_pairs={{0,4},{2,6},{4,0},{6,2},{1,5},{3,7},{5,1},{7,3},{8,12},{10,14},{12... | collective-permute-start | bytes 786440 | tf_op jit(solution)/shard_map/ppermute | solution.py:251
  211.7 23.6 %collective-permute-start.37 = (bf16[2,64,1024]{2,1,0:T(8,128)(2,1)S(1)}, bf16[2,64,1024]{2,1,0:T(8,128)(2,1)S(1)}, u32[]{:S(2)}, u32[]{:S(2)}) collective-permute-start(bf16[2,64,1024]{2,1,0:T(8,128)(2,1)S(1)} %get-tuple-element.366), channel_id=1, source_target_pairs={{0,6},{2,0},{4,2},{6,4},{1,7},{3,1},{5,3},{7,5},{8,14},{10,8},{12,... | collective-permute-start | bytes 786440 | tf_op jit(solution)/shard_map/ppermute | solution.py:251
  235.5 12.8 %collective-permute-start.40 = (bf16[2,64,1024]{2,1,0:T(8,128)(2,1)S(1)}, bf16[2,64,1024]{2,1,0:T(8,128)(2,1)S(1)}, u32[]{:S(2)}, u32[]{:S(2)}) collective-permute-start(bf16[2,64,1024]{2,1,0:T(8,128)(2,1)S(1)} %add_convert_fusion.2), channel_id=1, source_target_pairs={{0,16},{16,0},{1,17},{17,1},{2,18},{18,2},{3,19},{19,3},{4,20},{20... | collective-permute-start | bytes 786440 | tf_op jit(solution)/shard_map/ppermute | solution.py:56
  237.4 16.8 %collective-permute-start.38 = (bf16[4,32,2048]{2,1,0:T(8,128)(2,1)S(1)}, bf16[4,32,2048]{2,1,0:T(8,128)(2,1)S(1)}, u32[]{:S(2)}, u32[]{:S(2)}) collective-permute-start(bf16[4,32,2048]{2,1,0:T(8,128)(2,1)S(1)} %get-tuple-element.374), channel_id=1, source_target_pairs={{0,16},{16,0},{1,17},{17,1},{2,18},{18,2},{3,19},{19,3},{4,20},{20... | collective-permute-start | bytes 1572872 | tf_op jit(solution)/shard_map/ppermute | solution.py:56
  238.4 15.8 %collective-permute-start.39 = (bf16[4,32,2048]{2,1,0:T(8,128)(2,1)S(1)}, bf16[4,32,2048]{2,1,0:T(8,128)(2,1)S(1)}, u32[]{:S(2)}, u32[]{:S(2)}) collective-permute-start(bf16[4,32,2048]{2,1,0:T(8,128)(2,1)S(1)} %get-tuple-element.375), channel_id=1, source_target_pairs={{0,1},{1,0},{2,3},{3,2},{4,5},{5,4},{6,7},{7,6},{8,9},{9,8},{10,11... | collective-permute-start | bytes 1572872 | tf_op jit(solution)/shard_map/ppermute | solution.py:56
  255.2 24.8 %collective-permute-start.41 = (bf16[4,64,2176]{2,1,0:T(8,128)(2,1)S(1)}, bf16[4,64,2176]{2,1,0:T(8,128)(2,1)S(1)}, u32[]{:S(2)}, u32[]{:S(2)}) collective-permute-start(bf16[4,64,2176]{2,1,0:T(8,128)(2,1)S(1)} %get-tuple-element.404), channel_id=1, source_target_pairs={{0,1},{1,0},{2,3},{3,2},{4,5},{5,4},{6,7},{7,6},{8,9},{9,8},{10,11... | collective-permute-start | bytes 3342344 | tf_op jit(solution)/shard_map/ppermute | solution.py:56
  256.1 24.4 %collective-permute-start.42 = (bf16[4,2,32,2176]{3,2,1,0:T(8,128)(2,1)S(1)}, bf16[4,2,32,2176]{3,2,1,0:T(8,128)(2,1)S(1)}, u32[]{:S(2)}, u32[]{:S(2)}) collective-permute-start(bf16[4,2,32,2176]{3,2,1,0:T(8,128)(2,1)S(1)} %get-tuple-element.405), channel_id=1, source_target_pairs={{0,16},{16,0},{1,17},{17,1},{2,18},{18,2},{3,19},{19,3},{4,20},{20... | collective-permute-start | bytes 3342344 | tf_op jit(solution)/shard_map/ppermute | solution.py:56
  256.5 8.4 %collective-permute-start.43 = (bf16[2,32,2048]{2,1,0:T(8,128)(2,1)S(1)}, bf16[2,32,2048]{2,1,0:T(8,128)(2,1)S(1)}, u32[]{:S(2)}, u32[]{:S(2)}) collective-permute-start(bf16[2,32,2048]{2,1,0:T(8,128)(2,1)S(1)} %get-tuple-element.408), channel_id=1, source_target_pairs={{0,2},{2,4},{4,6},{6,0},{1,3},{3,5},{5,7},{7,1},{8,10},{10,12},{12... | collective-permute-start | bytes 786440 | tf_op jit(solution)/shard_map/ppermute | solution.py:251
  256.5 20.8 %collective-permute-start.44 = (bf16[2,32,2048]{2,1,0:T(8,128)(2,1)S(1)}, bf16[2,32,2048]{2,1,0:T(8,128)(2,1)S(1)}, u32[]{:S(2)}, u32[]{:S(2)}) collective-permute-start(bf16[2,32,2048]{2,1,0:T(8,128)(2,1)S(1)} %get-tuple-element.409), channel_id=1, source_target_pairs={{0,4},{2,6},{4,0},{6,2},{1,5},{3,7},{5,1},{7,3},{8,12},{10,14},{12... | collective-permute-start | bytes 786440 | tf_op jit(solution)/shard_map/ppermute | solution.py:251
  256.5 21.6 %collective-permute-start.45 = (bf16[2,32,2048]{2,1,0:T(8,128)(2,1)S(1)}, bf16[2,32,2048]{2,1,0:T(8,128)(2,1)S(1)}, u32[]{:S(2)}, u32[]{:S(2)}) collective-permute-start(bf16[2,32,2048]{2,1,0:T(8,128)(2,1)S(1)} %get-tuple-element.410), channel_id=1, source_target_pairs={{0,6},{2,0},{4,2},{6,4},{1,7},{3,1},{5,3},{7,5},{8,14},{10,8},{12,... | collective-permute-start | bytes 786440 | tf_op jit(solution)/shard_map/ppermute | solution.py:251
  264.9 38.1 %copy-start.18 = (bf16[2,256,1024]{2,1,0:T(8,128)(2,1)}, bf16[2,256,1024]{2,1,0:T(8,128)(2,1)S(1)}, u32[]{:S(2)}) copy-start(bf16[2,256,1024]{2,1,0:T(8,128)(2,1)S(1)} %fusion.12) | copy-start | bytes 3145732
  282.1 5.3 %collective-permute-start.49 = (bf16[2,32,2048]{2,1,0:T(8,128)(2,1)S(1)}, bf16[2,32,2048]{2,1,0:T(8,128)(2,1)S(1)}, u32[]{:S(2)}, u32[]{:S(2)}) collective-permute-start(bf16[2,32,2048]{2,1,0:T(8,128)(2,1)S(1)} %add_convert_fusion.1), channel_id=1, source_target_pairs={{0,16},{16,0},{1,17},{17,1},{2,18},{18,2},{3,19},{19,3},{4,20},{20... | collective-permute-start | bytes 786440 | tf_op jit(solution)/shard_map/ppermute | solution.py:56
  282.5 5.0 %collective-permute-start.50 = (bf16[256,1024]{1,0:T(8,128)(2,1)S(1)}, bf16[256,1024]{1,0:T(8,128)(2,1)S(1)}, u32[]{:S(2)}, u32[]{:S(2)}) collective-permute-start(bf16[256,1024]{1,0:T(8,128)(2,1)S(1)} %bitcast.167), channel_id=1, source_target_pairs={{0,8},{8,0},{1,9},{9,1},{2,10},{10,2},{3,11},{11,3},{4,12},{12,4},... | collective-permute-start | bytes 1572872 | tf_op jit(solution)/shard_map/ppermute | solution.py:56
  285.5 3.9 %collective-permute-start.48 = (bf16[2,256,1024]{2,1,0:T(8,128)(2,1)S(1)}, bf16[2,256,1024]{2,1,0:T(8,128)(2,1)S(1)}, u32[]{:S(2)}, u32[]{:S(2)}) collective-permute-start(bf16[2,256,1024]{2,1,0:T(8,128)(2,1)S(1)} %dynamic-slice_bitcast_fusion), channel_id=1, source_target_pairs={{0,8},{8,0},{1,9},{9,1},{2,10},{10,2},{3,11},{11,3},{4,12},{12,4},... | collective-permute-start | bytes 3145736 | tf_op jit(solution)/shard_map/ppermute | solution.py:56
  285.6 14.6 %collective-permute-start.46 = (bf16[4,32,2176]{2,1,0:T(8,128)(2,1)S(1)}, bf16[4,32,2176]{2,1,0:T(8,128)(2,1)S(1)}, u32[]{:S(2)}, u32[]{:S(2)}) collective-permute-start(bf16[4,32,2176]{2,1,0:T(8,128)(2,1)S(1)} %get-tuple-element.426), channel_id=1, source_target_pairs={{0,16},{16,0},{1,17},{17,1},{2,18},{18,2},{3,19},{19,3},{4,20},{20... | collective-permute-start | bytes 1671176 | tf_op jit(solution)/shard_map/ppermute | solution.py:56
  286.7 13.5 %collective-permute-start.47 = (bf16[4,32,2176]{2,1,0:T(8,128)(2,1)S(1)}, bf16[4,32,2176]{2,1,0:T(8,128)(2,1)S(1)}, u32[]{:S(2)}, u32[]{:S(2)}) collective-permute-start(bf16[4,32,2176]{2,1,0:T(8,128)(2,1)S(1)} %get-tuple-element.427), channel_id=1, source_target_pairs={{0,1},{1,0},{2,3},{3,2},{4,5},{5,4},{6,7},{7,6},{8,9},{9,8},{10,11... | collective-permute-start | bytes 1671176 | tf_op jit(solution)/shard_map/ppermute | solution.py:56
  300.2 6.2 %collective-permute-start.55 = (bf16[128,2048]{1,0:T(8,128)(2,1)S(1)}, bf16[128,2048]{1,0:T(8,128)(2,1)S(1)}, u32[]{:S(2)}, u32[]{:S(2)}) collective-permute-start(bf16[128,2048]{1,0:T(8,128)(2,1)S(1)} %bitcast.170), channel_id=1, source_target_pairs={{0,8},{8,0},{1,9},{9,1},{2,10},{10,2},{3,11},{11,3},{4,12},{12,4},... | collective-permute-start | bytes 1572872 | tf_op jit(solution)/shard_map/ppermute | solution.py:56
  303.8 27.5 %collective-permute-start.56 = (bf16[256,1024]{1,0:T(8,128)(2,1)}, bf16[256,1024]{1,0:T(8,128)(2,1)}, u32[]{:S(2)}, u32[]{:S(2)}) collective-permute-start(bf16[256,1024]{1,0:T(8,128)(2,1)} %dynamic-slice_bitcast_fusion.1), channel_id=1, source_target_pairs={{0,16},{16,0},{1,17},{17,1},{2,18},{18,2},{3,19},{19,3},{4,20},{20... | collective-permute-start | bytes 1572872 | tf_op jit(solution)/shard_map/ppermute | solution.py:56
  304.2 27.1 %collective-permute-start.54 = (bf16[256,1024]{1,0:T(8,128)(2,1)}, bf16[256,1024]{1,0:T(8,128)(2,1)}, u32[]{:S(2)}, u32[]{:S(2)}) collective-permute-start(bf16[256,1024]{1,0:T(8,128)(2,1)} %fusion.16), channel_id=1, source_target_pairs={{0,16},{16,0},{1,17},{17,1},{2,18},{18,2},{3,19},{19,3},{4,20},{20... | collective-permute-start | bytes 1572872 | tf_op jit(solution)/shard_map/ppermute | solution.py:56
  306.3 7.8 %collective-permute-start.51 = (bf16[2,32,2176]{2,1,0:T(8,128)(2,1)S(1)}, bf16[2,32,2176]{2,1,0:T(8,128)(2,1)S(1)}, u32[]{:S(2)}, u32[]{:S(2)}) collective-permute-start(bf16[2,32,2176]{2,1,0:T(8,128)(2,1)S(1)} %get-tuple-element.435), channel_id=1, source_target_pairs={{0,2},{2,4},{4,6},{6,0},{1,3},{3,5},{5,7},{7,1},{8,10},{10,12},{12... | collective-permute-start | bytes 835592 | tf_op jit(solution)/shard_map/ppermute | solution.py:251
  306.3 23.6 %collective-permute-start.52 = (bf16[2,32,2176]{2,1,0:T(8,128)(2,1)S(1)}, bf16[2,32,2176]{2,1,0:T(8,128)(2,1)S(1)}, u32[]{:S(2)}, u32[]{:S(2)}) collective-permute-start(bf16[2,32,2176]{2,1,0:T(8,128)(2,1)S(1)} %get-tuple-element.436), channel_id=1, source_target_pairs={{0,4},{2,6},{4,0},{6,2},{1,5},{3,7},{5,1},{7,3},{8,12},{10,14},{12... | collective-permute-start | bytes 835592 | tf_op jit(solution)/shard_map/ppermute | solution.py:251
  307.2 24.1 %collective-permute-start.53 = (bf16[2,32,2176]{2,1,0:T(8,128)(2,1)S(1)}, bf16[2,32,2176]{2,1,0:T(8,128)(2,1)S(1)}, u32[]{:S(2)}, u32[]{:S(2)}) collective-permute-start(bf16[2,32,2176]{2,1,0:T(8,128)(2,1)S(1)} %get-tuple-element.437), channel_id=1, source_target_pairs={{0,6},{2,0},{4,2},{6,4},{1,7},{3,1},{5,3},{7,5},{8,14},{10,8},{12,... | collective-permute-start | bytes 835592 | tf_op jit(solution)/shard_map/ppermute | solution.py:251
  332.6 7.8 %collective-permute-start.57 = (bf16[2,32,2176]{2,1,0:T(8,128)(2,1)S(1)}, bf16[2,32,2176]{2,1,0:T(8,128)(2,1)S(1)}, u32[]{:S(2)}, u32[]{:S(2)}) collective-permute-start(bf16[2,32,2176]{2,1,0:T(8,128)(2,1)S(1)} %add_convert_fusion), channel_id=1, source_target_pairs={{0,16},{16,0},{1,17},{17,1},{2,18},{18,2},{3,19},{19,3},{4,20},{20... | collective-permute-start | bytes 835592 | tf_op jit(solution)/shard_map/ppermute | solution.py:56
  340.6 3.0 collective-permute-start.58
  (46 other events, 368.1 us)
